TPU v7x, 32 devices: a whole 2x2x4 slice. The times are simulated.
32 devices in a mesh: layer: 4 (over z), row: 2 (over y), col: 4 (over x, core).
Axes of the slice: x: 2, y: 2, z: 4, core: 2. Of those that a mesh axis runs over, the one named last changes fastest.
Arguments:
- sources: bfloat16 [4, 64, 4, 16, 128], P('layer', None, 'row', 'col'), may hold values from -3 to 3
- adjoint_sources: bfloat16 [4, 64, 4, 16, 128], P('layer', None, 'row', 'col'), may hold values from -3 to 3
- blocks: bfloat16 [4, 4, 16, 9, 128, 128], P('layer', 'row', 'col'), may hold values from -0.2 to 1.4
- pattern: int32 [4, 4, 16, 9], P('layer', 'row', 'col'), may hold values 0 or 1
- coupling: float32 [4], replicated, may hold values from 0.7 to 0.9
- layer_group: int32 [4], replicated, may hold values from 0 to 3
- port_cells: int32 [64], replicated, may hold values from 0 to 8191
Outputs:
- forward_field: bfloat16 [4, 64, 4, 16, 128], P('layer', None, 'row', 'col')
- adjoint_field: bfloat16 [4, 64, 4, 16, 128], P('layer', None, 'row', 'col')
- gradient: float32 [4, 4, 16, 128], P(None, 'row', 'col')
All inputs are finite; a program needn't handle non-finite values. No bound on the sum of `pattern` on one device may be relied on, other than what follows from the above.
Results may differ from a plain program's by a relative error of at most 0.01.
Values may be sent and summed in bfloat16 or wider, within the bound.
No kernel may reach another device: no remote copies, remote signals or barrier semaphores. Data moves between devices by JAX's collectives and lax.ppermute only.
A program may use at most 64 MiB of HBM per device.

v0:
```python
import jax
import jax.numpy as jnp
from jax import lax
from jax.sharding import PartitionSpec as P

port_strength = 4.0
intersection_scale = 0.125


def extended(array, sides, width):
    for axis, dim in sides:
        peers, length = (lax.axis_size(axis), array.shape[dim])
        up = [(i, (i + 1) % peers) for i in range(peers - 1)]
        down = [(j, i) for i, j in up]
        last = lax.slice_in_dim(array, length - width, length, axis=dim)
        initial = lax.slice_in_dim(array, 0, width, axis=dim)
        before = lax.ppermute(last, axis, up)
        after = lax.ppermute(initial, axis, down)
        array = jnp.concatenate([before, array, after], axis=dim)
    return array


def shifted(block, axis, distance):
    devices = range(lax.axis_size(axis))
    route = [(i - distance, i) for i in devices if i - distance in devices]
    return lax.ppermute(block, axis, route)


def local(sources, adjoint_sources, blocks, pattern, coupling, layer_group, port_cells):
    port_count = sources.shape[1]
    tiles_x = sources.shape[2]
    tiles_y = sources.shape[3]
    tile_cells = sources.shape[4]
    groups = coupling.shape[0]
    layer_count = lax.axis_size("layer")
    layer_pos = lax.axis_index("layer")
    row_pos = lax.axis_index("row")
    col_pos = lax.axis_index("col")
    member = (layer_group[:, None] == jnp.arange(groups, dtype=jnp.int32)[None, :]).astype(
        jnp.float32
    )
    kappa = jnp.dot(member, coupling, precision=lax.Precision.HIGHEST)
    kappa_own = lax.dynamic_index_in_dim(kappa, layer_pos, 0, keepdims=False)
    kappa_next = lax.dynamic_index_in_dim(
        kappa, jnp.minimum(layer_pos + 1, layer_count - 1), 0, keepdims=False
    )
    tiles_y_total = tiles_y * lax.axis_size("col")
    tile_xpos = row_pos * tiles_x + jnp.arange(tiles_x, dtype=jnp.int32)
    tile_ypos = col_pos * tiles_y + jnp.arange(tiles_y, dtype=jnp.int32)
    tile_ids = tile_xpos[:, None] * tiles_y_total + tile_ypos[None, :]
    cell_ids = (
        tile_ids[:, :, None] * tile_cells + jnp.arange(tile_cells, dtype=jnp.int32)[None, None, :]
    )
    port_map = (cell_ids[None] == port_cells[:, None, None, None]).astype(
        jnp.float32
    ) * port_strength
    first_flag = jnp.where(layer_pos == 0, 1.0, 0.0).astype(jnp.float32)
    last_flag = jnp.where(layer_pos == layer_count - 1, 1.0, 0.0).astype(jnp.float32)
    forward_rhs = sources[0].astype(jnp.float32) + first_flag * port_map
    adjoint_rhs = adjoint_sources[0].astype(jnp.float32) + last_flag * port_map
    front_blocks = blocks[0]
    front_mask = pattern[0].astype(jnp.float32)

    def apply_front(stacked):
        padded = extended(stacked, (("row", 1), ("col", 2)), 1)
        summed = jnp.zeros(stacked.shape, jnp.float32)
        for offset in range(9):
            step_x = offset // 3 - 1
            step_y = offset % 3 - 1
            beside = padded[
                :, 1 + step_x : 1 + step_x + tiles_x, 1 + step_y : 1 + step_y + tiles_y, :
            ]
            product_term = jnp.einsum(
                "pijc,ijcd->pijd",
                beside,
                front_blocks[:, :, offset],
                preferred_element_type=jnp.float32,
            )
            summed = summed + front_mask[None, :, :, offset, None] * product_term
        return summed

    def advance(forward_prev, adjoint_prev, forward_part, adjoint_part):
        forward_in = shifted(forward_prev, "layer", 1)
        adjoint_in = shifted(adjoint_prev, "layer", -1)
        forward_wave = (forward_part + kappa_own * forward_in.astype(jnp.float32)).astype(
            jnp.bfloat16
        )
        adjoint_wave = (adjoint_part + kappa_next * adjoint_in.astype(jnp.float32)).astype(
            jnp.bfloat16
        )
        rows_forward = forward_wave.shape[0]
        result = apply_front(jnp.concatenate([forward_wave, adjoint_wave], 0)).astype(jnp.bfloat16)
        return (result[:rows_forward], result[rows_forward:])

    adjoint_layer = layer_count - 1 - layer_pos
    empty = jnp.zeros((port_count, tiles_x, tiles_y, tile_cells), jnp.bfloat16)

    def section_step(step_index, state_pair):
        forward_now, adjoint_now = state_pair
        forward_new, adjoint_new = advance(forward_now, adjoint_now, forward_rhs, adjoint_rhs)
        forward_now = jnp.where(step_index == layer_pos, forward_new, forward_now)
        adjoint_now = jnp.where(step_index == adjoint_layer, adjoint_new, adjoint_now)
        return (forward_now, adjoint_now)

    forward_field, adjoint_field = lax.fori_loop(0, layer_count, section_step, (empty, empty))
    intersection = (
        jnp.sum(forward_field.astype(jnp.float32) * adjoint_field.astype(jnp.float32), axis=0)
        * intersection_scale
    )
    own_group = lax.dynamic_index_in_dim(layer_group, layer_pos, 0, keepdims=False)
    selector = (jnp.arange(groups, dtype=jnp.int32) == own_group).astype(jnp.float32)
    contribution = selector[:, None, None, None] * intersection[None]
    gradient = lax.psum(contribution, "layer")
    return (forward_field[None], adjoint_field[None], gradient)


def solution(mesh):
    placed = (
        P("layer", None, "row", "col", None),
        P("layer", None, "row", "col", None),
        P("layer", "row", "col", None, None, None),
        P("layer", "row", "col", None),
        P(),
        P(),
        P(),
    )
    return jax.shard_map(
        local,
        mesh=mesh,
        in_specs=placed,
        out_specs=(
            P("layer", None, "row", "col", None),
            P("layer", None, "row", "col", None),
            P(None, "row", "col", None),
        ),
        check_vma=False,
    )
```

profile of v0, /device:TPU:6, one launch (start us, length us, event | category | flops | bytes accessed | tf_op | source)
XLA Modules:
  0.0 143.9 jit_solution(7524878533196764084)
XLA Ops:
  3.0 1.1 fusion.44
  4.1 1.8 %copy.21 = bf16[1,2,4,9,128,128]{5,4,2,1,3,0:T(8,128)(2,1)S(1)} copy(bf16[1,2,4,9,128,128]{5,4,3,2,1,0:T(8,128)(2,1)} %param.11) | data formatting | bytes 4718592 | tf_op args[2]
  6.1 118.8 %while.16 = (s32[]{:T(128)}, bf16[64,2,4,128]{3,0,2,1:T(8,128)(2,1)S(1)}, bf16[64,2,4,128]{3,0,2,1:T(8,128)(2,1)S(1)}, s32[]{:T(128)}, f32[2,4,9]{1,0,2:T(2,128)...) while((s32[]{:T(128)}, ...), condition=%wide.region_1.2_spmd.clone, body=%wide.region_0.1_spmd.clone.sunk | while | flops 329383936 | bytes 22816724 | solution.py:105
  6.7 3.5 %collective-permute-start = (bf16[64,2,4,128]{3,0,2,1:T(8,128)(2,1)}, bf16[64,2,4,128]{3,0,2,1:T(8,128)(2,1)S(1)}, u32[]{:S(2)}, u32[]{:S(2)}) collective-permute-start(bf16[64,2,4,128]{3,0,2,1:T(8,128)(2,1)} %broadcast_select_fusion.4), channel_id=1, source_target_pairs={{0,8},{8,16},{16,24},{1,9},{9,17},{17,25},{2,10},{10,18},{18,26},{... | collective-permute-start | bytes 393224 | tf_op jit(solution)/shard_map/while/body/eval_jaxpr/ppermute | solution.py:26
  10.2 1.3 collective-permute-start.1
  11.6 1.7 %collective-permute-done = bf16[64,2,4,128]{3,0,2,1:T(8,128)(2,1)S(1)} collective-permute-done((bf16[64,2,4,128]{3,0,2,1:T(8,128)(2,1)}, bf16[64,2,4,128]{3,0,2,1:T(8,128)(2,1)S(1)}, u32[]{:S(2)}, u32[]{:S(2)}) %collective-permute-start) | collective-permute-done | bytes 131104 | tf_op jit(solution)/shard_map/while/body/eval_jaxpr/ppermute | solution.py:26
  13.9 3.2 %collective-permute-done.1 = bf16[64,2,4,128]{3,0,2,1:T(8,128)(2,1)S(1)} collective-permute-done((bf16[64,2,4,128]{3,0,2,1:T(8,128)(2,1)S(1)}, bf16[64,2,4,128]{3,0,2,1:T(8,128)(2,1)S(1)}, u32[]{:S(2)}, u32[]{:S(2)}) %collective-permute-start.1) | collective-permute-done | bytes 131104 | tf_op jit(solution)/shard_map/while/body/eval_jaxpr/ppermute | solution.py:26
  17.8 2.4 %collective-permute-start.2 = (bf16[128,1,4,128]{3,0,2,1:T(8,128)(2,1)S(1)}, bf16[128,1,4,128]{3,0,2,1:T(8,128)(2,1)S(1)}, u32[]{:S(2)}, u32[]{:S(2)}) collective-permute-start(bf16[128,1,4,128]{3,0,2,1:T(8,128)(2,1)S(1)} %get-tuple-element.363), channel_id=1, source_target_pairs={{4,0},{5,1},{6,2},{7,3},{12,8},{13,9},{14,10},{15,11},{20,16},{21,... | collective-permute-start | bytes 393224 | tf_op jit(solution)/shard_map/while/body/eval_jaxpr/ppermute | solution.py:18
  20.2 1.3 collective-permute-start.3
  21.8 1.0 collective-permute-done.2
  22.7 4.4 %collective-permute-done.3 = bf16[128,1,4,128]{3,0,2,1:T(8,128)(2,1)S(1)} collective-permute-done((bf16[128,1,4,128]{3,0,2,1:T(8,128)(2,1)S(1)}, bf16[128,1,4,128]{3,0,2,1:T(8,128)(2,1)S(1)}, u32[]{:S(2)}, u32[]{:S(2)}) %collective-permute-start.3) | collective-permute-done | bytes 131104 | tf_op jit(solution)/shard_map/while/body/eval_jaxpr/ppermute | solution.py:17
  27.1 1.9 %collective-permute-start.4 = (bf16[128,4,1,128]{3,0,2,1:T(8,128)(2,1)S(1)}, bf16[128,4,1,128]{3,0,2,1:T(8,128)(2,1)S(1)}, u32[]{:S(2)}, u32[]{:S(2)}) collective-permute-start(bf16[128,4,1,128]{3,0,2,1:T(8,128)(2,1)S(1)} %get-tuple-element.365), channel_id=1, source_target_pairs={{1,0},{2,1},{3,2},{5,4},{6,5},{7,6},{9,8},{10,9},{11,10},{13,12},{... | collective-permute-start | bytes 393224 | tf_op jit(solution)/shard_map/while/body/eval_jaxpr/ppermute | solution.py:18
  29.0 2.4 %collective-permute-start.5 = (bf16[128,4,1,128]{3,0,2,1:T(8,128)(2,1)S(1)}, bf16[128,4,1,128]{3,0,2,1:T(8,128)(2,1)S(1)}, u32[]{:S(2)}, u32[]{:S(2)}) collective-permute-start(bf16[128,4,1,128]{3,0,2,1:T(8,128)(2,1)S(1)} %get-tuple-element.368), channel_id=1, source_target_pairs={{0,1},{1,2},{2,3},{4,5},{5,6},{6,7},{8,9},{9,10},{10,11},{12,13},{... | collective-permute-start | bytes 393224 | tf_op jit(solution)/shard_map/while/body/eval_jaxpr/ppermute | solution.py:17
  31.9 3.4 %collective-permute-done.5 = bf16[128,4,1,128]{3,0,2,1:T(8,128)(2,1)S(1)} collective-permute-done((bf16[128,4,1,128]{3,0,2,1:T(8,128)(2,1)S(1)}, bf16[128,4,1,128]{3,0,2,1:T(8,128)(2,1)S(1)}, u32[]{:S(2)}, u32[]{:S(2)}) %collective-permute-start.5) | collective-permute-done | bytes 131104 | tf_op jit(solution)/shard_map/while/body/eval_jaxpr/ppermute | solution.py:17
  37.5 3.5 %collective-permute-start = (bf16[64,2,4,128]{3,0,2,1:T(8,128)(2,1)}, bf16[64,2,4,128]{3,0,2,1:T(8,128)(2,1)S(1)}, u32[]{:S(2)}, u32[]{:S(2)}) collective-permute-start(bf16[64,2,4,128]{3,0,2,1:T(8,128)(2,1)} %broadcast_select_fusion.4), channel_id=1, source_target_pairs={{0,8},{8,16},{16,24},{1,9},{9,17},{17,25},{2,10},{10,18},{18,26},{... | collective-permute-start | bytes 393224 | tf_op jit(solution)/shard_map/while/body/eval_jaxpr/ppermute | solution.py:26
  41.0 1.3 collective-permute-start.1
  42.4 1.5 %collective-permute-done = bf16[64,2,4,128]{3,0,2,1:T(8,128)(2,1)S(1)} collective-permute-done((bf16[64,2,4,128]{3,0,2,1:T(8,128)(2,1)}, bf16[64,2,4,128]{3,0,2,1:T(8,128)(2,1)S(1)}, u32[]{:S(2)}, u32[]{:S(2)}) %collective-permute-start) | collective-permute-done | bytes 131104 | tf_op jit(solution)/shard_map/while/body/eval_jaxpr/ppermute | solution.py:26
  44.5 3.4 %collective-permute-done.1 = bf16[64,2,4,128]{3,0,2,1:T(8,128)(2,1)S(1)} collective-permute-done((bf16[64,2,4,128]{3,0,2,1:T(8,128)(2,1)S(1)}, bf16[64,2,4,128]{3,0,2,1:T(8,128)(2,1)S(1)}, u32[]{:S(2)}, u32[]{:S(2)}) %collective-permute-start.1) | collective-permute-done | bytes 131104 | tf_op jit(solution)/shard_map/while/body/eval_jaxpr/ppermute | solution.py:26
  48.6 1.5 %collective-permute-start.2 = (bf16[128,1,4,128]{3,0,2,1:T(8,128)(2,1)S(1)}, bf16[128,1,4,128]{3,0,2,1:T(8,128)(2,1)S(1)}, u32[]{:S(2)}, u32[]{:S(2)}) collective-permute-start(bf16[128,1,4,128]{3,0,2,1:T(8,128)(2,1)S(1)} %get-tuple-element.363), channel_id=1, source_target_pairs={{4,0},{5,1},{6,2},{7,3},{12,8},{13,9},{14,10},{15,11},{20,16},{21,... | collective-permute-start | bytes 393224 | tf_op jit(solution)/shard_map/while/body/eval_jaxpr/ppermute | solution.py:18
  50.1 1.3 collective-permute-start.3
  51.6 1.0 collective-permute-done.2
  52.6 4.4 %collective-permute-done.3 = bf16[128,1,4,128]{3,0,2,1:T(8,128)(2,1)S(1)} collective-permute-done((bf16[128,1,4,128]{3,0,2,1:T(8,128)(2,1)S(1)}, bf16[128,1,4,128]{3,0,2,1:T(8,128)(2,1)S(1)}, u32[]{:S(2)}, u32[]{:S(2)}) %collective-permute-start.3) | collective-permute-done | bytes 131104 | tf_op jit(solution)/shard_map/while/body/eval_jaxpr/ppermute | solution.py:17
  57.0 1.9 %collective-permute-start.4 = (bf16[128,4,1,128]{3,0,2,1:T(8,128)(2,1)S(1)}, bf16[128,4,1,128]{3,0,2,1:T(8,128)(2,1)S(1)}, u32[]{:S(2)}, u32[]{:S(2)}) collective-permute-start(bf16[128,4,1,128]{3,0,2,1:T(8,128)(2,1)S(1)} %get-tuple-element.365), channel_id=1, source_target_pairs={{1,0},{2,1},{3,2},{5,4},{6,5},{7,6},{9,8},{10,9},{11,10},{13,12},{... | collective-permute-start | bytes 393224 | tf_op jit(solution)/shard_map/while/body/eval_jaxpr/ppermute | solution.py:18
  58.9 2.4 %collective-permute-start.5 = (bf16[128,4,1,128]{3,0,2,1:T(8,128)(2,1)S(1)}, bf16[128,4,1,128]{3,0,2,1:T(8,128)(2,1)S(1)}, u32[]{:S(2)}, u32[]{:S(2)}) collective-permute-start(bf16[128,4,1,128]{3,0,2,1:T(8,128)(2,1)S(1)} %get-tuple-element.368), channel_id=1, source_target_pairs={{0,1},{1,2},{2,3},{4,5},{5,6},{6,7},{8,9},{9,10},{10,11},{12,13},{... | collective-permute-start | bytes 393224 | tf_op jit(solution)/shard_map/while/body/eval_jaxpr/ppermute | solution.py:17
  61.8 3.4 %collective-permute-done.5 = bf16[128,4,1,128]{3,0,2,1:T(8,128)(2,1)S(1)} collective-permute-done((bf16[128,4,1,128]{3,0,2,1:T(8,128)(2,1)S(1)}, bf16[128,4,1,128]{3,0,2,1:T(8,128)(2,1)S(1)}, u32[]{:S(2)}, u32[]{:S(2)}) %collective-permute-start.5) | collective-permute-done | bytes 131104 | tf_op jit(solution)/shard_map/while/body/eval_jaxpr/ppermute | solution.py:17
  67.4 3.5 %collective-permute-start = (bf16[64,2,4,128]{3,0,2,1:T(8,128)(2,1)}, bf16[64,2,4,128]{3,0,2,1:T(8,128)(2,1)S(1)}, u32[]{:S(2)}, u32[]{:S(2)}) collective-permute-start(bf16[64,2,4,128]{3,0,2,1:T(8,128)(2,1)} %broadcast_select_fusion.4), channel_id=1, source_target_pairs={{0,8},{8,16},{16,24},{1,9},{9,17},{17,25},{2,10},{10,18},{18,26},{... | collective-permute-start | bytes 393224 | tf_op jit(solution)/shard_map/while/body/eval_jaxpr/ppermute | solution.py:26
  70.9 1.3 collective-permute-start.1
  72.2 1.5 %collective-permute-done = bf16[64,2,4,128]{3,0,2,1:T(8,128)(2,1)S(1)} collective-permute-done((bf16[64,2,4,128]{3,0,2,1:T(8,128)(2,1)}, bf16[64,2,4,128]{3,0,2,1:T(8,128)(2,1)S(1)}, u32[]{:S(2)}, u32[]{:S(2)}) %collective-permute-start) | collective-permute-done | bytes 131104 | tf_op jit(solution)/shard_map/while/body/eval_jaxpr/ppermute | solution.py:26
  74.3 3.4 %collective-permute-done.1 = bf16[64,2,4,128]{3,0,2,1:T(8,128)(2,1)S(1)} collective-permute-done((bf16[64,2,4,128]{3,0,2,1:T(8,128)(2,1)S(1)}, bf16[64,2,4,128]{3,0,2,1:T(8,128)(2,1)S(1)}, u32[]{:S(2)}, u32[]{:S(2)}) %collective-permute-start.1) | collective-permute-done | bytes 131104 | tf_op jit(solution)/shard_map/while/body/eval_jaxpr/ppermute | solution.py:26
  78.5 1.5 %collective-permute-start.2 = (bf16[128,1,4,128]{3,0,2,1:T(8,128)(2,1)S(1)}, bf16[128,1,4,128]{3,0,2,1:T(8,128)(2,1)S(1)}, u32[]{:S(2)}, u32[]{:S(2)}) collective-permute-start(bf16[128,1,4,128]{3,0,2,1:T(8,128)(2,1)S(1)} %get-tuple-element.363), channel_id=1, source_target_pairs={{4,0},{5,1},{6,2},{7,3},{12,8},{13,9},{14,10},{15,11},{20,16},{21,... | collective-permute-start | bytes 393224 | tf_op jit(solution)/shard_map/while/body/eval_jaxpr/ppermute | solution.py:18
  80.0 1.3 collective-permute-start.3
  82.5 4.4 %collective-permute-done.3 = bf16[128,1,4,128]{3,0,2,1:T(8,128)(2,1)S(1)} collective-permute-done((bf16[128,1,4,128]{3,0,2,1:T(8,128)(2,1)S(1)}, bf16[128,1,4,128]{3,0,2,1:T(8,128)(2,1)S(1)}, u32[]{:S(2)}, u32[]{:S(2)}) %collective-permute-start.3) | collective-permute-done | bytes 131104 | tf_op jit(solution)/shard_map/while/body/eval_jaxpr/ppermute | solution.py:17
  86.8 1.9 %collective-permute-start.4 = (bf16[128,4,1,128]{3,0,2,1:T(8,128)(2,1)S(1)}, bf16[128,4,1,128]{3,0,2,1:T(8,128)(2,1)S(1)}, u32[]{:S(2)}, u32[]{:S(2)}) collective-permute-start(bf16[128,4,1,128]{3,0,2,1:T(8,128)(2,1)S(1)} %get-tuple-element.365), channel_id=1, source_target_pairs={{1,0},{2,1},{3,2},{5,4},{6,5},{7,6},{9,8},{10,9},{11,10},{13,12},{... | collective-permute-start | bytes 393224 | tf_op jit(solution)/shard_map/while/body/eval_jaxpr/ppermute | solution.py:18
  88.8 2.4 %collective-permute-start.5 = (bf16[128,4,1,128]{3,0,2,1:T(8,128)(2,1)S(1)}, bf16[128,4,1,128]{3,0,2,1:T(8,128)(2,1)S(1)}, u32[]{:S(2)}, u32[]{:S(2)}) collective-permute-start(bf16[128,4,1,128]{3,0,2,1:T(8,128)(2,1)S(1)} %get-tuple-element.368), channel_id=1, source_target_pairs={{0,1},{1,2},{2,3},{4,5},{5,6},{6,7},{8,9},{9,10},{10,11},{12,13},{... | collective-permute-start | bytes 393224 | tf_op jit(solution)/shard_map/while/body/eval_jaxpr/ppermute | solution.py:17
  91.6 3.4 %collective-permute-done.5 = bf16[128,4,1,128]{3,0,2,1:T(8,128)(2,1)S(1)} collective-permute-done((bf16[128,4,1,128]{3,0,2,1:T(8,128)(2,1)S(1)}, bf16[128,4,1,128]{3,0,2,1:T(8,128)(2,1)S(1)}, u32[]{:S(2)}, u32[]{:S(2)}) %collective-permute-start.5) | collective-permute-done | bytes 131104 | tf_op jit(solution)/shard_map/while/body/eval_jaxpr/ppermute | solution.py:17
  97.3 1.9 %collective-permute-start = (bf16[64,2,4,128]{3,0,2,1:T(8,128)(2,1)}, bf16[64,2,4,128]{3,0,2,1:T(8,128)(2,1)S(1)}, u32[]{:S(2)}, u32[]{:S(2)}) collective-permute-start(bf16[64,2,4,128]{3,0,2,1:T(8,128)(2,1)} %broadcast_select_fusion.4), channel_id=1, source_target_pairs={{0,8},{8,16},{16,24},{1,9},{9,17},{17,25},{2,10},{10,18},{18,26},{... | collective-permute-start | bytes 393224 | tf_op jit(solution)/shard_map/while/body/eval_jaxpr/ppermute | solution.py:26
  99.2 1.3 collective-permute-start.1
  100.5 1.5 %collective-permute-done = bf16[64,2,4,128]{3,0,2,1:T(8,128)(2,1)S(1)} collective-permute-done((bf16[64,2,4,128]{3,0,2,1:T(8,128)(2,1)}, bf16[64,2,4,128]{3,0,2,1:T(8,128)(2,1)S(1)}, u32[]{:S(2)}, u32[]{:S(2)}) %collective-permute-start) | collective-permute-done | bytes 131104 | tf_op jit(solution)/shard_map/while/body/eval_jaxpr/ppermute | solution.py:26
  102.6 3.4 %collective-permute-done.1 = bf16[64,2,4,128]{3,0,2,1:T(8,128)(2,1)S(1)} collective-permute-done((bf16[64,2,4,128]{3,0,2,1:T(8,128)(2,1)S(1)}, bf16[64,2,4,128]{3,0,2,1:T(8,128)(2,1)S(1)}, u32[]{:S(2)}, u32[]{:S(2)}) %collective-permute-start.1) | collective-permute-done | bytes 131104 | tf_op jit(solution)/shard_map/while/body/eval_jaxpr/ppermute | solution.py:26
  106.8 1.5 %collective-permute-start.2 = (bf16[128,1,4,128]{3,0,2,1:T(8,128)(2,1)S(1)}, bf16[128,1,4,128]{3,0,2,1:T(8,128)(2,1)S(1)}, u32[]{:S(2)}, u32[]{:S(2)}) collective-permute-start(bf16[128,1,4,128]{3,0,2,1:T(8,128)(2,1)S(1)} %get-tuple-element.363), channel_id=1, source_target_pairs={{4,0},{5,1},{6,2},{7,3},{12,8},{13,9},{14,10},{15,11},{20,16},{21,... | collective-permute-start | bytes 393224 | tf_op jit(solution)/shard_map/while/body/eval_jaxpr/ppermute | solution.py:18
  108.3 1.3 collective-permute-start.3
  109.8 1.0 collective-permute-done.2
  110.8 4.4 %collective-permute-done.3 = bf16[128,1,4,128]{3,0,2,1:T(8,128)(2,1)S(1)} collective-permute-done((bf16[128,1,4,128]{3,0,2,1:T(8,128)(2,1)S(1)}, bf16[128,1,4,128]{3,0,2,1:T(8,128)(2,1)S(1)}, u32[]{:S(2)}, u32[]{:S(2)}) %collective-permute-start.3) | collective-permute-done | bytes 131104 | tf_op jit(solution)/shard_map/while/body/eval_jaxpr/ppermute | solution.py:17
  115.1 1.9 %collective-permute-start.4 = (bf16[128,4,1,128]{3,0,2,1:T(8,128)(2,1)S(1)}, bf16[128,4,1,128]{3,0,2,1:T(8,128)(2,1)S(1)}, u32[]{:S(2)}, u32[]{:S(2)}) collective-permute-start(bf16[128,4,1,128]{3,0,2,1:T(8,128)(2,1)S(1)} %get-tuple-element.365), channel_id=1, source_target_pairs={{1,0},{2,1},{3,2},{5,4},{6,5},{7,6},{9,8},{10,9},{11,10},{13,12},{... | collective-permute-start | bytes 393224 | tf_op jit(solution)/shard_map/while/body/eval_jaxpr/ppermute | solution.py:18
  117.1 2.4 %collective-permute-start.5 = (bf16[128,4,1,128]{3,0,2,1:T(8,128)(2,1)S(1)}, bf16[128,4,1,128]{3,0,2,1:T(8,128)(2,1)S(1)}, u32[]{:S(2)}, u32[]{:S(2)}) collective-permute-start(bf16[128,4,1,128]{3,0,2,1:T(8,128)(2,1)S(1)} %get-tuple-element.368), channel_id=1, source_target_pairs={{0,1},{1,2},{2,3},{4,5},{5,6},{6,7},{8,9},{9,10},{10,11},{12,13},{... | collective-permute-start | bytes 393224 | tf_op jit(solution)/shard_map/while/body/eval_jaxpr/ppermute | solution.py:17
  119.9 3.4 %collective-permute-done.5 = bf16[128,4,1,128]{3,0,2,1:T(8,128)(2,1)S(1)} collective-permute-done((bf16[128,4,1,128]{3,0,2,1:T(8,128)(2,1)S(1)}, bf16[128,4,1,128]{3,0,2,1:T(8,128)(2,1)S(1)}, u32[]{:S(2)}, u32[]{:S(2)}) %collective-permute-start.5) | collective-permute-done | bytes 131104 | tf_op jit(solution)/shard_map/while/body/eval_jaxpr/ppermute | solution.py:17
  124.9 1.2 dynamic_slice.13
  126.9 16.1 %psum.7 = f32[4,2,4,128]{3,2,1,0:T(4,128)} all-reduce(f32[4,2,4,128]{3,2,1,0:T(4,128)S(1)} %broadcast_multiply_fusion), channel_id=1, replica_groups=mesh['layer'=4,'row'=2,'col'=4] {'layer'}, use_global_device_ids=true, to_apply=%region_3.4 | all-reduce | flops 4096 | bytes 32768 | tf_op jit(solution)/shard_map/psum | solution.py:113
  (92 shorter events, 21.8 us)
Async XLA Ops:
  0.6 0.7 copy-start
  4.1 1.9 %copy-start.1 = (s32[1,2,4,9]{3,2,1,0:T(4,128)S(1)}, s32[1,2,4,9]{3,2,1,0:T(4,128)}, u32[]{:S(2)}) copy-start(s32[1,2,4,9]{3,2,1,0:T(4,128)} %param.12) | copy-start | bytes 868
  6.7 6.5 %collective-permute-start = (bf16[64,2,4,128]{3,0,2,1:T(8,128)(2,1)}, bf16[64,2,4,128]{3,0,2,1:T(8,128)(2,1)S(1)}, u32[]{:S(2)}, u32[]{:S(2)}) collective-permute-start(bf16[64,2,4,128]{3,0,2,1:T(8,128)(2,1)} %broadcast_select_fusion.4), channel_id=1, source_target_pairs={{0,8},{8,16},{16,24},{1,9},{9,17},{17,25},{2,10},{10,18},{18,26},{... | collective-permute-start | bytes 393224 | tf_op jit(solution)/shard_map/while/body/eval_jaxpr/ppermute | solution.py:26
  10.2 6.9 %collective-permute-start.1 = (bf16[64,2,4,128]{3,0,2,1:T(8,128)(2,1)S(1)}, bf16[64,2,4,128]{3,0,2,1:T(8,128)(2,1)S(1)}, u32[]{:S(2)}, u32[]{:S(2)}) collective-permute-start(bf16[64,2,4,128]{3,0,2,1:T(8,128)(2,1)S(1)} %broadcast_select_fusion.5), channel_id=1, source_target_pairs={{8,0},{16,8},{24,16},{9,1},{17,9},{25,17},{10,2},{18,10},{26,18},{... | collective-permute-start | bytes 393224 | tf_op jit(solution)/shard_map/while/body/eval_jaxpr/ppermute | solution.py:26
  17.8 4.9 %collective-permute-start.2 = (bf16[128,1,4,128]{3,0,2,1:T(8,128)(2,1)S(1)}, bf16[128,1,4,128]{3,0,2,1:T(8,128)(2,1)S(1)}, u32[]{:S(2)}, u32[]{:S(2)}) collective-permute-start(bf16[128,1,4,128]{3,0,2,1:T(8,128)(2,1)S(1)} %get-tuple-element.363), channel_id=1, source_target_pairs={{4,0},{5,1},{6,2},{7,3},{12,8},{13,9},{14,10},{15,11},{20,16},{21,... | collective-permute-start | bytes 393224 | tf_op jit(solution)/shard_map/while/body/eval_jaxpr/ppermute | solution.py:18
  20.2 6.9 %collective-permute-start.3 = (bf16[128,1,4,128]{3,0,2,1:T(8,128)(2,1)S(1)}, bf16[128,1,4,128]{3,0,2,1:T(8,128)(2,1)S(1)}, u32[]{:S(2)}, u32[]{:S(2)}) collective-permute-start(bf16[128,1,4,128]{3,0,2,1:T(8,128)(2,1)S(1)} %get-tuple-element.364), channel_id=1, source_target_pairs={{0,4},{1,5},{2,6},{3,7},{8,12},{9,13},{10,14},{11,15},{16,20},{17,... | collective-permute-start | bytes 393224 | tf_op jit(solution)/shard_map/while/body/eval_jaxpr/ppermute | solution.py:17
  27.1 8.7 %collective-permute-start.4 = (bf16[128,4,1,128]{3,0,2,1:T(8,128)(2,1)S(1)}, bf16[128,4,1,128]{3,0,2,1:T(8,128)(2,1)S(1)}, u32[]{:S(2)}, u32[]{:S(2)}) collective-permute-start(bf16[128,4,1,128]{3,0,2,1:T(8,128)(2,1)S(1)} %get-tuple-element.365), channel_id=1, source_target_pairs={{1,0},{2,1},{3,2},{5,4},{6,5},{7,6},{9,8},{10,9},{11,10},{13,12},{... | collective-permute-start | bytes 393224 | tf_op jit(solution)/shard_map/while/body/eval_jaxpr/ppermute | solution.py:18
  29.0 6.3 %collective-permute-start.5 = (bf16[128,4,1,128]{3,0,2,1:T(8,128)(2,1)S(1)}, bf16[128,4,1,128]{3,0,2,1:T(8,128)(2,1)S(1)}, u32[]{:S(2)}, u32[]{:S(2)}) collective-permute-start(bf16[128,4,1,128]{3,0,2,1:T(8,128)(2,1)S(1)} %get-tuple-element.368), channel_id=1, source_target_pairs={{0,1},{1,2},{2,3},{4,5},{5,6},{6,7},{8,9},{9,10},{10,11},{12,13},{... | collective-permute-start | bytes 393224 | tf_op jit(solution)/shard_map/while/body/eval_jaxpr/ppermute | solution.py:17
  37.5 6.3 %collective-permute-start = (bf16[64,2,4,128]{3,0,2,1:T(8,128)(2,1)}, bf16[64,2,4,128]{3,0,2,1:T(8,128)(2,1)S(1)}, u32[]{:S(2)}, u32[]{:S(2)}) collective-permute-start(bf16[64,2,4,128]{3,0,2,1:T(8,128)(2,1)} %broadcast_select_fusion.4), channel_id=1, source_target_pairs={{0,8},{8,16},{16,24},{1,9},{9,17},{17,25},{2,10},{10,18},{18,26},{... | collective-permute-start | bytes 393224 | tf_op jit(solution)/shard_map/while/body/eval_jaxpr/ppermute | solution.py:26
  41.0 6.9 %collective-permute-start.1 = (bf16[64,2,4,128]{3,0,2,1:T(8,128)(2,1)S(1)}, bf16[64,2,4,128]{3,0,2,1:T(8,128)(2,1)S(1)}, u32[]{:S(2)}, u32[]{:S(2)}) collective-permute-start(bf16[64,2,4,128]{3,0,2,1:T(8,128)(2,1)S(1)} %broadcast_select_fusion.5), channel_id=1, source_target_pairs={{8,0},{16,8},{24,16},{9,1},{17,9},{25,17},{10,2},{18,10},{26,18},{... | collective-permute-start | bytes 393224 | tf_op jit(solution)/shard_map/while/body/eval_jaxpr/ppermute | solution.py:26
  48.6 4.0 %collective-permute-start.2 = (bf16[128,1,4,128]{3,0,2,1:T(8,128)(2,1)S(1)}, bf16[128,1,4,128]{3,0,2,1:T(8,128)(2,1)S(1)}, u32[]{:S(2)}, u32[]{:S(2)}) collective-permute-start(bf16[128,1,4,128]{3,0,2,1:T(8,128)(2,1)S(1)} %get-tuple-element.363), channel_id=1, source_target_pairs={{4,0},{5,1},{6,2},{7,3},{12,8},{13,9},{14,10},{15,11},{20,16},{21,... | collective-permute-start | bytes 393224 | tf_op jit(solution)/shard_map/while/body/eval_jaxpr/ppermute | solution.py:18
  50.1 6.9 %collective-permute-start.3 = (bf16[128,1,4,128]{3,0,2,1:T(8,128)(2,1)S(1)}, bf16[128,1,4,128]{3,0,2,1:T(8,128)(2,1)S(1)}, u32[]{:S(2)}, u32[]{:S(2)}) collective-permute-start(bf16[128,1,4,128]{3,0,2,1:T(8,128)(2,1)S(1)} %get-tuple-element.364), channel_id=1, source_target_pairs={{0,4},{1,5},{2,6},{3,7},{8,12},{9,13},{10,14},{11,15},{16,20},{17,... | collective-permute-start | bytes 393224 | tf_op jit(solution)/shard_map/while/body/eval_jaxpr/ppermute | solution.py:17
  57.0 8.7 %collective-permute-start.4 = (bf16[128,4,1,128]{3,0,2,1:T(8,128)(2,1)S(1)}, bf16[128,4,1,128]{3,0,2,1:T(8,128)(2,1)S(1)}, u32[]{:S(2)}, u32[]{:S(2)}) collective-permute-start(bf16[128,4,1,128]{3,0,2,1:T(8,128)(2,1)S(1)} %get-tuple-element.365), channel_id=1, source_target_pairs={{1,0},{2,1},{3,2},{5,4},{6,5},{7,6},{9,8},{10,9},{11,10},{13,12},{... | collective-permute-start | bytes 393224 | tf_op jit(solution)/shard_map/while/body/eval_jaxpr/ppermute | solution.py:18
  58.9 6.3 %collective-permute-start.5 = (bf16[128,4,1,128]{3,0,2,1:T(8,128)(2,1)S(1)}, bf16[128,4,1,128]{3,0,2,1:T(8,128)(2,1)S(1)}, u32[]{:S(2)}, u32[]{:S(2)}) collective-permute-start(bf16[128,4,1,128]{3,0,2,1:T(8,128)(2,1)S(1)} %get-tuple-element.368), channel_id=1, source_target_pairs={{0,1},{1,2},{2,3},{4,5},{5,6},{6,7},{8,9},{9,10},{10,11},{12,13},{... | collective-permute-start | bytes 393224 | tf_op jit(solution)/shard_map/while/body/eval_jaxpr/ppermute | solution.py:17
  67.4 6.3 %collective-permute-start = (bf16[64,2,4,128]{3,0,2,1:T(8,128)(2,1)}, bf16[64,2,4,128]{3,0,2,1:T(8,128)(2,1)S(1)}, u32[]{:S(2)}, u32[]{:S(2)}) collective-permute-start(bf16[64,2,4,128]{3,0,2,1:T(8,128)(2,1)} %broadcast_select_fusion.4), channel_id=1, source_target_pairs={{0,8},{8,16},{16,24},{1,9},{9,17},{17,25},{2,10},{10,18},{18,26},{... | collective-permute-start | bytes 393224 | tf_op jit(solution)/shard_map/while/body/eval_jaxpr/ppermute | solution.py:26
  70.9 6.9 %collective-permute-start.1 = (bf16[64,2,4,128]{3,0,2,1:T(8,128)(2,1)S(1)}, bf16[64,2,4,128]{3,0,2,1:T(8,128)(2,1)S(1)}, u32[]{:S(2)}, u32[]{:S(2)}) collective-permute-start(bf16[64,2,4,128]{3,0,2,1:T(8,128)(2,1)S(1)} %broadcast_select_fusion.5), channel_id=1, source_target_pairs={{8,0},{16,8},{24,16},{9,1},{17,9},{25,17},{10,2},{18,10},{26,18},{... | collective-permute-start | bytes 393224 | tf_op jit(solution)/shard_map/while/body/eval_jaxpr/ppermute | solution.py:26
  78.5 4.0 %collective-permute-start.2 = (bf16[128,1,4,128]{3,0,2,1:T(8,128)(2,1)S(1)}, bf16[128,1,4,128]{3,0,2,1:T(8,128)(2,1)S(1)}, u32[]{:S(2)}, u32[]{:S(2)}) collective-permute-start(bf16[128,1,4,128]{3,0,2,1:T(8,128)(2,1)S(1)} %get-tuple-element.363), channel_id=1, source_target_pairs={{4,0},{5,1},{6,2},{7,3},{12,8},{13,9},{14,10},{15,11},{20,16},{21,... | collective-permute-start | bytes 393224 | tf_op jit(solution)/shard_map/while/body/eval_jaxpr/ppermute | solution.py:18
  80.0 6.9 %collective-permute-start.3 = (bf16[128,1,4,128]{3,0,2,1:T(8,128)(2,1)S(1)}, bf16[128,1,4,128]{3,0,2,1:T(8,128)(2,1)S(1)}, u32[]{:S(2)}, u32[]{:S(2)}) collective-permute-start(bf16[128,1,4,128]{3,0,2,1:T(8,128)(2,1)S(1)} %get-tuple-element.364), channel_id=1, source_target_pairs={{0,4},{1,5},{2,6},{3,7},{8,12},{9,13},{10,14},{11,15},{16,20},{17,... | collective-permute-start | bytes 393224 | tf_op jit(solution)/shard_map/while/body/eval_jaxpr/ppermute | solution.py:17
  86.8 8.7 %collective-permute-start.4 = (bf16[128,4,1,128]{3,0,2,1:T(8,128)(2,1)S(1)}, bf16[128,4,1,128]{3,0,2,1:T(8,128)(2,1)S(1)}, u32[]{:S(2)}, u32[]{:S(2)}) collective-permute-start(bf16[128,4,1,128]{3,0,2,1:T(8,128)(2,1)S(1)} %get-tuple-element.365), channel_id=1, source_target_pairs={{1,0},{2,1},{3,2},{5,4},{6,5},{7,6},{9,8},{10,9},{11,10},{13,12},{... | collective-permute-start | bytes 393224 | tf_op jit(solution)/shard_map/while/body/eval_jaxpr/ppermute | solution.py:18
  88.8 6.3 %collective-permute-start.5 = (bf16[128,4,1,128]{3,0,2,1:T(8,128)(2,1)S(1)}, bf16[128,4,1,128]{3,0,2,1:T(8,128)(2,1)S(1)}, u32[]{:S(2)}, u32[]{:S(2)}) collective-permute-start(bf16[128,4,1,128]{3,0,2,1:T(8,128)(2,1)S(1)} %get-tuple-element.368), channel_id=1, source_target_pairs={{0,1},{1,2},{2,3},{4,5},{5,6},{6,7},{8,9},{9,10},{10,11},{12,13},{... | collective-permute-start | bytes 393224 | tf_op jit(solution)/shard_map/while/body/eval_jaxpr/ppermute | solution.py:17
  97.3 4.7 %collective-permute-start = (bf16[64,2,4,128]{3,0,2,1:T(8,128)(2,1)}, bf16[64,2,4,128]{3,0,2,1:T(8,128)(2,1)S(1)}, u32[]{:S(2)}, u32[]{:S(2)}) collective-permute-start(bf16[64,2,4,128]{3,0,2,1:T(8,128)(2,1)} %broadcast_select_fusion.4), channel_id=1, source_target_pairs={{0,8},{8,16},{16,24},{1,9},{9,17},{17,25},{2,10},{10,18},{18,26},{... | collective-permute-start | bytes 393224 | tf_op jit(solution)/shard_map/while/body/eval_jaxpr/ppermute | solution.py:26
  99.2 6.9 %collective-permute-start.1 = (bf16[64,2,4,128]{3,0,2,1:T(8,128)(2,1)S(1)}, bf16[64,2,4,128]{3,0,2,1:T(8,128)(2,1)S(1)}, u32[]{:S(2)}, u32[]{:S(2)}) collective-permute-start(bf16[64,2,4,128]{3,0,2,1:T(8,128)(2,1)S(1)} %broadcast_select_fusion.5), channel_id=1, source_target_pairs={{8,0},{16,8},{24,16},{9,1},{17,9},{25,17},{10,2},{18,10},{26,18},{... | collective-permute-start | bytes 393224 | tf_op jit(solution)/shard_map/while/body/eval_jaxpr/ppermute | solution.py:26
  106.8 4.0 %collective-permute-start.2 = (bf16[128,1,4,128]{3,0,2,1:T(8,128)(2,1)S(1)}, bf16[128,1,4,128]{3,0,2,1:T(8,128)(2,1)S(1)}, u32[]{:S(2)}, u32[]{:S(2)}) collective-permute-start(bf16[128,1,4,128]{3,0,2,1:T(8,128)(2,1)S(1)} %get-tuple-element.363), channel_id=1, source_target_pairs={{4,0},{5,1},{6,2},{7,3},{12,8},{13,9},{14,10},{15,11},{20,16},{21,... | collective-permute-start | bytes 393224 | tf_op jit(solution)/shard_map/while/body/eval_jaxpr/ppermute | solution.py:18
  108.3 6.9 %collective-permute-start.3 = (bf16[128,1,4,128]{3,0,2,1:T(8,128)(2,1)S(1)}, bf16[128,1,4,128]{3,0,2,1:T(8,128)(2,1)S(1)}, u32[]{:S(2)}, u32[]{:S(2)}) collective-permute-start(bf16[128,1,4,128]{3,0,2,1:T(8,128)(2,1)S(1)} %get-tuple-element.364), channel_id=1, source_target_pairs={{0,4},{1,5},{2,6},{3,7},{8,12},{9,13},{10,14},{11,15},{16,20},{17,... | collective-permute-start | bytes 393224 | tf_op jit(solution)/shard_map/while/body/eval_jaxpr/ppermute | solution.py:17
  115.1 8.7 %collective-permute-start.4 = (bf16[128,4,1,128]{3,0,2,1:T(8,128)(2,1)S(1)}, bf16[128,4,1,128]{3,0,2,1:T(8,128)(2,1)S(1)}, u32[]{:S(2)}, u32[]{:S(2)}) collective-permute-start(bf16[128,4,1,128]{3,0,2,1:T(8,128)(2,1)S(1)} %get-tuple-element.365), channel_id=1, source_target_pairs={{1,0},{2,1},{3,2},{5,4},{6,5},{7,6},{9,8},{10,9},{11,10},{13,12},{... | collective-permute-start | bytes 393224 | tf_op jit(solution)/shard_map/while/body/eval_jaxpr/ppermute | solution.py:18
  117.1 6.3 %collective-permute-start.5 = (bf16[128,4,1,128]{3,0,2,1:T(8,128)(2,1)S(1)}, bf16[128,4,1,128]{3,0,2,1:T(8,128)(2,1)S(1)}, u32[]{:S(2)}, u32[]{:S(2)}) collective-permute-start(bf16[128,4,1,128]{3,0,2,1:T(8,128)(2,1)S(1)} %get-tuple-element.368), channel_id=1, source_target_pairs={{0,1},{1,2},{2,3},{4,5},{5,6},{6,7},{8,9},{9,10},{10,11},{12,13},{... | collective-permute-start | bytes 393224 | tf_op jit(solution)/shard_map/while/body/eval_jaxpr/ppermute | solution.py:17
where the time goes:
time: 145 us; the launch traced here: 144 us
  waiting for transfers between devices  54.5 us (38%)
  starting transfers between devices  46.9 us (32%)
  blocking collectives  16.1 us (11%)
  other arithmetic  10.5 us (7%)
  matrix products  9.04 us (6%)
  local copies, waits for them, and re-layouts  5.42 us (4%)
    ppermute x8, waiting for transfers between devices, extended(): before = lax.ppermute(last, axis, up)  31.1 us
    ppermute x8, waiting for transfers between devices, shifted(): return lax.ppermute(block, axis, route)  19.5 us
    ppermute x8, starting transfers between devices, shifted(): return lax.ppermute(block, axis, route)  17.5 us
    psum x1, blocking collectives, local(): gradient = lax.psum(contribution, 'layer')  16.1 us
    ppermute x8, starting transfers between devices, extended(): before = lax.ppermute(last, axis, up)  14.8 us
    ppermute x8, starting transfers between devices, extended(): after = lax.ppermute(initial, axis, down)  14.6 us
    dot_general x36, matrix products, apply_front(): jnp.einsum('pijc,ijcd->pijd', beside, front_blocks[:, :, offset], preferr...  8.21 us
    ppermute x8, waiting for transfers between devices, extended(): after = lax.ppermute(initial, axis, down)  3.89 us
  transfers between devices with their start and end apart: 24, of which 20 were waited for; matrix products, arithmetic and copies ran while one was open for 5% of the time, Pallas kernels for 0%

commit v1 on v0

v1 whole, which is shorter than its diff:
```python
import functools

import jax
import jax.numpy as jnp
from jax import lax
from jax.experimental import pallas as pl
from jax.experimental.pallas import tpu as pltpu
from jax.sharding import PartitionSpec as P

port_strength = 4.0
intersection_scale = 0.125
AXES = ("layer", "row", "col")
OFFSETS = 9
VMEM_BYTES = 24 * 1024 * 1024

VM = pl.BlockSpec(memory_space=pltpu.VMEM)
SM = pl.BlockSpec(memory_space=pltpu.SMEM)


def call(kernel, outs, *args, smem=0, scratch=(), aliases=None):
    return pl.pallas_call(
        kernel,
        out_shape=[jax.ShapeDtypeStruct(shape, dtype) for shape, dtype in outs],
        in_specs=[SM] * smem + [VM] * (len(args) - smem),
        out_specs=[VM] * len(outs),
        scratch_shapes=list(scratch),
        input_output_aliases=aliases or {},
        compiler_params=pltpu.CompilerParams(vmem_limit_bytes=VMEM_BYTES),
    )(*args)


def near(i, n):
    return i ^ 1


def far(i, n):
    return (((i + 1) ^ 1) - 1) % n


def pairings(n):
    return [near] if n == 2 else [near, far]


class Side:
    def __init__(self, pairing, axis, tiles):
        pos, count = lax.axis_index(axis), lax.axis_size(axis)
        even = lax.rem(pos, 2) == 0
        after = even if pairing is near else jnp.logical_not(even)
        self.step = jnp.where(after, 1, -1)
        self.edge = jnp.where(after, tiles - 1, 0)
        self.real = None
        if pairing is far:
            self.real = jnp.logical_not(
                jnp.logical_or(jnp.logical_and(after, pos == count - 1), jnp.logical_and(jnp.logical_not(after), pos == 0))
            )

    def when(self, body):
        if self.real is None:
            body()
        else:
            pl.when(self.real)(body)


def local(sources, adjoint_sources, blocks, pattern, coupling, layer_group, port_cells):
    ports, tiles_x, tiles_y, cells = sources.shape[1:]
    tiles = tiles_x * tiles_y
    groups = coupling.shape[0]
    layers, rows, cols = (lax.axis_size(axis) for axis in AXES)
    row_pairs, col_pairs = pairings(rows), pairings(cols)
    ext = tiles_x + len(row_pairs)
    bf16, f32 = jnp.bfloat16, jnp.float32

    def route(of_layer=None, of_row=None, of_col=None):
        pairs = []
        for l in range(layers):
            for r in range(rows):
                for c in range(cols):
                    a = of_layer(l) if of_layer else l
                    b = of_row(r, rows) if of_row else r
                    d = of_col(c, cols) if of_col else c
                    pairs.append(((l * rows + r) * cols + c, (a * rows + b) * cols + d))
        return pairs

    def swapped(array, **where):
        return lax.ppermute(array, AXES, route(**where))

    def is_active(step):
        pos = lax.axis_index("layer")
        return jnp.logical_or(pos == step, pos == layers - 1 - step)

    def sweep_of(step):
        return jnp.where(lax.axis_index("layer") == step, 0, 1)

    def port_map(cells_ref, x, y):
        x_pos = lax.axis_index("row") * tiles_x + x
        y_pos = lax.axis_index("col") * tiles_y + y
        first = (x_pos * (tiles_y * cols) + y_pos) * cells
        row = jnp.broadcast_to(cells_ref[...], (ports, ports))
        diagonal = lax.broadcasted_iota(jnp.int32, (ports, ports), 0) == lax.broadcasted_iota(
            jnp.int32, (ports, ports), 1
        )
        column = jnp.sum(jnp.where(diagonal, row, 0), axis=1, keepdims=True)
        lane = lax.broadcasted_iota(jnp.int32, (ports, cells), 1)
        return jnp.where(column - first == lane, port_strength, 0.0).astype(f32)

    def source_tile(flat_ref, cells_ref, sweep, x, y):
        tile = flat_ref[sweep, pl.ds(x * tiles_y + y, ports, stride=tiles), :]
        pos = lax.axis_index("layer")
        end = pos == (0 if sweep == 0 else layers - 1)
        return (tile + jnp.where(end, port_map(cells_ref, x, y), 0.0)).astype(bf16)

    def rims_kernel(forward_ref, adjoint_ref, cells_ref, flat_ref, *rim_refs):
        flat_ref[0] = forward_ref[...].astype(f32).reshape(ports * tiles, cells)
        flat_ref[1] = adjoint_ref[...].astype(f32).reshape(ports * tiles, cells)
        for pairing, rim_ref in zip(row_pairs, rim_refs):
            side = Side(pairing, "row", tiles_x)
            for sweep in range(2):
                for y in range(tiles_y):
                    rim_ref[sweep, y] = source_tile(flat_ref, cells_ref, sweep, side.edge, y)

    port_row = port_cells.reshape(1, ports)
    flat, *rims = call(
        rims_kernel,
        [((2, ports * tiles, cells), f32)] + [((2, tiles_y, ports, cells), bf16)] * len(row_pairs),
        sources.reshape(ports, tiles, cells),
        adjoint_sources.reshape(ports, tiles, cells),
        port_row,
    )
    source_rims = [swapped(rim, of_row=pairing) for rim, pairing in zip(rims, row_pairs)]

    def setup_kernel(pattern_ref, coupling_ref, group_ref, flat_ref, cells_ref, blocks_ref, source_ref, front_ref, kappa_ref, member_ref):
        for sweep in range(2):
            for x in range(tiles_x):
                for y in range(tiles_y):
                    source_ref[sweep, x * tiles_y + y] = source_tile(flat_ref, cells_ref, sweep, x, y)

        def mask_block(index, carry):
            for offset in range(OFFSETS):
                present = pattern_ref[index, offset] > 0
                front_ref[index, offset] = jnp.where(present, blocks_ref[index, offset], jnp.zeros((cells, cells), bf16))
            return carry

        lax.fori_loop(0, tiles, mask_block, 0)
        pos = lax.axis_index("layer")
        own = coupling_ref[group_ref[pos]]
        following = coupling_ref[group_ref[jnp.minimum(pos + 1, layers - 1)]]
        kappa_ref[0] = jnp.full((8, cells), own, f32)
        kappa_ref[1] = jnp.full((8, cells), following, f32)
        for g in range(groups):
            for l in range(layers):
                member_ref[g, l] = jnp.full((tiles, cells), jnp.where(group_ref[l] == g, 1.0, 0.0), f32)

    source, front, kappa, member = call(
        setup_kernel,
        [
            ((2, tiles, ports, cells), bf16),
            ((tiles, OFFSETS, cells, cells), bf16),
            ((2, 8, cells), f32),
            ((groups, layers, tiles, cells), f32),
        ],
        pattern.reshape(tiles, OFFSETS),
        coupling,
        layer_group,
        flat,
        port_row,
        blocks.reshape(tiles, OFFSETS, cells, cells),
        smem=3,
    )

    def wave_kernel(step, *refs):
        source_ref, kappa_ref = refs[:2]
        refs = refs[2:]
        halo_refs, refs = refs[: len(row_pairs)], refs[len(row_pairs) :]
        if step > 0:
            field_ref, refs = refs[0], refs[1:]
            field_rims, refs = refs[: len(row_pairs)], refs[len(row_pairs) :]
        wave_ref, rim_refs = refs[0], refs[1:]

        @pl.when(is_active(step))
        def _():
            sweep = sweep_of(step)

            def wave(base, field):
                if step == 0:
                    return base
                factor = kappa_ref[sweep, 0:1, :]
                return (base.astype(f32) + factor * field.astype(f32)).astype(bf16)

            for x in range(tiles_x):
                for y in range(tiles_y):
                    t = x * tiles_y + y
                    wave_ref[x, y] = wave(source_ref[sweep, t], field_ref[t] if step > 0 else None)
            for h, pairing in enumerate(row_pairs):
                side = Side(pairing, "row", tiles_x)
                for y in range(tiles_y):
                    value = wave(halo_refs[h][sweep, y], field_rims[h][y] if step > 0 else None)
                    if side.real is not None:
                        value = jnp.where(side.real, value, jnp.zeros_like(value))
                    wave_ref[tiles_x + h, y] = value
            for pairing, rim_ref in zip(col_pairs, rim_refs):
                edge = Side(pairing, "col", tiles_y).edge
                for x in range(ext):
                    rim_ref[x] = wave_ref[x, edge]

    def product(lhs, rhs):
        return jnp.dot(lhs, rhs, preferred_element_type=f32)

    def inner_kernel(step, wave_ref, front_ref, sum_ref):
        @pl.when(is_active(step))
        def _():
            for y in range(tiles_y):
                low, high = max(y - 1, 0), min(y + 1, tiles_y - 1)
                width = high - low + 1
                first = low - y + 1
                beside = [
                    jnp.concatenate([wave_ref[x, j] for j in range(low, high + 1)], axis=1) for x in range(ext)
                ]
                for x in range(tiles_x):
                    reach = [a for a in (-1, 0, 1) if 0 <= x + a < tiles_x]
                    lhs = jnp.concatenate([beside[x + a] for a in reach], axis=1)
                    rhs = jnp.concatenate(
                        [
                            front_ref[x * tiles_y + y, 3 * (a + 1) + first : 3 * (a + 1) + first + width].reshape(
                                width * cells, cells
                            )
                            for a in reach
                        ],
                        axis=0,
                    )
                    sum_ref[x * tiles_y + y] = product(lhs, rhs)
                for h, pairing in enumerate(row_pairs):
                    side = Side(pairing, "row", tiles_x)
                    t = side.edge * tiles_y + y
                    rhs = front_ref[t, pl.ds(3 * (side.step + 1) + first, width)].reshape(width * cells, cells)
                    sum_ref[t] += product(beside[tiles_x + h], rhs)

    def outer_kernel(step, *refs):
        front_ref = refs[1]
        halo_refs, refs = refs[2 : 2 + len(col_pairs)], refs[2 + len(col_pairs) :]
        if step == layers - 1:
            earlier, refs = refs[: layers - 1], refs[layers - 1 :]
        sum_ref, field_ref, refs = refs[0], refs[1], refs[2:]

        @pl.when(is_active(step))
        def _():
            for pairing, halo_ref in zip(col_pairs, halo_refs):
                across = Side(pairing, "col", tiles_y)

                def add(across=across, halo_ref=halo_ref):
                    for x in range(tiles_x):
                        t = x * tiles_y + across.edge
                        reach = [a for a in (-1, 0, 1) if 0 <= x + a < tiles_x]
                        lhs = jnp.concatenate([halo_ref[x + a] for a in reach], axis=1)
                        rhs = jnp.concatenate([front_ref[t, 3 * (a + 1) + 1 + across.step] for a in reach], axis=0)
                        sum_ref[t] += product(lhs, rhs)
                    for h, row_pairing in enumerate(row_pairs):
                        side = Side(row_pairing, "row", tiles_x)
                        t = side.edge * tiles_y + across.edge
                        sum_ref[t] += product(halo_ref[tiles_x + h], front_ref[t, 3 * (side.step + 1) + 1 + across.step])

                across.when(add)
            for t in range(tiles):
                field_ref[t] = sum_ref[t].astype(bf16)
            if step < layers - 1:
                for pairing, rim_ref in zip(row_pairs, refs):
                    edge = Side(pairing, "row", tiles_x).edge
                    rim_ref[...] = field_ref[pl.ds(edge * tiles_y, tiles_y)]

        if step == layers - 1:
            pos = lax.axis_index("layer")
            first = jnp.minimum(pos, layers - 1 - pos)
            for k in range(layers // 2):

                @pl.when(first == k)
                def _(k=k):
                    one, other = earlier[k], field_ref if k == 0 else earlier[layers - 1 - k]
                    for t in range(tiles):
                        both = one[t].astype(f32) * other[t].astype(f32)
                        refs[0][t : t + 1, :] = jnp.sum(both, axis=0, keepdims=True) * intersection_scale

    fields, received, received_rims = [], None, []
    for step in range(layers):
        wave, *rims = call(
            functools.partial(wave_kernel, step),
            [((ext, tiles_y, ports, cells), bf16)] + [((ext, ports, cells), bf16)] * len(col_pairs),
            source,
            kappa,
            *source_rims,
            *([received, *received_rims] if step > 0 else []),
        )
        halos = [swapped(rim, of_col=pairing) for rim, pairing in zip(rims, col_pairs)]
        (summed,) = call(
            functools.partial(inner_kernel, step), [((tiles, ports, cells), f32)], wave, front
        )
        last = step == layers - 1
        _, field, *extra = call(
            functools.partial(outer_kernel, step),
            [((tiles, ports, cells), f32), ((tiles, ports, cells), bf16)]
            + ([((tiles, cells), f32)] if last else [((tiles_y, ports, cells), bf16)] * len(row_pairs)),
            summed,
            front,
            *halos,
            *(fields if last else []),
            aliases={0: 0},
        )
        fields.append(field)
        if not last:
            partner = lambda l: l ^ 1 if step % 2 == 0 else (((l + 1) ^ 1) - 1) % layers
            received = swapped(field, of_layer=partner)
            received_rims = [
                swapped(rim, of_layer=partner, of_row=pairing) for rim, pairing in zip(extra, row_pairs)
            ]
    intersection = extra[0]

    def fields_kernel(*refs):
        field_refs, (forward_ref, adjoint_ref, flat_ref) = refs[:layers], refs[layers:]
        pos = lax.axis_index("layer")
        for out_ref, active in ((forward_ref, lambda s: s), (adjoint_ref, lambda s: layers - 1 - s)):
            for step in range(layers):

                @pl.when(pos == active(step))
                def _(step=step):
                    for t in range(tiles):
                        flat_ref[pl.ds(t, ports, stride=tiles), :] = field_refs[step][t].astype(f32)

            out_ref[...] = flat_ref[...].reshape(ports, tiles, cells).astype(bf16)

    forward, adjoint = call(
        fields_kernel,
        [((ports, tiles, cells), bf16)] * 2,
        *fields,
        scratch=[pltpu.VMEM((ports * tiles, cells), f32)],
    )

    if layers == 4:
        parts = [intersection] + [swapped(intersection, of_layer=lambda l, m=m: l ^ m) for m in range(1, layers)]

        def gradient_kernel(*refs):
            part_refs, member_ref, out_ref = refs[:layers], refs[layers], refs[layers + 1]
            pos = lax.axis_index("layer")
            for g in range(groups):
                total = jnp.zeros((tiles, cells), f32)
                for m in range(layers):
                    total = total + member_ref[g, pos ^ m] * part_refs[m][...]
                for x in range(tiles_x):
                    out_ref[g, x] = total[x * tiles_y : (x + 1) * tiles_y]

        (gradient,) = call(
            gradient_kernel, [((groups, tiles_x, tiles_y, cells), f32)], *parts, member
        )
    else:
        selected = lax.dynamic_index_in_dim(member, lax.axis_index("layer"), 1, keepdims=False)
        gradient = lax.psum(selected * intersection[None], "layer").reshape(groups, tiles_x, tiles_y, cells)
    shape = (1, ports, tiles_x, tiles_y, cells)
    return (forward.reshape(shape), adjoint.reshape(shape), gradient)


def solution(mesh):
    placed = (
        P("layer", None, "row", "col", None),
        P("layer", None, "row", "col", None),
        P("layer", "row", "col", None, None, None),
        P("layer", "row", "col", None),
        P(),
        P(),
        P(),
    )
    return jax.shard_map(
        local,
        mesh=mesh,
        in_specs=placed,
        out_specs=(
            P("layer", None, "row", "col", None),
            P("layer", None, "row", "col", None),
            P(None, "row", "col", None),
        ),
        check_vma=False,
    )
```

time: 145 us -> 62.4 us (0.43)
  the two profiles are of different devices: /device:TPU:6 before, /device:TPU:0 now
where the time goes in v1:
time: 62.4 us; the launch traced here: 62.2 us
  waiting for transfers between devices  25.8 us (41%)
  starting transfers between devices  24.8 us (40%)
  local copies, waits for them, and re-layouts  6.12 us (10%)
  Pallas kernels  4.65 us (7%)
  between operations  0.75 us (1%)
    ppermute x18, waiting for transfers between devices, swapped(): return lax.ppermute(array, AXES, route(**where))  25.8 us
    ppermute x18, starting transfers between devices, swapped(): return lax.ppermute(array, AXES, route(**where))  24.8 us
    unnamed x14, local copies, waits for them, and re-layouts  6.12 us
    pallas_call x16, Pallas kernels, call(): pl.pallas_call(kernel, out_shape=[jax.ShapeDtypeStruct(shape, dtype) for...  4.65 us
  transfers between devices with their start and end apart: 18, of which 9 were waited for; matrix products, arithmetic and copies ran while one was open for 0% of the time, Pallas kernels for 5%

profile of v1, /device:TPU:0, one launch (start us, length us, event | category | flops | bytes accessed | tf_op | source)
XLA Modules:
  0.0 62.2 jit_solution(13828942698127661155)
XLA Ops:
  0.6 0.9 %copy-done.1 = bf16[1,64,2,4,128]{4,3,2,1,0:T(4,128)(2,1)S(1)} copy-done((bf16[1,64,2,4,128]{4,3,2,1,0:T(4,128)(2,1)S(1)}, bf16[1,64,2,4,128]{4,3,2,1,0:T(4,128)(2,1)}, u32[]{:S(2)}) %copy-start.1) | copy-done | bytes 131096
  1.5 0.9 %copy-done.2 = bf16[1,64,2,4,128]{4,3,2,1,0:T(4,128)(2,1)S(1)} copy-done((bf16[1,64,2,4,128]{4,3,2,1,0:T(4,128)(2,1)S(1)}, bf16[1,64,2,4,128]{4,3,2,1,0:T(4,128)(2,1)}, u32[]{:S(2)}) %copy-start.2) | copy-done | bytes 131096
  2.4 0.7 %copy-done.4 = s32[64]{0:T(128)S(1)} copy-done((s32[64]{0:T(128)S(1)}, s32[64]{0:T(128)}, u32[]{:S(2)}) %copy-start.4) | copy-done | bytes 280
  3.1 0.2 shard_map.94
  3.3 3.0 %collective-permute-start = (bf16[2,4,64,128]{3,2,1,0:T(8,128)(2,1)S(1)}, bf16[2,4,64,128]{3,2,1,0:T(8,128)(2,1)S(1)}, u32[]{:S(2)}, u32[]{:S(2)}) collective-permute-start(bf16[2,4,64,128]{3,2,1,0:T(8,128)(2,1)S(1)} %get-tuple-element.34), channel_id=1, source_target_pairs={{0,4},{1,5},{2,6},{3,7},{4,0},{5,1},{6,2},{7,3},{8,12},{9,13},{10,... | collective-permute-start | bytes 393224 | tf_op jit(solution)/shard_map/ppermute | solution.py:85
  6.4 1.7 %copy-done = bf16[1,2,4,9,128,128]{5,4,3,2,1,0:T(8,128)(2,1)S(1)} copy-done((bf16[1,2,4,9,128,128]{5,4,3,2,1,0:T(8,128)(2,1)S(1)}, bf16[1,2,4,9,128,128]{5,4,3,2,1,0:T(8,128)(2,1)}, u32[]{:S(2)}) %copy-start) | copy-done | bytes 2359320
  8.0 0.7 %copy-done.3 = s32[1,2,4,9]{3,2,1,0:T(4,128)S(1)} copy-done((s32[1,2,4,9]{3,2,1,0:T(4,128)S(1)}, s32[1,2,4,9]{3,2,1,0:T(4,128)}, u32[]{:S(2)}) %copy-start.3) | copy-done | bytes 312
  8.7 0.7 %copy-done.5 = f32[4]{0:T(128)S(1)} copy-done((f32[4]{0:T(128)S(1)}, f32[4]{0:T(128)}, u32[]{:S(2)}) %copy-start.5) | copy-done | bytes 40
  9.4 0.7 %copy-done.6 = s32[4]{0:T(128)S(1)} copy-done((s32[4]{0:T(128)S(1)}, s32[4]{0:T(128)}, u32[]{:S(2)}) %copy-start.6) | copy-done | bytes 40
  10.0 1.5 %shard_map.95 = (bf16[2,8,64,128]{3,2,1,0:T(8,128)(2,1)S(1)}, bf16[8,9,128,128]{3,2,1,0:T(8,128)(2,1)S(1)}, f32[2,8,128]{2,1,0:T(8,128)S(1)}, f32[4,4,8,128]{3,2,1,0:T(8,128)S(1)}) custom-call(s32[8,9]{1,0:T(8,128)S(1)} %bitcast.10, f32[4]{0:T(128)S(1)} %copy-done.5, s32[4]{0:T(128)S(1)} %copy-done.6, f32[2,512,128]{2,1,0:T(8,128)S(1)} %get-tuple-element.31.flat_ref, ...), custom_call_target="tpu_custom_call" | custom-call | tf_op jit(solution)/shard_map/pallas_call | solution.py:21
  11.6 0.1 collective-permute-start.1
  11.7 1.6 %collective-permute-start.2 = (bf16[3,64,128]{2,1,0:T(8,128)(2,1)S(1)}, bf16[3,64,128]{2,1,0:T(8,128)(2,1)S(1)}, u32[]{:S(2)}, u32[]{:S(2)}) collective-permute-start(bf16[3,64,128]{2,1,0:T(8,128)(2,1)S(1)} %get-tuple-element.38), channel_id=1, source_target_pairs={{0,3},{1,2},{2,1},{3,0},{4,7},{5,6},{6,5},{7,4},{8,11},{9,10},{10,... | collective-permute-start | bytes 147464 | tf_op jit(solution)/shard_map/ppermute | solution.py:85
  13.3 0.4 shard_map.97.refs_0_
  13.8 0.0 collective-permute-done.1.refs_2_
  13.8 1.5 %collective-permute-done.2.refs_3_ = bf16[3,64,128]{2,1,0:T(8,128)(2,1)S(1)} collective-permute-done((bf16[3,64,128]{2,1,0:T(8,128)(2,1)S(1)}, bf16[3,64,128]{2,1,0:T(8,128)(2,1)S(1)}, u32[]{:S(2)}, u32[]{:S(2)}) %collective-permute-start.2) | collective-permute-done | bytes 49184 | tf_op jit(solution)/shard_map/ppermute | solution.py:85
  15.3 0.2 shard_map.98
  15.5 1.4 %collective-permute-start.3 = (bf16[8,64,128]{2,1,0:T(8,128)(2,1)S(1)}, bf16[8,64,128]{2,1,0:T(8,128)(2,1)S(1)}, u32[]{:S(2)}, u32[]{:S(2)}) collective-permute-start(bf16[8,64,128]{2,1,0:T(8,128)(2,1)S(1)} %get-tuple-element.39.refs_4_.refs_0_), channel_id=1, source_target_pairs={{0,8},{1,9},{2,10},{3,11},{4,12},{5,13},{6,14},{7,15},{8,0},{9,1},... | collective-permute-start | bytes 393224 | tf_op jit(solution)/shard_map/ppermute | solution.py:85
  16.9 0.7 %collective-permute-start.4 = (bf16[4,64,128]{2,1,0:T(8,128)(2,1)S(1)}, bf16[4,64,128]{2,1,0:T(8,128)(2,1)S(1)}, u32[]{:S(2)}, u32[]{:S(2)}) collective-permute-start(bf16[4,64,128]{2,1,0:T(8,128)(2,1)S(1)} %get-tuple-element.40), channel_id=1, source_target_pairs={{0,12},{1,13},{2,14},{3,15},{4,8},{5,9},{6,10},{7,11},{8,4},{9,5},... | collective-permute-start | bytes 196616 | tf_op jit(solution)/shard_map/ppermute | solution.py:85
  17.6 5.0 %collective-permute-done.4.refs_4_ = bf16[4,64,128]{2,1,0:T(8,128)(2,1)S(1)} collective-permute-done((bf16[4,64,128]{2,1,0:T(8,128)(2,1)S(1)}, bf16[4,64,128]{2,1,0:T(8,128)(2,1)S(1)}, u32[]{:S(2)}, u32[]{:S(2)}) %collective-permute-start.4) | collective-permute-done | bytes 65568 | tf_op jit(solution)/shard_map/ppermute | solution.py:85
  22.6 0.0 collective-permute-done.3.refs_3_
  22.6 1.7 %collective-permute-start.6 = (bf16[3,64,128]{2,1,0:T(8,128)(2,1)S(1)}, bf16[3,64,128]{2,1,0:T(8,128)(2,1)S(1)}, u32[]{:S(2)}, u32[]{:S(2)}) collective-permute-start(bf16[3,64,128]{2,1,0:T(8,128)(2,1)S(1)} %get-tuple-element.43), channel_id=1, source_target_pairs={{0,3},{1,2},{2,1},{3,0},{4,7},{5,6},{6,5},{7,4},{8,11},{9,10},{10,... | collective-permute-start | bytes 147464 | tf_op jit(solution)/shard_map/ppermute | solution.py:85
  24.4 0.0 collective-permute-done.5.refs_2_
  24.4 1.8 %collective-permute-done.6.refs_3_ = bf16[3,64,128]{2,1,0:T(8,128)(2,1)S(1)} collective-permute-done((bf16[3,64,128]{2,1,0:T(8,128)(2,1)S(1)}, bf16[3,64,128]{2,1,0:T(8,128)(2,1)S(1)}, u32[]{:S(2)}, u32[]{:S(2)}) %collective-permute-start.6) | collective-permute-done | bytes 49184 | tf_op jit(solution)/shard_map/ppermute | solution.py:85
  26.2 3.9 %collective-permute-start.7 = (bf16[8,64,128]{2,1,0:T(8,128)(2,1)S(1)}, bf16[8,64,128]{2,1,0:T(8,128)(2,1)S(1)}, u32[]{:S(2)}, u32[]{:S(2)}) collective-permute-start(bf16[8,64,128]{2,1,0:T(8,128)(2,1)S(1)} %get-tuple-element.44.refs_5_.refs_1_), channel_id=1, source_target_pairs={{0,24},{1,25},{2,26},{3,27},{4,28},{5,29},{6,30},{7,31},{8,16},{9,... | collective-permute-start | bytes 393224 | tf_op jit(solution)/shard_map/ppermute | solution.py:85
  30.1 1.2 %collective-permute-start.8 = (bf16[4,64,128]{2,1,0:T(8,128)(2,1)S(1)}, bf16[4,64,128]{2,1,0:T(8,128)(2,1)S(1)}, u32[]{:S(2)}, u32[]{:S(2)}) collective-permute-start(bf16[4,64,128]{2,1,0:T(8,128)(2,1)S(1)} %get-tuple-element.45), channel_id=1, source_target_pairs={{0,28},{1,29},{2,30},{3,31},{4,24},{5,25},{6,26},{7,27},{8,20},{9,... | collective-permute-start | bytes 196616 | tf_op jit(solution)/shard_map/ppermute | solution.py:85
  31.3 5.8 %collective-permute-done.8.refs_4_ = bf16[4,64,128]{2,1,0:T(8,128)(2,1)S(1)} collective-permute-done((bf16[4,64,128]{2,1,0:T(8,128)(2,1)S(1)}, bf16[4,64,128]{2,1,0:T(8,128)(2,1)S(1)}, u32[]{:S(2)}, u32[]{:S(2)}) %collective-permute-start.8) | collective-permute-done | bytes 65568 | tf_op jit(solution)/shard_map/ppermute | solution.py:85
  37.1 0.0 collective-permute-start.9
  37.1 1.5 %collective-permute-start.10 = (bf16[3,64,128]{2,1,0:T(8,128)(2,1)S(1)}, bf16[3,64,128]{2,1,0:T(8,128)(2,1)S(1)}, u32[]{:S(2)}, u32[]{:S(2)}) collective-permute-start(bf16[3,64,128]{2,1,0:T(8,128)(2,1)S(1)} %get-tuple-element.48), channel_id=1, source_target_pairs={{0,3},{1,2},{2,1},{3,0},{4,7},{5,6},{6,5},{7,4},{8,11},{9,10},{10,... | collective-permute-start | bytes 147464 | tf_op jit(solution)/shard_map/ppermute | solution.py:85
  38.6 0.0 collective-permute-done.9.refs_2_
  38.6 2.1 %collective-permute-done.10.refs_3_ = bf16[3,64,128]{2,1,0:T(8,128)(2,1)S(1)} collective-permute-done((bf16[3,64,128]{2,1,0:T(8,128)(2,1)S(1)}, bf16[3,64,128]{2,1,0:T(8,128)(2,1)S(1)}, u32[]{:S(2)}, u32[]{:S(2)}) %collective-permute-start.10) | collective-permute-done | bytes 49184 | tf_op jit(solution)/shard_map/ppermute | solution.py:85
  40.7 4.0 %collective-permute-start.11 = (bf16[8,64,128]{2,1,0:T(8,128)(2,1)S(1)}, bf16[8,64,128]{2,1,0:T(8,128)(2,1)S(1)}, u32[]{:S(2)}, u32[]{:S(2)}) collective-permute-start(bf16[8,64,128]{2,1,0:T(8,128)(2,1)S(1)} %get-tuple-element.49.refs_6_.refs_2_), channel_id=1, source_target_pairs={{0,8},{1,9},{2,10},{3,11},{4,12},{5,13},{6,14},{7,15},{8,0},{9,1},... | collective-permute-start | bytes 393224 | tf_op jit(solution)/shard_map/ppermute | solution.py:85
  44.7 0.0 collective-permute-start.12
  44.8 5.6 %collective-permute-done.12.refs_4_ = bf16[4,64,128]{2,1,0:T(8,128)(2,1)S(1)} collective-permute-done((bf16[4,64,128]{2,1,0:T(8,128)(2,1)S(1)}, bf16[4,64,128]{2,1,0:T(8,128)(2,1)S(1)}, u32[]{:S(2)}, u32[]{:S(2)}) %collective-permute-start.12) | collective-permute-done | bytes 65568 | tf_op jit(solution)/shard_map/ppermute | solution.py:85
  50.3 0.0 collective-permute-done.11.refs_3_
  50.3 0.1 shard_map.105
  50.4 0.1 collective-permute-start.13
  50.5 1.2 %collective-permute-start.14 = (bf16[3,64,128]{2,1,0:T(8,128)(2,1)S(1)}, bf16[3,64,128]{2,1,0:T(8,128)(2,1)S(1)}, u32[]{:S(2)}, u32[]{:S(2)}) collective-permute-start(bf16[3,64,128]{2,1,0:T(8,128)(2,1)S(1)} %get-tuple-element.53), channel_id=1, source_target_pairs={{0,3},{1,2},{2,1},{3,0},{4,7},{5,6},{6,5},{7,4},{8,11},{9,10},{10,... | collective-permute-start | bytes 147464 | tf_op jit(solution)/shard_map/ppermute | solution.py:85
  51.7 0.4 shard_map.106.refs_0_
  52.1 0.0 collective-permute-done.13.refs_2_
  52.1 1.9 %collective-permute-done.14.refs_3_ = bf16[3,64,128]{2,1,0:T(8,128)(2,1)S(1)} collective-permute-done((bf16[3,64,128]{2,1,0:T(8,128)(2,1)S(1)}, bf16[3,64,128]{2,1,0:T(8,128)(2,1)S(1)}, u32[]{:S(2)}, u32[]{:S(2)}) %collective-permute-start.14) | collective-permute-done | bytes 49184 | tf_op jit(solution)/shard_map/ppermute | solution.py:85
  54.1 0.2 shard_map.107
  54.3 2.7 %collective-permute-start.17 = (f32[8,128]{1,0:T(8,128)S(1)}, f32[8,128]{1,0:T(8,128)S(1)}, u32[]{:S(2)}, u32[]{:S(2)}) collective-permute-start(f32[8,128]{1,0:T(8,128)S(1)} %get-tuple-element.57.refs_0_), channel_id=1, source_target_pairs={{0,24},{1,25},{2,26},{3,27},{4,28},{5,29},{6,30},{7,31},{8,16},{9,... | collective-permute-start | bytes 12296 | tf_op jit(solution)/shard_map/ppermute | solution.py:85
  57.0 0.2 collective-permute-start.16
  57.2 1.5 %collective-permute-start.15 = (f32[8,128]{1,0:T(8,128)S(1)}, f32[8,128]{1,0:T(8,128)S(1)}, u32[]{:S(2)}, u32[]{:S(2)}) collective-permute-start(f32[8,128]{1,0:T(8,128)S(1)} %get-tuple-element.57.refs_0_), channel_id=1, source_target_pairs={{0,8},{1,9},{2,10},{3,11},{4,12},{5,13},{6,14},{7,15},{8,0},{9,1},... | collective-permute-start | bytes 12296 | tf_op jit(solution)/shard_map/ppermute | solution.py:85
  58.8 0.8 %shard_map.108 = (bf16[64,8,128]{2,1,0:T(8,128)(2,1)}, bf16[64,8,128]{2,1,0:T(8,128)(2,1)}) custom-call(bf16[8,64,128]{2,1,0:T(8,128)(2,1)S(1)} %get-tuple-element.39.refs_4_.refs_0_, bf16[8,64,128]{2,1,0:T(8,128)(2,1)S(1)} %get-tuple-element.44.refs_5_.refs_1_, bf16[8,64,128]{2,1,0:T(8,128)(2,1)S(1)} %get-tuple-element.49.refs_6_.refs_2_, ...), custom_call_target="tpu_custom_call" | custom-call | tf_op jit(solution)/shard_map/pallas_call | solution.py:21
  59.6 0.2 collective-permute-done.17.refs_3_
  59.8 1.7 %collective-permute-done.16.refs_2_ = f32[8,128]{1,0:T(8,128)S(1)} collective-permute-done((f32[8,128]{1,0:T(8,128)S(1)}, f32[8,128]{1,0:T(8,128)S(1)}, u32[]{:S(2)}, u32[]{:S(2)}) %collective-permute-start.16) | collective-permute-done | bytes 4128 | tf_op jit(solution)/shard_map/ppermute | solution.py:85
  61.5 0.6 shard_map.109
  (18 shorter events, 0.1 us)
Async XLA Ops:
  0.6 0.9 %copy-start.1 = (bf16[1,64,2,4,128]{4,3,2,1,0:T(4,128)(2,1)S(1)}, bf16[1,64,2,4,128]{4,3,2,1,0:T(4,128)(2,1)}, u32[]{:S(2)}) copy-start(bf16[1,64,2,4,128]{4,3,2,1,0:T(4,128)(2,1)} %param.7) | copy-start | bytes 393220
  1.5 0.9 %copy-start.2 = (bf16[1,64,2,4,128]{4,3,2,1,0:T(4,128)(2,1)S(1)}, bf16[1,64,2,4,128]{4,3,2,1,0:T(4,128)(2,1)}, u32[]{:S(2)}) copy-start(bf16[1,64,2,4,128]{4,3,2,1,0:T(4,128)(2,1)} %param.8) | copy-start | bytes 393220
  2.4 0.7 %copy-start.4 = (s32[64]{0:T(128)S(1)}, s32[64]{0:T(128)}, u32[]{:S(2)}) copy-start(s32[64]{0:T(128)} %param.13) | copy-start | bytes 772
  3.3 8.3 %collective-permute-start = (bf16[2,4,64,128]{3,2,1,0:T(8,128)(2,1)S(1)}, bf16[2,4,64,128]{3,2,1,0:T(8,128)(2,1)S(1)}, u32[]{:S(2)}, u32[]{:S(2)}) collective-permute-start(bf16[2,4,64,128]{3,2,1,0:T(8,128)(2,1)S(1)} %get-tuple-element.34), channel_id=1, source_target_pairs={{0,4},{1,5},{2,6},{3,7},{4,0},{5,1},{6,2},{7,3},{8,12},{9,13},{10,... | collective-permute-start | bytes 393224 | tf_op jit(solution)/shard_map/ppermute | solution.py:85
  6.4 1.7 %copy-start = (bf16[1,2,4,9,128,128]{5,4,3,2,1,0:T(8,128)(2,1)S(1)}, bf16[1,2,4,9,128,128]{5,4,3,2,1,0:T(8,128)(2,1)}, u32[]{:S(2)}) copy-start(bf16[1,2,4,9,128,128]{5,4,3,2,1,0:T(8,128)(2,1)} %param.9) | copy-start | bytes 7077892
  8.0 0.7 %copy-start.3 = (s32[1,2,4,9]{3,2,1,0:T(4,128)S(1)}, s32[1,2,4,9]{3,2,1,0:T(4,128)}, u32[]{:S(2)}) copy-start(s32[1,2,4,9]{3,2,1,0:T(4,128)} %param.10) | copy-start | bytes 868
  8.7 0.7 %copy-start.5 = (f32[4]{0:T(128)S(1)}, f32[4]{0:T(128)}, u32[]{:S(2)}) copy-start(f32[4]{0:T(128)} %coupling_ref.1) | copy-start | bytes 52
  9.4 0.7 %copy-start.6 = (s32[4]{0:T(128)S(1)}, s32[4]{0:T(128)}, u32[]{:S(2)}) copy-start(s32[4]{0:T(128)} %group_ref.1) | copy-start | bytes 52
  11.6 2.1 %collective-permute-start.1 = (bf16[3,64,128]{2,1,0:T(8,128)(2,1)S(1)}, bf16[3,64,128]{2,1,0:T(8,128)(2,1)S(1)}, u32[]{:S(2)}, u32[]{:S(2)}) collective-permute-start(bf16[3,64,128]{2,1,0:T(8,128)(2,1)S(1)} %get-tuple-element.37), channel_id=1, source_target_pairs={{0,1},{1,0},{2,3},{3,2},{4,5},{5,4},{6,7},{7,6},{8,9},{9,8},{10,11... | collective-permute-start | bytes 147464 | tf_op jit(solution)/shard_map/ppermute | solution.py:85
  11.7 3.6 %collective-permute-start.2 = (bf16[3,64,128]{2,1,0:T(8,128)(2,1)S(1)}, bf16[3,64,128]{2,1,0:T(8,128)(2,1)S(1)}, u32[]{:S(2)}, u32[]{:S(2)}) collective-permute-start(bf16[3,64,128]{2,1,0:T(8,128)(2,1)S(1)} %get-tuple-element.38), channel_id=1, source_target_pairs={{0,3},{1,2},{2,1},{3,0},{4,7},{5,6},{6,5},{7,4},{8,11},{9,10},{10,... | collective-permute-start | bytes 147464 | tf_op jit(solution)/shard_map/ppermute | solution.py:85
  15.5 7.1 %collective-permute-start.3 = (bf16[8,64,128]{2,1,0:T(8,128)(2,1)S(1)}, bf16[8,64,128]{2,1,0:T(8,128)(2,1)S(1)}, u32[]{:S(2)}, u32[]{:S(2)}) collective-permute-start(bf16[8,64,128]{2,1,0:T(8,128)(2,1)S(1)} %get-tuple-element.39.refs_4_.refs_0_), channel_id=1, source_target_pairs={{0,8},{1,9},{2,10},{3,11},{4,12},{5,13},{6,14},{7,15},{8,0},{9,1},... | collective-permute-start | bytes 393224 | tf_op jit(solution)/shard_map/ppermute | solution.py:85
  16.9 5.8 %collective-permute-start.4 = (bf16[4,64,128]{2,1,0:T(8,128)(2,1)S(1)}, bf16[4,64,128]{2,1,0:T(8,128)(2,1)S(1)}, u32[]{:S(2)}, u32[]{:S(2)}) collective-permute-start(bf16[4,64,128]{2,1,0:T(8,128)(2,1)S(1)} %get-tuple-element.40), channel_id=1, source_target_pairs={{0,12},{1,13},{2,14},{3,15},{4,8},{5,9},{6,10},{7,11},{8,4},{9,5},... | collective-permute-start | bytes 196616 | tf_op jit(solution)/shard_map/ppermute | solution.py:85
  22.6 1.7 %collective-permute-start.5 = (bf16[3,64,128]{2,1,0:T(8,128)(2,1)S(1)}, bf16[3,64,128]{2,1,0:T(8,128)(2,1)S(1)}, u32[]{:S(2)}, u32[]{:S(2)}) collective-permute-start(bf16[3,64,128]{2,1,0:T(8,128)(2,1)S(1)} %get-tuple-element.42), channel_id=1, source_target_pairs={{0,1},{1,0},{2,3},{3,2},{4,5},{5,4},{6,7},{7,6},{8,9},{9,8},{10,11... | collective-permute-start | bytes 147464 | tf_op jit(solution)/shard_map/ppermute | solution.py:85
  22.6 3.6 %collective-permute-start.6 = (bf16[3,64,128]{2,1,0:T(8,128)(2,1)S(1)}, bf16[3,64,128]{2,1,0:T(8,128)(2,1)S(1)}, u32[]{:S(2)}, u32[]{:S(2)}) collective-permute-start(bf16[3,64,128]{2,1,0:T(8,128)(2,1)S(1)} %get-tuple-element.43), channel_id=1, source_target_pairs={{0,3},{1,2},{2,1},{3,0},{4,7},{5,6},{6,5},{7,4},{8,11},{9,10},{10,... | collective-permute-start | bytes 147464 | tf_op jit(solution)/shard_map/ppermute | solution.py:85
  26.2 10.9 %collective-permute-start.7 = (bf16[8,64,128]{2,1,0:T(8,128)(2,1)S(1)}, bf16[8,64,128]{2,1,0:T(8,128)(2,1)S(1)}, u32[]{:S(2)}, u32[]{:S(2)}) collective-permute-start(bf16[8,64,128]{2,1,0:T(8,128)(2,1)S(1)} %get-tuple-element.44.refs_5_.refs_1_), channel_id=1, source_target_pairs={{0,24},{1,25},{2,26},{3,27},{4,28},{5,29},{6,30},{7,31},{8,16},{9,... | collective-permute-start | bytes 393224 | tf_op jit(solution)/shard_map/ppermute | solution.py:85
  30.1 7.0 %collective-permute-start.8 = (bf16[4,64,128]{2,1,0:T(8,128)(2,1)S(1)}, bf16[4,64,128]{2,1,0:T(8,128)(2,1)S(1)}, u32[]{:S(2)}, u32[]{:S(2)}) collective-permute-start(bf16[4,64,128]{2,1,0:T(8,128)(2,1)S(1)} %get-tuple-element.45), channel_id=1, source_target_pairs={{0,28},{1,29},{2,30},{3,31},{4,24},{5,25},{6,26},{7,27},{8,20},{9,... | collective-permute-start | bytes 196616 | tf_op jit(solution)/shard_map/ppermute | solution.py:85
  37.1 1.5 %collective-permute-start.9 = (bf16[3,64,128]{2,1,0:T(8,128)(2,1)S(1)}, bf16[3,64,128]{2,1,0:T(8,128)(2,1)S(1)}, u32[]{:S(2)}, u32[]{:S(2)}) collective-permute-start(bf16[3,64,128]{2,1,0:T(8,128)(2,1)S(1)} %get-tuple-element.47), channel_id=1, source_target_pairs={{0,1},{1,0},{2,3},{3,2},{4,5},{5,4},{6,7},{7,6},{8,9},{9,8},{10,11... | collective-permute-start | bytes 147464 | tf_op jit(solution)/shard_map/ppermute | solution.py:85
  37.1 3.6 %collective-permute-start.10 = (bf16[3,64,128]{2,1,0:T(8,128)(2,1)S(1)}, bf16[3,64,128]{2,1,0:T(8,128)(2,1)S(1)}, u32[]{:S(2)}, u32[]{:S(2)}) collective-permute-start(bf16[3,64,128]{2,1,0:T(8,128)(2,1)S(1)} %get-tuple-element.48), channel_id=1, source_target_pairs={{0,3},{1,2},{2,1},{3,0},{4,7},{5,6},{6,5},{7,4},{8,11},{9,10},{10,... | collective-permute-start | bytes 147464 | tf_op jit(solution)/shard_map/ppermute | solution.py:85
  40.7 9.6 %collective-permute-start.11 = (bf16[8,64,128]{2,1,0:T(8,128)(2,1)S(1)}, bf16[8,64,128]{2,1,0:T(8,128)(2,1)S(1)}, u32[]{:S(2)}, u32[]{:S(2)}) collective-permute-start(bf16[8,64,128]{2,1,0:T(8,128)(2,1)S(1)} %get-tuple-element.49.refs_6_.refs_2_), channel_id=1, source_target_pairs={{0,8},{1,9},{2,10},{3,11},{4,12},{5,13},{6,14},{7,15},{8,0},{9,1},... | collective-permute-start | bytes 393224 | tf_op jit(solution)/shard_map/ppermute | solution.py:85
  44.7 5.6 %collective-permute-start.12 = (bf16[4,64,128]{2,1,0:T(8,128)(2,1)S(1)}, bf16[4,64,128]{2,1,0:T(8,128)(2,1)S(1)}, u32[]{:S(2)}, u32[]{:S(2)}) collective-permute-start(bf16[4,64,128]{2,1,0:T(8,128)(2,1)S(1)} %get-tuple-element.50), channel_id=1, source_target_pairs={{0,12},{1,13},{2,14},{3,15},{4,8},{5,9},{6,10},{7,11},{8,4},{9,5},... | collective-permute-start | bytes 196616 | tf_op jit(solution)/shard_map/ppermute | solution.py:85
  50.4 1.7 %collective-permute-start.13 = (bf16[3,64,128]{2,1,0:T(8,128)(2,1)S(1)}, bf16[3,64,128]{2,1,0:T(8,128)(2,1)S(1)}, u32[]{:S(2)}, u32[]{:S(2)}) collective-permute-start(bf16[3,64,128]{2,1,0:T(8,128)(2,1)S(1)} %get-tuple-element.52), channel_id=1, source_target_pairs={{0,1},{1,0},{2,3},{3,2},{4,5},{5,4},{6,7},{7,6},{8,9},{9,8},{10,11... | collective-permute-start | bytes 147464 | tf_op jit(solution)/shard_map/ppermute | solution.py:85
  50.5 3.6 %collective-permute-start.14 = (bf16[3,64,128]{2,1,0:T(8,128)(2,1)S(1)}, bf16[3,64,128]{2,1,0:T(8,128)(2,1)S(1)}, u32[]{:S(2)}, u32[]{:S(2)}) collective-permute-start(bf16[3,64,128]{2,1,0:T(8,128)(2,1)S(1)} %get-tuple-element.53), channel_id=1, source_target_pairs={{0,3},{1,2},{2,1},{3,0},{4,7},{5,6},{6,5},{7,4},{8,11},{9,10},{10,... | collective-permute-start | bytes 147464 | tf_op jit(solution)/shard_map/ppermute | solution.py:85
  54.3 5.5 %collective-permute-start.17 = (f32[8,128]{1,0:T(8,128)S(1)}, f32[8,128]{1,0:T(8,128)S(1)}, u32[]{:S(2)}, u32[]{:S(2)}) collective-permute-start(f32[8,128]{1,0:T(8,128)S(1)} %get-tuple-element.57.refs_0_), channel_id=1, source_target_pairs={{0,24},{1,25},{2,26},{3,27},{4,28},{5,29},{6,30},{7,31},{8,16},{9,... | collective-permute-start | bytes 12296 | tf_op jit(solution)/shard_map/ppermute | solution.py:85
  57.0 4.5 %collective-permute-start.16 = (f32[8,128]{1,0:T(8,128)S(1)}, f32[8,128]{1,0:T(8,128)S(1)}, u32[]{:S(2)}, u32[]{:S(2)}) collective-permute-start(f32[8,128]{1,0:T(8,128)S(1)} %get-tuple-element.57.refs_0_), channel_id=1, source_target_pairs={{0,16},{1,17},{2,18},{3,19},{4,20},{5,21},{6,22},{7,23},{8,24},{9,... | collective-permute-start | bytes 12296 | tf_op jit(solution)/shard_map/ppermute | solution.py:85
  57.2 4.3 %collective-permute-start.15 = (f32[8,128]{1,0:T(8,128)S(1)}, f32[8,128]{1,0:T(8,128)S(1)}, u32[]{:S(2)}, u32[]{:S(2)}) collective-permute-start(f32[8,128]{1,0:T(8,128)S(1)} %get-tuple-element.57.refs_0_), channel_id=1, source_target_pairs={{0,8},{1,9},{2,10},{3,11},{4,12},{5,13},{6,14},{7,15},{8,0},{9,1},... | collective-permute-start | bytes 12296 | tf_op jit(solution)/shard_map/ppermute | solution.py:85

commit v2 on v1

--- a/solution.py
+++ b/solution.py
@@ -14,14 +14,14 @@
 VMEM_BYTES = 24 * 1024 * 1024
 
 VM = pl.BlockSpec(memory_space=pltpu.VMEM)
-SM = pl.BlockSpec(memory_space=pltpu.SMEM)
-
-
-def call(kernel, outs, *args, smem=0, scratch=(), aliases=None):
+
+
+def call(kernel, outs, *args, far_args=0, scratch=(), aliases=None):
+    args = [pltpu.with_memory_space_constraint(a, pltpu.HBM) for a in args[:far_args]] + list(args[far_args:])
     return pl.pallas_call(
         kernel,
         out_shape=[jax.ShapeDtypeStruct(shape, dtype) for shape, dtype in outs],
-        in_specs=[SM] * smem + [VM] * (len(args) - smem),
+        in_specs=[pl.BlockSpec(memory_space=pltpu.HBM)] * far_args + [VM] * (len(args) - far_args),
         out_specs=[VM] * len(outs),
         scratch_shapes=list(scratch),
         input_output_aliases=aliases or {},
@@ -84,6 +84,19 @@
     def swapped(array, **where):
         return lax.ppermute(array, AXES, route(**where))
 
+    def to_next(step, array, of_row=None):
+        pairs = []
+        for l in range(layers):
+            a = (near if step % 2 == 0 else far)(l, layers)
+            for r in range(rows):
+                for c in range(cols):
+                    if abs(a - l) == 1:
+                        target = (a, of_row(r, rows) if of_row else r, c)
+                    else:
+                        target = (l, r, near(c, cols))
+                    pairs.append(((l * rows + r) * cols + c, (target[0] * rows + target[1]) * cols + target[2]))
+        return lax.ppermute(array, AXES, pairs)
+
     def is_active(step):
         pos = lax.axis_index("layer")
         return jnp.logical_or(pos == step, pos == layers - 1 - step)
@@ -109,7 +122,18 @@
         end = pos == (0 if sweep == 0 else layers - 1)
         return (tile + jnp.where(end, port_map(cells_ref, x, y), 0.0)).astype(bf16)
 
-    def rims_kernel(forward_ref, adjoint_ref, cells_ref, flat_ref, *rim_refs):
+    def rims_kernel(forward_hbm, adjoint_hbm, cells_hbm, flat_ref, cells_ref, *refs):
+        rim_refs, (forward_ref, adjoint_ref, sems) = refs[: len(row_pairs)], refs[len(row_pairs) :]
+        copies = [
+            pltpu.make_async_copy(src, dst, sems.at[i])
+            for i, (src, dst) in enumerate(
+                ((forward_hbm, forward_ref), (adjoint_hbm, adjoint_ref), (cells_hbm, cells_ref))
+            )
+        ]
+        for copy in copies:
+            copy.start()
+        for copy in copies:
+            copy.wait()
         flat_ref[0] = forward_ref[...].astype(f32).reshape(ports * tiles, cells)
         flat_ref[1] = adjoint_ref[...].astype(f32).reshape(ports * tiles, cells)
         for pairing, rim_ref in zip(row_pairs, rim_refs):
@@ -119,28 +143,60 @@
                     rim_ref[sweep, y] = source_tile(flat_ref, cells_ref, sweep, side.edge, y)
 
     port_row = port_cells.reshape(1, ports)
-    flat, *rims = call(
+    raw = (ports, tiles, cells)
+    flat, port_row, *rims = call(
         rims_kernel,
-        [((2, ports * tiles, cells), f32)] + [((2, tiles_y, ports, cells), bf16)] * len(row_pairs),
-        sources.reshape(ports, tiles, cells),
-        adjoint_sources.reshape(ports, tiles, cells),
+        [((2, ports * tiles, cells), f32), ((1, ports), jnp.int32)]
+        + [((2, tiles_y, ports, cells), bf16)] * len(row_pairs),
+        sources.reshape(raw),
+        adjoint_sources.reshape(raw),
         port_row,
+        far_args=3,
+        scratch=[pltpu.VMEM(raw, bf16), pltpu.VMEM(raw, bf16), pltpu.SemaphoreType.DMA((3,))],
     )
     source_rims = [swapped(rim, of_row=pairing) for rim, pairing in zip(rims, row_pairs)]
 
-    def setup_kernel(pattern_ref, coupling_ref, group_ref, flat_ref, cells_ref, blocks_ref, source_ref, front_ref, kappa_ref, member_ref):
+    def setup_kernel(
+        pattern_hbm,
+        coupling_hbm,
+        group_hbm,
+        blocks_hbm,
+        flat_ref,
+        cells_ref,
+        source_ref,
+        front_ref,
+        kappa_ref,
+        member_ref,
+        pattern_ref,
+        coupling_ref,
+        group_ref,
+        blocks_ref,
+        sems,
+        block_sems,
+    ):
+        scalars = [
+            pltpu.make_async_copy(src, dst, sems.at[i])
+            for i, (src, dst) in enumerate(
+                ((pattern_hbm, pattern_ref), (coupling_hbm, coupling_ref), (group_hbm, group_ref))
+            )
+        ]
+        loads = [
+            pltpu.make_async_copy(blocks_hbm.at[t], blocks_ref.at[t], block_sems.at[t]) for t in range(tiles)
+        ]
+        for copy in scalars + loads:
+            copy.start()
         for sweep in range(2):
             for x in range(tiles_x):
                 for y in range(tiles_y):
                     source_ref[sweep, x * tiles_y + y] = source_tile(flat_ref, cells_ref, sweep, x, y)
 
-        def mask_block(index, carry):
+        for copy in scalars:
+            copy.wait()
+        for t in range(tiles):
+            loads[t].wait()
             for offset in range(OFFSETS):
-                present = pattern_ref[index, offset] > 0
-                front_ref[index, offset] = jnp.where(present, blocks_ref[index, offset], jnp.zeros((cells, cells), bf16))
-            return carry
-
-        lax.fori_loop(0, tiles, mask_block, 0)
+                present = pattern_ref[t // tiles_y, t % tiles_y, offset] > 0
+                front_ref[t, offset] = jnp.where(present, blocks_ref[t, offset], jnp.zeros((cells, cells), bf16))
         pos = lax.axis_index("layer")
         own = coupling_ref[group_ref[pos]]
         following = coupling_ref[group_ref[jnp.minimum(pos + 1, layers - 1)]]
@@ -158,13 +214,21 @@
             ((2, 8, cells), f32),
             ((groups, layers, tiles, cells), f32),
         ],
-        pattern.reshape(tiles, OFFSETS),
+        pattern[0],
         coupling,
         layer_group,
+        blocks.reshape(tiles, OFFSETS, cells, cells),
         flat,
         port_row,
-        blocks.reshape(tiles, OFFSETS, cells, cells),
-        smem=3,
+        far_args=4,
+        scratch=[
+            pltpu.SMEM(pattern.shape[1:], jnp.int32),
+            pltpu.SMEM(coupling.shape, f32),
+            pltpu.SMEM(layer_group.shape, jnp.int32),
+            pltpu.VMEM((tiles, OFFSETS, cells, cells), bf16),
+            pltpu.SemaphoreType.DMA((3,)),
+            pltpu.SemaphoreType.DMA((tiles,)),
+        ],
     )
 
     def wave_kernel(step, *refs):
@@ -305,11 +369,8 @@
         )
         fields.append(field)
         if not last:
-            partner = lambda l: l ^ 1 if step % 2 == 0 else (((l + 1) ^ 1) - 1) % layers
-            received = swapped(field, of_layer=partner)
-            received_rims = [
-                swapped(rim, of_layer=partner, of_row=pairing) for rim, pairing in zip(extra, row_pairs)
-            ]
+            received = to_next(step, field)
+            received_rims = [to_next(step, rim, pairing) for rim, pairing in zip(extra, row_pairs)]
     intersection = extra[0]
 
     def fields_kernel(*refs):

time: 62.4 us -> 56.2 us (0.901)
  local copies, waits for them, and re-layouts: 6.12 us -> 0 us
  waiting for transfers between devices: 25.8 us -> 23.4 us
  Pallas kernels: 4.65 us -> 5.98 us
  starting transfers between devices: 24.8 us -> 25.8 us
    ppermute x18 -> x12, waiting for transfers between devices: 25.8 us -> 11.3 us  [swapped(): return lax.ppermute(array, AXES, route(**where))]
    ppermute x0 -> x6, starting transfers between devices: none -> 12.3 us  [to_next(): return lax.ppermute(array, AXES, pairs)]
    ppermute x0 -> x6, waiting for transfers between devices: none -> 12.2 us  [to_next(): return lax.ppermute(array, AXES, pairs)]
    ppermute x18 -> x12, starting transfers between devices: 24.8 us -> 13.5 us  [swapped(): return lax.ppermute(array, AXES, route(**where))]
    unnamed x14 -> x0, local copies, waits for them, and re-layouts: 6.12 us -> none
    pallas_call x16, Pallas kernels: 4.65 us -> 5.98 us  [call(): pl.pallas_call(kernel, out_shape=[jax.ShapeDtypeStruct(shape, dtype) for...]
  transfers between devices with their start and end apart: 18 -> 18, of which waited for: 9 -> 10; matrix products, arithmetic and copies ran while one was open for 0% -> 0% of each run, Pallas kernels for 5% -> 6%
where the time goes in v2:
time: 56.2 us; the launch traced here: 56 us
  starting transfers between devices  25.8 us (46%)
  waiting for transfers between devices  23.4 us (42%)
  Pallas kernels  5.98 us (11%)
  between operations  0.71 us (1%)
    ppermute x12, starting transfers between devices, swapped(): return lax.ppermute(array, AXES, route(**where))  13.5 us
    ppermute x6, starting transfers between devices, to_next(): return lax.ppermute(array, AXES, pairs)  12.3 us
    ppermute x6, waiting for transfers between devices, to_next(): return lax.ppermute(array, AXES, pairs)  12.2 us
    ppermute x12, waiting for transfers between devices, swapped(): return lax.ppermute(array, AXES, route(**where))  11.3 us
    pallas_call x16, Pallas kernels, call(): pl.pallas_call(kernel, out_shape=[jax.ShapeDtypeStruct(shape, dtype) for...  5.98 us
  transfers between devices with their start and end apart: 18, of which 10 were waited for; matrix products, arithmetic and copies ran while one was open for 0% of the time, Pallas kernels for 6%

profile of v2, /device:TPU:0, one launch (start us, length us, event | category | flops | bytes accessed | tf_op | source)
XLA Modules:
  0.0 56.0 jit_solution(2889917654610131620)
XLA Ops:
  0.6 1.2 %shard_map.94 = (f32[2,512,128]{2,1,0:T(8,128)S(1)}, s32[1,64]{1,0:T(1,128)S(1)}, bf16[2,4,64,128]{3,2,1,0:T(8,128)(2,1)S(1)}) custom-call(bf16[64,8,128]{2,1,0:T(8,128)(2,1)} %bitcast.8, bf16[64,8,128]{2,1,0:T(8,128)(2,1)} %bitcast.9, s32[1,64]{1,0:T(1,128)} %bitcast.11), custom_call_target="tpu_custom_call" | custom-call | tf_op jit(solution)/shard_map/pallas_call | solution.py:21
  1.9 3.0 %collective-permute-start = (bf16[2,4,64,128]{3,2,1,0:T(8,128)(2,1)S(1)}, bf16[2,4,64,128]{3,2,1,0:T(8,128)(2,1)S(1)}, u32[]{:S(2)}, u32[]{:S(2)}) collective-permute-start(bf16[2,4,64,128]{3,2,1,0:T(8,128)(2,1)S(1)} %get-tuple-element.36), channel_id=1, source_target_pairs={{0,4},{1,5},{2,6},{3,7},{4,0},{5,1},{6,2},{7,3},{8,12},{9,13},{10,... | collective-permute-start | bytes 393224 | tf_op jit(solution)/shard_map/ppermute | solution.py:85
  4.9 1.9 %shard_map.95 = (bf16[2,8,64,128]{3,2,1,0:T(8,128)(2,1)S(1)}, bf16[8,9,128,128]{3,2,1,0:T(8,128)(2,1)S(1)}, f32[2,8,128]{2,1,0:T(8,128)S(1)}, f32[4,4,8,128]{3,2,1,0:T(8,128)S(1)}) custom-call(s32[2,4,9]{2,1,0:T(4,128)} %bitcast.10, f32[4]{0:T(128)} %coupling_hbm.1, s32[4]{0:T(128)} %group_hbm.1, bf16[8,9,128,128]{3,2,1,0:T(8,128)(2,1)} %bitcast.7, ...), custom_call_target="tpu_custom_call" | custom-call | tf_op jit(solution)/shard_map/pallas_call | solution.py:21
  6.8 1.6 %collective-permute-done.refs_2_ = bf16[2,4,64,128]{3,2,1,0:T(8,128)(2,1)S(1)} collective-permute-done((bf16[2,4,64,128]{3,2,1,0:T(8,128)(2,1)S(1)}, bf16[2,4,64,128]{3,2,1,0:T(8,128)(2,1)S(1)}, u32[]{:S(2)}, u32[]{:S(2)}) %collective-permute-start) | collective-permute-done | bytes 131104 | tf_op jit(solution)/shard_map/ppermute | solution.py:85
  8.4 0.1 collective-permute-start.1
  8.5 1.8 %collective-permute-start.2 = (bf16[3,64,128]{2,1,0:T(8,128)(2,1)S(1)}, bf16[3,64,128]{2,1,0:T(8,128)(2,1)S(1)}, u32[]{:S(2)}, u32[]{:S(2)}) collective-permute-start(bf16[3,64,128]{2,1,0:T(8,128)(2,1)S(1)} %get-tuple-element.40), channel_id=1, source_target_pairs={{0,3},{1,2},{2,1},{3,0},{4,7},{5,6},{6,5},{7,4},{8,11},{9,10},{10,... | collective-permute-start | bytes 147464 | tf_op jit(solution)/shard_map/ppermute | solution.py:85
  10.3 0.4 shard_map.97.refs_0_
  10.8 0.0 collective-permute-done.1.refs_2_
  10.8 1.3 %collective-permute-done.2.refs_3_ = bf16[3,64,128]{2,1,0:T(8,128)(2,1)S(1)} collective-permute-done((bf16[3,64,128]{2,1,0:T(8,128)(2,1)S(1)}, bf16[3,64,128]{2,1,0:T(8,128)(2,1)S(1)}, u32[]{:S(2)}, u32[]{:S(2)}) %collective-permute-start.2) | collective-permute-done | bytes 49184 | tf_op jit(solution)/shard_map/ppermute | solution.py:85
  12.1 0.2 shard_map.98
  12.3 1.4 %collective-permute-start.3 = (bf16[8,64,128]{2,1,0:T(8,128)(2,1)S(1)}, bf16[8,64,128]{2,1,0:T(8,128)(2,1)S(1)}, u32[]{:S(2)}, u32[]{:S(2)}) collective-permute-start(bf16[8,64,128]{2,1,0:T(8,128)(2,1)S(1)} %get-tuple-element.41.refs_4_.refs_0_), channel_id=1, source_target_pairs={{0,8},{1,9},{2,10},{3,11},{4,12},{5,13},{6,14},{7,15},{8,0},{9,1},... | collective-permute-start | bytes 393224 | tf_op jit(solution)/shard_map/ppermute | solution.py:98
  13.7 1.8 %collective-permute-start.4 = (bf16[4,64,128]{2,1,0:T(8,128)(2,1)S(1)}, bf16[4,64,128]{2,1,0:T(8,128)(2,1)S(1)}, u32[]{:S(2)}, u32[]{:S(2)}) collective-permute-start(bf16[4,64,128]{2,1,0:T(8,128)(2,1)S(1)} %get-tuple-element.42), channel_id=1, source_target_pairs={{0,12},{1,13},{2,14},{3,15},{4,8},{5,9},{6,10},{7,11},{8,4},{9,5},... | collective-permute-start | bytes 196616 | tf_op jit(solution)/shard_map/ppermute | solution.py:98
  15.5 5.4 %collective-permute-done.4.refs_4_ = bf16[4,64,128]{2,1,0:T(8,128)(2,1)S(1)} collective-permute-done((bf16[4,64,128]{2,1,0:T(8,128)(2,1)S(1)}, bf16[4,64,128]{2,1,0:T(8,128)(2,1)S(1)}, u32[]{:S(2)}, u32[]{:S(2)}) %collective-permute-start.4) | collective-permute-done | bytes 65568 | tf_op jit(solution)/shard_map/ppermute | solution.py:98
  20.9 0.0 collective-permute-done.3.refs_3_
  20.9 0.0 collective-permute-start.5
  20.9 1.5 %collective-permute-start.6 = (bf16[3,64,128]{2,1,0:T(8,128)(2,1)S(1)}, bf16[3,64,128]{2,1,0:T(8,128)(2,1)S(1)}, u32[]{:S(2)}, u32[]{:S(2)}) collective-permute-start(bf16[3,64,128]{2,1,0:T(8,128)(2,1)S(1)} %get-tuple-element.45), channel_id=1, source_target_pairs={{0,3},{1,2},{2,1},{3,0},{4,7},{5,6},{6,5},{7,4},{8,11},{9,10},{10,... | collective-permute-start | bytes 147464 | tf_op jit(solution)/shard_map/ppermute | solution.py:85
  22.4 0.0 collective-permute-done.5.refs_2_
  22.4 2.1 %collective-permute-done.6.refs_3_ = bf16[3,64,128]{2,1,0:T(8,128)(2,1)S(1)} collective-permute-done((bf16[3,64,128]{2,1,0:T(8,128)(2,1)S(1)}, bf16[3,64,128]{2,1,0:T(8,128)(2,1)S(1)}, u32[]{:S(2)}, u32[]{:S(2)}) %collective-permute-start.6) | collective-permute-done | bytes 49184 | tf_op jit(solution)/shard_map/ppermute | solution.py:85
  24.5 0.4 collective-permute-start.7
  25.0 0.1 collective-permute-start.8
  25.0 1.2 %collective-permute-done.8.refs_4_ = bf16[4,64,128]{2,1,0:T(8,128)(2,1)S(1)} collective-permute-done((bf16[4,64,128]{2,1,0:T(8,128)(2,1)S(1)}, bf16[4,64,128]{2,1,0:T(8,128)(2,1)S(1)}, u32[]{:S(2)}, u32[]{:S(2)}) %collective-permute-start.8) | collective-permute-done | bytes 65568 | tf_op jit(solution)/shard_map/ppermute | solution.py:98
  26.2 0.0 collective-permute-done.7.refs_3_
  26.2 0.2 collective-permute-start.9
  26.4 1.3 %collective-permute-start.10 = (bf16[3,64,128]{2,1,0:T(8,128)(2,1)S(1)}, bf16[3,64,128]{2,1,0:T(8,128)(2,1)S(1)}, u32[]{:S(2)}, u32[]{:S(2)}) collective-permute-start(bf16[3,64,128]{2,1,0:T(8,128)(2,1)S(1)} %get-tuple-element.50), channel_id=1, source_target_pairs={{0,3},{1,2},{2,1},{3,0},{4,7},{5,6},{6,5},{7,4},{8,11},{9,10},{10,... | collective-permute-start | bytes 147464 | tf_op jit(solution)/shard_map/ppermute | solution.py:85
  27.7 0.0 collective-permute-done.9.refs_2_
  27.7 2.3 %collective-permute-done.10.refs_3_ = bf16[3,64,128]{2,1,0:T(8,128)(2,1)S(1)} collective-permute-done((bf16[3,64,128]{2,1,0:T(8,128)(2,1)S(1)}, bf16[3,64,128]{2,1,0:T(8,128)(2,1)S(1)}, u32[]{:S(2)}, u32[]{:S(2)}) %collective-permute-start.10) | collective-permute-done | bytes 49184 | tf_op jit(solution)/shard_map/ppermute | solution.py:85
  30.0 7.5 %collective-permute-start.11 = (bf16[8,64,128]{2,1,0:T(8,128)(2,1)S(1)}, bf16[8,64,128]{2,1,0:T(8,128)(2,1)S(1)}, u32[]{:S(2)}, u32[]{:S(2)}) collective-permute-start(bf16[8,64,128]{2,1,0:T(8,128)(2,1)S(1)} %get-tuple-element.51.refs_6_.refs_2_), channel_id=1, source_target_pairs={{0,8},{1,9},{2,10},{3,11},{4,12},{5,13},{6,14},{7,15},{8,0},{9,1},... | collective-permute-start | bytes 393224 | tf_op jit(solution)/shard_map/ppermute | solution.py:98
  37.5 1.0 %collective-permute-start.12 = (bf16[4,64,128]{2,1,0:T(8,128)(2,1)S(1)}, bf16[4,64,128]{2,1,0:T(8,128)(2,1)S(1)}, u32[]{:S(2)}, u32[]{:S(2)}) collective-permute-start(bf16[4,64,128]{2,1,0:T(8,128)(2,1)S(1)} %get-tuple-element.52), channel_id=1, source_target_pairs={{0,12},{1,13},{2,14},{3,15},{4,8},{5,9},{6,10},{7,11},{8,4},{9,5},... | collective-permute-start | bytes 196616 | tf_op jit(solution)/shard_map/ppermute | solution.py:98
  38.6 5.6 %collective-permute-done.12.refs_4_ = bf16[4,64,128]{2,1,0:T(8,128)(2,1)S(1)} collective-permute-done((bf16[4,64,128]{2,1,0:T(8,128)(2,1)S(1)}, bf16[4,64,128]{2,1,0:T(8,128)(2,1)S(1)}, u32[]{:S(2)}, u32[]{:S(2)}) %collective-permute-start.12) | collective-permute-done | bytes 65568 | tf_op jit(solution)/shard_map/ppermute | solution.py:98
  44.1 0.0 collective-permute-done.11.refs_3_
  44.1 0.1 shard_map.105
  44.2 0.1 collective-permute-start.13
  44.3 1.1 %collective-permute-start.14 = (bf16[3,64,128]{2,1,0:T(8,128)(2,1)S(1)}, bf16[3,64,128]{2,1,0:T(8,128)(2,1)S(1)}, u32[]{:S(2)}, u32[]{:S(2)}) collective-permute-start(bf16[3,64,128]{2,1,0:T(8,128)(2,1)S(1)} %get-tuple-element.55), channel_id=1, source_target_pairs={{0,3},{1,2},{2,1},{3,0},{4,7},{5,6},{6,5},{7,4},{8,11},{9,10},{10,... | collective-permute-start | bytes 147464 | tf_op jit(solution)/shard_map/ppermute | solution.py:85
  45.5 0.4 shard_map.106.refs_0_
  45.9 0.0 collective-permute-done.13.refs_2_
  45.9 2.0 %collective-permute-done.14.refs_3_ = bf16[3,64,128]{2,1,0:T(8,128)(2,1)S(1)} collective-permute-done((bf16[3,64,128]{2,1,0:T(8,128)(2,1)S(1)}, bf16[3,64,128]{2,1,0:T(8,128)(2,1)S(1)}, u32[]{:S(2)}, u32[]{:S(2)}) %collective-permute-start.14) | collective-permute-done | bytes 49184 | tf_op jit(solution)/shard_map/ppermute | solution.py:85
  47.9 0.2 shard_map.107
  48.1 2.7 %collective-permute-start.17 = (f32[8,128]{1,0:T(8,128)S(1)}, f32[8,128]{1,0:T(8,128)S(1)}, u32[]{:S(2)}, u32[]{:S(2)}) collective-permute-start(f32[8,128]{1,0:T(8,128)S(1)} %get-tuple-element.59.refs_0_), channel_id=1, source_target_pairs={{0,24},{1,25},{2,26},{3,27},{4,28},{5,29},{6,30},{7,31},{8,16},{9,... | collective-permute-start | bytes 12296 | tf_op jit(solution)/shard_map/ppermute | solution.py:85
  50.8 0.2 collective-permute-start.16
  51.1 1.5 %collective-permute-start.15 = (f32[8,128]{1,0:T(8,128)S(1)}, f32[8,128]{1,0:T(8,128)S(1)}, u32[]{:S(2)}, u32[]{:S(2)}) collective-permute-start(f32[8,128]{1,0:T(8,128)S(1)} %get-tuple-element.59.refs_0_), channel_id=1, source_target_pairs={{0,8},{1,9},{2,10},{3,11},{4,12},{5,13},{6,14},{7,15},{8,0},{9,1},... | collective-permute-start | bytes 12296 | tf_op jit(solution)/shard_map/ppermute | solution.py:85
  52.6 0.8 %shard_map.108 = (bf16[64,8,128]{2,1,0:T(8,128)(2,1)}, bf16[64,8,128]{2,1,0:T(8,128)(2,1)}) custom-call(bf16[8,64,128]{2,1,0:T(8,128)(2,1)S(1)} %get-tuple-element.41.refs_4_.refs_0_, bf16[8,64,128]{2,1,0:T(8,128)(2,1)S(1)} %get-tuple-element.46.refs_5_.refs_1_, bf16[8,64,128]{2,1,0:T(8,128)(2,1)S(1)} %get-tuple-element.51.refs_6_.refs_2_, ...), custom_call_target="tpu_custom_call" | custom-call | tf_op jit(solution)/shard_map/pallas_call | solution.py:21
  53.4 0.2 collective-permute-done.17.refs_3_
  53.6 1.7 %collective-permute-done.16.refs_2_ = f32[8,128]{1,0:T(8,128)S(1)} collective-permute-done((f32[8,128]{1,0:T(8,128)S(1)}, f32[8,128]{1,0:T(8,128)S(1)}, u32[]{:S(2)}, u32[]{:S(2)}) %collective-permute-start.16) | collective-permute-done | bytes 4128 | tf_op jit(solution)/shard_map/ppermute | solution.py:85
  55.3 0.0 collective-permute-done.15.refs_1_
  55.3 0.6 %shard_map.109 = f32[4,2,4,128]{3,2,1,0:T(4,128)} custom-call(f32[8,128]{1,0:T(8,128)S(1)} %get-tuple-element.59.refs_0_, f32[8,128]{1,0:T(8,128)S(1)} %collective-permute-done.15.refs_1_, f32[8,128]{1,0:T(8,128)S(1)} %collective-permute-done.16.refs_2_, f32[8,128]{1,0:T(8,128)S(1)} %collective-permute-done.17.refs_3_, ...), custom_call_target="tpu_custom_call" | custom-call | tf_op jit(solution)/shard_map/pallas_call | solution.py:21
  (7 shorter events, 0.0 us)
Async XLA Ops:
  1.9 6.5 %collective-permute-start = (bf16[2,4,64,128]{3,2,1,0:T(8,128)(2,1)S(1)}, bf16[2,4,64,128]{3,2,1,0:T(8,128)(2,1)S(1)}, u32[]{:S(2)}, u32[]{:S(2)}) collective-permute-start(bf16[2,4,64,128]{3,2,1,0:T(8,128)(2,1)S(1)} %get-tuple-element.36), channel_id=1, source_target_pairs={{0,4},{1,5},{2,6},{3,7},{4,0},{5,1},{6,2},{7,3},{8,12},{9,13},{10,... | collective-permute-start | bytes 393224 | tf_op jit(solution)/shard_map/ppermute | solution.py:85
  8.4 2.3 %collective-permute-start.1 = (bf16[3,64,128]{2,1,0:T(8,128)(2,1)S(1)}, bf16[3,64,128]{2,1,0:T(8,128)(2,1)S(1)}, u32[]{:S(2)}, u32[]{:S(2)}) collective-permute-start(bf16[3,64,128]{2,1,0:T(8,128)(2,1)S(1)} %get-tuple-element.39), channel_id=1, source_target_pairs={{0,1},{1,0},{2,3},{3,2},{4,5},{5,4},{6,7},{7,6},{8,9},{9,8},{10,11... | collective-permute-start | bytes 147464 | tf_op jit(solution)/shard_map/ppermute | solution.py:85
  8.5 3.6 %collective-permute-start.2 = (bf16[3,64,128]{2,1,0:T(8,128)(2,1)S(1)}, bf16[3,64,128]{2,1,0:T(8,128)(2,1)S(1)}, u32[]{:S(2)}, u32[]{:S(2)}) collective-permute-start(bf16[3,64,128]{2,1,0:T(8,128)(2,1)S(1)} %get-tuple-element.40), channel_id=1, source_target_pairs={{0,3},{1,2},{2,1},{3,0},{4,7},{5,6},{6,5},{7,4},{8,11},{9,10},{10,... | collective-permute-start | bytes 147464 | tf_op jit(solution)/shard_map/ppermute | solution.py:85
  12.3 8.6 %collective-permute-start.3 = (bf16[8,64,128]{2,1,0:T(8,128)(2,1)S(1)}, bf16[8,64,128]{2,1,0:T(8,128)(2,1)S(1)}, u32[]{:S(2)}, u32[]{:S(2)}) collective-permute-start(bf16[8,64,128]{2,1,0:T(8,128)(2,1)S(1)} %get-tuple-element.41.refs_4_.refs_0_), channel_id=1, source_target_pairs={{0,8},{1,9},{2,10},{3,11},{4,12},{5,13},{6,14},{7,15},{8,0},{9,1},... | collective-permute-start | bytes 393224 | tf_op jit(solution)/shard_map/ppermute | solution.py:98
  13.7 7.2 %collective-permute-start.4 = (bf16[4,64,128]{2,1,0:T(8,128)(2,1)S(1)}, bf16[4,64,128]{2,1,0:T(8,128)(2,1)S(1)}, u32[]{:S(2)}, u32[]{:S(2)}) collective-permute-start(bf16[4,64,128]{2,1,0:T(8,128)(2,1)S(1)} %get-tuple-element.42), channel_id=1, source_target_pairs={{0,12},{1,13},{2,14},{3,15},{4,8},{5,9},{6,10},{7,11},{8,4},{9,5},... | collective-permute-start | bytes 196616 | tf_op jit(solution)/shard_map/ppermute | solution.py:98
  20.9 1.5 %collective-permute-start.5 = (bf16[3,64,128]{2,1,0:T(8,128)(2,1)S(1)}, bf16[3,64,128]{2,1,0:T(8,128)(2,1)S(1)}, u32[]{:S(2)}, u32[]{:S(2)}) collective-permute-start(bf16[3,64,128]{2,1,0:T(8,128)(2,1)S(1)} %get-tuple-element.44), channel_id=1, source_target_pairs={{0,1},{1,0},{2,3},{3,2},{4,5},{5,4},{6,7},{7,6},{8,9},{9,8},{10,11... | collective-permute-start | bytes 147464 | tf_op jit(solution)/shard_map/ppermute | solution.py:85
  20.9 3.6 %collective-permute-start.6 = (bf16[3,64,128]{2,1,0:T(8,128)(2,1)S(1)}, bf16[3,64,128]{2,1,0:T(8,128)(2,1)S(1)}, u32[]{:S(2)}, u32[]{:S(2)}) collective-permute-start(bf16[3,64,128]{2,1,0:T(8,128)(2,1)S(1)} %get-tuple-element.45), channel_id=1, source_target_pairs={{0,3},{1,2},{2,1},{3,0},{4,7},{5,6},{6,5},{7,4},{8,11},{9,10},{10,... | collective-permute-start | bytes 147464 | tf_op jit(solution)/shard_map/ppermute | solution.py:85
  24.5 1.7 %collective-permute-start.7 = (bf16[8,64,128]{2,1,0:T(8,128)(2,1)S(1)}, bf16[8,64,128]{2,1,0:T(8,128)(2,1)S(1)}, u32[]{:S(2)}, u32[]{:S(2)}) collective-permute-start(bf16[8,64,128]{2,1,0:T(8,128)(2,1)S(1)} %get-tuple-element.46.refs_5_.refs_1_), channel_id=1, source_target_pairs={{0,1},{1,0},{2,3},{3,2},{4,5},{5,4},{6,7},{7,6},{8,16},{9,17},{10,... | collective-permute-start | bytes 393224 | tf_op jit(solution)/shard_map/ppermute | solution.py:98
  25.0 1.3 %collective-permute-start.8 = (bf16[4,64,128]{2,1,0:T(8,128)(2,1)S(1)}, bf16[4,64,128]{2,1,0:T(8,128)(2,1)S(1)}, u32[]{:S(2)}, u32[]{:S(2)}) collective-permute-start(bf16[4,64,128]{2,1,0:T(8,128)(2,1)S(1)} %get-tuple-element.47), channel_id=1, source_target_pairs={{0,1},{1,0},{2,3},{3,2},{4,5},{5,4},{6,7},{7,6},{8,20},{9,21},{10,... | collective-permute-start | bytes 196616 | tf_op jit(solution)/shard_map/ppermute | solution.py:98
  26.2 1.5 %collective-permute-start.9 = (bf16[3,64,128]{2,1,0:T(8,128)(2,1)S(1)}, bf16[3,64,128]{2,1,0:T(8,128)(2,1)S(1)}, u32[]{:S(2)}, u32[]{:S(2)}) collective-permute-start(bf16[3,64,128]{2,1,0:T(8,128)(2,1)S(1)} %get-tuple-element.49), channel_id=1, source_target_pairs={{0,1},{1,0},{2,3},{3,2},{4,5},{5,4},{6,7},{7,6},{8,9},{9,8},{10,11... | collective-permute-start | bytes 147464 | tf_op jit(solution)/shard_map/ppermute | solution.py:85
  26.4 3.6 %collective-permute-start.10 = (bf16[3,64,128]{2,1,0:T(8,128)(2,1)S(1)}, bf16[3,64,128]{2,1,0:T(8,128)(2,1)S(1)}, u32[]{:S(2)}, u32[]{:S(2)}) collective-permute-start(bf16[3,64,128]{2,1,0:T(8,128)(2,1)S(1)} %get-tuple-element.50), channel_id=1, source_target_pairs={{0,3},{1,2},{2,1},{3,0},{4,7},{5,6},{6,5},{7,4},{8,11},{9,10},{10,... | collective-permute-start | bytes 147464 | tf_op jit(solution)/shard_map/ppermute | solution.py:85
  30.0 14.1 %collective-permute-start.11 = (bf16[8,64,128]{2,1,0:T(8,128)(2,1)S(1)}, bf16[8,64,128]{2,1,0:T(8,128)(2,1)S(1)}, u32[]{:S(2)}, u32[]{:S(2)}) collective-permute-start(bf16[8,64,128]{2,1,0:T(8,128)(2,1)S(1)} %get-tuple-element.51.refs_6_.refs_2_), channel_id=1, source_target_pairs={{0,8},{1,9},{2,10},{3,11},{4,12},{5,13},{6,14},{7,15},{8,0},{9,1},... | collective-permute-start | bytes 393224 | tf_op jit(solution)/shard_map/ppermute | solution.py:98
  37.5 6.6 %collective-permute-start.12 = (bf16[4,64,128]{2,1,0:T(8,128)(2,1)S(1)}, bf16[4,64,128]{2,1,0:T(8,128)(2,1)S(1)}, u32[]{:S(2)}, u32[]{:S(2)}) collective-permute-start(bf16[4,64,128]{2,1,0:T(8,128)(2,1)S(1)} %get-tuple-element.52), channel_id=1, source_target_pairs={{0,12},{1,13},{2,14},{3,15},{4,8},{5,9},{6,10},{7,11},{8,4},{9,5},... | collective-permute-start | bytes 196616 | tf_op jit(solution)/shard_map/ppermute | solution.py:98
  44.2 1.7 %collective-permute-start.13 = (bf16[3,64,128]{2,1,0:T(8,128)(2,1)S(1)}, bf16[3,64,128]{2,1,0:T(8,128)(2,1)S(1)}, u32[]{:S(2)}, u32[]{:S(2)}) collective-permute-start(bf16[3,64,128]{2,1,0:T(8,128)(2,1)S(1)} %get-tuple-element.54), channel_id=1, source_target_pairs={{0,1},{1,0},{2,3},{3,2},{4,5},{5,4},{6,7},{7,6},{8,9},{9,8},{10,11... | collective-permute-start | bytes 147464 | tf_op jit(solution)/shard_map/ppermute | solution.py:85
  44.3 3.6 %collective-permute-start.14 = (bf16[3,64,128]{2,1,0:T(8,128)(2,1)S(1)}, bf16[3,64,128]{2,1,0:T(8,128)(2,1)S(1)}, u32[]{:S(2)}, u32[]{:S(2)}) collective-permute-start(bf16[3,64,128]{2,1,0:T(8,128)(2,1)S(1)} %get-tuple-element.55), channel_id=1, source_target_pairs={{0,3},{1,2},{2,1},{3,0},{4,7},{5,6},{6,5},{7,4},{8,11},{9,10},{10,... | collective-permute-start | bytes 147464 | tf_op jit(solution)/shard_map/ppermute | solution.py:85
  48.1 5.5 %collective-permute-start.17 = (f32[8,128]{1,0:T(8,128)S(1)}, f32[8,128]{1,0:T(8,128)S(1)}, u32[]{:S(2)}, u32[]{:S(2)}) collective-permute-start(f32[8,128]{1,0:T(8,128)S(1)} %get-tuple-element.59.refs_0_), channel_id=1, source_target_pairs={{0,24},{1,25},{2,26},{3,27},{4,28},{5,29},{6,30},{7,31},{8,16},{9,... | collective-permute-start | bytes 12296 | tf_op jit(solution)/shard_map/ppermute | solution.py:85
  50.8 4.5 %collective-permute-start.16 = (f32[8,128]{1,0:T(8,128)S(1)}, f32[8,128]{1,0:T(8,128)S(1)}, u32[]{:S(2)}, u32[]{:S(2)}) collective-permute-start(f32[8,128]{1,0:T(8,128)S(1)} %get-tuple-element.59.refs_0_), channel_id=1, source_target_pairs={{0,16},{1,17},{2,18},{3,19},{4,20},{5,21},{6,22},{7,23},{8,24},{9,... | collective-permute-start | bytes 12296 | tf_op jit(solution)/shard_map/ppermute | solution.py:85
  51.1 4.3 %collective-permute-start.15 = (f32[8,128]{1,0:T(8,128)S(1)}, f32[8,128]{1,0:T(8,128)S(1)}, u32[]{:S(2)}, u32[]{:S(2)}) collective-permute-start(f32[8,128]{1,0:T(8,128)S(1)} %get-tuple-element.59.refs_0_), channel_id=1, source_target_pairs={{0,8},{1,9},{2,10},{3,11},{4,12},{5,13},{6,14},{7,15},{8,0},{9,1},... | collective-permute-start | bytes 12296 | tf_op jit(solution)/shard_map/ppermute | solution.py:85

commit v3 on v2

v3 whole, which is shorter than its diff:
```python
import functools

import jax
import jax.numpy as jnp
from jax import lax
from jax.experimental import pallas as pl
from jax.experimental.pallas import tpu as pltpu
from jax.sharding import PartitionSpec as P

port_strength = 4.0
intersection_scale = 0.125
AXES = ("layer", "row", "col")
OFFSETS = 9
VMEM_BYTES = 24 * 1024 * 1024
SPARE = 2

VM = pl.BlockSpec(memory_space=pltpu.VMEM)


def call(kernel, outs, *args, far_args=0, scratch=(), aliases=None):
    args = [pltpu.with_memory_space_constraint(a, pltpu.HBM) for a in args[:far_args]] + list(args[far_args:])
    return pl.pallas_call(
        kernel,
        out_shape=[jax.ShapeDtypeStruct(shape, dtype) for shape, dtype in outs],
        in_specs=[pl.BlockSpec(memory_space=pltpu.HBM)] * far_args + [VM] * (len(args) - far_args),
        out_specs=[VM] * len(outs),
        scratch_shapes=list(scratch),
        input_output_aliases=aliases or {},
        compiler_params=pltpu.CompilerParams(vmem_limit_bytes=VMEM_BYTES),
    )(*args)


def near(i, n):
    return i ^ 1


def far(i, n):
    return (((i + 1) ^ 1) - 1) % n


def pairings(n):
    return [near] if n == 2 else [near, far]


class Side:
    def __init__(self, pairing, axis, tiles):
        pos, count = lax.axis_index(axis), lax.axis_size(axis)
        even = lax.rem(pos, 2) == 0
        after = even if pairing is near else jnp.logical_not(even)
        self.step = jnp.where(after, 1, -1)
        self.edge = jnp.where(after, tiles - 1, 0)
        self.real = None
        if pairing is far:
            self.real = jnp.logical_not(
                jnp.logical_or(jnp.logical_and(after, pos == count - 1), jnp.logical_and(jnp.logical_not(after), pos == 0))
            )

    def when(self, body):
        if self.real is None:
            body()
        else:
            pl.when(self.real)(body)


def local(sources, adjoint_sources, blocks, pattern, coupling, layer_group, port_cells):
    ports, tiles_x, tiles_y, cells = sources.shape[1:]
    tiles = tiles_x * tiles_y
    groups = coupling.shape[0]
    layers, rows, cols = (lax.axis_size(axis) for axis in AXES)
    if cols != 4 or layers % 2 or rows % 2:
        raise ValueError("unsupported mesh")
    row_pairs = pairings(rows)
    halos = len(row_pairs)
    ext = tiles_x + halos
    bf16, f32 = jnp.bfloat16, jnp.float32
    tile = (ports, cells)

    def permuted(array, target):
        pairs = []
        for l in range(layers):
            for r in range(rows):
                for c in range(cols):
                    a, b, d = target(l, r, c)
                    pairs.append(((l * rows + r) * cols + c, (a * rows + b) * cols + d))
        return lax.ppermute(array, AXES, pairs)

    def to_core(array):
        return permuted(array, lambda l, r, c: (l, r, near(c, cols)))

    def to_layer(step, beside):
        def target(l, r, c):
            if step is None:
                return l, *beside(r, c)
            a = (near if step % 2 == 0 else far)(l, layers)
            return (a, *beside(r, c)) if abs(a - l) == 1 else (l, r, near(c, cols))

        return lambda array: permuted(array, target)

    def same(r, c):
        return r, c

    def other_row(pairing):
        return lambda r, c: (pairing(r, rows), c)

    def other_chip(pairing):
        def beside(r, c):
            d = far(c, cols)
            return (r if abs(d - c) == 1 else pairing(r, rows)), d

        return beside

    def is_active(step):
        pos = lax.axis_index("layer")
        return jnp.logical_or(pos == step, pos == layers - 1 - step)

    def taker(refs):
        refs = list(refs)

        def take(count=None):
            taken = refs[: 1 if count is None else count]
            del refs[: len(taken)]
            return taken[0] if count is None else taken

        return take

    def first_sweep():
        return jnp.where(lax.axis_index("layer") < layers // 2, 0, 1)

    def port_map(cells_ref, x, y):
        x_pos = lax.axis_index("row") * tiles_x + x
        y_pos = lax.axis_index("col") * tiles_y + y
        first = (x_pos * (tiles_y * cols) + y_pos) * cells
        row = jnp.broadcast_to(cells_ref[...], (ports, ports))
        diagonal = lax.broadcasted_iota(jnp.int32, (ports, ports), 0) == lax.broadcasted_iota(
            jnp.int32, (ports, ports), 1
        )
        column = jnp.sum(jnp.where(diagonal, row, 0), axis=1, keepdims=True)
        lane = lax.broadcasted_iota(jnp.int32, tile, 1)
        return jnp.where(column - first == lane, port_strength, 0.0).astype(f32)

    def source_tile(flat_ref, cells_ref, phase, x, y):
        value = flat_ref[phase, pl.ds(x * tiles_y + y, ports, stride=tiles), :]
        if phase == 0:
            pos = lax.axis_index("layer")
            end = jnp.logical_or(pos == 0, pos == layers - 1)
            value = value + jnp.where(end, port_map(cells_ref, x, y), 0.0)
        return value.astype(bf16)

    def corner_kernel(forward_hbm, adjoint_hbm, cells_hbm, flat_ref, cells_ref, corner_ref, raw_ref, sems):
        copies = [
            pltpu.make_async_copy(src, dst, sems.at[i])
            for i, (src, dst) in enumerate(
                ((forward_hbm, raw_ref.at[0]), (adjoint_hbm, raw_ref.at[1]), (cells_hbm, cells_ref))
            )
        ]
        for copy in copies:
            copy.start()
        for copy in copies:
            copy.wait()
        edge = Side(far, "col", tiles_y).edge
        for phase in range(2):
            flat_ref[phase] = raw_ref[first_sweep() ^ phase].astype(f32).reshape(ports * tiles, cells)
            for h, pairing in enumerate(row_pairs):
                row = Side(pairing, "row", tiles_x).edge
                corner_ref[h, phase] = source_tile(flat_ref, cells_ref, phase, row, edge)

    def rims_kernel(flat_ref, cells_ref, *refs):
        take = taker(refs)
        rim_refs, column_ref = take(halos), take()
        edge = Side(far, "col", tiles_y).edge
        for phase in range(2):
            for x in range(tiles_x):
                column_ref[phase, x] = source_tile(flat_ref, cells_ref, phase, x, edge)
            for h, pairing in enumerate(row_pairs):
                row = Side(pairing, "row", tiles_x).edge
                for y in range(tiles_y):
                    rim_refs[h][phase, y] = source_tile(flat_ref, cells_ref, phase, row, y)

    raw_shape = (ports, tiles, cells)
    flat, port_row, corner = call(
        corner_kernel,
        [((2, ports * tiles, cells), f32), ((1, ports), jnp.int32), ((SPARE * halos, 2, *tile), bf16)],
        sources.reshape(raw_shape),
        adjoint_sources.reshape(raw_shape),
        port_cells.reshape(1, ports),
        far_args=3,
        scratch=[pltpu.VMEM((2, *raw_shape), bf16), pltpu.SemaphoreType.DMA((3,))],
    )
    corner = to_core(corner)
    outward = call(
        rims_kernel, [((2, tiles_y, *tile), bf16)] * halos + [((2, tiles_x, *tile), bf16)], flat, port_row
    )

    def relay_kernel(*refs):
        take = taker(refs)
        column_ref, corner_ref, out_refs = take(), take(), take(halos)
        inner = Side(far, "col", tiles_y).real

        @pl.when(inner)
        def _():
            for out_ref in out_refs:
                out_ref[...] = column_ref[...]

        @pl.when(jnp.logical_not(inner))
        def _():
            for h, out_ref in enumerate(out_refs):
                if len(out_ref.shape) == 4:
                    for phase in range(2):
                        out_ref[phase, 0] = corner_ref[h, phase]
                else:
                    out_ref[0] = corner_ref[h]

    def exchange(step, corner, outward, field=None):
        rims, column = outward[:halos], outward[halos]
        arrived = [] if field is None else [to_layer(step, same)(field)]
        arrived += [to_layer(step, other_row(pairing))(rim) for rim, pairing in zip(rims, row_pairs)]
        carried = call(relay_kernel, [(column.shape, bf16)] * halos, column, corner)
        return arrived + [to_layer(step, other_chip(pairing))(part) for part, pairing in zip(carried, row_pairs)]

    source_beside = exchange(None, corner, outward)

    def setup_kernel(pattern_hbm, coupling_hbm, group_hbm, blocks_hbm, *refs):
        take = taker(refs)
        flat_ref, cells_ref, source_ref, front_ref, kappa_ref, member_ref = (take() for _ in range(6))
        pattern_ref, coupling_ref, group_ref, blocks_ref, sems, block_sems = (take() for _ in range(6))
        scalars = [
            pltpu.make_async_copy(src, dst, sems.at[i])
            for i, (src, dst) in enumerate(
                ((pattern_hbm, pattern_ref), (coupling_hbm, coupling_ref), (group_hbm, group_ref))
            )
        ]
        loads = [
            pltpu.make_async_copy(blocks_hbm.at[t], blocks_ref.at[t], block_sems.at[t]) for t in range(tiles)
        ]
        for copy in scalars + loads:
            copy.start()
        for phase in range(2):
            for x in range(tiles_x):
                for y in range(tiles_y):
                    source_ref[phase, x * tiles_y + y] = source_tile(flat_ref, cells_ref, phase, x, y)
        for copy in scalars:
            copy.wait()
        for t in range(tiles):
            loads[t].wait()
            for offset in range(OFFSETS):
                present = pattern_ref[t // tiles_y, t % tiles_y, offset] > 0
                front_ref[t, offset] = jnp.where(present, blocks_ref[t, offset], jnp.zeros((cells, cells), bf16))
        pos = lax.axis_index("layer")
        own = coupling_ref[group_ref[pos]]
        following = coupling_ref[group_ref[jnp.minimum(pos + 1, layers - 1)]]
        early = first_sweep() == 0
        kappa_ref[0] = jnp.full((8, cells), jnp.where(early, own, following), f32)
        kappa_ref[1] = jnp.full((8, cells), jnp.where(early, following, own), f32)
        for g in range(groups):
            for l in range(layers):
                member_ref[g, l] = jnp.full((tiles, cells), jnp.where(group_ref[l] == g, 1.0, 0.0), f32)

    source, front, kappa, member = call(
        setup_kernel,
        [
            ((2, tiles, *tile), bf16),
            ((tiles, OFFSETS, cells, cells), bf16),
            ((2, 8, cells), f32),
            ((groups, layers, tiles, cells), f32),
        ],
        pattern[0],
        coupling,
        layer_group,
        blocks.reshape(tiles, OFFSETS, cells, cells),
        flat,
        port_row,
        far_args=4,
        scratch=[
            pltpu.SMEM(pattern.shape[1:], jnp.int32),
            pltpu.SMEM(coupling.shape, f32),
            pltpu.SMEM(layer_group.shape, jnp.int32),
            pltpu.VMEM((tiles, OFFSETS, cells, cells), bf16),
            pltpu.SemaphoreType.DMA((3,)),
            pltpu.SemaphoreType.DMA((tiles,)),
        ],
    )

    def waves(phase, kappa_ref):
        def wave(base, field=None, real=None):
            if field is not None:
                factor = kappa_ref[phase, 0:1, :]
                base = (base.astype(f32) + factor * field.astype(f32)).astype(bf16)
            return base if real is None else jnp.where(real, base, jnp.zeros_like(base))

        return wave

    def row_real():
        return [Side(pairing, "row", tiles_x).real for pairing in row_pairs]

    def wave_kernel(step, *refs):
        take = taker(refs)
        phase = int(step >= layers // 2)
        source_ref, kappa_ref, rim_refs, column_refs = take(), take(), take(halos), take(halos)
        field_ref, field_rims, carried = None, [None] * halos, column_refs
        if step > 0:
            field_ref, field_rims, carried = take(), take(halos), take(halos)
        wave_ref, core_ref, side_ref = take(), take(), take()
        if step > 0:
            for h in range(halos):
                core_ref[ext + h] = carried[h][0]
        else:
            for h in range(halos):
                for p in range(2):
                    core_ref[ext + p * halos + h] = column_refs[h][p, 0]

        @pl.when(is_active(step))
        def _():
            wave = waves(phase, kappa_ref)
            real = row_real()
            for x in range(tiles_x):
                for y in range(tiles_y):
                    t = x * tiles_y + y
                    wave_ref[x, y] = wave(source_ref[phase, t], None if step == 0 else field_ref[t])
                side_ref[x] = wave(column_refs[0][phase, x], None if step == 0 else carried[0][x])
            for h in range(halos):
                for y in range(tiles_y):
                    wave_ref[tiles_x + h, y] = wave(
                        rim_refs[h][phase, y], None if step == 0 else field_rims[h][y], real[h]
                    )
            edge = Side(near, "col", tiles_y).edge
            for x in range(ext):
                core_ref[x] = wave_ref[x, edge]

    def product(lhs, rhs):
        return jnp.dot(lhs, rhs, preferred_element_type=f32)

    def add_column(across, sum_ref, front_ref, halo_ref):
        for x in range(tiles_x):
            t = x * tiles_y + across.edge
            reach = [a for a in (-1, 0, 1) if 0 <= x + a < tiles_x]
            lhs = jnp.concatenate([halo_ref[x + a] for a in reach], axis=1)
            rhs = jnp.concatenate([front_ref[t, 3 * (a + 1) + 1 + across.step] for a in reach], axis=0)
            sum_ref[t] += product(lhs, rhs)

    def add_corner(across, pairing, sum_ref, front_ref, corner):
        side = Side(pairing, "row", tiles_x)
        t = side.edge * tiles_y + across.edge
        sum_ref[t] += product(corner, front_ref[t, 3 * (side.step + 1) + 1 + across.step])

    def inner_kernel(step, wave_ref, side_ref, front_ref, sum_ref):
        @pl.when(is_active(step))
        def _():
            for y in range(tiles_y):
                low, high = max(y - 1, 0), min(y + 1, tiles_y - 1)
                width = high - low + 1
                first = low - y + 1
                beside = [
                    jnp.concatenate([wave_ref[x, j] for j in range(low, high + 1)], axis=1) for x in range(ext)
                ]
                for x in range(tiles_x):
                    reach = [a for a in (-1, 0, 1) if 0 <= x + a < tiles_x]
                    lhs = jnp.concatenate([beside[x + a] for a in reach], axis=1)
                    rhs = jnp.concatenate(
                        [
                            front_ref[x * tiles_y + y, 3 * (a + 1) + first : 3 * (a + 1) + first + width].reshape(
                                width * cells, cells
                            )
                            for a in reach
                        ],
                        axis=0,
                    )
                    sum_ref[x * tiles_y + y] = product(lhs, rhs)
                for h, pairing in enumerate(row_pairs):
                    side = Side(pairing, "row", tiles_x)
                    t = side.edge * tiles_y + y
                    rhs = front_ref[t, pl.ds(3 * (side.step + 1) + first, width)].reshape(width * cells, cells)
                    sum_ref[t] += product(beside[tiles_x + h], rhs)
            across = Side(far, "col", tiles_y)
            across.when(lambda: add_column(across, sum_ref, front_ref, side_ref))

    def add_far_corners(step, sum_ref, front_ref, kappa_ref, core_ref, base_ref):
        phase = int(step >= layers // 2)
        wave = waves(phase, kappa_ref)
        real = row_real()
        beyond = Side(far, "col", tiles_y)

        def corners():
            for h, pairing in enumerate(row_pairs):
                base = base_ref[ext + phase * halos + h]
                corner = wave(base, None if step == 0 else core_ref[ext + h], real[h])
                add_corner(beyond, pairing, sum_ref, front_ref, corner)

        beyond.when(corners)

    def corner_front_kernel(step, *refs):
        take = taker(refs)
        take()
        front_ref, kappa_ref, core_ref, base_ref, sum_ref, corner_ref = (take() for _ in range(6))

        @pl.when(is_active(step))
        def _():
            add_far_corners(step, sum_ref, front_ref, kappa_ref, core_ref, base_ref)
            edge = Side(far, "col", tiles_y).edge
            for h, pairing in enumerate(row_pairs):
                row = Side(pairing, "row", tiles_x).edge
                corner_ref[h] = sum_ref[row * tiles_y + edge].astype(bf16)

    def outer_kernel(step, *refs):
        take = taker(refs)
        take()
        front_ref, core_ref = take(), take()
        last = step == layers - 1
        kappa_ref, base_ref = (take(), take()) if last else (None, None)
        earlier = take(layers - 1) if last else []
        sum_ref, field_ref, rest = take(), take(), take(halos + 1)

        @pl.when(is_active(step))
        def _():
            if last:
                add_far_corners(step, sum_ref, front_ref, kappa_ref, core_ref, base_ref)
            across = Side(near, "col", tiles_y)
            add_column(across, sum_ref, front_ref, core_ref)
            for h, pairing in enumerate(row_pairs):
                add_corner(across, pairing, sum_ref, front_ref, core_ref[tiles_x + h])
            for t in range(tiles):
                field_ref[t] = sum_ref[t].astype(bf16)
            if not last:
                edge = Side(far, "col", tiles_y).edge
                for x in range(tiles_x):
                    rest[halos][x] = field_ref[x * tiles_y + edge]
                for h, pairing in enumerate(row_pairs):
                    row = Side(pairing, "row", tiles_x).edge
                    rest[h][...] = field_ref[pl.ds(row * tiles_y, tiles_y)]

        if step == layers - 1:
            pos = lax.axis_index("layer")
            first = jnp.minimum(pos, layers - 1 - pos)
            for k in range(layers // 2):

                @pl.when(first == k)
                def _(k=k):
                    one, other = earlier[k], field_ref if k == 0 else earlier[layers - 1 - k]
                    for t in range(tiles):
                        both = one[t].astype(f32) * other[t].astype(f32)
                        rest[0][t : t + 1, :] = jnp.sum(both, axis=0, keepdims=True) * intersection_scale

    fields, field_arrived, first_core = [], [], None
    for step in range(layers):
        last = step == layers - 1
        wave, core, side = call(
            functools.partial(wave_kernel, step),
            [
                ((ext, tiles_y, *tile), bf16),
                ((ext + halos * (2 if step == 0 else 1), *tile), bf16),
                ((tiles_x, *tile), bf16),
            ],
            source,
            kappa,
            *source_beside,
            *field_arrived,
        )
        core = to_core(core)
        if step == 0:
            first_core = core
        (summed,) = call(
            functools.partial(inner_kernel, step), [((tiles, *tile), f32)], wave, side, front
        )
        base = core if step == 0 else first_core
        if not last:
            summed, corner = call(
                functools.partial(corner_front_kernel, step),
                [((tiles, *tile), f32), ((SPARE * halos, *tile), bf16)],
                summed,
                front,
                kappa,
                core,
                base,
                aliases={0: 0},
            )
            corner = to_core(corner)
        _, field, *extra = call(
            functools.partial(outer_kernel, step),
            [((tiles, *tile), f32), ((tiles, *tile), bf16)]
            + (
                [((tiles, cells), f32)]
                if last
                else [((tiles_y, *tile), bf16)] * halos + [((tiles_x, *tile), bf16)]
            ),
            summed,
            front,
            core,
            *([kappa, base, *fields] if last else []),
            aliases={0: 0},
        )
        fields.append(field)
        if not last:
            field_arrived = exchange(step, corner, extra, field)
    intersection = extra[0]

    def fields_kernel(*refs):
        field_refs, (forward_ref, adjoint_ref, flat_ref) = refs[:layers], refs[layers:]
        pos = lax.axis_index("layer")
        for out_ref, active in ((forward_ref, lambda s: s), (adjoint_ref, lambda s: layers - 1 - s)):
            for step in range(layers):

                @pl.when(pos == active(step))
                def _(step=step):
                    for t in range(tiles):
                        flat_ref[pl.ds(t, ports, stride=tiles), :] = field_refs[step][t].astype(f32)

            out_ref[...] = flat_ref[...].reshape(ports, tiles, cells).astype(bf16)

    forward, adjoint = call(
        fields_kernel,
        [((ports, tiles, cells), bf16)] * 2,
        *fields,
        scratch=[pltpu.VMEM((ports * tiles, cells), f32)],
    )

    if layers == 4:
        parts = [intersection] + [
            permuted(intersection, lambda l, r, c, m=m: (l ^ m, r, c)) for m in range(1, layers)
        ]

        def gradient_kernel(*refs):
            part_refs, member_ref, out_ref = refs[:layers], refs[layers], refs[layers + 1]
            pos = lax.axis_index("layer")
            for g in range(groups):
                total = jnp.zeros((tiles, cells), f32)
                for m in range(layers):
                    total = total + member_ref[g, pos ^ m] * part_refs[m][...]
                for x in range(tiles_x):
                    out_ref[g, x] = total[x * tiles_y : (x + 1) * tiles_y]

        (gradient,) = call(
            gradient_kernel, [((groups, tiles_x, tiles_y, cells), f32)], *parts, member
        )
    else:
        selected = lax.dynamic_index_in_dim(member, lax.axis_index("layer"), 1, keepdims=False)
        gradient = lax.psum(selected * intersection[None], "layer").reshape(groups, tiles_x, tiles_y, cells)
    shape = (1, ports, tiles_x, tiles_y, cells)
    return (forward.reshape(shape), adjoint.reshape(shape), gradient)


def solution(mesh):
    placed = (
        P("layer", None, "row", "col", None),
        P("layer", None, "row", "col", None),
        P("layer", "row", "col", None, None, None),
        P("layer", "row", "col", None),
        P(),
        P(),
        P(),
    )
    return jax.shard_map(
        local,
        mesh=mesh,
        in_specs=placed,
        out_specs=(
            P("layer", None, "row", "col", None),
            P("layer", None, "row", "col", None),
            P(None, "row", "col", None),
        ),
        check_vma=False,
    )
```

time: 56.2 us -> 49.9 us (0.89)
  waiting for transfers between devices: 23.4 us -> 16.1 us
  starting transfers between devices: 25.8 us -> 26.8 us
    ppermute x18 -> x22, waiting for transfers between devices: 23.4 us -> 16.1 us  [permuted(): return lax.ppermute(array, AXES, pairs)]
    ppermute x18 -> x22, starting transfers between devices: 25.8 us -> 26.8 us  [permuted(): return lax.ppermute(array, AXES, pairs)]
    pallas_call x16 -> x24, Pallas kernels: 5.98 us -> 6.05 us  [call(): pl.pallas_call(kernel, out_shape=[jax.ShapeDtypeStruct(shape, dtype) for...]
  transfers between devices with their start and end apart: 18 -> 22, of which waited for: 10 -> 13; matrix products, arithmetic and copies ran while one was open for 0% -> 0% of each run, Pallas kernels for 6% -> 8%
where the time goes in v3:
time: 49.9 us; the launch traced here: 49.7 us
  starting transfers between devices  26.8 us (54%)
  waiting for transfers between devices  16.1 us (32%)
  Pallas kernels  6.05 us (12%)
  between operations  0.75 us (2%)
    ppermute x22, starting transfers between devices, permuted(): return lax.ppermute(array, AXES, pairs)  26.8 us
    ppermute x22, waiting for transfers between devices, permuted(): return lax.ppermute(array, AXES, pairs)  16.1 us
    pallas_call x24, Pallas kernels, call(): pl.pallas_call(kernel, out_shape=[jax.ShapeDtypeStruct(shape, dtype) for...  6.05 us
  transfers between devices with their start and end apart: 22, of which 13 were waited for; matrix products, arithmetic and copies ran while one was open for 0% of the time, Pallas kernels for 8%

profile of v3, /device:TPU:0, one launch (start us, length us, event | category | flops | bytes accessed | tf_op | source)
XLA Modules:
  0.0 49.7 jit_solution(11688474391009894120)
XLA Ops:
  0.6 1.1 %shard_map.94 = (f32[2,512,128]{2,1,0:T(8,128)S(1)}, s32[1,64]{1,0:T(1,128)S(1)}, bf16[2,2,64,128]{3,2,1,0:T(8,128)(2,1)S(1)}) custom-call(bf16[64,8,128]{2,1,0:T(8,128)(2,1)} %bitcast.8, bf16[64,8,128]{2,1,0:T(8,128)(2,1)} %bitcast.9, s32[1,64]{1,0:T(1,128)} %bitcast.11), custom_call_target="tpu_custom_call" | custom-call | tf_op jit(solution)/shard_map/pallas_call | solution.py:22
  1.7 0.5 %collective-permute-start.1 = (bf16[2,2,64,128]{3,2,1,0:T(8,128)(2,1)S(1)}, bf16[2,2,64,128]{3,2,1,0:T(8,128)(2,1)S(1)}, u32[]{:S(2)}, u32[]{:S(2)}) collective-permute-start(bf16[2,2,64,128]{3,2,1,0:T(8,128)(2,1)S(1)} %get-tuple-element.49), channel_id=1, source_target_pairs={{0,1},{1,0},{2,3},{3,2},{4,5},{5,4},{6,7},{7,6},{8,9},{9,8},{10,11... | collective-permute-start | bytes 196616 | tf_op jit(solution)/shard_map/ppermute | solution.py:85
  2.3 0.2 shard_map.96
  2.5 2.6 %collective-permute-start = (bf16[2,4,64,128]{3,2,1,0:T(8,128)(2,1)S(1)}, bf16[2,4,64,128]{3,2,1,0:T(8,128)(2,1)S(1)}, u32[]{:S(2)}, u32[]{:S(2)}) collective-permute-start(bf16[2,4,64,128]{3,2,1,0:T(8,128)(2,1)S(1)} %get-tuple-element.47), channel_id=1, source_target_pairs={{0,4},{1,5},{2,6},{3,7},{4,0},{5,1},{6,2},{7,3},{8,12},{9,13},{10,... | collective-permute-start | bytes 393224 | tf_op jit(solution)/shard_map/ppermute | solution.py:85
  5.1 0.0 collective-permute-done.1.refs_1_
  5.1 1.7 %collective-permute-start.2 = (bf16[2,2,64,128]{3,2,1,0:T(8,128)(2,1)S(1)}, bf16[2,2,64,128]{3,2,1,0:T(8,128)(2,1)S(1)}, u32[]{:S(2)}, u32[]{:S(2)}) collective-permute-start(bf16[2,2,64,128]{3,2,1,0:T(8,128)(2,1)S(1)} %shard_map.97), channel_id=1, source_target_pairs={{0,7},{1,2},{2,1},{3,4},{4,3},{5,6},{6,5},{7,0},{8,15},{9,10},{10,... | collective-permute-start | bytes 196616 | tf_op jit(solution)/shard_map/ppermute | solution.py:85
  6.7 1.8 %shard_map.95 = (bf16[2,8,64,128]{3,2,1,0:T(8,128)(2,1)S(1)}, bf16[8,9,128,128]{3,2,1,0:T(8,128)(2,1)S(1)}, f32[2,8,128]{2,1,0:T(8,128)S(1)}, f32[4,4,8,128]{3,2,1,0:T(8,128)S(1)}) custom-call(s32[2,4,9]{2,1,0:T(4,128)} %bitcast.10, f32[4]{0:T(128)} %coupling_hbm.1, s32[4]{0:T(128)} %group_hbm.1, bf16[8,9,128,128]{3,2,1,0:T(8,128)(2,1)} %bitcast.7, ...), custom_call_target="tpu_custom_call" | custom-call | tf_op jit(solution)/shard_map/pallas_call | solution.py:22
  8.5 1.7 %collective-permute-done.2.refs_3_ = bf16[2,2,64,128]{3,2,1,0:T(8,128)(2,1)S(1)} collective-permute-done((bf16[2,2,64,128]{3,2,1,0:T(8,128)(2,1)S(1)}, bf16[2,2,64,128]{3,2,1,0:T(8,128)(2,1)S(1)}, u32[]{:S(2)}, u32[]{:S(2)}) %collective-permute-start.2) | collective-permute-done | bytes 65568 | tf_op jit(solution)/shard_map/ppermute | solution.py:85
  10.2 0.1 collective-permute-start.3
  10.3 0.5 shard_map.99.refs_0_
  10.8 0.8 %collective-permute-done.3.refs_3_.refs_4_.refs_2_ = bf16[5,64,128]{2,1,0:T(8,128)(2,1)S(1)} collective-permute-done((bf16[5,64,128]{2,1,0:T(8,128)(2,1)S(1)}, bf16[5,64,128]{2,1,0:T(8,128)(2,1)S(1)}, u32[]{:S(2)}, u32[]{:S(2)}) %collective-permute-start.3) | collective-permute-done | bytes 81952 | tf_op jit(solution)/shard_map/ppermute | solution.py:85
  11.6 0.2 shard_map.101
  11.8 1.3 %collective-permute-start.4 = (bf16[8,64,128]{2,1,0:T(8,128)(2,1)S(1)}, bf16[8,64,128]{2,1,0:T(8,128)(2,1)S(1)}, u32[]{:S(2)}, u32[]{:S(2)}) collective-permute-start(bf16[8,64,128]{2,1,0:T(8,128)(2,1)S(1)} %get-tuple-element.55.refs_5_.refs_0_), channel_id=1, source_target_pairs={{0,8},{1,9},{2,10},{3,11},{4,12},{5,13},{6,14},{7,15},{8,0},{9,1},... | collective-permute-start | bytes 393224 | tf_op jit(solution)/shard_map/ppermute | solution.py:85
  13.1 1.7 %collective-permute-start.5 = (bf16[4,64,128]{2,1,0:T(8,128)(2,1)S(1)}, bf16[4,64,128]{2,1,0:T(8,128)(2,1)S(1)}, u32[]{:S(2)}, u32[]{:S(2)}) collective-permute-start(bf16[4,64,128]{2,1,0:T(8,128)(2,1)S(1)} %get-tuple-element.56), channel_id=1, source_target_pairs={{0,12},{1,13},{2,14},{3,15},{4,8},{5,9},{6,10},{7,11},{8,4},{9,5},... | collective-permute-start | bytes 196616 | tf_op jit(solution)/shard_map/ppermute | solution.py:85
  14.8 0.0 collective-permute-done.6.refs_1_
  14.8 2.0 %collective-permute-start.7 = (bf16[2,64,128]{2,1,0:T(8,128)(2,1)S(1)}, bf16[2,64,128]{2,1,0:T(8,128)(2,1)S(1)}, u32[]{:S(2)}, u32[]{:S(2)}) collective-permute-start(bf16[2,64,128]{2,1,0:T(8,128)(2,1)S(1)} %shard_map.102), channel_id=1, source_target_pairs={{0,15},{1,10},{2,9},{3,12},{4,11},{5,14},{6,13},{7,8},{8,7},{9,2},... | collective-permute-start | bytes 98312 | tf_op jit(solution)/shard_map/ppermute | solution.py:85
  16.8 3.6 %collective-permute-done.7.refs_6_ = bf16[2,64,128]{2,1,0:T(8,128)(2,1)S(1)} collective-permute-done((bf16[2,64,128]{2,1,0:T(8,128)(2,1)S(1)}, bf16[2,64,128]{2,1,0:T(8,128)(2,1)S(1)}, u32[]{:S(2)}, u32[]{:S(2)}) %collective-permute-start.7) | collective-permute-done | bytes 32800 | tf_op jit(solution)/shard_map/ppermute | solution.py:85
  20.4 0.0 collective-permute-done.5.refs_5_
  20.4 0.1 collective-permute-start.8
  20.5 1.2 %collective-permute-done.8.refs_3_.refs_2_ = bf16[4,64,128]{2,1,0:T(8,128)(2,1)S(1)} collective-permute-done((bf16[4,64,128]{2,1,0:T(8,128)(2,1)S(1)}, bf16[4,64,128]{2,1,0:T(8,128)(2,1)S(1)}, u32[]{:S(2)}, u32[]{:S(2)}) %collective-permute-start.8) | collective-permute-done | bytes 65568 | tf_op jit(solution)/shard_map/ppermute | solution.py:85
  21.8 0.2 collective-permute-start.9
  21.9 0.4 collective-permute-start.11
  22.3 0.2 collective-permute-start.10
  22.4 0.7 %collective-permute-done.11.refs_1_ = bf16[2,64,128]{2,1,0:T(8,128)(2,1)S(1)} collective-permute-done((bf16[2,64,128]{2,1,0:T(8,128)(2,1)S(1)}, bf16[2,64,128]{2,1,0:T(8,128)(2,1)S(1)}, u32[]{:S(2)}, u32[]{:S(2)}) %collective-permute-start.11) | collective-permute-done | bytes 32800 | tf_op jit(solution)/shard_map/ppermute | solution.py:85
  23.2 0.3 collective-permute-start.12
  23.5 0.0 collective-permute-done.10.refs_5_
  23.5 0.8 %collective-permute-done.12.refs_6_ = bf16[2,64,128]{2,1,0:T(8,128)(2,1)S(1)} collective-permute-done((bf16[2,64,128]{2,1,0:T(8,128)(2,1)S(1)}, bf16[2,64,128]{2,1,0:T(8,128)(2,1)S(1)}, u32[]{:S(2)}, u32[]{:S(2)}) %collective-permute-start.12) | collective-permute-done | bytes 32800 | tf_op jit(solution)/shard_map/ppermute | solution.py:85
  24.4 0.3 collective-permute-start.13
  24.7 0.9 %collective-permute-done.13.refs_3_.refs_2_ = bf16[4,64,128]{2,1,0:T(8,128)(2,1)S(1)} collective-permute-done((bf16[4,64,128]{2,1,0:T(8,128)(2,1)S(1)}, bf16[4,64,128]{2,1,0:T(8,128)(2,1)S(1)}, u32[]{:S(2)}, u32[]{:S(2)}) %collective-permute-start.13) | collective-permute-done | bytes 65568 | tf_op jit(solution)/shard_map/ppermute | solution.py:85
  25.6 8.1 %collective-permute-start.14 = (bf16[8,64,128]{2,1,0:T(8,128)(2,1)S(1)}, bf16[8,64,128]{2,1,0:T(8,128)(2,1)S(1)}, u32[]{:S(2)}, u32[]{:S(2)}) collective-permute-start(bf16[8,64,128]{2,1,0:T(8,128)(2,1)S(1)} %get-tuple-element.71.refs_7_.refs_2_), channel_id=1, source_target_pairs={{0,8},{1,9},{2,10},{3,11},{4,12},{5,13},{6,14},{7,15},{8,0},{9,1},... | collective-permute-start | bytes 393224 | tf_op jit(solution)/shard_map/ppermute | solution.py:85
  33.8 0.0 collective-permute-start.16
  33.8 0.9 %collective-permute-start.15 = (bf16[4,64,128]{2,1,0:T(8,128)(2,1)S(1)}, bf16[4,64,128]{2,1,0:T(8,128)(2,1)S(1)}, u32[]{:S(2)}, u32[]{:S(2)}) collective-permute-start(bf16[4,64,128]{2,1,0:T(8,128)(2,1)S(1)} %get-tuple-element.72), channel_id=1, source_target_pairs={{0,12},{1,13},{2,14},{3,15},{4,8},{5,9},{6,10},{7,11},{8,4},{9,5},... | collective-permute-start | bytes 196616 | tf_op jit(solution)/shard_map/ppermute | solution.py:85
  34.7 0.3 collective-permute-done.16.refs_1_
  35.0 2.0 %collective-permute-start.17 = (bf16[2,64,128]{2,1,0:T(8,128)(2,1)S(1)}, bf16[2,64,128]{2,1,0:T(8,128)(2,1)S(1)}, u32[]{:S(2)}, u32[]{:S(2)}) collective-permute-start(bf16[2,64,128]{2,1,0:T(8,128)(2,1)S(1)} %shard_map.112), channel_id=1, source_target_pairs={{0,15},{1,10},{2,9},{3,12},{4,11},{5,14},{6,13},{7,8},{8,7},{9,2},... | collective-permute-start | bytes 98312 | tf_op jit(solution)/shard_map/ppermute | solution.py:85
  36.9 3.0 %collective-permute-done.15.refs_5_ = bf16[4,64,128]{2,1,0:T(8,128)(2,1)S(1)} collective-permute-done((bf16[4,64,128]{2,1,0:T(8,128)(2,1)S(1)}, bf16[4,64,128]{2,1,0:T(8,128)(2,1)S(1)}, u32[]{:S(2)}, u32[]{:S(2)}) %collective-permute-start.15) | collective-permute-done | bytes 65568 | tf_op jit(solution)/shard_map/ppermute | solution.py:85
  40.0 0.5 %collective-permute-done.17.refs_6_ = bf16[2,64,128]{2,1,0:T(8,128)(2,1)S(1)} collective-permute-done((bf16[2,64,128]{2,1,0:T(8,128)(2,1)S(1)}, bf16[2,64,128]{2,1,0:T(8,128)(2,1)S(1)}, u32[]{:S(2)}, u32[]{:S(2)}) %collective-permute-start.17) | collective-permute-done | bytes 32800 | tf_op jit(solution)/shard_map/ppermute | solution.py:85
  40.5 0.1 shard_map.113
  40.5 0.1 collective-permute-start.18
  40.6 0.5 shard_map.114.refs_0_
  41.1 0.8 %collective-permute-done.18.refs_2_ = bf16[4,64,128]{2,1,0:T(8,128)(2,1)S(1)} collective-permute-done((bf16[4,64,128]{2,1,0:T(8,128)(2,1)S(1)}, bf16[4,64,128]{2,1,0:T(8,128)(2,1)S(1)}, u32[]{:S(2)}, u32[]{:S(2)}) %collective-permute-start.18) | collective-permute-done | bytes 65568 | tf_op jit(solution)/shard_map/ppermute | solution.py:85
  41.9 0.2 shard_map.115
  42.1 2.5 %collective-permute-start.21 = (f32[8,128]{1,0:T(8,128)S(1)}, f32[8,128]{1,0:T(8,128)S(1)}, u32[]{:S(2)}, u32[]{:S(2)}) collective-permute-start(f32[8,128]{1,0:T(8,128)S(1)} %get-tuple-element.81.refs_0_), channel_id=1, source_target_pairs={{0,24},{1,25},{2,26},{3,27},{4,28},{5,29},{6,30},{7,31},{8,16},{9,... | collective-permute-start | bytes 12296 | tf_op jit(solution)/shard_map/ppermute | solution.py:85
  44.6 0.2 collective-permute-start.20
  44.8 1.8 %collective-permute-start.19 = (f32[8,128]{1,0:T(8,128)S(1)}, f32[8,128]{1,0:T(8,128)S(1)}, u32[]{:S(2)}, u32[]{:S(2)}) collective-permute-start(f32[8,128]{1,0:T(8,128)S(1)} %get-tuple-element.81.refs_0_), channel_id=1, source_target_pairs={{0,8},{1,9},{2,10},{3,11},{4,12},{5,13},{6,14},{7,15},{8,0},{9,1},... | collective-permute-start | bytes 12296 | tf_op jit(solution)/shard_map/ppermute | solution.py:85
  46.6 0.8 %shard_map.116 = (bf16[64,8,128]{2,1,0:T(8,128)(2,1)}, bf16[64,8,128]{2,1,0:T(8,128)(2,1)}) custom-call(bf16[8,64,128]{2,1,0:T(8,128)(2,1)S(1)} %get-tuple-element.55.refs_5_.refs_0_, bf16[8,64,128]{2,1,0:T(8,128)(2,1)S(1)} %get-tuple-element.63.refs_6_.refs_1_, bf16[8,64,128]{2,1,0:T(8,128)(2,1)S(1)} %get-tuple-element.71.refs_7_.refs_2_, ...), custom_call_target="tpu_custom_call" | custom-call | tf_op jit(solution)/shard_map/pallas_call | solution.py:22
  47.4 0.2 collective-permute-done.21.refs_3_
  47.6 1.5 %collective-permute-done.20.refs_2_ = f32[8,128]{1,0:T(8,128)S(1)} collective-permute-done((f32[8,128]{1,0:T(8,128)S(1)}, f32[8,128]{1,0:T(8,128)S(1)}, u32[]{:S(2)}, u32[]{:S(2)}) %collective-permute-start.20) | collective-permute-done | bytes 4128 | tf_op jit(solution)/shard_map/ppermute | solution.py:85
  49.1 0.6 %shard_map.117 = f32[4,2,4,128]{3,2,1,0:T(4,128)} custom-call(f32[8,128]{1,0:T(8,128)S(1)} %get-tuple-element.81.refs_0_, f32[8,128]{1,0:T(8,128)S(1)} %collective-permute-done.19.refs_1_, f32[8,128]{1,0:T(8,128)S(1)} %collective-permute-done.20.refs_2_, f32[8,128]{1,0:T(8,128)S(1)} %collective-permute-done.21.refs_3_, ...), custom_call_target="tpu_custom_call" | custom-call | tf_op jit(solution)/shard_map/pallas_call | solution.py:22
  (20 shorter events, 0.1 us)
Async XLA Ops:
  1.7 3.3 %collective-permute-start.1 = (bf16[2,2,64,128]{3,2,1,0:T(8,128)(2,1)S(1)}, bf16[2,2,64,128]{3,2,1,0:T(8,128)(2,1)S(1)}, u32[]{:S(2)}, u32[]{:S(2)}) collective-permute-start(bf16[2,2,64,128]{3,2,1,0:T(8,128)(2,1)S(1)} %get-tuple-element.49), channel_id=1, source_target_pairs={{0,1},{1,0},{2,3},{3,2},{4,5},{5,4},{6,7},{7,6},{8,9},{9,8},{10,11... | collective-permute-start | bytes 196616 | tf_op jit(solution)/shard_map/ppermute | solution.py:85
  2.5 7.8 %collective-permute-start = (bf16[2,4,64,128]{3,2,1,0:T(8,128)(2,1)S(1)}, bf16[2,4,64,128]{3,2,1,0:T(8,128)(2,1)S(1)}, u32[]{:S(2)}, u32[]{:S(2)}) collective-permute-start(bf16[2,4,64,128]{3,2,1,0:T(8,128)(2,1)S(1)} %get-tuple-element.47), channel_id=1, source_target_pairs={{0,4},{1,5},{2,6},{3,7},{4,0},{5,1},{6,2},{7,3},{8,12},{9,13},{10,... | collective-permute-start | bytes 393224 | tf_op jit(solution)/shard_map/ppermute | solution.py:85
  5.1 5.1 %collective-permute-start.2 = (bf16[2,2,64,128]{3,2,1,0:T(8,128)(2,1)S(1)}, bf16[2,2,64,128]{3,2,1,0:T(8,128)(2,1)S(1)}, u32[]{:S(2)}, u32[]{:S(2)}) collective-permute-start(bf16[2,2,64,128]{3,2,1,0:T(8,128)(2,1)S(1)} %shard_map.97), channel_id=1, source_target_pairs={{0,7},{1,2},{2,1},{3,4},{4,3},{5,6},{6,5},{7,0},{8,15},{9,10},{10,... | collective-permute-start | bytes 196616 | tf_op jit(solution)/shard_map/ppermute | solution.py:85
  10.2 1.3 %collective-permute-start.3 = (bf16[5,64,128]{2,1,0:T(8,128)(2,1)S(1)}, bf16[5,64,128]{2,1,0:T(8,128)(2,1)S(1)}, u32[]{:S(2)}, u32[]{:S(2)}) collective-permute-start(bf16[5,64,128]{2,1,0:T(8,128)(2,1)S(1)} %get-tuple-element.53), channel_id=1, source_target_pairs={{0,1},{1,0},{2,3},{3,2},{4,5},{5,4},{6,7},{7,6},{8,9},{9,8},{10,11... | collective-permute-start | bytes 245768 | tf_op jit(solution)/shard_map/ppermute | solution.py:85
  11.8 8.6 %collective-permute-start.4 = (bf16[8,64,128]{2,1,0:T(8,128)(2,1)S(1)}, bf16[8,64,128]{2,1,0:T(8,128)(2,1)S(1)}, u32[]{:S(2)}, u32[]{:S(2)}) collective-permute-start(bf16[8,64,128]{2,1,0:T(8,128)(2,1)S(1)} %get-tuple-element.55.refs_5_.refs_0_), channel_id=1, source_target_pairs={{0,8},{1,9},{2,10},{3,11},{4,12},{5,13},{6,14},{7,15},{8,0},{9,1},... | collective-permute-start | bytes 393224 | tf_op jit(solution)/shard_map/ppermute | solution.py:85
  13.1 1.7 %collective-permute-start.6 = (bf16[2,64,128]{2,1,0:T(8,128)(2,1)S(1)}, bf16[2,64,128]{2,1,0:T(8,128)(2,1)S(1)}, u32[]{:S(2)}, u32[]{:S(2)}) collective-permute-start(bf16[2,64,128]{2,1,0:T(8,128)(2,1)S(1)} %get-tuple-element.58), channel_id=1, source_target_pairs={{0,1},{1,0},{2,3},{3,2},{4,5},{5,4},{6,7},{7,6},{8,9},{9,8},{10,11... | collective-permute-start | bytes 98312 | tf_op jit(solution)/shard_map/ppermute | solution.py:85
  13.1 7.3 %collective-permute-start.5 = (bf16[4,64,128]{2,1,0:T(8,128)(2,1)S(1)}, bf16[4,64,128]{2,1,0:T(8,128)(2,1)S(1)}, u32[]{:S(2)}, u32[]{:S(2)}) collective-permute-start(bf16[4,64,128]{2,1,0:T(8,128)(2,1)S(1)} %get-tuple-element.56), channel_id=1, source_target_pairs={{0,12},{1,13},{2,14},{3,15},{4,8},{5,9},{6,10},{7,11},{8,4},{9,5},... | collective-permute-start | bytes 196616 | tf_op jit(solution)/shard_map/ppermute | solution.py:85
  14.8 5.6 %collective-permute-start.7 = (bf16[2,64,128]{2,1,0:T(8,128)(2,1)S(1)}, bf16[2,64,128]{2,1,0:T(8,128)(2,1)S(1)}, u32[]{:S(2)}, u32[]{:S(2)}) collective-permute-start(bf16[2,64,128]{2,1,0:T(8,128)(2,1)S(1)} %shard_map.102), channel_id=1, source_target_pairs={{0,15},{1,10},{2,9},{3,12},{4,11},{5,14},{6,13},{7,8},{8,7},{9,2},... | collective-permute-start | bytes 98312 | tf_op jit(solution)/shard_map/ppermute | solution.py:85
  20.4 1.3 %collective-permute-start.8 = (bf16[4,64,128]{2,1,0:T(8,128)(2,1)S(1)}, bf16[4,64,128]{2,1,0:T(8,128)(2,1)S(1)}, u32[]{:S(2)}, u32[]{:S(2)}) collective-permute-start(bf16[4,64,128]{2,1,0:T(8,128)(2,1)S(1)} %get-tuple-element.61), channel_id=1, source_target_pairs={{0,1},{1,0},{2,3},{3,2},{4,5},{5,4},{6,7},{7,6},{8,9},{9,8},{10,11... | collective-permute-start | bytes 196616 | tf_op jit(solution)/shard_map/ppermute | solution.py:85
  21.8 2.6 %collective-permute-start.9 = (bf16[8,64,128]{2,1,0:T(8,128)(2,1)S(1)}, bf16[8,64,128]{2,1,0:T(8,128)(2,1)S(1)}, u32[]{:S(2)}, u32[]{:S(2)}) collective-permute-start(bf16[8,64,128]{2,1,0:T(8,128)(2,1)S(1)} %get-tuple-element.63.refs_6_.refs_1_), channel_id=1, source_target_pairs={{0,1},{1,0},{2,3},{3,2},{4,5},{5,4},{6,7},{7,6},{8,16},{9,17},{10,... | collective-permute-start | bytes 393224 | tf_op jit(solution)/shard_map/ppermute | solution.py:85
  21.9 1.2 %collective-permute-start.11 = (bf16[2,64,128]{2,1,0:T(8,128)(2,1)S(1)}, bf16[2,64,128]{2,1,0:T(8,128)(2,1)S(1)}, u32[]{:S(2)}, u32[]{:S(2)}) collective-permute-start(bf16[2,64,128]{2,1,0:T(8,128)(2,1)S(1)} %get-tuple-element.66), channel_id=1, source_target_pairs={{0,1},{1,0},{2,3},{3,2},{4,5},{5,4},{6,7},{7,6},{8,9},{9,8},{10,11... | collective-permute-start | bytes 98312 | tf_op jit(solution)/shard_map/ppermute | solution.py:85
  22.3 1.3 %collective-permute-start.10 = (bf16[4,64,128]{2,1,0:T(8,128)(2,1)S(1)}, bf16[4,64,128]{2,1,0:T(8,128)(2,1)S(1)}, u32[]{:S(2)}, u32[]{:S(2)}) collective-permute-start(bf16[4,64,128]{2,1,0:T(8,128)(2,1)S(1)} %get-tuple-element.64), channel_id=1, source_target_pairs={{0,1},{1,0},{2,3},{3,2},{4,5},{5,4},{6,7},{7,6},{8,20},{9,21},{10,... | collective-permute-start | bytes 196616 | tf_op jit(solution)/shard_map/ppermute | solution.py:85
  23.2 1.2 %collective-permute-start.12 = (bf16[2,64,128]{2,1,0:T(8,128)(2,1)S(1)}, bf16[2,64,128]{2,1,0:T(8,128)(2,1)S(1)}, u32[]{:S(2)}, u32[]{:S(2)}) collective-permute-start(bf16[2,64,128]{2,1,0:T(8,128)(2,1)S(1)} %shard_map.107), channel_id=1, source_target_pairs={{0,1},{1,0},{2,3},{3,2},{4,5},{5,4},{6,7},{7,6},{8,23},{9,18},{10,... | collective-permute-start | bytes 98312 | tf_op jit(solution)/shard_map/ppermute | solution.py:85
  24.4 1.3 %collective-permute-start.13 = (bf16[4,64,128]{2,1,0:T(8,128)(2,1)S(1)}, bf16[4,64,128]{2,1,0:T(8,128)(2,1)S(1)}, u32[]{:S(2)}, u32[]{:S(2)}) collective-permute-start(bf16[4,64,128]{2,1,0:T(8,128)(2,1)S(1)} %get-tuple-element.69), channel_id=1, source_target_pairs={{0,1},{1,0},{2,3},{3,2},{4,5},{5,4},{6,7},{7,6},{8,9},{9,8},{10,11... | collective-permute-start | bytes 196616 | tf_op jit(solution)/shard_map/ppermute | solution.py:85
  25.6 14.8 %collective-permute-start.14 = (bf16[8,64,128]{2,1,0:T(8,128)(2,1)S(1)}, bf16[8,64,128]{2,1,0:T(8,128)(2,1)S(1)}, u32[]{:S(2)}, u32[]{:S(2)}) collective-permute-start(bf16[8,64,128]{2,1,0:T(8,128)(2,1)S(1)} %get-tuple-element.71.refs_7_.refs_2_), channel_id=1, source_target_pairs={{0,8},{1,9},{2,10},{3,11},{4,12},{5,13},{6,14},{7,15},{8,0},{9,1},... | collective-permute-start | bytes 393224 | tf_op jit(solution)/shard_map/ppermute | solution.py:85
  33.8 1.2 %collective-permute-start.16 = (bf16[2,64,128]{2,1,0:T(8,128)(2,1)S(1)}, bf16[2,64,128]{2,1,0:T(8,128)(2,1)S(1)}, u32[]{:S(2)}, u32[]{:S(2)}) collective-permute-start(bf16[2,64,128]{2,1,0:T(8,128)(2,1)S(1)} %get-tuple-element.74), channel_id=1, source_target_pairs={{0,1},{1,0},{2,3},{3,2},{4,5},{5,4},{6,7},{7,6},{8,9},{9,8},{10,11... | collective-permute-start | bytes 98312 | tf_op jit(solution)/shard_map/ppermute | solution.py:85
  33.8 6.2 %collective-permute-start.15 = (bf16[4,64,128]{2,1,0:T(8,128)(2,1)S(1)}, bf16[4,64,128]{2,1,0:T(8,128)(2,1)S(1)}, u32[]{:S(2)}, u32[]{:S(2)}) collective-permute-start(bf16[4,64,128]{2,1,0:T(8,128)(2,1)S(1)} %get-tuple-element.72), channel_id=1, source_target_pairs={{0,12},{1,13},{2,14},{3,15},{4,8},{5,9},{6,10},{7,11},{8,4},{9,5},... | collective-permute-start | bytes 196616 | tf_op jit(solution)/shard_map/ppermute | solution.py:85
  35.0 5.5 %collective-permute-start.17 = (bf16[2,64,128]{2,1,0:T(8,128)(2,1)S(1)}, bf16[2,64,128]{2,1,0:T(8,128)(2,1)S(1)}, u32[]{:S(2)}, u32[]{:S(2)}) collective-permute-start(bf16[2,64,128]{2,1,0:T(8,128)(2,1)S(1)} %shard_map.112), channel_id=1, source_target_pairs={{0,15},{1,10},{2,9},{3,12},{4,11},{5,14},{6,13},{7,8},{8,7},{9,2},... | collective-permute-start | bytes 98312 | tf_op jit(solution)/shard_map/ppermute | solution.py:85
  40.5 1.3 %collective-permute-start.18 = (bf16[4,64,128]{2,1,0:T(8,128)(2,1)S(1)}, bf16[4,64,128]{2,1,0:T(8,128)(2,1)S(1)}, u32[]{:S(2)}, u32[]{:S(2)}) collective-permute-start(bf16[4,64,128]{2,1,0:T(8,128)(2,1)S(1)} %get-tuple-element.77), channel_id=1, source_target_pairs={{0,1},{1,0},{2,3},{3,2},{4,5},{5,4},{6,7},{7,6},{8,9},{9,8},{10,11... | collective-permute-start | bytes 196616 | tf_op jit(solution)/shard_map/ppermute | solution.py:85
  42.1 5.5 %collective-permute-start.21 = (f32[8,128]{1,0:T(8,128)S(1)}, f32[8,128]{1,0:T(8,128)S(1)}, u32[]{:S(2)}, u32[]{:S(2)}) collective-permute-start(f32[8,128]{1,0:T(8,128)S(1)} %get-tuple-element.81.refs_0_), channel_id=1, source_target_pairs={{0,24},{1,25},{2,26},{3,27},{4,28},{5,29},{6,30},{7,31},{8,16},{9,... | collective-permute-start | bytes 12296 | tf_op jit(solution)/shard_map/ppermute | solution.py:85
  44.6 4.5 %collective-permute-start.20 = (f32[8,128]{1,0:T(8,128)S(1)}, f32[8,128]{1,0:T(8,128)S(1)}, u32[]{:S(2)}, u32[]{:S(2)}) collective-permute-start(f32[8,128]{1,0:T(8,128)S(1)} %get-tuple-element.81.refs_0_), channel_id=1, source_target_pairs={{0,16},{1,17},{2,18},{3,19},{4,20},{5,21},{6,22},{7,23},{8,24},{9,... | collective-permute-start | bytes 12296 | tf_op jit(solution)/shard_map/ppermute | solution.py:85
  44.8 4.3 %collective-permute-start.19 = (f32[8,128]{1,0:T(8,128)S(1)}, f32[8,128]{1,0:T(8,128)S(1)}, u32[]{:S(2)}, u32[]{:S(2)}) collective-permute-start(f32[8,128]{1,0:T(8,128)S(1)} %get-tuple-element.81.refs_0_), channel_id=1, source_target_pairs={{0,8},{1,9},{2,10},{3,11},{4,12},{5,13},{6,14},{7,15},{8,0},{9,1},... | collective-permute-start | bytes 12296 | tf_op jit(solution)/shard_map/ppermute | solution.py:85

commit v4 on v3

--- a/solution.py
+++ b/solution.py
@@ -168,13 +168,12 @@
         take = taker(refs)
         rim_refs, column_ref = take(halos), take()
         edge = Side(far, "col", tiles_y).edge
-        for phase in range(2):
-            for x in range(tiles_x):
-                column_ref[phase, x] = source_tile(flat_ref, cells_ref, phase, x, edge)
-            for h, pairing in enumerate(row_pairs):
-                row = Side(pairing, "row", tiles_x).edge
-                for y in range(tiles_y):
-                    rim_refs[h][phase, y] = source_tile(flat_ref, cells_ref, phase, row, y)
+        for x in range(tiles_x):
+            column_ref[x] = source_tile(flat_ref, cells_ref, 0, x, edge)
+        for h, pairing in enumerate(row_pairs):
+            row = Side(pairing, "row", tiles_x).edge
+            for y in range(tiles_y):
+                rim_refs[h][y] = source_tile(flat_ref, cells_ref, 0, row, y)
 
     raw_shape = (ports, tiles, cells)
     flat, port_row, corner = call(
@@ -187,11 +186,9 @@
         scratch=[pltpu.VMEM((2, *raw_shape), bf16), pltpu.SemaphoreType.DMA((3,))],
     )
     corner = to_core(corner)
-    outward = call(
-        rims_kernel, [((2, tiles_y, *tile), bf16)] * halos + [((2, tiles_x, *tile), bf16)], flat, port_row
-    )
-
-    def relay_kernel(*refs):
+    outward = call(rims_kernel, [((tiles_y, *tile), bf16)] * halos + [((tiles_x, *tile), bf16)], flat, port_row)
+
+    def relay_kernel(phase, *refs):
         take = taker(refs)
         column_ref, corner_ref, out_refs = take(), take(), take(halos)
         inner = Side(far, "col", tiles_y).real
@@ -199,29 +196,27 @@
         @pl.when(inner)
         def _():
             for out_ref in out_refs:
-                out_ref[...] = column_ref[...]
+                out_ref[:tiles_x] = column_ref[...]
 
         @pl.when(jnp.logical_not(inner))
         def _():
             for h, out_ref in enumerate(out_refs):
-                if len(out_ref.shape) == 4:
-                    for phase in range(2):
-                        out_ref[phase, 0] = corner_ref[h, phase]
-                else:
-                    out_ref[0] = corner_ref[h]
+                out_ref[0] = corner_ref[h] if phase is None else corner_ref[h, phase]
 
     def exchange(step, corner, outward, field=None):
         rims, column = outward[:halos], outward[halos]
         arrived = [] if field is None else [to_layer(step, same)(field)]
         arrived += [to_layer(step, other_row(pairing))(rim) for rim, pairing in zip(rims, row_pairs)]
-        carried = call(relay_kernel, [(column.shape, bf16)] * halos, column, corner)
+        kernel = functools.partial(relay_kernel, 0 if step is None else None)
+        carried = call(kernel, [(column.shape, bf16)] * halos, column, corner)
         return arrived + [to_layer(step, other_chip(pairing))(part) for part, pairing in zip(carried, row_pairs)]
 
     source_beside = exchange(None, corner, outward)
 
     def setup_kernel(pattern_hbm, coupling_hbm, group_hbm, blocks_hbm, *refs):
         take = taker(refs)
-        flat_ref, cells_ref, source_ref, front_ref, kappa_ref, member_ref = (take() for _ in range(6))
+        flat_ref, cells_ref, corner_ref, source_ref, front_ref, kappa_ref, member_ref = (take() for _ in range(7))
+        late_refs, carried_refs = take(halos), take(halos)
         pattern_ref, coupling_ref, group_ref, blocks_ref, sems, block_sems = (take() for _ in range(6))
         scalars = [
             pltpu.make_async_copy(src, dst, sems.at[i])
@@ -238,6 +233,18 @@
             for x in range(tiles_x):
                 for y in range(tiles_y):
                     source_ref[phase, x * tiles_y + y] = source_tile(flat_ref, cells_ref, phase, x, y)
+        for pairing, rim_ref in zip(row_pairs, late_refs):
+            row = Side(pairing, "row", tiles_x).edge
+            rim_ref[...] = source_ref[1, pl.ds(row * tiles_y, tiles_y)]
+        beyond = Side(far, "col", tiles_y)
+        for h, carried_ref in enumerate(carried_refs):
+            for x in range(tiles_x):
+                carried_ref[x] = source_ref[1, x * tiles_y + beyond.edge]
+
+            @pl.when(jnp.logical_not(beyond.real))
+            def _(h=h, carried_ref=carried_ref):
+                carried_ref[0] = corner_ref[h, 1]
+
         for copy in scalars:
             copy.wait()
         for t in range(tiles):
@@ -255,20 +262,23 @@
             for l in range(layers):
                 member_ref[g, l] = jnp.full((tiles, cells), jnp.where(group_ref[l] == g, 1.0, 0.0), f32)
 
-    source, front, kappa, member = call(
+    source, front, kappa, member, *late = call(
         setup_kernel,
         [
             ((2, tiles, *tile), bf16),
             ((tiles, OFFSETS, cells, cells), bf16),
             ((2, 8, cells), f32),
             ((groups, layers, tiles, cells), f32),
-        ],
+        ]
+        + [((tiles_y, *tile), bf16)] * halos
+        + [((max(tiles_x, tiles_y), *tile), bf16)] * halos,
         pattern[0],
         coupling,
         layer_group,
         blocks.reshape(tiles, OFFSETS, cells, cells),
         flat,
         port_row,
+        corner,
         far_args=4,
         scratch=[
             pltpu.SMEM(pattern.shape[1:], jnp.int32),
@@ -280,6 +290,11 @@
         ],
     )
 
+    late = [
+        to_layer(None, beside(pairing))(part)
+        for part, (beside, pairing) in zip(late, [(b, p) for b in (other_row, other_chip) for p in row_pairs])
+    ]
+
     def waves(phase, kappa_ref):
         def wave(base, field=None, real=None):
             if field is not None:
@@ -300,13 +315,10 @@
         if step > 0:
             field_ref, field_rims, carried = take(), take(halos), take(halos)
         wave_ref, core_ref, side_ref = take(), take(), take()
-        if step > 0:
-            for h in range(halos):
-                core_ref[ext + h] = carried[h][0]
-        else:
-            for h in range(halos):
-                for p in range(2):
-                    core_ref[ext + p * halos + h] = column_refs[h][p, 0]
+        for h in range(halos):
+            core_ref[ext + h] = carried[h][0]
+            if step == layers // 2:
+                core_ref[ext + halos + h] = column_refs[h][0]
 
         @pl.when(is_active(step))
         def _():
@@ -316,11 +328,11 @@
                 for y in range(tiles_y):
                     t = x * tiles_y + y
                     wave_ref[x, y] = wave(source_ref[phase, t], None if step == 0 else field_ref[t])
-                side_ref[x] = wave(column_refs[0][phase, x], None if step == 0 else carried[0][x])
+                side_ref[x] = wave(column_refs[0][x], None if step == 0 else carried[0][x])
             for h in range(halos):
                 for y in range(tiles_y):
                     wave_ref[tiles_x + h, y] = wave(
-                        rim_refs[h][phase, y], None if step == 0 else field_rims[h][y], real[h]
+                        rim_refs[h][y], None if step == 0 else field_rims[h][y], real[h]
                     )
             edge = Side(near, "col", tiles_y).edge
             for x in range(ext):
@@ -390,7 +402,10 @@
     def corner_front_kernel(step, *refs):
         take = taker(refs)
         take()
-        front_ref, kappa_ref, core_ref, base_ref, sum_ref, corner_ref = (take() for _ in range(6))
+        front_ref, kappa_ref, core_ref, base_ref = (take() for _ in range(4))
+        if step == 1:
+            take(2 * halos)
+        sum_ref, corner_ref = take(), take()
 
         @pl.when(is_active(step))
         def _():
@@ -439,28 +454,27 @@
                         both = one[t].astype(f32) * other[t].astype(f32)
                         rest[0][t : t + 1, :] = jnp.sum(both, axis=0, keepdims=True) * intersection_scale
 
-    fields, field_arrived, first_core = [], [], None
+    fields, field_arrived = [], []
     for step in range(layers):
         last = step == layers - 1
         wave, core, side = call(
             functools.partial(wave_kernel, step),
             [
                 ((ext, tiles_y, *tile), bf16),
-                ((ext + halos * (2 if step == 0 else 1), *tile), bf16),
+                ((ext + halos * (2 if step == layers // 2 else 1), *tile), bf16),
                 ((tiles_x, *tile), bf16),
             ],
             source,
             kappa,
-            *source_beside,
+            *(source_beside if step < layers // 2 else late),
             *field_arrived,
         )
         core = to_core(core)
-        if step == 0:
-            first_core = core
         (summed,) = call(
             functools.partial(inner_kernel, step), [((tiles, *tile), f32)], wave, side, front
         )
-        base = core if step == 0 else first_core
+        if step in (0, layers // 2):
+            base = core
         if not last:
             summed, corner = call(
                 functools.partial(corner_front_kernel, step),
@@ -470,6 +484,7 @@
                 kappa,
                 core,
                 base,
+                *(late if step == 1 else []),
                 aliases={0: 0},
             )
             corner = to_core(corner)

time: 49.9 us -> 49.5 us (level)
  waiting for transfers between devices: 16.1 us -> 14.7 us
  starting transfers between devices: 26.8 us -> 27.8 us
    ppermute x22 -> x24, waiting for transfers between devices: 16.1 us -> 14.7 us  [permuted(): return lax.ppermute(array, AXES, pairs)]
    ppermute x22 -> x24, starting transfers between devices: 26.8 us -> 27.8 us  [permuted(): return lax.ppermute(array, AXES, pairs)]
  transfers between devices with their start and end apart: 22 -> 24, of which waited for: 13 -> 14; matrix products, arithmetic and copies ran while one was open for 0% -> 0% of each run, Pallas kernels for 8% -> 8%
where the time goes in v4:
time: 49.5 us; the launch traced here: 49.3 us
  starting transfers between devices  27.8 us (56%)
  waiting for transfers between devices  14.7 us (30%)
  Pallas kernels  6.09 us (12%)
  between operations  0.76 us (2%)
    ppermute x24, starting transfers between devices, permuted(): return lax.ppermute(array, AXES, pairs)  27.8 us
    ppermute x24, waiting for transfers between devices, permuted(): return lax.ppermute(array, AXES, pairs)  14.7 us
    pallas_call x24, Pallas kernels, call(): pl.pallas_call(kernel, out_shape=[jax.ShapeDtypeStruct(shape, dtype) for...  6.09 us
  transfers between devices with their start and end apart: 24, of which 14 were waited for; matrix products, arithmetic and copies ran while one was open for 0% of the time, Pallas kernels for 8%

profile of v4, /device:TPU:0, one launch (start us, length us, event | category | flops | bytes accessed | tf_op | source)
XLA Modules:
  0.0 49.3 jit_solution(5256558098224213891)
XLA Ops:
  0.6 1.1 %shard_map.94 = (f32[2,512,128]{2,1,0:T(8,128)S(1)}, s32[1,64]{1,0:T(1,128)S(1)}, bf16[2,2,64,128]{3,2,1,0:T(8,128)(2,1)S(1)}) custom-call(bf16[64,8,128]{2,1,0:T(8,128)(2,1)} %bitcast.8, bf16[64,8,128]{2,1,0:T(8,128)(2,1)} %bitcast.9, s32[1,64]{1,0:T(1,128)} %bitcast.11), custom_call_target="tpu_custom_call" | custom-call | tf_op jit(solution)/shard_map/pallas_call | solution.py:22
  1.7 0.5 %collective-permute-start = (bf16[2,2,64,128]{3,2,1,0:T(8,128)(2,1)S(1)}, bf16[2,2,64,128]{3,2,1,0:T(8,128)(2,1)S(1)}, u32[]{:S(2)}, u32[]{:S(2)}) collective-permute-start(bf16[2,2,64,128]{3,2,1,0:T(8,128)(2,1)S(1)} %get-tuple-element.47), channel_id=1, source_target_pairs={{0,1},{1,0},{2,3},{3,2},{4,5},{5,4},{6,7},{7,6},{8,9},{9,8},{10,11... | collective-permute-start | bytes 196616 | tf_op jit(solution)/shard_map/ppermute | solution.py:85
  2.3 0.2 shard_map.96
  2.5 2.6 %collective-permute-start.1 = (bf16[4,64,128]{2,1,0:T(8,128)(2,1)S(1)}, bf16[4,64,128]{2,1,0:T(8,128)(2,1)S(1)}, u32[]{:S(2)}, u32[]{:S(2)}) collective-permute-start(bf16[4,64,128]{2,1,0:T(8,128)(2,1)S(1)} %get-tuple-element.50), channel_id=1, source_target_pairs={{0,4},{1,5},{2,6},{3,7},{4,0},{5,1},{6,2},{7,3},{8,12},{9,13},{10,... | collective-permute-start | bytes 196616 | tf_op jit(solution)/shard_map/ppermute | solution.py:85
  5.1 0.0 collective-permute-done.refs_2_.refs_1_
  5.1 1.7 %collective-permute-start.2 = (bf16[2,64,128]{2,1,0:T(8,128)(2,1)S(1)}, bf16[2,64,128]{2,1,0:T(8,128)(2,1)S(1)}, u32[]{:S(2)}, u32[]{:S(2)}) collective-permute-start(bf16[2,64,128]{2,1,0:T(8,128)(2,1)S(1)} %shard_map.97), channel_id=1, source_target_pairs={{0,7},{1,2},{2,1},{3,4},{4,3},{5,6},{6,5},{7,0},{8,15},{9,10},{10,... | collective-permute-start | bytes 98312 | tf_op jit(solution)/shard_map/ppermute | solution.py:85
  6.7 1.9 %shard_map.95 = (bf16[2,8,64,128]{3,2,1,0:T(8,128)(2,1)S(1)}, bf16[8,9,128,128]{3,2,1,0:T(8,128)(2,1)S(1)}, f32[2,8,128]{2,1,0:T(8,128)S(1)}, f32[4,4,8,128]{3,2...) custom-call(s32[2,4,9]{2,1,0:T(4,128)} %bitcast.10, f32[4]{0:T(128)} %coupling_hbm.1, ...), custom_call_target="tpu_custom_call" | custom-call | tf_op jit(solution)/shard_map/pallas_call | solution.py:22
  8.6 0.9 %collective-permute-done.2.refs_3_ = bf16[2,64,128]{2,1,0:T(8,128)(2,1)S(1)} collective-permute-done((bf16[2,64,128]{2,1,0:T(8,128)(2,1)S(1)}, bf16[2,64,128]{2,1,0:T(8,128)(2,1)S(1)}, u32[]{:S(2)}, u32[]{:S(2)}) %collective-permute-start.2) | collective-permute-done | bytes 32800 | tf_op jit(solution)/shard_map/ppermute | solution.py:85
  9.5 0.1 collective-permute-start.3
  9.6 0.4 shard_map.99.refs_0_
  10.1 0.8 %collective-permute-done.3.refs_3_.refs_4_.refs_2_ = bf16[4,64,128]{2,1,0:T(8,128)(2,1)S(1)} collective-permute-done((bf16[4,64,128]{2,1,0:T(8,128)(2,1)S(1)}, bf16[4,64,128]{2,1,0:T(8,128)(2,1)S(1)}, u32[]{:S(2)}, u32[]{:S(2)}) %collective-permute-start.3) | collective-permute-done | bytes 65568 | tf_op jit(solution)/shard_map/ppermute | solution.py:85
  10.9 0.2 shard_map.101
  11.1 1.3 %collective-permute-start.4 = (bf16[8,64,128]{2,1,0:T(8,128)(2,1)S(1)}, bf16[8,64,128]{2,1,0:T(8,128)(2,1)S(1)}, u32[]{:S(2)}, u32[]{:S(2)}) collective-permute-start(bf16[8,64,128]{2,1,0:T(8,128)(2,1)S(1)} %get-tuple-element.57.refs_5_.refs_0_), channel_id=1, source_target_pairs={{0,8},{1,9},{2,10},{3,11},{4,12},{5,13},{6,14},{7,15},{8,0},{9,1},... | collective-permute-start | bytes 393224 | tf_op jit(solution)/shard_map/ppermute | solution.py:85
  12.3 0.0 collective-permute-start.6
  12.3 1.4 %collective-permute-start.5 = (bf16[4,64,128]{2,1,0:T(8,128)(2,1)S(1)}, bf16[4,64,128]{2,1,0:T(8,128)(2,1)S(1)}, u32[]{:S(2)}, u32[]{:S(2)}) collective-permute-start(bf16[4,64,128]{2,1,0:T(8,128)(2,1)S(1)} %get-tuple-element.58), channel_id=1, source_target_pairs={{0,12},{1,13},{2,14},{3,15},{4,8},{5,9},{6,10},{7,11},{8,4},{9,5},... | collective-permute-start | bytes 196616 | tf_op jit(solution)/shard_map/ppermute | solution.py:85
  13.7 2.0 %collective-permute-start.7 = (bf16[2,64,128]{2,1,0:T(8,128)(2,1)S(1)}, bf16[2,64,128]{2,1,0:T(8,128)(2,1)S(1)}, u32[]{:S(2)}, u32[]{:S(2)}) collective-permute-start(bf16[2,64,128]{2,1,0:T(8,128)(2,1)S(1)} %shard_map.102), channel_id=1, source_target_pairs={{0,15},{1,10},{2,9},{3,12},{4,11},{5,14},{6,13},{7,8},{8,7},{9,2},... | collective-permute-start | bytes 98312 | tf_op jit(solution)/shard_map/ppermute | solution.py:85
  15.7 0.9 %collective-permute-start.9 = (bf16[4,64,128]{2,1,0:T(8,128)(2,1)S(1)}, bf16[4,64,128]{2,1,0:T(8,128)(2,1)S(1)}, u32[]{:S(2)}, u32[]{:S(2)}) collective-permute-start(bf16[4,64,128]{2,1,0:T(8,128)(2,1)S(1)} %get-tuple-element.64), channel_id=1, source_target_pairs={{0,4},{1,5},{2,6},{3,7},{4,0},{5,1},{6,2},{7,3},{8,12},{9,13},{10,... | collective-permute-start | bytes 196616 | tf_op jit(solution)/shard_map/ppermute | solution.py:85
  16.6 1.0 %collective-permute-start.10 = (bf16[4,64,128]{2,1,0:T(8,128)(2,1)S(1)}, bf16[4,64,128]{2,1,0:T(8,128)(2,1)S(1)}, u32[]{:S(2)}, u32[]{:S(2)}) collective-permute-start(bf16[4,64,128]{2,1,0:T(8,128)(2,1)S(1)} %get-tuple-element.65), channel_id=1, source_target_pairs={{0,7},{1,2},{2,1},{3,4},{4,3},{5,6},{6,5},{7,0},{8,15},{9,10},{10,... | collective-permute-start | bytes 196616 | tf_op jit(solution)/shard_map/ppermute | solution.py:85
  17.6 1.7 %collective-permute-done.7.refs_6_ = bf16[2,64,128]{2,1,0:T(8,128)(2,1)S(1)} collective-permute-done((bf16[2,64,128]{2,1,0:T(8,128)(2,1)S(1)}, bf16[2,64,128]{2,1,0:T(8,128)(2,1)S(1)}, u32[]{:S(2)}, u32[]{:S(2)}) %collective-permute-start.7) | collective-permute-done | bytes 32800 | tf_op jit(solution)/shard_map/ppermute | solution.py:85
  19.4 0.1 collective-permute-start.8
  19.5 1.0 %collective-permute-done.9.refs_5_.refs_2_ = bf16[4,64,128]{2,1,0:T(8,128)(2,1)S(1)} collective-permute-done((bf16[4,64,128]{2,1,0:T(8,128)(2,1)S(1)}, bf16[4,64,128]{2,1,0:T(8,128)(2,1)S(1)}, u32[]{:S(2)}, u32[]{:S(2)}) %collective-permute-start.9) | collective-permute-done | bytes 65568 | tf_op jit(solution)/shard_map/ppermute | solution.py:85
  20.5 0.8 %collective-permute-done.10.refs_6_.refs_3_ = bf16[4,64,128]{2,1,0:T(8,128)(2,1)S(1)} collective-permute-done((bf16[4,64,128]{2,1,0:T(8,128)(2,1)S(1)}, bf16[4,64,128]{2,1,0:T(8,128)(2,1)S(1)}, u32[]{:S(2)}, u32[]{:S(2)}) %collective-permute-start.10) | collective-permute-done | bytes 65568 | tf_op jit(solution)/shard_map/ppermute | solution.py:85
  21.3 0.5 %collective-permute-start.13 = (bf16[2,64,128]{2,1,0:T(8,128)(2,1)S(1)}, bf16[2,64,128]{2,1,0:T(8,128)(2,1)S(1)}, u32[]{:S(2)}, u32[]{:S(2)}) collective-permute-start(bf16[2,64,128]{2,1,0:T(8,128)(2,1)S(1)} %get-tuple-element.70), channel_id=1, source_target_pairs={{0,1},{1,0},{2,3},{3,2},{4,5},{5,4},{6,7},{7,6},{8,9},{9,8},{10,11... | collective-permute-start | bytes 98312 | tf_op jit(solution)/shard_map/ppermute | solution.py:85
  21.8 0.1 collective-permute-start.12
  21.9 0.8 %collective-permute-done.13.refs_1_ = bf16[2,64,128]{2,1,0:T(8,128)(2,1)S(1)} collective-permute-done((bf16[2,64,128]{2,1,0:T(8,128)(2,1)S(1)}, bf16[2,64,128]{2,1,0:T(8,128)(2,1)S(1)}, u32[]{:S(2)}, u32[]{:S(2)}) %collective-permute-start.13) | collective-permute-done | bytes 32800 | tf_op jit(solution)/shard_map/ppermute | solution.py:85
  22.7 0.3 collective-permute-start.14
  23.1 0.9 %collective-permute-done.14.refs_6_ = bf16[2,64,128]{2,1,0:T(8,128)(2,1)S(1)} collective-permute-done((bf16[2,64,128]{2,1,0:T(8,128)(2,1)S(1)}, bf16[2,64,128]{2,1,0:T(8,128)(2,1)S(1)}, u32[]{:S(2)}, u32[]{:S(2)}) %collective-permute-start.14) | collective-permute-done | bytes 32800 | tf_op jit(solution)/shard_map/ppermute | solution.py:85
  24.0 0.4 collective-permute-start.15
  24.4 1.0 %collective-permute-done.15.refs_3_.refs_4_.refs_2_ = bf16[5,64,128]{2,1,0:T(8,128)(2,1)S(1)} collective-permute-done((bf16[5,64,128]{2,1,0:T(8,128)(2,1)S(1)}, bf16[5,64,128]{2,1,0:T(8,128)(2,1)S(1)}, u32[]{:S(2)}, u32[]{:S(2)}) %collective-permute-start.15) | collective-permute-done | bytes 81952 | tf_op jit(solution)/shard_map/ppermute | solution.py:85
  25.3 8.2 %collective-permute-start.16 = (bf16[8,64,128]{2,1,0:T(8,128)(2,1)S(1)}, bf16[8,64,128]{2,1,0:T(8,128)(2,1)S(1)}, u32[]{:S(2)}, u32[]{:S(2)}) collective-permute-start(bf16[8,64,128]{2,1,0:T(8,128)(2,1)S(1)} %get-tuple-element.75.refs_7_.refs_2_), channel_id=1, source_target_pairs={{0,8},{1,9},{2,10},{3,11},{4,12},{5,13},{6,14},{7,15},{8,0},{9,1},... | collective-permute-start | bytes 393224 | tf_op jit(solution)/shard_map/ppermute | solution.py:85
  33.5 0.0 collective-permute-start.18
  33.5 0.7 %collective-permute-start.17 = (bf16[4,64,128]{2,1,0:T(8,128)(2,1)S(1)}, bf16[4,64,128]{2,1,0:T(8,128)(2,1)S(1)}, u32[]{:S(2)}, u32[]{:S(2)}) collective-permute-start(bf16[4,64,128]{2,1,0:T(8,128)(2,1)S(1)} %get-tuple-element.76), channel_id=1, source_target_pairs={{0,12},{1,13},{2,14},{3,15},{4,8},{5,9},{6,10},{7,11},{8,4},{9,5},... | collective-permute-start | bytes 196616 | tf_op jit(solution)/shard_map/ppermute | solution.py:85
  34.3 0.5 collective-permute-done.18.refs_1_
  34.7 1.5 %collective-permute-start.19 = (bf16[2,64,128]{2,1,0:T(8,128)(2,1)S(1)}, bf16[2,64,128]{2,1,0:T(8,128)(2,1)S(1)}, u32[]{:S(2)}, u32[]{:S(2)}) collective-permute-start(bf16[2,64,128]{2,1,0:T(8,128)(2,1)S(1)} %shard_map.112), channel_id=1, source_target_pairs={{0,15},{1,10},{2,9},{3,12},{4,11},{5,14},{6,13},{7,8},{8,7},{9,2},... | collective-permute-start | bytes 98312 | tf_op jit(solution)/shard_map/ppermute | solution.py:85
  36.2 3.3 %collective-permute-done.17.refs_5_ = bf16[4,64,128]{2,1,0:T(8,128)(2,1)S(1)} collective-permute-done((bf16[4,64,128]{2,1,0:T(8,128)(2,1)S(1)}, bf16[4,64,128]{2,1,0:T(8,128)(2,1)S(1)}, u32[]{:S(2)}, u32[]{:S(2)}) %collective-permute-start.17) | collective-permute-done | bytes 65568 | tf_op jit(solution)/shard_map/ppermute | solution.py:85
  39.6 0.5 collective-permute-done.19.refs_6_
  40.0 0.1 shard_map.113
  40.1 0.1 collective-permute-start.20
  40.2 0.5 shard_map.114.refs_0_
  40.7 0.8 %collective-permute-done.20.refs_2_ = bf16[4,64,128]{2,1,0:T(8,128)(2,1)S(1)} collective-permute-done((bf16[4,64,128]{2,1,0:T(8,128)(2,1)S(1)}, bf16[4,64,128]{2,1,0:T(8,128)(2,1)S(1)}, u32[]{:S(2)}, u32[]{:S(2)}) %collective-permute-start.20) | collective-permute-done | bytes 65568 | tf_op jit(solution)/shard_map/ppermute | solution.py:85
  41.4 0.2 shard_map.115
  41.7 2.5 %collective-permute-start.23 = (f32[8,128]{1,0:T(8,128)S(1)}, f32[8,128]{1,0:T(8,128)S(1)}, u32[]{:S(2)}, u32[]{:S(2)}) collective-permute-start(f32[8,128]{1,0:T(8,128)S(1)} %get-tuple-element.85.refs_0_), channel_id=1, source_target_pairs={{0,24},{1,25},{2,26},{3,27},{4,28},{5,29},{6,30},{7,31},{8,16},{9,... | collective-permute-start | bytes 12296 | tf_op jit(solution)/shard_map/ppermute | solution.py:85
  44.2 0.2 collective-permute-start.22
  44.4 1.7 %collective-permute-start.21 = (f32[8,128]{1,0:T(8,128)S(1)}, f32[8,128]{1,0:T(8,128)S(1)}, u32[]{:S(2)}, u32[]{:S(2)}) collective-permute-start(f32[8,128]{1,0:T(8,128)S(1)} %get-tuple-element.85.refs_0_), channel_id=1, source_target_pairs={{0,8},{1,9},{2,10},{3,11},{4,12},{5,13},{6,14},{7,15},{8,0},{9,1},... | collective-permute-start | bytes 12296 | tf_op jit(solution)/shard_map/ppermute | solution.py:85
  46.1 0.8 %shard_map.116 = (bf16[64,8,128]{2,1,0:T(8,128)(2,1)}, bf16[64,8,128]{2,1,0:T(8,128)(2,1)}) custom-call(bf16[8,64,128]{2,1,0:T(8,128)(2,1)S(1)} %get-tuple-element.57.refs_5_.refs_0_, bf16[8,64,128]{2,1,0:T(8,128)(2,1)S(1)} %get-tuple-element.67.refs_6_.refs_1_, bf16[8,64,128]{2,1,0:T(8,128)(2,1)S(1)} %get-tuple-element.75.refs_7_.refs_2_, ...), custom_call_target="tpu_custom_call" | custom-call | tf_op jit(solution)/shard_map/pallas_call | solution.py:22
  47.0 0.2 collective-permute-done.23.refs_3_
  47.2 1.5 %collective-permute-done.22.refs_2_ = f32[8,128]{1,0:T(8,128)S(1)} collective-permute-done((f32[8,128]{1,0:T(8,128)S(1)}, f32[8,128]{1,0:T(8,128)S(1)}, u32[]{:S(2)}, u32[]{:S(2)}) %collective-permute-start.22) | collective-permute-done | bytes 4128 | tf_op jit(solution)/shard_map/ppermute | solution.py:85
  48.7 0.6 %shard_map.117 = f32[4,2,4,128]{3,2,1,0:T(4,128)} custom-call(f32[8,128]{1,0:T(8,128)S(1)} %get-tuple-element.85.refs_0_, f32[8,128]{1,0:T(8,128)S(1)} %collective-permute-done.21.refs_1_, f32[8,128]{1,0:T(8,128)S(1)} %collective-permute-done.22.refs_2_, f32[8,128]{1,0:T(8,128)S(1)} %collective-permute-done.23.refs_3_, ...), custom_call_target="tpu_custom_call" | custom-call | tf_op jit(solution)/shard_map/pallas_call | solution.py:22
  (24 shorter events, 0.1 us)
Async XLA Ops:
  1.7 3.3 %collective-permute-start = (bf16[2,2,64,128]{3,2,1,0:T(8,128)(2,1)S(1)}, bf16[2,2,64,128]{3,2,1,0:T(8,128)(2,1)S(1)}, u32[]{:S(2)}, u32[]{:S(2)}) collective-permute-start(bf16[2,2,64,128]{3,2,1,0:T(8,128)(2,1)S(1)} %get-tuple-element.47), channel_id=1, source_target_pairs={{0,1},{1,0},{2,3},{3,2},{4,5},{5,4},{6,7},{7,6},{8,9},{9,8},{10,11... | collective-permute-start | bytes 196616 | tf_op jit(solution)/shard_map/ppermute | solution.py:85
  2.5 6.1 %collective-permute-start.1 = (bf16[4,64,128]{2,1,0:T(8,128)(2,1)S(1)}, bf16[4,64,128]{2,1,0:T(8,128)(2,1)S(1)}, u32[]{:S(2)}, u32[]{:S(2)}) collective-permute-start(bf16[4,64,128]{2,1,0:T(8,128)(2,1)S(1)} %get-tuple-element.50), channel_id=1, source_target_pairs={{0,4},{1,5},{2,6},{3,7},{4,0},{5,1},{6,2},{7,3},{8,12},{9,13},{10,... | collective-permute-start | bytes 196616 | tf_op jit(solution)/shard_map/ppermute | solution.py:85
  5.1 4.4 %collective-permute-start.2 = (bf16[2,64,128]{2,1,0:T(8,128)(2,1)S(1)}, bf16[2,64,128]{2,1,0:T(8,128)(2,1)S(1)}, u32[]{:S(2)}, u32[]{:S(2)}) collective-permute-start(bf16[2,64,128]{2,1,0:T(8,128)(2,1)S(1)} %shard_map.97), channel_id=1, source_target_pairs={{0,7},{1,2},{2,1},{3,4},{4,3},{5,6},{6,5},{7,0},{8,15},{9,10},{10,... | collective-permute-start | bytes 98312 | tf_op jit(solution)/shard_map/ppermute | solution.py:85
  9.5 1.3 %collective-permute-start.3 = (bf16[4,64,128]{2,1,0:T(8,128)(2,1)S(1)}, bf16[4,64,128]{2,1,0:T(8,128)(2,1)S(1)}, u32[]{:S(2)}, u32[]{:S(2)}) collective-permute-start(bf16[4,64,128]{2,1,0:T(8,128)(2,1)S(1)} %get-tuple-element.55), channel_id=1, source_target_pairs={{0,1},{1,0},{2,3},{3,2},{4,5},{5,4},{6,7},{7,6},{8,9},{9,8},{10,11... | collective-permute-start | bytes 196616 | tf_op jit(solution)/shard_map/ppermute | solution.py:85
  11.1 8.3 %collective-permute-start.4 = (bf16[8,64,128]{2,1,0:T(8,128)(2,1)S(1)}, bf16[8,64,128]{2,1,0:T(8,128)(2,1)S(1)}, u32[]{:S(2)}, u32[]{:S(2)}) collective-permute-start(bf16[8,64,128]{2,1,0:T(8,128)(2,1)S(1)} %get-tuple-element.57.refs_5_.refs_0_), channel_id=1, source_target_pairs={{0,8},{1,9},{2,10},{3,11},{4,12},{5,13},{6,14},{7,15},{8,0},{9,1},... | collective-permute-start | bytes 393224 | tf_op jit(solution)/shard_map/ppermute | solution.py:85
  12.3 1.4 %collective-permute-start.6 = (bf16[2,64,128]{2,1,0:T(8,128)(2,1)S(1)}, bf16[2,64,128]{2,1,0:T(8,128)(2,1)S(1)}, u32[]{:S(2)}, u32[]{:S(2)}) collective-permute-start(bf16[2,64,128]{2,1,0:T(8,128)(2,1)S(1)} %get-tuple-element.60), channel_id=1, source_target_pairs={{0,1},{1,0},{2,3},{3,2},{4,5},{5,4},{6,7},{7,6},{8,9},{9,8},{10,11... | collective-permute-start | bytes 98312 | tf_op jit(solution)/shard_map/ppermute | solution.py:85
  12.3 7.0 %collective-permute-start.5 = (bf16[4,64,128]{2,1,0:T(8,128)(2,1)S(1)}, bf16[4,64,128]{2,1,0:T(8,128)(2,1)S(1)}, u32[]{:S(2)}, u32[]{:S(2)}) collective-permute-start(bf16[4,64,128]{2,1,0:T(8,128)(2,1)S(1)} %get-tuple-element.58), channel_id=1, source_target_pairs={{0,12},{1,13},{2,14},{3,15},{4,8},{5,9},{6,10},{7,11},{8,4},{9,5},... | collective-permute-start | bytes 196616 | tf_op jit(solution)/shard_map/ppermute | solution.py:85
  13.7 5.7 %collective-permute-start.7 = (bf16[2,64,128]{2,1,0:T(8,128)(2,1)S(1)}, bf16[2,64,128]{2,1,0:T(8,128)(2,1)S(1)}, u32[]{:S(2)}, u32[]{:S(2)}) collective-permute-start(bf16[2,64,128]{2,1,0:T(8,128)(2,1)S(1)} %shard_map.102), channel_id=1, source_target_pairs={{0,15},{1,10},{2,9},{3,12},{4,11},{5,14},{6,13},{7,8},{8,7},{9,2},... | collective-permute-start | bytes 98312 | tf_op jit(solution)/shard_map/ppermute | solution.py:85
  15.7 4.8 %collective-permute-start.9 = (bf16[4,64,128]{2,1,0:T(8,128)(2,1)S(1)}, bf16[4,64,128]{2,1,0:T(8,128)(2,1)S(1)}, u32[]{:S(2)}, u32[]{:S(2)}) collective-permute-start(bf16[4,64,128]{2,1,0:T(8,128)(2,1)S(1)} %get-tuple-element.64), channel_id=1, source_target_pairs={{0,4},{1,5},{2,6},{3,7},{4,0},{5,1},{6,2},{7,3},{8,12},{9,13},{10,... | collective-permute-start | bytes 196616 | tf_op jit(solution)/shard_map/ppermute | solution.py:85
  16.6 4.7 %collective-permute-start.10 = (bf16[4,64,128]{2,1,0:T(8,128)(2,1)S(1)}, bf16[4,64,128]{2,1,0:T(8,128)(2,1)S(1)}, u32[]{:S(2)}, u32[]{:S(2)}) collective-permute-start(bf16[4,64,128]{2,1,0:T(8,128)(2,1)S(1)} %get-tuple-element.65), channel_id=1, source_target_pairs={{0,7},{1,2},{2,1},{3,4},{4,3},{5,6},{6,5},{7,0},{8,15},{9,10},{10,... | collective-permute-start | bytes 196616 | tf_op jit(solution)/shard_map/ppermute | solution.py:85
  19.4 1.9 %collective-permute-start.8 = (bf16[4,64,128]{2,1,0:T(8,128)(2,1)S(1)}, bf16[4,64,128]{2,1,0:T(8,128)(2,1)S(1)}, u32[]{:S(2)}, u32[]{:S(2)}) collective-permute-start(bf16[4,64,128]{2,1,0:T(8,128)(2,1)S(1)} %get-tuple-element.63), channel_id=1, source_target_pairs={{0,1},{1,0},{2,3},{3,2},{4,5},{5,4},{6,7},{7,6},{8,9},{9,8},{10,11... | collective-permute-start | bytes 196616 | tf_op jit(solution)/shard_map/ppermute | solution.py:85
  21.3 2.6 %collective-permute-start.11 = (bf16[8,64,128]{2,1,0:T(8,128)(2,1)S(1)}, bf16[8,64,128]{2,1,0:T(8,128)(2,1)S(1)}, u32[]{:S(2)}, u32[]{:S(2)}) collective-permute-start(bf16[8,64,128]{2,1,0:T(8,128)(2,1)S(1)} %get-tuple-element.67.refs_6_.refs_1_), channel_id=1, source_target_pairs={{0,1},{1,0},{2,3},{3,2},{4,5},{5,4},{6,7},{7,6},{8,16},{9,17},{10,... | collective-permute-start | bytes 393224 | tf_op jit(solution)/shard_map/ppermute | solution.py:85
  21.3 1.4 %collective-permute-start.13 = (bf16[2,64,128]{2,1,0:T(8,128)(2,1)S(1)}, bf16[2,64,128]{2,1,0:T(8,128)(2,1)S(1)}, u32[]{:S(2)}, u32[]{:S(2)}) collective-permute-start(bf16[2,64,128]{2,1,0:T(8,128)(2,1)S(1)} %get-tuple-element.70), channel_id=1, source_target_pairs={{0,1},{1,0},{2,3},{3,2},{4,5},{5,4},{6,7},{7,6},{8,9},{9,8},{10,11... | collective-permute-start | bytes 98312 | tf_op jit(solution)/shard_map/ppermute | solution.py:85
  21.8 2.1 %collective-permute-start.12 = (bf16[4,64,128]{2,1,0:T(8,128)(2,1)S(1)}, bf16[4,64,128]{2,1,0:T(8,128)(2,1)S(1)}, u32[]{:S(2)}, u32[]{:S(2)}) collective-permute-start(bf16[4,64,128]{2,1,0:T(8,128)(2,1)S(1)} %get-tuple-element.68), channel_id=1, source_target_pairs={{0,1},{1,0},{2,3},{3,2},{4,5},{5,4},{6,7},{7,6},{8,20},{9,21},{10,... | collective-permute-start | bytes 196616 | tf_op jit(solution)/shard_map/ppermute | solution.py:85
  22.7 1.2 %collective-permute-start.14 = (bf16[2,64,128]{2,1,0:T(8,128)(2,1)S(1)}, bf16[2,64,128]{2,1,0:T(8,128)(2,1)S(1)}, u32[]{:S(2)}, u32[]{:S(2)}) collective-permute-start(bf16[2,64,128]{2,1,0:T(8,128)(2,1)S(1)} %shard_map.107), channel_id=1, source_target_pairs={{0,1},{1,0},{2,3},{3,2},{4,5},{5,4},{6,7},{7,6},{8,23},{9,18},{10,... | collective-permute-start | bytes 98312 | tf_op jit(solution)/shard_map/ppermute | solution.py:85
  24.0 1.3 %collective-permute-start.15 = (bf16[5,64,128]{2,1,0:T(8,128)(2,1)S(1)}, bf16[5,64,128]{2,1,0:T(8,128)(2,1)S(1)}, u32[]{:S(2)}, u32[]{:S(2)}) collective-permute-start(bf16[5,64,128]{2,1,0:T(8,128)(2,1)S(1)} %get-tuple-element.73), channel_id=1, source_target_pairs={{0,1},{1,0},{2,3},{3,2},{4,5},{5,4},{6,7},{7,6},{8,9},{9,8},{10,11... | collective-permute-start | bytes 245768 | tf_op jit(solution)/shard_map/ppermute | solution.py:85
  25.3 14.7 %collective-permute-start.16 = (bf16[8,64,128]{2,1,0:T(8,128)(2,1)S(1)}, bf16[8,64,128]{2,1,0:T(8,128)(2,1)S(1)}, u32[]{:S(2)}, u32[]{:S(2)}) collective-permute-start(bf16[8,64,128]{2,1,0:T(8,128)(2,1)S(1)} %get-tuple-element.75.refs_7_.refs_2_), channel_id=1, source_target_pairs={{0,8},{1,9},{2,10},{3,11},{4,12},{5,13},{6,14},{7,15},{8,0},{9,1},... | collective-permute-start | bytes 393224 | tf_op jit(solution)/shard_map/ppermute | solution.py:85
  33.5 1.2 %collective-permute-start.18 = (bf16[2,64,128]{2,1,0:T(8,128)(2,1)S(1)}, bf16[2,64,128]{2,1,0:T(8,128)(2,1)S(1)}, u32[]{:S(2)}, u32[]{:S(2)}) collective-permute-start(bf16[2,64,128]{2,1,0:T(8,128)(2,1)S(1)} %get-tuple-element.78), channel_id=1, source_target_pairs={{0,1},{1,0},{2,3},{3,2},{4,5},{5,4},{6,7},{7,6},{8,9},{9,8},{10,11... | collective-permute-start | bytes 98312 | tf_op jit(solution)/shard_map/ppermute | solution.py:85
  33.5 6.0 %collective-permute-start.17 = (bf16[4,64,128]{2,1,0:T(8,128)(2,1)S(1)}, bf16[4,64,128]{2,1,0:T(8,128)(2,1)S(1)}, u32[]{:S(2)}, u32[]{:S(2)}) collective-permute-start(bf16[4,64,128]{2,1,0:T(8,128)(2,1)S(1)} %get-tuple-element.76), channel_id=1, source_target_pairs={{0,12},{1,13},{2,14},{3,15},{4,8},{5,9},{6,10},{7,11},{8,4},{9,5},... | collective-permute-start | bytes 196616 | tf_op jit(solution)/shard_map/ppermute | solution.py:85
  34.7 5.3 %collective-permute-start.19 = (bf16[2,64,128]{2,1,0:T(8,128)(2,1)S(1)}, bf16[2,64,128]{2,1,0:T(8,128)(2,1)S(1)}, u32[]{:S(2)}, u32[]{:S(2)}) collective-permute-start(bf16[2,64,128]{2,1,0:T(8,128)(2,1)S(1)} %shard_map.112), channel_id=1, source_target_pairs={{0,15},{1,10},{2,9},{3,12},{4,11},{5,14},{6,13},{7,8},{8,7},{9,2},... | collective-permute-start | bytes 98312 | tf_op jit(solution)/shard_map/ppermute | solution.py:85
  40.1 1.3 %collective-permute-start.20 = (bf16[4,64,128]{2,1,0:T(8,128)(2,1)S(1)}, bf16[4,64,128]{2,1,0:T(8,128)(2,1)S(1)}, u32[]{:S(2)}, u32[]{:S(2)}) collective-permute-start(bf16[4,64,128]{2,1,0:T(8,128)(2,1)S(1)} %get-tuple-element.81), channel_id=1, source_target_pairs={{0,1},{1,0},{2,3},{3,2},{4,5},{5,4},{6,7},{7,6},{8,9},{9,8},{10,11... | collective-permute-start | bytes 196616 | tf_op jit(solution)/shard_map/ppermute | solution.py:85
  41.7 5.5 %collective-permute-start.23 = (f32[8,128]{1,0:T(8,128)S(1)}, f32[8,128]{1,0:T(8,128)S(1)}, u32[]{:S(2)}, u32[]{:S(2)}) collective-permute-start(f32[8,128]{1,0:T(8,128)S(1)} %get-tuple-element.85.refs_0_), channel_id=1, source_target_pairs={{0,24},{1,25},{2,26},{3,27},{4,28},{5,29},{6,30},{7,31},{8,16},{9,... | collective-permute-start | bytes 12296 | tf_op jit(solution)/shard_map/ppermute | solution.py:85
  44.2 4.5 %collective-permute-start.22 = (f32[8,128]{1,0:T(8,128)S(1)}, f32[8,128]{1,0:T(8,128)S(1)}, u32[]{:S(2)}, u32[]{:S(2)}) collective-permute-start(f32[8,128]{1,0:T(8,128)S(1)} %get-tuple-element.85.refs_0_), channel_id=1, source_target_pairs={{0,16},{1,17},{2,18},{3,19},{4,20},{5,21},{6,22},{7,23},{8,24},{9,... | collective-permute-start | bytes 12296 | tf_op jit(solution)/shard_map/ppermute | solution.py:85
  44.4 4.3 %collective-permute-start.21 = (f32[8,128]{1,0:T(8,128)S(1)}, f32[8,128]{1,0:T(8,128)S(1)}, u32[]{:S(2)}, u32[]{:S(2)}) collective-permute-start(f32[8,128]{1,0:T(8,128)S(1)} %get-tuple-element.85.refs_0_), channel_id=1, source_target_pairs={{0,8},{1,9},{2,10},{3,11},{4,12},{5,13},{6,14},{7,15},{8,0},{9,1},... | collective-permute-start | bytes 12296 | tf_op jit(solution)/shard_map/ppermute | solution.py:85

commit v5 on v4

--- a/solution.py
+++ b/solution.py
@@ -307,18 +307,79 @@
     def row_real():
         return [Side(pairing, "row", tiles_x).real for pairing in row_pairs]
 
-    def wave_kernel(step, *refs):
+    def step_inputs(step, take):
+        source_ref, kappa_ref, rim_refs, column_refs = take(), take(), take(halos), take(halos)
+        if step == 0:
+            return source_ref, kappa_ref, rim_refs, column_refs, None, [None] * halos, column_refs
+        return source_ref, kappa_ref, rim_refs, column_refs, take(), take(halos), take(halos)
+
+    def core_kernel(step, *refs):
         take = taker(refs)
         phase = int(step >= layers // 2)
-        source_ref, kappa_ref, rim_refs, column_refs = take(), take(), take(halos), take(halos)
-        field_ref, field_rims, carried = None, [None] * halos, column_refs
-        if step > 0:
-            field_ref, field_rims, carried = take(), take(halos), take(halos)
-        wave_ref, core_ref, side_ref = take(), take(), take()
+        source_ref, kappa_ref, rim_refs, column_refs, field_ref, field_rims, carried = step_inputs(step, take)
+        core_ref = take()
         for h in range(halos):
             core_ref[ext + h] = carried[h][0]
             if step == layers // 2:
                 core_ref[ext + halos + h] = column_refs[h][0]
+
+        @pl.when(is_active(step))
+        def _():
+            wave = waves(phase, kappa_ref)
+            real = row_real()
+            edge = Side(near, "col", tiles_y).edge
+            for x in range(tiles_x):
+                t = x * tiles_y + edge
+                core_ref[x] = wave(source_ref[phase, t], None if step == 0 else field_ref[t])
+            for h in range(halos):
+                core_ref[tiles_x + h] = wave(
+                    rim_refs[h][edge], None if step == 0 else field_rims[h][edge], real[h]
+                )
+
+    def product(lhs, rhs):
+        return jnp.dot(lhs, rhs, preferred_element_type=f32)
+
+    def column_products(across, front_ref, halo_ref):
+        totals = []
+        for x in range(tiles_x):
+            t = x * tiles_y + across.edge
+            reach = [a for a in (-1, 0, 1) if 0 <= x + a < tiles_x]
+            lhs = jnp.concatenate([halo_ref[x + a] for a in reach], axis=1)
+            rhs = jnp.concatenate([front_ref[t, 3 * (a + 1) + 1 + across.step] for a in reach], axis=0)
+            totals.append(product(lhs, rhs))
+        return totals
+
+    def corner_product(across, pairing, front_ref, corner):
+        side = Side(pairing, "row", tiles_x)
+        t = side.edge * tiles_y + across.edge
+        return t, product(corner, front_ref[t, 3 * (side.step + 1) + 1 + across.step])
+
+    def early_tiles():
+        edge = Side(far, "col", tiles_y).edge
+        inside = [(x, y) for x in range(tiles_x) for y in range(1, tiles_y - 1)]
+        if halos > 1:
+            return inside + [(x, edge) for x in range(1, tiles_x - 1)]
+        low = jnp.where(Side(near, "row", tiles_x).edge == 0, 1, 0)
+        return inside + [(low + i, edge) for i in range(tiles_x - 1)]
+
+    def late_tiles():
+        beside, beyond = (Side(pairing, "col", tiles_y).edge for pairing in (near, far))
+        corners = [(Side(pairing, "row", tiles_x).edge, beyond) for pairing in row_pairs]
+        return [(x, beside) for x in range(tiles_x)] + corners
+
+    def add_parts(some, one_ref, other_ref, part_ref):
+        for x, y in some:
+            t = x * tiles_y + y
+            both = one_ref[t].astype(f32) * other_ref[t].astype(f32)
+            part_ref[pl.ds(t, 1), :] = jnp.sum(both, axis=0, keepdims=True) * intersection_scale
+
+    def inner_kernel(step, *refs):
+        take = taker(refs)
+        phase, last = int(step >= layers // 2), step == layers - 1
+        source_ref, kappa_ref, rim_refs, column_refs, field_ref, field_rims, carried = step_inputs(step, take)
+        take()
+        front_ref, earlier = take(), take(layers - 1 if last else 0)
+        sum_ref, out_ref, rest, wave_ref, side_ref = take(), take(), take(1 if last else halos + 1), take(), take()
 
         @pl.when(is_active(step))
         def _():
@@ -334,29 +395,6 @@
                     wave_ref[tiles_x + h, y] = wave(
                         rim_refs[h][y], None if step == 0 else field_rims[h][y], real[h]
                     )
-            edge = Side(near, "col", tiles_y).edge
-            for x in range(ext):
-                core_ref[x] = wave_ref[x, edge]
-
-    def product(lhs, rhs):
-        return jnp.dot(lhs, rhs, preferred_element_type=f32)
-
-    def add_column(across, sum_ref, front_ref, halo_ref):
-        for x in range(tiles_x):
-            t = x * tiles_y + across.edge
-            reach = [a for a in (-1, 0, 1) if 0 <= x + a < tiles_x]
-            lhs = jnp.concatenate([halo_ref[x + a] for a in reach], axis=1)
-            rhs = jnp.concatenate([front_ref[t, 3 * (a + 1) + 1 + across.step] for a in reach], axis=0)
-            sum_ref[t] += product(lhs, rhs)
-
-    def add_corner(across, pairing, sum_ref, front_ref, corner):
-        side = Side(pairing, "row", tiles_x)
-        t = side.edge * tiles_y + across.edge
-        sum_ref[t] += product(corner, front_ref[t, 3 * (side.step + 1) + 1 + across.step])
-
-    def inner_kernel(step, wave_ref, side_ref, front_ref, sum_ref):
-        @pl.when(is_active(step))
-        def _():
             for y in range(tiles_y):
                 low, high = max(y - 1, 0), min(y + 1, tiles_y - 1)
                 width = high - low + 1
@@ -383,7 +421,33 @@
                     rhs = front_ref[t, pl.ds(3 * (side.step + 1) + first, width)].reshape(width * cells, cells)
                     sum_ref[t] += product(beside[tiles_x + h], rhs)
             across = Side(far, "col", tiles_y)
-            across.when(lambda: add_column(across, sum_ref, front_ref, side_ref))
+
+            def beyond():
+                for x, total in enumerate(column_products(across, front_ref, side_ref)):
+                    sum_ref[x * tiles_y + across.edge] += total
+
+            across.when(beyond)
+            some = early_tiles()
+            for x, y in some:
+                out_ref[x * tiles_y + y] = sum_ref[x * tiles_y + y].astype(bf16)
+            if last:
+                add_parts(some, earlier[0], out_ref, rest[0])
+            else:
+                for x in range(tiles_x):
+                    rest[halos][x] = out_ref[x * tiles_y + across.edge]
+                for h, pairing in enumerate(row_pairs):
+                    row = Side(pairing, "row", tiles_x).edge
+                    rest[h][1 : tiles_y - 1] = out_ref[pl.ds(row * tiles_y + 1, tiles_y - 2)]
+
+        if last:
+            pos = lax.axis_index("layer")
+            first = jnp.minimum(pos, layers - 1 - pos)
+            whole = [(x, y) for x in range(tiles_x) for y in range(tiles_y)]
+            for k in range(1, layers // 2):
+
+                @pl.when(first == k)
+                def _(k=k):
+                    add_parts(whole, earlier[k], earlier[layers - 1 - k], rest[0])
 
     def add_far_corners(step, sum_ref, front_ref, kappa_ref, core_ref, base_ref):
         phase = int(step >= layers // 2)
@@ -395,7 +459,8 @@
             for h, pairing in enumerate(row_pairs):
                 base = base_ref[ext + phase * halos + h]
                 corner = wave(base, None if step == 0 else core_ref[ext + h], real[h])
-                add_corner(beyond, pairing, sum_ref, front_ref, corner)
+                t, total = corner_product(beyond, pairing, front_ref, corner)
+                sum_ref[t] += total
 
         beyond.when(corners)
 
@@ -417,61 +482,61 @@
 
     def outer_kernel(step, *refs):
         take = taker(refs)
-        take()
+        last = step == layers - 1
+        take(2 + (1 if last else halos + 1))
         front_ref, core_ref = take(), take()
-        last = step == layers - 1
-        kappa_ref, base_ref = (take(), take()) if last else (None, None)
-        earlier = take(layers - 1) if last else []
-        sum_ref, field_ref, rest = take(), take(), take(halos + 1)
+        kappa_ref, base_ref, first_ref = (take(), take(), take()) if last else (None, None, None)
+        sum_ref, field_ref, rest = take(), take(), take(1 if last else halos + 1)
 
         @pl.when(is_active(step))
         def _():
             if last:
                 add_far_corners(step, sum_ref, front_ref, kappa_ref, core_ref, base_ref)
-            across = Side(near, "col", tiles_y)
-            add_column(across, sum_ref, front_ref, core_ref)
-            for h, pairing in enumerate(row_pairs):
-                add_corner(across, pairing, sum_ref, front_ref, core_ref[tiles_x + h])
-            for t in range(tiles):
+            across, beyond = Side(near, "col", tiles_y), Side(far, "col", tiles_y)
+            totals = column_products(across, front_ref, core_ref)
+            corners = [
+                corner_product(across, pairing, front_ref, core_ref[tiles_x + h])[1]
+                for h, pairing in enumerate(row_pairs)
+            ]
+            edges = [Side(pairing, "row", tiles_x).edge for pairing in row_pairs]
+            for x, total in enumerate(totals):
+                t = x * tiles_y + across.edge
+                total = sum_ref[t] + total
+                for edge, corner in zip(edges, corners):
+                    total = total + jnp.where(edge == x, corner, 0.0)
+                field_ref[t] = total.astype(bf16)
+            for edge in edges:
+                t = edge * tiles_y + beyond.edge
                 field_ref[t] = sum_ref[t].astype(bf16)
-            if not last:
-                edge = Side(far, "col", tiles_y).edge
-                for x in range(tiles_x):
-                    rest[halos][x] = field_ref[x * tiles_y + edge]
+            some = late_tiles()
+            if last:
+                add_parts(some, first_ref, field_ref, rest[0])
+            else:
                 for h, pairing in enumerate(row_pairs):
                     row = Side(pairing, "row", tiles_x).edge
-                    rest[h][...] = field_ref[pl.ds(row * tiles_y, tiles_y)]
-
-        if step == layers - 1:
-            pos = lax.axis_index("layer")
-            first = jnp.minimum(pos, layers - 1 - pos)
-            for k in range(layers // 2):
-
-                @pl.when(first == k)
-                def _(k=k):
-                    one, other = earlier[k], field_ref if k == 0 else earlier[layers - 1 - k]
-                    for t in range(tiles):
-                        both = one[t].astype(f32) * other[t].astype(f32)
-                        rest[0][t : t + 1, :] = jnp.sum(both, axis=0, keepdims=True) * intersection_scale
+                    rest[halos][row] = field_ref[row * tiles_y + beyond.edge]
+                    for edge in (across.edge, beyond.edge):
+                        rest[h][edge] = field_ref[row * tiles_y + edge]
 
     fields, field_arrived = [], []
     for step in range(layers):
         last = step == layers - 1
-        wave, core, side = call(
-            functools.partial(wave_kernel, step),
-            [
-                ((ext, tiles_y, *tile), bf16),
-                ((ext + halos * (2 if step == layers // 2 else 1), *tile), bf16),
-                ((tiles_x, *tile), bf16),
-            ],
-            source,
-            kappa,
-            *(source_beside if step < layers // 2 else late),
-            *field_arrived,
+        inputs = [source, kappa, *(source_beside if step < layers // 2 else late), *field_arrived]
+        (core_out,) = call(
+            functools.partial(core_kernel, step),
+            [((ext + halos * (2 if step == layers // 2 else 1), *tile), bf16)],
+            *inputs,
         )
-        core = to_core(core)
-        (summed,) = call(
-            functools.partial(inner_kernel, step), [((tiles, *tile), f32)], wave, side, front
+        core = to_core(core_out)
+        summed, *partial_out = call(
+            functools.partial(inner_kernel, step),
+            [((tiles, *tile), f32), ((tiles, *tile), bf16)]
+            + ([((tiles, cells), f32)] if last else [((tiles_y, *tile), bf16)] * halos + [((tiles_x, *tile), bf16)]),
+            *inputs,
+            core_out,
+            front,
+            *(fields if last else []),
+            scratch=[pltpu.VMEM((ext, tiles_y, *tile), bf16), pltpu.VMEM((tiles_x, *tile), bf16)],
         )
         if step in (0, layers // 2):
             base = core
@@ -490,17 +555,13 @@
             corner = to_core(corner)
         _, field, *extra = call(
             functools.partial(outer_kernel, step),
-            [((tiles, *tile), f32), ((tiles, *tile), bf16)]
-            + (
-                [((tiles, cells), f32)]
-                if last
-                else [((tiles_y, *tile), bf16)] * halos + [((tiles_x, *tile), bf16)]
-            ),
+            [(part.shape, part.dtype) for part in (summed, *partial_out)],
             summed,
+            *partial_out,
             front,
             core,
-            *([kappa, base, *fields] if last else []),
-            aliases={0: 0},
+            *([kappa, base, fields[0]] if last else []),
+            aliases={i: i for i in range(1 + len(partial_out))},
         )
         fields.append(field)
         if not last:

time: 49.5 us -> 49.2 us (level)
  no operation moved by 1% of the time
where the time goes in v5:
time: 49.2 us; the launch traced here: 49.1 us
  starting transfers between devices  27.7 us (56%)
  waiting for transfers between devices  14.5 us (29%)
  Pallas kernels  6.1 us (12%)
  between operations  0.77 us (2%)
    ppermute x24, starting transfers between devices, permuted(): return lax.ppermute(array, AXES, pairs)  27.7 us
    ppermute x24, waiting for transfers between devices, permuted(): return lax.ppermute(array, AXES, pairs)  14.5 us
    pallas_call x24, Pallas kernels, call(): pl.pallas_call(kernel, out_shape=[jax.ShapeDtypeStruct(shape, dtype) for...  6.1 us
  transfers between devices with their start and end apart: 24, of which 14 were waited for; matrix products, arithmetic and copies ran while one was open for 0% of the time, Pallas kernels for 8%

profile of v5, /device:TPU:0, one launch (start us, length us, event | category | flops | bytes accessed | tf_op | source)
XLA Modules:
  0.0 49.1 jit_solution(5194775052956291940)
XLA Ops:
  0.6 1.1 %shard_map.94 = (f32[2,512,128]{2,1,0:T(8,128)S(1)}, s32[1,64]{1,0:T(1,128)S(1)}, bf16[2,2,64,128]{3,2,1,0:T(8,128)(2,1)S(1)}) custom-call(bf16[64,8,128]{2,1,0:T(8,128)(2,1)} %bitcast.8, bf16[64,8,128]{2,1,0:T(8,128)(2,1)} %bitcast.9, s32[1,64]{1,0:T(1,128)} %bitcast.11), custom_call_target="tpu_custom_call" | custom-call | tf_op jit(solution)/shard_map/pallas_call | solution.py:22
  1.7 0.5 %collective-permute-start = (bf16[2,2,64,128]{3,2,1,0:T(8,128)(2,1)S(1)}, bf16[2,2,64,128]{3,2,1,0:T(8,128)(2,1)S(1)}, u32[]{:S(2)}, u32[]{:S(2)}) collective-permute-start(bf16[2,2,64,128]{3,2,1,0:T(8,128)(2,1)S(1)} %get-tuple-element.50), channel_id=1, source_target_pairs={{0,1},{1,0},{2,3},{3,2},{4,5},{5,4},{6,7},{7,6},{8,9},{9,8},{10,11... | collective-permute-start | bytes 196616 | tf_op jit(solution)/shard_map/ppermute | solution.py:85
  2.3 0.2 shard_map.96
  2.5 2.6 %collective-permute-start.1 = (bf16[4,64,128]{2,1,0:T(8,128)(2,1)S(1)}, bf16[4,64,128]{2,1,0:T(8,128)(2,1)S(1)}, u32[]{:S(2)}, u32[]{:S(2)}) collective-permute-start(bf16[4,64,128]{2,1,0:T(8,128)(2,1)S(1)} %get-tuple-element.53), channel_id=1, source_target_pairs={{0,4},{1,5},{2,6},{3,7},{4,0},{5,1},{6,2},{7,3},{8,12},{9,13},{10,... | collective-permute-start | bytes 196616 | tf_op jit(solution)/shard_map/ppermute | solution.py:85
  5.1 0.0 collective-permute-done.refs_2_.refs_1_
  5.1 1.7 %collective-permute-start.2 = (bf16[2,64,128]{2,1,0:T(8,128)(2,1)S(1)}, bf16[2,64,128]{2,1,0:T(8,128)(2,1)S(1)}, u32[]{:S(2)}, u32[]{:S(2)}) collective-permute-start(bf16[2,64,128]{2,1,0:T(8,128)(2,1)S(1)} %shard_map.97), channel_id=1, source_target_pairs={{0,7},{1,2},{2,1},{3,4},{4,3},{5,6},{6,5},{7,0},{8,15},{9,10},{10,... | collective-permute-start | bytes 98312 | tf_op jit(solution)/shard_map/ppermute | solution.py:85
  6.7 1.9 %shard_map.95 = (bf16[2,8,64,128]{3,2,1,0:T(8,128)(2,1)S(1)}, bf16[8,9,128,128]{3,2,1,0:T(8,128)(2,1)S(1)}, f32[2,8,128]{2,1,0:T(8,128)S(1)}, f32[4,4,8,128]{3,2...) custom-call(s32[2,4,9]{2,1,0:T(4,128)} %bitcast.10, f32[4]{0:T(128)} %coupling_hbm.1, ...), custom_call_target="tpu_custom_call" | custom-call | tf_op jit(solution)/shard_map/pallas_call | solution.py:22
  8.6 0.0 collective-permute-done.1.refs_2_
  8.6 0.9 %collective-permute-done.2.refs_3_ = bf16[2,64,128]{2,1,0:T(8,128)(2,1)S(1)} collective-permute-done((bf16[2,64,128]{2,1,0:T(8,128)(2,1)S(1)}, bf16[2,64,128]{2,1,0:T(8,128)(2,1)S(1)}, u32[]{:S(2)}, u32[]{:S(2)}) %collective-permute-start.2) | collective-permute-done | bytes 32800 | tf_op jit(solution)/shard_map/ppermute | solution.py:85
  9.5 0.0 collective-permute-start.3
  9.5 0.5 shard_map.99
  10.0 0.8 %collective-permute-done.3.refs_3_.refs_4_.refs_5_ = bf16[4,64,128]{2,1,0:T(8,128)(2,1)S(1)} collective-permute-done((bf16[4,64,128]{2,1,0:T(8,128)(2,1)S(1)}, bf16[4,64,128]{2,1,0:T(8,128)(2,1)S(1)}, u32[]{:S(2)}, u32[]{:S(2)}) %collective-permute-start.3) | collective-permute-done | bytes 65568 | tf_op jit(solution)/shard_map/ppermute | solution.py:85
  10.8 0.2 shard_map.101
  10.9 1.4 %collective-permute-start.4 = (bf16[8,64,128]{2,1,0:T(8,128)(2,1)S(1)}, bf16[8,64,128]{2,1,0:T(8,128)(2,1)S(1)}, u32[]{:S(2)}, u32[]{:S(2)}) collective-permute-start(bf16[8,64,128]{2,1,0:T(8,128)(2,1)S(1)} %get-tuple-element.61.refs_9_.refs_7_.refs_0_), channel_id=1, source_target_pairs={{0,8},{1,9},{2,10},{3,11},{4,12},{5,13},{6,14},{7,15},{8,0},{9,1},... | collective-permute-start | bytes 393224 | tf_op jit(solution)/shard_map/ppermute | solution.py:85
  12.3 0.0 collective-permute-start.6
  12.3 1.3 %collective-permute-start.5 = (bf16[4,64,128]{2,1,0:T(8,128)(2,1)S(1)}, bf16[4,64,128]{2,1,0:T(8,128)(2,1)S(1)}, u32[]{:S(2)}, u32[]{:S(2)}) collective-permute-start(bf16[4,64,128]{2,1,0:T(8,128)(2,1)S(1)} %get-tuple-element.62), channel_id=1, source_target_pairs={{0,12},{1,13},{2,14},{3,15},{4,8},{5,9},{6,10},{7,11},{8,4},{9,5},... | collective-permute-start | bytes 196616 | tf_op jit(solution)/shard_map/ppermute | solution.py:85
  13.6 2.1 %collective-permute-start.7 = (bf16[2,64,128]{2,1,0:T(8,128)(2,1)S(1)}, bf16[2,64,128]{2,1,0:T(8,128)(2,1)S(1)}, u32[]{:S(2)}, u32[]{:S(2)}) collective-permute-start(bf16[2,64,128]{2,1,0:T(8,128)(2,1)S(1)} %shard_map.102), channel_id=1, source_target_pairs={{0,15},{1,10},{2,9},{3,12},{4,11},{5,14},{6,13},{7,8},{8,7},{9,2},... | collective-permute-start | bytes 98312 | tf_op jit(solution)/shard_map/ppermute | solution.py:85
  15.7 0.9 %collective-permute-start.9 = (bf16[4,64,128]{2,1,0:T(8,128)(2,1)S(1)}, bf16[4,64,128]{2,1,0:T(8,128)(2,1)S(1)}, u32[]{:S(2)}, u32[]{:S(2)}) collective-permute-start(bf16[4,64,128]{2,1,0:T(8,128)(2,1)S(1)} %get-tuple-element.66), channel_id=1, source_target_pairs={{0,4},{1,5},{2,6},{3,7},{4,0},{5,1},{6,2},{7,3},{8,12},{9,13},{10,... | collective-permute-start | bytes 196616 | tf_op jit(solution)/shard_map/ppermute | solution.py:85
  16.6 1.0 %collective-permute-start.10 = (bf16[4,64,128]{2,1,0:T(8,128)(2,1)S(1)}, bf16[4,64,128]{2,1,0:T(8,128)(2,1)S(1)}, u32[]{:S(2)}, u32[]{:S(2)}) collective-permute-start(bf16[4,64,128]{2,1,0:T(8,128)(2,1)S(1)} %get-tuple-element.67), channel_id=1, source_target_pairs={{0,7},{1,2},{2,1},{3,4},{4,3},{5,6},{6,5},{7,0},{8,15},{9,10},{10,... | collective-permute-start | bytes 196616 | tf_op jit(solution)/shard_map/ppermute | solution.py:85
  17.6 1.7 %collective-permute-done.7.refs_6_ = bf16[2,64,128]{2,1,0:T(8,128)(2,1)S(1)} collective-permute-done((bf16[2,64,128]{2,1,0:T(8,128)(2,1)S(1)}, bf16[2,64,128]{2,1,0:T(8,128)(2,1)S(1)}, u32[]{:S(2)}, u32[]{:S(2)}) %collective-permute-start.7) | collective-permute-done | bytes 32800 | tf_op jit(solution)/shard_map/ppermute | solution.py:85
  19.4 0.1 collective-permute-start.8
  19.5 1.0 %collective-permute-done.9.refs_5_.refs_2_ = bf16[4,64,128]{2,1,0:T(8,128)(2,1)S(1)} collective-permute-done((bf16[4,64,128]{2,1,0:T(8,128)(2,1)S(1)}, bf16[4,64,128]{2,1,0:T(8,128)(2,1)S(1)}, u32[]{:S(2)}, u32[]{:S(2)}) %collective-permute-start.9) | collective-permute-done | bytes 65568 | tf_op jit(solution)/shard_map/ppermute | solution.py:85
  20.4 0.8 %collective-permute-done.10.refs_6_.refs_3_ = bf16[4,64,128]{2,1,0:T(8,128)(2,1)S(1)} collective-permute-done((bf16[4,64,128]{2,1,0:T(8,128)(2,1)S(1)}, bf16[4,64,128]{2,1,0:T(8,128)(2,1)S(1)}, u32[]{:S(2)}, u32[]{:S(2)}) %collective-permute-start.10) | collective-permute-done | bytes 65568 | tf_op jit(solution)/shard_map/ppermute | solution.py:85
  21.3 0.5 %collective-permute-start.13 = (bf16[2,64,128]{2,1,0:T(8,128)(2,1)S(1)}, bf16[2,64,128]{2,1,0:T(8,128)(2,1)S(1)}, u32[]{:S(2)}, u32[]{:S(2)}) collective-permute-start(bf16[2,64,128]{2,1,0:T(8,128)(2,1)S(1)} %get-tuple-element.75), channel_id=1, source_target_pairs={{0,1},{1,0},{2,3},{3,2},{4,5},{5,4},{6,7},{7,6},{8,9},{9,8},{10,11... | collective-permute-start | bytes 98312 | tf_op jit(solution)/shard_map/ppermute | solution.py:85
  21.8 0.1 collective-permute-start.12
  21.8 0.8 %collective-permute-done.13.refs_1_ = bf16[2,64,128]{2,1,0:T(8,128)(2,1)S(1)} collective-permute-done((bf16[2,64,128]{2,1,0:T(8,128)(2,1)S(1)}, bf16[2,64,128]{2,1,0:T(8,128)(2,1)S(1)}, u32[]{:S(2)}, u32[]{:S(2)}) %collective-permute-start.13) | collective-permute-done | bytes 32800 | tf_op jit(solution)/shard_map/ppermute | solution.py:85
  22.7 0.3 collective-permute-start.14
  23.0 0.9 %collective-permute-done.14.refs_6_ = bf16[2,64,128]{2,1,0:T(8,128)(2,1)S(1)} collective-permute-done((bf16[2,64,128]{2,1,0:T(8,128)(2,1)S(1)}, bf16[2,64,128]{2,1,0:T(8,128)(2,1)S(1)}, u32[]{:S(2)}, u32[]{:S(2)}) %collective-permute-start.14) | collective-permute-done | bytes 32800 | tf_op jit(solution)/shard_map/ppermute | solution.py:85
  23.9 0.4 collective-permute-start.15
  24.3 1.0 %collective-permute-done.15.refs_3_.refs_4_.refs_5_.refs_6_ = bf16[5,64,128]{2,1,0:T(8,128)(2,1)S(1)} collective-permute-done((bf16[5,64,128]{2,1,0:T(8,128)(2,1)S(1)}, bf16[5,64,128]{2,1,0:T(8,128)(2,1)S(1)}, u32[]{:S(2)}, u32[]{:S(2)}) %collective-permute-start.15) | collective-permute-done | bytes 81952 | tf_op jit(solution)/shard_map/ppermute | solution.py:85
  25.2 8.1 %collective-permute-start.16 = (bf16[8,64,128]{2,1,0:T(8,128)(2,1)S(1)}, bf16[8,64,128]{2,1,0:T(8,128)(2,1)S(1)}, u32[]{:S(2)}, u32[]{:S(2)}) collective-permute-start(bf16[8,64,128]{2,1,0:T(8,128)(2,1)S(1)} %get-tuple-element.81.refs_11_.refs_2_), channel_id=1, source_target_pairs={{0,8},{1,9},{2,10},{3,11},{4,12},{5,13},{6,14},{7,15},{8,0},{9,1},... | collective-permute-start | bytes 393224 | tf_op jit(solution)/shard_map/ppermute | solution.py:85
  33.4 0.0 collective-permute-start.18
  33.4 0.7 %collective-permute-start.17 = (bf16[4,64,128]{2,1,0:T(8,128)(2,1)S(1)}, bf16[4,64,128]{2,1,0:T(8,128)(2,1)S(1)}, u32[]{:S(2)}, u32[]{:S(2)}) collective-permute-start(bf16[4,64,128]{2,1,0:T(8,128)(2,1)S(1)} %get-tuple-element.82), channel_id=1, source_target_pairs={{0,12},{1,13},{2,14},{3,15},{4,8},{5,9},{6,10},{7,11},{8,4},{9,5},... | collective-permute-start | bytes 196616 | tf_op jit(solution)/shard_map/ppermute | solution.py:85
  34.1 0.5 collective-permute-done.18.refs_1_
  34.6 1.5 %collective-permute-start.19 = (bf16[2,64,128]{2,1,0:T(8,128)(2,1)S(1)}, bf16[2,64,128]{2,1,0:T(8,128)(2,1)S(1)}, u32[]{:S(2)}, u32[]{:S(2)}) collective-permute-start(bf16[2,64,128]{2,1,0:T(8,128)(2,1)S(1)} %shard_map.112), channel_id=1, source_target_pairs={{0,15},{1,10},{2,9},{3,12},{4,11},{5,14},{6,13},{7,8},{8,7},{9,2},... | collective-permute-start | bytes 98312 | tf_op jit(solution)/shard_map/ppermute | solution.py:85
  36.1 3.3 %collective-permute-done.17.refs_5_ = bf16[4,64,128]{2,1,0:T(8,128)(2,1)S(1)} collective-permute-done((bf16[4,64,128]{2,1,0:T(8,128)(2,1)S(1)}, bf16[4,64,128]{2,1,0:T(8,128)(2,1)S(1)}, u32[]{:S(2)}, u32[]{:S(2)}) %collective-permute-start.17) | collective-permute-done | bytes 65568 | tf_op jit(solution)/shard_map/ppermute | solution.py:85
  39.4 0.5 collective-permute-done.19.refs_6_
  39.9 0.1 collective-permute-start.20
  40.0 0.5 %shard_map.114 = (f32[8,64,128]{2,1,0:T(8,128)S(1)}, bf16[8,64,128]{2,1,0:T(8,128)(2,1)S(1)}, f32[8,128]{1,0:T(8,128)S(1)}) custom-call(bf16[2,8,64,128]{3,2,1,0:T(8,128)(2,1)S(1)} %get-tuple-element.51.refs_0_, f32[2,8,128]{2,1,0:T(8,128)S(1)} %get-tuple-element.52.refs_1_.refs_2_.refs_5_, bf16[4,64,128]{2,1,0:T(8,128)(2,1)S(1)} %collective-permute-done.9.refs_5_.refs_2_, ...), custom_call_target="tpu_custom_call" | custom-call | tf_op jit(solution)/shard_map/pallas_call | solution.py:22
  40.5 0.7 %collective-permute-done.20.refs_4_ = bf16[4,64,128]{2,1,0:T(8,128)(2,1)S(1)} collective-permute-done((bf16[4,64,128]{2,1,0:T(8,128)(2,1)S(1)}, bf16[4,64,128]{2,1,0:T(8,128)(2,1)S(1)}, u32[]{:S(2)}, u32[]{:S(2)}) %collective-permute-start.20) | collective-permute-done | bytes 65568 | tf_op jit(solution)/shard_map/ppermute | solution.py:85
  41.2 0.2 shard_map.115
  41.4 2.5 %collective-permute-start.23 = (f32[8,128]{1,0:T(8,128)S(1)}, f32[8,128]{1,0:T(8,128)S(1)}, u32[]{:S(2)}, u32[]{:S(2)}) collective-permute-start(f32[8,128]{1,0:T(8,128)S(1)} %get-tuple-element.91.refs_0_), channel_id=1, source_target_pairs={{0,24},{1,25},{2,26},{3,27},{4,28},{5,29},{6,30},{7,31},{8,16},{9,... | collective-permute-start | bytes 12296 | tf_op jit(solution)/shard_map/ppermute | solution.py:85
  43.9 0.2 collective-permute-start.22
  44.1 1.7 %collective-permute-start.21 = (f32[8,128]{1,0:T(8,128)S(1)}, f32[8,128]{1,0:T(8,128)S(1)}, u32[]{:S(2)}, u32[]{:S(2)}) collective-permute-start(f32[8,128]{1,0:T(8,128)S(1)} %get-tuple-element.91.refs_0_), channel_id=1, source_target_pairs={{0,8},{1,9},{2,10},{3,11},{4,12},{5,13},{6,14},{7,15},{8,0},{9,1},... | collective-permute-start | bytes 12296 | tf_op jit(solution)/shard_map/ppermute | solution.py:85
  45.8 0.8 %shard_map.116 = (bf16[64,8,128]{2,1,0:T(8,128)(2,1)}, bf16[64,8,128]{2,1,0:T(8,128)(2,1)}) custom-call(bf16[8,64,128]{2,1,0:T(8,128)(2,1)S(1)} %get-tuple-element.61.refs_9_.refs_7_.refs_0_, bf16[8,64,128]{2,1,0:T(8,128)(2,1)S(1)} %get-tuple-element.72.refs_10_.refs_1_, bf16[8,64,128]{2,1,0:T(8,128)(2,1)S(1)} %get-tuple-element.81.refs_11_.refs_2_, ...), custom_call_target="tpu_custom_call" | custom-call | tf_op jit(solution)/shard_map/pallas_call | solution.py:22
  46.7 0.2 collective-permute-done.23.refs_3_
  46.9 1.6 %collective-permute-done.22.refs_2_ = f32[8,128]{1,0:T(8,128)S(1)} collective-permute-done((f32[8,128]{1,0:T(8,128)S(1)}, f32[8,128]{1,0:T(8,128)S(1)}, u32[]{:S(2)}, u32[]{:S(2)}) %collective-permute-start.22) | collective-permute-done | bytes 4128 | tf_op jit(solution)/shard_map/ppermute | solution.py:85
  48.4 0.6 %shard_map.117 = f32[4,2,4,128]{3,2,1,0:T(4,128)} custom-call(f32[8,128]{1,0:T(8,128)S(1)} %get-tuple-element.91.refs_0_, f32[8,128]{1,0:T(8,128)S(1)} %collective-permute-done.21.refs_1_, f32[8,128]{1,0:T(8,128)S(1)} %collective-permute-done.22.refs_2_, f32[8,128]{1,0:T(8,128)S(1)} %collective-permute-done.23.refs_3_, ...), custom_call_target="tpu_custom_call" | custom-call | tf_op jit(solution)/shard_map/pallas_call | solution.py:22
  (24 shorter events, 0.1 us)
Async XLA Ops:
  1.7 3.3 %collective-permute-start = (bf16[2,2,64,128]{3,2,1,0:T(8,128)(2,1)S(1)}, bf16[2,2,64,128]{3,2,1,0:T(8,128)(2,1)S(1)}, u32[]{:S(2)}, u32[]{:S(2)}) collective-permute-start(bf16[2,2,64,128]{3,2,1,0:T(8,128)(2,1)S(1)} %get-tuple-element.50), channel_id=1, source_target_pairs={{0,1},{1,0},{2,3},{3,2},{4,5},{5,4},{6,7},{7,6},{8,9},{9,8},{10,11... | collective-permute-start | bytes 196616 | tf_op jit(solution)/shard_map/ppermute | solution.py:85
  2.5 6.1 %collective-permute-start.1 = (bf16[4,64,128]{2,1,0:T(8,128)(2,1)S(1)}, bf16[4,64,128]{2,1,0:T(8,128)(2,1)S(1)}, u32[]{:S(2)}, u32[]{:S(2)}) collective-permute-start(bf16[4,64,128]{2,1,0:T(8,128)(2,1)S(1)} %get-tuple-element.53), channel_id=1, source_target_pairs={{0,4},{1,5},{2,6},{3,7},{4,0},{5,1},{6,2},{7,3},{8,12},{9,13},{10,... | collective-permute-start | bytes 196616 | tf_op jit(solution)/shard_map/ppermute | solution.py:85
  5.1 4.4 %collective-permute-start.2 = (bf16[2,64,128]{2,1,0:T(8,128)(2,1)S(1)}, bf16[2,64,128]{2,1,0:T(8,128)(2,1)S(1)}, u32[]{:S(2)}, u32[]{:S(2)}) collective-permute-start(bf16[2,64,128]{2,1,0:T(8,128)(2,1)S(1)} %shard_map.97), channel_id=1, source_target_pairs={{0,7},{1,2},{2,1},{3,4},{4,3},{5,6},{6,5},{7,0},{8,15},{9,10},{10,... | collective-permute-start | bytes 98312 | tf_op jit(solution)/shard_map/ppermute | solution.py:85
  9.5 1.3 %collective-permute-start.3 = (bf16[4,64,128]{2,1,0:T(8,128)(2,1)S(1)}, bf16[4,64,128]{2,1,0:T(8,128)(2,1)S(1)}, u32[]{:S(2)}, u32[]{:S(2)}) collective-permute-start(bf16[4,64,128]{2,1,0:T(8,128)(2,1)S(1)} %shard_map.98.refs_4_), channel_id=1, source_target_pairs={{0,1},{1,0},{2,3},{3,2},{4,5},{5,4},{6,7},{7,6},{8,9},{9,8},{10,11... | collective-permute-start | bytes 196616 | tf_op jit(solution)/shard_map/ppermute | solution.py:85
  10.9 8.4 %collective-permute-start.4 = (bf16[8,64,128]{2,1,0:T(8,128)(2,1)S(1)}, bf16[8,64,128]{2,1,0:T(8,128)(2,1)S(1)}, u32[]{:S(2)}, u32[]{:S(2)}) collective-permute-start(bf16[8,64,128]{2,1,0:T(8,128)(2,1)S(1)} %get-tuple-element.61.refs_9_.refs_7_.refs_0_), channel_id=1, source_target_pairs={{0,8},{1,9},{2,10},{3,11},{4,12},{5,13},{6,14},{7,15},{8,0},{9,1},... | collective-permute-start | bytes 393224 | tf_op jit(solution)/shard_map/ppermute | solution.py:85
  12.3 1.3 %collective-permute-start.6 = (bf16[2,64,128]{2,1,0:T(8,128)(2,1)S(1)}, bf16[2,64,128]{2,1,0:T(8,128)(2,1)S(1)}, u32[]{:S(2)}, u32[]{:S(2)}) collective-permute-start(bf16[2,64,128]{2,1,0:T(8,128)(2,1)S(1)} %get-tuple-element.64), channel_id=1, source_target_pairs={{0,1},{1,0},{2,3},{3,2},{4,5},{5,4},{6,7},{7,6},{8,9},{9,8},{10,11... | collective-permute-start | bytes 98312 | tf_op jit(solution)/shard_map/ppermute | solution.py:85
  12.3 7.0 %collective-permute-start.5 = (bf16[4,64,128]{2,1,0:T(8,128)(2,1)S(1)}, bf16[4,64,128]{2,1,0:T(8,128)(2,1)S(1)}, u32[]{:S(2)}, u32[]{:S(2)}) collective-permute-start(bf16[4,64,128]{2,1,0:T(8,128)(2,1)S(1)} %get-tuple-element.62), channel_id=1, source_target_pairs={{0,12},{1,13},{2,14},{3,15},{4,8},{5,9},{6,10},{7,11},{8,4},{9,5},... | collective-permute-start | bytes 196616 | tf_op jit(solution)/shard_map/ppermute | solution.py:85
  13.6 5.7 %collective-permute-start.7 = (bf16[2,64,128]{2,1,0:T(8,128)(2,1)S(1)}, bf16[2,64,128]{2,1,0:T(8,128)(2,1)S(1)}, u32[]{:S(2)}, u32[]{:S(2)}) collective-permute-start(bf16[2,64,128]{2,1,0:T(8,128)(2,1)S(1)} %shard_map.102), channel_id=1, source_target_pairs={{0,15},{1,10},{2,9},{3,12},{4,11},{5,14},{6,13},{7,8},{8,7},{9,2},... | collective-permute-start | bytes 98312 | tf_op jit(solution)/shard_map/ppermute | solution.py:85
  15.7 4.8 %collective-permute-start.9 = (bf16[4,64,128]{2,1,0:T(8,128)(2,1)S(1)}, bf16[4,64,128]{2,1,0:T(8,128)(2,1)S(1)}, u32[]{:S(2)}, u32[]{:S(2)}) collective-permute-start(bf16[4,64,128]{2,1,0:T(8,128)(2,1)S(1)} %get-tuple-element.66), channel_id=1, source_target_pairs={{0,4},{1,5},{2,6},{3,7},{4,0},{5,1},{6,2},{7,3},{8,12},{9,13},{10,... | collective-permute-start | bytes 196616 | tf_op jit(solution)/shard_map/ppermute | solution.py:85
  16.6 4.6 %collective-permute-start.10 = (bf16[4,64,128]{2,1,0:T(8,128)(2,1)S(1)}, bf16[4,64,128]{2,1,0:T(8,128)(2,1)S(1)}, u32[]{:S(2)}, u32[]{:S(2)}) collective-permute-start(bf16[4,64,128]{2,1,0:T(8,128)(2,1)S(1)} %get-tuple-element.67), channel_id=1, source_target_pairs={{0,7},{1,2},{2,1},{3,4},{4,3},{5,6},{6,5},{7,0},{8,15},{9,10},{10,... | collective-permute-start | bytes 196616 | tf_op jit(solution)/shard_map/ppermute | solution.py:85
  19.4 1.9 %collective-permute-start.8 = (bf16[4,64,128]{2,1,0:T(8,128)(2,1)S(1)}, bf16[4,64,128]{2,1,0:T(8,128)(2,1)S(1)}, u32[]{:S(2)}, u32[]{:S(2)}) collective-permute-start(bf16[4,64,128]{2,1,0:T(8,128)(2,1)S(1)} %shard_map.103.refs_7_), channel_id=1, source_target_pairs={{0,1},{1,0},{2,3},{3,2},{4,5},{5,4},{6,7},{7,6},{8,9},{9,8},{10,11... | collective-permute-start | bytes 196616 | tf_op jit(solution)/shard_map/ppermute | solution.py:85
  21.3 2.6 %collective-permute-start.11 = (bf16[8,64,128]{2,1,0:T(8,128)(2,1)S(1)}, bf16[8,64,128]{2,1,0:T(8,128)(2,1)S(1)}, u32[]{:S(2)}, u32[]{:S(2)}) collective-permute-start(bf16[8,64,128]{2,1,0:T(8,128)(2,1)S(1)} %get-tuple-element.72.refs_10_.refs_1_), channel_id=1, source_target_pairs={{0,1},{1,0},{2,3},{3,2},{4,5},{5,4},{6,7},{7,6},{8,16},{9,17},{10,... | collective-permute-start | bytes 393224 | tf_op jit(solution)/shard_map/ppermute | solution.py:85
  21.3 1.4 %collective-permute-start.13 = (bf16[2,64,128]{2,1,0:T(8,128)(2,1)S(1)}, bf16[2,64,128]{2,1,0:T(8,128)(2,1)S(1)}, u32[]{:S(2)}, u32[]{:S(2)}) collective-permute-start(bf16[2,64,128]{2,1,0:T(8,128)(2,1)S(1)} %get-tuple-element.75), channel_id=1, source_target_pairs={{0,1},{1,0},{2,3},{3,2},{4,5},{5,4},{6,7},{7,6},{8,9},{9,8},{10,11... | collective-permute-start | bytes 98312 | tf_op jit(solution)/shard_map/ppermute | solution.py:85
  21.8 2.1 %collective-permute-start.12 = (bf16[4,64,128]{2,1,0:T(8,128)(2,1)S(1)}, bf16[4,64,128]{2,1,0:T(8,128)(2,1)S(1)}, u32[]{:S(2)}, u32[]{:S(2)}) collective-permute-start(bf16[4,64,128]{2,1,0:T(8,128)(2,1)S(1)} %get-tuple-element.73), channel_id=1, source_target_pairs={{0,1},{1,0},{2,3},{3,2},{4,5},{5,4},{6,7},{7,6},{8,20},{9,21},{10,... | collective-permute-start | bytes 196616 | tf_op jit(solution)/shard_map/ppermute | solution.py:85
  22.7 1.2 %collective-permute-start.14 = (bf16[2,64,128]{2,1,0:T(8,128)(2,1)S(1)}, bf16[2,64,128]{2,1,0:T(8,128)(2,1)S(1)}, u32[]{:S(2)}, u32[]{:S(2)}) collective-permute-start(bf16[2,64,128]{2,1,0:T(8,128)(2,1)S(1)} %shard_map.107), channel_id=1, source_target_pairs={{0,1},{1,0},{2,3},{3,2},{4,5},{5,4},{6,7},{7,6},{8,23},{9,18},{10,... | collective-permute-start | bytes 98312 | tf_op jit(solution)/shard_map/ppermute | solution.py:85
  23.9 1.3 %collective-permute-start.15 = (bf16[5,64,128]{2,1,0:T(8,128)(2,1)S(1)}, bf16[5,64,128]{2,1,0:T(8,128)(2,1)S(1)}, u32[]{:S(2)}, u32[]{:S(2)}) collective-permute-start(bf16[5,64,128]{2,1,0:T(8,128)(2,1)S(1)} %shard_map.108.refs_7_), channel_id=1, source_target_pairs={{0,1},{1,0},{2,3},{3,2},{4,5},{5,4},{6,7},{7,6},{8,9},{9,8},{10,11... | collective-permute-start | bytes 245768 | tf_op jit(solution)/shard_map/ppermute | solution.py:85
  25.2 14.6 %collective-permute-start.16 = (bf16[8,64,128]{2,1,0:T(8,128)(2,1)S(1)}, bf16[8,64,128]{2,1,0:T(8,128)(2,1)S(1)}, u32[]{:S(2)}, u32[]{:S(2)}) collective-permute-start(bf16[8,64,128]{2,1,0:T(8,128)(2,1)S(1)} %get-tuple-element.81.refs_11_.refs_2_), channel_id=1, source_target_pairs={{0,8},{1,9},{2,10},{3,11},{4,12},{5,13},{6,14},{7,15},{8,0},{9,1},... | collective-permute-start | bytes 393224 | tf_op jit(solution)/shard_map/ppermute | solution.py:85
  33.4 1.2 %collective-permute-start.18 = (bf16[2,64,128]{2,1,0:T(8,128)(2,1)S(1)}, bf16[2,64,128]{2,1,0:T(8,128)(2,1)S(1)}, u32[]{:S(2)}, u32[]{:S(2)}) collective-permute-start(bf16[2,64,128]{2,1,0:T(8,128)(2,1)S(1)} %get-tuple-element.84), channel_id=1, source_target_pairs={{0,1},{1,0},{2,3},{3,2},{4,5},{5,4},{6,7},{7,6},{8,9},{9,8},{10,11... | collective-permute-start | bytes 98312 | tf_op jit(solution)/shard_map/ppermute | solution.py:85
  33.4 6.0 %collective-permute-start.17 = (bf16[4,64,128]{2,1,0:T(8,128)(2,1)S(1)}, bf16[4,64,128]{2,1,0:T(8,128)(2,1)S(1)}, u32[]{:S(2)}, u32[]{:S(2)}) collective-permute-start(bf16[4,64,128]{2,1,0:T(8,128)(2,1)S(1)} %get-tuple-element.82), channel_id=1, source_target_pairs={{0,12},{1,13},{2,14},{3,15},{4,8},{5,9},{6,10},{7,11},{8,4},{9,5},... | collective-permute-start | bytes 196616 | tf_op jit(solution)/shard_map/ppermute | solution.py:85
  34.6 5.3 %collective-permute-start.19 = (bf16[2,64,128]{2,1,0:T(8,128)(2,1)S(1)}, bf16[2,64,128]{2,1,0:T(8,128)(2,1)S(1)}, u32[]{:S(2)}, u32[]{:S(2)}) collective-permute-start(bf16[2,64,128]{2,1,0:T(8,128)(2,1)S(1)} %shard_map.112), channel_id=1, source_target_pairs={{0,15},{1,10},{2,9},{3,12},{4,11},{5,14},{6,13},{7,8},{8,7},{9,2},... | collective-permute-start | bytes 98312 | tf_op jit(solution)/shard_map/ppermute | solution.py:85
  39.9 1.3 %collective-permute-start.20 = (bf16[4,64,128]{2,1,0:T(8,128)(2,1)S(1)}, bf16[4,64,128]{2,1,0:T(8,128)(2,1)S(1)}, u32[]{:S(2)}, u32[]{:S(2)}) collective-permute-start(bf16[4,64,128]{2,1,0:T(8,128)(2,1)S(1)} %shard_map.113.refs_7_), channel_id=1, source_target_pairs={{0,1},{1,0},{2,3},{3,2},{4,5},{5,4},{6,7},{7,6},{8,9},{9,8},{10,11... | collective-permute-start | bytes 196616 | tf_op jit(solution)/shard_map/ppermute | solution.py:85
  41.4 5.5 %collective-permute-start.23 = (f32[8,128]{1,0:T(8,128)S(1)}, f32[8,128]{1,0:T(8,128)S(1)}, u32[]{:S(2)}, u32[]{:S(2)}) collective-permute-start(f32[8,128]{1,0:T(8,128)S(1)} %get-tuple-element.91.refs_0_), channel_id=1, source_target_pairs={{0,24},{1,25},{2,26},{3,27},{4,28},{5,29},{6,30},{7,31},{8,16},{9,... | collective-permute-start | bytes 12296 | tf_op jit(solution)/shard_map/ppermute | solution.py:85
  43.9 4.5 %collective-permute-start.22 = (f32[8,128]{1,0:T(8,128)S(1)}, f32[8,128]{1,0:T(8,128)S(1)}, u32[]{:S(2)}, u32[]{:S(2)}) collective-permute-start(f32[8,128]{1,0:T(8,128)S(1)} %get-tuple-element.91.refs_0_), channel_id=1, source_target_pairs={{0,16},{1,17},{2,18},{3,19},{4,20},{5,21},{6,22},{7,23},{8,24},{9,... | collective-permute-start | bytes 12296 | tf_op jit(solution)/shard_map/ppermute | solution.py:85
  44.1 4.3 %collective-permute-start.21 = (f32[8,128]{1,0:T(8,128)S(1)}, f32[8,128]{1,0:T(8,128)S(1)}, u32[]{:S(2)}, u32[]{:S(2)}) collective-permute-start(f32[8,128]{1,0:T(8,128)S(1)} %get-tuple-element.91.refs_0_), channel_id=1, source_target_pairs={{0,8},{1,9},{2,10},{3,11},{4,12},{5,13},{6,14},{7,15},{8,0},{9,1},... | collective-permute-start | bytes 12296 | tf_op jit(solution)/shard_map/ppermute | solution.py:85

commit v6 on v5

--- a/solution.py
+++ b/solution.py
@@ -12,6 +12,7 @@
 AXES = ("layer", "row", "col")
 OFFSETS = 9
 VMEM_BYTES = 24 * 1024 * 1024
+BESIDE = 16
 SPARE = 2
 
 VM = pl.BlockSpec(memory_space=pltpu.VMEM)
@@ -485,6 +486,8 @@
         last = step == layers - 1
         take(2 + (1 if last else halos + 1))
         front_ref, core_ref = take(), take()
+        if last and layers == 4:
+            take()
         kappa_ref, base_ref, first_ref = (take(), take(), take()) if last else (None, None, None)
         sum_ref, field_ref, rest = take(), take(), take(1 if last else halos + 1)
 
@@ -517,6 +520,14 @@
                     rest[halos][row] = field_ref[row * tiles_y + beyond.edge]
                     for edge in (across.edge, beyond.edge):
                         rest[h][edge] = field_ref[row * tiles_y + edge]
+
+    def middle_kernel(one_ref, other_ref, part_ref):
+        pos = lax.axis_index("layer")
+
+        @pl.when(jnp.logical_and(pos > 0, pos < layers - 1))
+        def _():
+            whole = [(x, y) for x in range(tiles_x) for y in range(tiles_y)]
+            add_parts(whole, one_ref, other_ref, part_ref)
 
     fields, field_arrived = [], []
     for step in range(layers):
@@ -560,12 +571,16 @@
             *partial_out,
             front,
             core,
+            *([beside] if last and layers == 4 else []),
             *([kappa, base, fields[0]] if last else []),
             aliases={i: i for i in range(1 + len(partial_out))},
         )
         fields.append(field)
         if not last:
             field_arrived = exchange(step, corner, extra, field)
+        if layers == 4 and step == 2:
+            (beside,) = call(middle_kernel, [((BESIDE * tiles, cells), f32)], fields[1], fields[2])
+            beside = permuted(beside, lambda l, r, c: (l ^ 1, r, c))
     intersection = extra[0]
 
     def fields_kernel(*refs):
@@ -589,22 +604,63 @@
     )
 
     if layers == 4:
-        parts = [intersection] + [
-            permuted(intersection, lambda l, r, c, m=m: (l ^ m, r, c)) for m in range(1, layers)
-        ]
-
-        def gradient_kernel(*refs):
-            part_refs, member_ref, out_ref = refs[:layers], refs[layers], refs[layers + 1]
-            pos = lax.axis_index("layer")
+
+        def pair_kernel(own_ref, beside_ref, out_ref):
+            out_ref[0] = own_ref[...]
+            out_ref[1] = beside_ref[:tiles]
+
+        def gather(parts, member_ref, out_ref):
             for g in range(groups):
                 total = jnp.zeros((tiles, cells), f32)
-                for m in range(layers):
-                    total = total + member_ref[g, pos ^ m] * part_refs[m][...]
+                for layer, part in parts:
+                    total = total + member_ref[g, layer] * part
                 for x in range(tiles_x):
                     out_ref[g, x] = total[x * tiles_y : (x + 1) * tiles_y]
 
-        (gradient,) = call(
-            gradient_kernel, [((groups, tiles_x, tiles_y, cells), f32)], *parts, member
+        def ends_kernel(own_ref, beside_ref, across_ref, member_ref, out_ref):
+            pos = lax.axis_index("layer")
+            end = layers - 1 - pos
+            parts = [(pos, own_ref[...]), (pos ^ 1, beside_ref[:tiles]), (end, across_ref[0]), (end ^ 1, across_ref[1])]
+            gather(parts, member_ref, out_ref)
+
+        def middle_layers_kernel(ends_ref, own_ref, across_ref, next_ref, other_ref, member_ref, out_ref, sum_ref, sem):
+            pos = lax.axis_index("layer")
+
+            @pl.when(jnp.logical_and(pos > 0, pos < layers - 1))
+            def _():
+                parts = [
+                    (pos, own_ref[...]),
+                    (layers - 1 - pos, across_ref[0]),
+                    (pos ^ 1, next_ref[...]),
+                    (pos ^ 2, other_ref[...]),
+                ]
+                gather(parts, member_ref, sum_ref)
+                copy = pltpu.make_async_copy(sum_ref, out_ref, sem)
+                copy.start()
+                copy.wait()
+
+        out_shape = (groups, tiles_x, tiles_y, cells)
+        (both,) = call(pair_kernel, [((2, tiles, cells), f32)], intersection, beside)
+        across = permuted(both, lambda l, r, c: (layers - 1 - l, r, c))
+        following = permuted(intersection, lambda l, r, c: (l ^ 1, r, c))
+        other = permuted(intersection, lambda l, r, c: (l ^ 2, r, c))
+        (gradient,) = call(ends_kernel, [(out_shape, f32)], intersection, beside, across, member)
+        hbm = pl.BlockSpec(memory_space=pltpu.HBM)
+        gradient = pl.pallas_call(
+            middle_layers_kernel,
+            out_shape=jax.ShapeDtypeStruct(out_shape, f32),
+            in_specs=[hbm] + [VM] * 5,
+            out_specs=hbm,
+            scratch_shapes=[pltpu.VMEM(out_shape, f32), pltpu.SemaphoreType.DMA],
+            input_output_aliases={0: 0},
+            compiler_params=pltpu.CompilerParams(vmem_limit_bytes=VMEM_BYTES),
+        )(
+            pltpu.with_memory_space_constraint(gradient, pltpu.HBM),
+            intersection,
+            across,
+            following,
+            other,
+            member,
         )
     else:
         selected = lax.dynamic_index_in_dim(member, lax.axis_index("layer"), 1, keepdims=False)

time: 49.2 us -> 48.6 us (0.988)
  waiting for transfers between devices: 14.5 us -> 13 us
  starting transfers between devices: 27.7 us -> 28.6 us
    ppermute x24 -> x25, waiting for transfers between devices: 14.5 us -> 13 us  [permuted(): return lax.ppermute(array, AXES, pairs)]
    ppermute x24 -> x25, starting transfers between devices: 27.7 us -> 28.6 us  [permuted(): return lax.ppermute(array, AXES, pairs)]
    pallas_call x24 -> x26, Pallas kernels: 6.1 us -> 6.11 us  [call(): pl.pallas_call(kernel, out_shape=[jax.ShapeDtypeStruct(shape, dtype) for...]
  transfers between devices with their start and end apart: 24 -> 25, of which waited for: 14 -> 15; matrix products, arithmetic and copies ran while one was open for 0% -> 0% of each run, Pallas kernels for 8% -> 9%
where the time goes in v6:
time: 48.6 us; the launch traced here: 48.5 us
  starting transfers between devices  28.6 us (59%)
  waiting for transfers between devices  13 us (27%)
  Pallas kernels  6.12 us (13%)
  between operations  0.78 us (2%)
    ppermute x25, starting transfers between devices, permuted(): return lax.ppermute(array, AXES, pairs)  28.6 us
    ppermute x25, waiting for transfers between devices, permuted(): return lax.ppermute(array, AXES, pairs)  13 us
    pallas_call x26, Pallas kernels, call(): pl.pallas_call(kernel, out_shape=[jax.ShapeDtypeStruct(shape, dtype) for...  6.11 us
  transfers between devices with their start and end apart: 25, of which 15 were waited for; matrix products, arithmetic and copies ran while one was open for 0% of the time, Pallas kernels for 9%

profile of v6, /device:TPU:0, one launch (start us, length us, event | category | flops | bytes accessed | tf_op | source)
XLA Modules:
  0.0 48.5 jit_solution(6363292353614687354)
XLA Ops:
  0.6 1.1 %shard_map.94 = (f32[2,512,128]{2,1,0:T(8,128)S(1)}, s32[1,64]{1,0:T(1,128)S(1)}, bf16[2,2,64,128]{3,2,1,0:T(8,128)(2,1)S(1)}) custom-call(bf16[64,8,128]{2,1,0:T(8,128)(2,1)} %bitcast.8, bf16[64,8,128]{2,1,0:T(8,128)(2,1)} %bitcast.9, s32[1,64]{1,0:T(1,128)} %bitcast.11), custom_call_target="tpu_custom_call" | custom-call | tf_op jit(solution)/shard_map/pallas_call | solution.py:23
  1.7 0.5 %collective-permute-start = (bf16[2,2,64,128]{3,2,1,0:T(8,128)(2,1)S(1)}, bf16[2,2,64,128]{3,2,1,0:T(8,128)(2,1)S(1)}, u32[]{:S(2)}, u32[]{:S(2)}) collective-permute-start(bf16[2,2,64,128]{3,2,1,0:T(8,128)(2,1)S(1)} %get-tuple-element.50), channel_id=1, source_target_pairs={{0,1},{1,0},{2,3},{3,2},{4,5},{5,4},{6,7},{7,6},{8,9},{9,8},{10,11... | collective-permute-start | bytes 196616 | tf_op jit(solution)/shard_map/ppermute | solution.py:86
  2.3 0.2 shard_map.96
  2.5 2.6 %collective-permute-start.1 = (bf16[4,64,128]{2,1,0:T(8,128)(2,1)S(1)}, bf16[4,64,128]{2,1,0:T(8,128)(2,1)S(1)}, u32[]{:S(2)}, u32[]{:S(2)}) collective-permute-start(bf16[4,64,128]{2,1,0:T(8,128)(2,1)S(1)} %get-tuple-element.53), channel_id=1, source_target_pairs={{0,4},{1,5},{2,6},{3,7},{4,0},{5,1},{6,2},{7,3},{8,12},{9,13},{10,... | collective-permute-start | bytes 196616 | tf_op jit(solution)/shard_map/ppermute | solution.py:86
  5.1 1.7 %collective-permute-start.2 = (bf16[2,64,128]{2,1,0:T(8,128)(2,1)S(1)}, bf16[2,64,128]{2,1,0:T(8,128)(2,1)S(1)}, u32[]{:S(2)}, u32[]{:S(2)}) collective-permute-start(bf16[2,64,128]{2,1,0:T(8,128)(2,1)S(1)} %shard_map.97), channel_id=1, source_target_pairs={{0,7},{1,2},{2,1},{3,4},{4,3},{5,6},{6,5},{7,0},{8,15},{9,10},{10,... | collective-permute-start | bytes 98312 | tf_op jit(solution)/shard_map/ppermute | solution.py:86
  6.7 1.9 %shard_map.95 = (bf16[2,8,64,128]{3,2,1,0:T(8,128)(2,1)S(1)}, bf16[8,9,128,128]{3,2,1,0:T(8,128)(2,1)S(1)}, f32[2,8,128]{2,1,0:T(8,128)S(1)}, f32[4,4,8,128]{3,2...) custom-call(s32[2,4,9]{2,1,0:T(4,128)} %bitcast.10, f32[4]{0:T(128)} %coupling_hbm.1, ...), custom_call_target="tpu_custom_call" | custom-call | tf_op jit(solution)/shard_map/pallas_call | solution.py:23
  8.6 0.0 collective-permute-done.1.refs_2_
  8.6 0.9 %collective-permute-done.2.refs_3_ = bf16[2,64,128]{2,1,0:T(8,128)(2,1)S(1)} collective-permute-done((bf16[2,64,128]{2,1,0:T(8,128)(2,1)S(1)}, bf16[2,64,128]{2,1,0:T(8,128)(2,1)S(1)}, u32[]{:S(2)}, u32[]{:S(2)}) %collective-permute-start.2) | collective-permute-done | bytes 32800 | tf_op jit(solution)/shard_map/ppermute | solution.py:86
  9.5 0.0 collective-permute-start.3
  9.5 0.5 %shard_map.99 = (f32[8,64,128]{2,1,0:T(8,128)S(1)}, bf16[8,64,128]{2,1,0:T(8,128)(2,1)S(1)}, bf16[4,64,128]{2,1,0:T(8,128)(2,1)S(1)}, bf16[2,64,128]{2,1,0:T(8,128)(2,1)S(1)}) custom-call(bf16[2,8,64,128]{3,2,1,0:T(8,128)(2,1)S(1)} %get-tuple-element.51.refs_0_, f32[2,8,128]{2,1,0:T(8,128)S(1)} %get-tuple-element.52.refs_1_.refs_2_.refs_6_, ...), custom_call_target="tpu_custom_call" | custom-call | tf_op jit(solution)/shard_map/pallas_call | solution.py:23
  10.0 0.8 %collective-permute-done.3.refs_3_.refs_4_.refs_5_ = bf16[4,64,128]{2,1,0:T(8,128)(2,1)S(1)} collective-permute-done((bf16[4,64,128]{2,1,0:T(8,128)(2,1)S(1)}, bf16[4,64,128]{2,1,0:T(8,128)(2,1)S(1)}, u32[]{:S(2)}, u32[]{:S(2)}) %collective-permute-start.3) | collective-permute-done | bytes 65568 | tf_op jit(solution)/shard_map/ppermute | solution.py:86
  10.8 0.2 shard_map.101
  10.9 1.4 %collective-permute-start.4 = (bf16[8,64,128]{2,1,0:T(8,128)(2,1)S(1)}, bf16[8,64,128]{2,1,0:T(8,128)(2,1)S(1)}, u32[]{:S(2)}, u32[]{:S(2)}) collective-permute-start(bf16[8,64,128]{2,1,0:T(8,128)(2,1)S(1)} %get-tuple-element.61.refs_9_.refs_8_.refs_0_), channel_id=1, source_target_pairs={{0,8},{1,9},{2,10},{3,11},{4,12},{5,13},{6,14},{7,15},{8,0},{9,1},... | collective-permute-start | bytes 393224 | tf_op jit(solution)/shard_map/ppermute | solution.py:86
  12.3 1.3 %collective-permute-start.5 = (bf16[4,64,128]{2,1,0:T(8,128)(2,1)S(1)}, bf16[4,64,128]{2,1,0:T(8,128)(2,1)S(1)}, u32[]{:S(2)}, u32[]{:S(2)}) collective-permute-start(bf16[4,64,128]{2,1,0:T(8,128)(2,1)S(1)} %get-tuple-element.62), channel_id=1, source_target_pairs={{0,12},{1,13},{2,14},{3,15},{4,8},{5,9},{6,10},{7,11},{8,4},{9,5},... | collective-permute-start | bytes 196616 | tf_op jit(solution)/shard_map/ppermute | solution.py:86
  13.6 2.1 %collective-permute-start.7 = (bf16[2,64,128]{2,1,0:T(8,128)(2,1)S(1)}, bf16[2,64,128]{2,1,0:T(8,128)(2,1)S(1)}, u32[]{:S(2)}, u32[]{:S(2)}) collective-permute-start(bf16[2,64,128]{2,1,0:T(8,128)(2,1)S(1)} %shard_map.102), channel_id=1, source_target_pairs={{0,15},{1,10},{2,9},{3,12},{4,11},{5,14},{6,13},{7,8},{8,7},{9,2},... | collective-permute-start | bytes 98312 | tf_op jit(solution)/shard_map/ppermute | solution.py:86
  15.7 0.9 %collective-permute-start.9 = (bf16[4,64,128]{2,1,0:T(8,128)(2,1)S(1)}, bf16[4,64,128]{2,1,0:T(8,128)(2,1)S(1)}, u32[]{:S(2)}, u32[]{:S(2)}) collective-permute-start(bf16[4,64,128]{2,1,0:T(8,128)(2,1)S(1)} %get-tuple-element.66), channel_id=1, source_target_pairs={{0,4},{1,5},{2,6},{3,7},{4,0},{5,1},{6,2},{7,3},{8,12},{9,13},{10,... | collective-permute-start | bytes 196616 | tf_op jit(solution)/shard_map/ppermute | solution.py:86
  16.6 1.0 %collective-permute-start.10 = (bf16[4,64,128]{2,1,0:T(8,128)(2,1)S(1)}, bf16[4,64,128]{2,1,0:T(8,128)(2,1)S(1)}, u32[]{:S(2)}, u32[]{:S(2)}) collective-permute-start(bf16[4,64,128]{2,1,0:T(8,128)(2,1)S(1)} %get-tuple-element.67), channel_id=1, source_target_pairs={{0,7},{1,2},{2,1},{3,4},{4,3},{5,6},{6,5},{7,0},{8,15},{9,10},{10,... | collective-permute-start | bytes 196616 | tf_op jit(solution)/shard_map/ppermute | solution.py:86
  17.6 1.7 %collective-permute-done.7.refs_6_ = bf16[2,64,128]{2,1,0:T(8,128)(2,1)S(1)} collective-permute-done((bf16[2,64,128]{2,1,0:T(8,128)(2,1)S(1)}, bf16[2,64,128]{2,1,0:T(8,128)(2,1)S(1)}, u32[]{:S(2)}, u32[]{:S(2)}) %collective-permute-start.7) | collective-permute-done | bytes 32800 | tf_op jit(solution)/shard_map/ppermute | solution.py:86
  19.4 0.1 collective-permute-start.8
  19.5 1.0 %collective-permute-done.9.refs_5_.refs_2_ = bf16[4,64,128]{2,1,0:T(8,128)(2,1)S(1)} collective-permute-done((bf16[4,64,128]{2,1,0:T(8,128)(2,1)S(1)}, bf16[4,64,128]{2,1,0:T(8,128)(2,1)S(1)}, u32[]{:S(2)}, u32[]{:S(2)}) %collective-permute-start.9) | collective-permute-done | bytes 65568 | tf_op jit(solution)/shard_map/ppermute | solution.py:86
  20.4 0.8 %collective-permute-done.10.refs_6_.refs_3_ = bf16[4,64,128]{2,1,0:T(8,128)(2,1)S(1)} collective-permute-done((bf16[4,64,128]{2,1,0:T(8,128)(2,1)S(1)}, bf16[4,64,128]{2,1,0:T(8,128)(2,1)S(1)}, u32[]{:S(2)}, u32[]{:S(2)}) %collective-permute-start.10) | collective-permute-done | bytes 65568 | tf_op jit(solution)/shard_map/ppermute | solution.py:86
  21.3 0.5 %collective-permute-start.13 = (bf16[2,64,128]{2,1,0:T(8,128)(2,1)S(1)}, bf16[2,64,128]{2,1,0:T(8,128)(2,1)S(1)}, u32[]{:S(2)}, u32[]{:S(2)}) collective-permute-start(bf16[2,64,128]{2,1,0:T(8,128)(2,1)S(1)} %get-tuple-element.75), channel_id=1, source_target_pairs={{0,1},{1,0},{2,3},{3,2},{4,5},{5,4},{6,7},{7,6},{8,9},{9,8},{10,11... | collective-permute-start | bytes 98312 | tf_op jit(solution)/shard_map/ppermute | solution.py:86
  21.8 0.1 collective-permute-start.12
  21.8 0.8 %collective-permute-done.13.refs_1_ = bf16[2,64,128]{2,1,0:T(8,128)(2,1)S(1)} collective-permute-done((bf16[2,64,128]{2,1,0:T(8,128)(2,1)S(1)}, bf16[2,64,128]{2,1,0:T(8,128)(2,1)S(1)}, u32[]{:S(2)}, u32[]{:S(2)}) %collective-permute-start.13) | collective-permute-done | bytes 32800 | tf_op jit(solution)/shard_map/ppermute | solution.py:86
  22.7 0.3 collective-permute-start.14
  23.0 0.9 %collective-permute-done.14.refs_6_ = bf16[2,64,128]{2,1,0:T(8,128)(2,1)S(1)} collective-permute-done((bf16[2,64,128]{2,1,0:T(8,128)(2,1)S(1)}, bf16[2,64,128]{2,1,0:T(8,128)(2,1)S(1)}, u32[]{:S(2)}, u32[]{:S(2)}) %collective-permute-start.14) | collective-permute-done | bytes 32800 | tf_op jit(solution)/shard_map/ppermute | solution.py:86
  23.9 0.4 collective-permute-start.15
  24.3 1.0 %collective-permute-done.15.refs_3_.refs_4_.refs_5_.refs_7_ = bf16[5,64,128]{2,1,0:T(8,128)(2,1)S(1)} collective-permute-done((bf16[5,64,128]{2,1,0:T(8,128)(2,1)S(1)}, bf16[5,64,128]{2,1,0:T(8,128)(2,1)S(1)}, u32[]{:S(2)}, u32[]{:S(2)}) %collective-permute-start.15) | collective-permute-done | bytes 81952 | tf_op jit(solution)/shard_map/ppermute | solution.py:86
  25.2 8.1 %collective-permute-start.16 = (bf16[8,64,128]{2,1,0:T(8,128)(2,1)S(1)}, bf16[8,64,128]{2,1,0:T(8,128)(2,1)S(1)}, u32[]{:S(2)}, u32[]{:S(2)}) collective-permute-start(bf16[8,64,128]{2,1,0:T(8,128)(2,1)S(1)} %get-tuple-element.81.refs_11_.other_ref.refs_2_), channel_id=1, source_target_pairs={{0,8},{1,9},{2,10},{3,11},{4,12},{5,13},{6,14},{7,15},{8,0},{9,1},... | collective-permute-start | bytes 393224 | tf_op jit(solution)/shard_map/ppermute | solution.py:86
  33.4 0.0 collective-permute-start.18
  33.4 0.7 %collective-permute-start.17 = (bf16[4,64,128]{2,1,0:T(8,128)(2,1)S(1)}, bf16[4,64,128]{2,1,0:T(8,128)(2,1)S(1)}, u32[]{:S(2)}, u32[]{:S(2)}) collective-permute-start(bf16[4,64,128]{2,1,0:T(8,128)(2,1)S(1)} %get-tuple-element.82), channel_id=1, source_target_pairs={{0,12},{1,13},{2,14},{3,15},{4,8},{5,9},{6,10},{7,11},{8,4},{9,5},... | collective-permute-start | bytes 196616 | tf_op jit(solution)/shard_map/ppermute | solution.py:86
  34.1 0.5 collective-permute-done.18.refs_1_
  34.6 1.5 %collective-permute-start.19 = (bf16[2,64,128]{2,1,0:T(8,128)(2,1)S(1)}, bf16[2,64,128]{2,1,0:T(8,128)(2,1)S(1)}, u32[]{:S(2)}, u32[]{:S(2)}) collective-permute-start(bf16[2,64,128]{2,1,0:T(8,128)(2,1)S(1)} %shard_map.112), channel_id=1, source_target_pairs={{0,15},{1,10},{2,9},{3,12},{4,11},{5,14},{6,13},{7,8},{8,7},{9,2},... | collective-permute-start | bytes 98312 | tf_op jit(solution)/shard_map/ppermute | solution.py:86
  36.1 0.9 %collective-permute-start.21 = (f32[128,128]{1,0:T(8,128)S(1)}, f32[128,128]{1,0:T(8,128)S(1)}, u32[]{:S(2)}, u32[]{:S(2)}) collective-permute-start(f32[128,128]{1,0:T(8,128)S(1)} %shard_map.115), channel_id=1, source_target_pairs={{0,8},{1,9},{2,10},{3,11},{4,12},{5,13},{6,14},{7,15},{8,0},{9,1},... | collective-permute-start | bytes 196616 | tf_op jit(solution)/shard_map/ppermute | solution.py:86
  36.9 2.4 %collective-permute-done.17.refs_5_ = bf16[4,64,128]{2,1,0:T(8,128)(2,1)S(1)} collective-permute-done((bf16[4,64,128]{2,1,0:T(8,128)(2,1)S(1)}, bf16[4,64,128]{2,1,0:T(8,128)(2,1)S(1)}, u32[]{:S(2)}, u32[]{:S(2)}) %collective-permute-start.17) | collective-permute-done | bytes 65568 | tf_op jit(solution)/shard_map/ppermute | solution.py:86
  39.4 0.5 collective-permute-done.19.refs_6_
  39.9 0.1 collective-permute-start.20
  40.0 0.5 %shard_map.114 = (f32[8,64,128]{2,1,0:T(8,128)S(1)}, bf16[8,64,128]{2,1,0:T(8,128)(2,1)S(1)}, f32[8,128]{1,0:T(8,128)S(1)}) custom-call(bf16[2,8,64,128]{3,2,1,0:T(8,128)(2,1)S(1)} %get-tuple-element.51.refs_0_, f32[2,8,128]{2,1,0:T(8,128)S(1)} %get-tuple-element.52.refs_1_.refs_2_.refs_6_, bf16[4,64,128]{2,1,0:T(8,128)(2,1)S(1)} %collective-permute-done.9.refs_5_.refs_2_, ...), custom_call_target="tpu_custom_call" | custom-call | tf_op jit(solution)/shard_map/pallas_call | solution.py:23
  40.5 0.3 collective-permute-done.21.refs_5_.beside_ref
  40.8 0.4 collective-permute-done.20.refs_4_
  41.2 0.2 shard_map.116
  41.4 2.5 %collective-permute-start.22 = (f32[2,8,128]{2,1,0:T(8,128)S(1)}, f32[2,8,128]{2,1,0:T(8,128)S(1)}, u32[]{:S(2)}, u32[]{:S(2)}) collective-permute-start(f32[2,8,128]{2,1,0:T(8,128)S(1)} %shard_map.118), channel_id=1, source_target_pairs={{0,24},{1,25},{2,26},{3,27},{4,28},{5,29},{6,30},{7,31},{8,16},{9,... | collective-permute-start | bytes 24584 | tf_op jit(solution)/shard_map/ppermute | solution.py:86
  44.0 0.3 collective-permute-start.24
  44.2 1.6 %collective-permute-start.23 = (f32[8,128]{1,0:T(8,128)S(1)}, f32[8,128]{1,0:T(8,128)S(1)}, u32[]{:S(2)}, u32[]{:S(2)}) collective-permute-start(f32[8,128]{1,0:T(8,128)S(1)} %get-tuple-element.91.own_ref), channel_id=1, source_target_pairs={{0,8},{1,9},{2,10},{3,11},{4,12},{5,13},{6,14},{7,15},{8,0},{9,1},... | collective-permute-start | bytes 12296 | tf_op jit(solution)/shard_map/ppermute | solution.py:86
  45.9 0.8 %shard_map.117 = (bf16[64,8,128]{2,1,0:T(8,128)(2,1)}, bf16[64,8,128]{2,1,0:T(8,128)(2,1)}) custom-call(bf16[8,64,128]{2,1,0:T(8,128)(2,1)S(1)} %get-tuple-element.61.refs_9_.refs_8_.refs_0_, bf16[8,64,128]{2,1,0:T(8,128)(2,1)S(1)} %get-tuple-element.72.refs_10_.one_ref.refs_1_, bf16[8,64,128]{2,1,0:T(8,128)(2,1)S(1)} %get-tuple-element.81.refs_11_.other_ref.refs_2_, ...), custom_call_target="tpu_custom_call" | custom-call | tf_op jit(solution)/shard_map/pallas_call | solution.py:23
  46.7 0.2 collective-permute-done.22.across_ref
  46.9 0.6 %shard_map.119.ends_ref = f32[4,2,4,128]{3,2,1,0:T(4,128)} custom-call(f32[8,128]{1,0:T(8,128)S(1)} %get-tuple-element.91.own_ref, f32[128,128]{1,0:T(8,128)S(1)} %collective-permute-done.21.refs_5_.beside_ref, f32[2,8,128]{2,1,0:T(8,128)S(1)} %collective-permute-done.22.across_ref, f32[4,4,8,128]{3,2,1,0:T(8,128)S(1)} %get-tuple-element.92.member_ref), custom_call_target="tpu_custom_call" | custom-call | tf_op jit(solution)/shard_map/pallas_call | solution.py:23
  47.5 0.9 %collective-permute-done.24.other_ref = f32[8,128]{1,0:T(8,128)S(1)} collective-permute-done((f32[8,128]{1,0:T(8,128)S(1)}, f32[8,128]{1,0:T(8,128)S(1)}, u32[]{:S(2)}, u32[]{:S(2)}) %collective-permute-start.24) | collective-permute-done | bytes 4128 | tf_op jit(solution)/shard_map/ppermute | solution.py:86
  (29 shorter events, 0.1 us)
Async XLA Ops:
  1.7 3.3 %collective-permute-start = (bf16[2,2,64,128]{3,2,1,0:T(8,128)(2,1)S(1)}, bf16[2,2,64,128]{3,2,1,0:T(8,128)(2,1)S(1)}, u32[]{:S(2)}, u32[]{:S(2)}) collective-permute-start(bf16[2,2,64,128]{3,2,1,0:T(8,128)(2,1)S(1)} %get-tuple-element.50), channel_id=1, source_target_pairs={{0,1},{1,0},{2,3},{3,2},{4,5},{5,4},{6,7},{7,6},{8,9},{9,8},{10,11... | collective-permute-start | bytes 196616 | tf_op jit(solution)/shard_map/ppermute | solution.py:86
  2.5 6.1 %collective-permute-start.1 = (bf16[4,64,128]{2,1,0:T(8,128)(2,1)S(1)}, bf16[4,64,128]{2,1,0:T(8,128)(2,1)S(1)}, u32[]{:S(2)}, u32[]{:S(2)}) collective-permute-start(bf16[4,64,128]{2,1,0:T(8,128)(2,1)S(1)} %get-tuple-element.53), channel_id=1, source_target_pairs={{0,4},{1,5},{2,6},{3,7},{4,0},{5,1},{6,2},{7,3},{8,12},{9,13},{10,... | collective-permute-start | bytes 196616 | tf_op jit(solution)/shard_map/ppermute | solution.py:86
  5.1 4.4 %collective-permute-start.2 = (bf16[2,64,128]{2,1,0:T(8,128)(2,1)S(1)}, bf16[2,64,128]{2,1,0:T(8,128)(2,1)S(1)}, u32[]{:S(2)}, u32[]{:S(2)}) collective-permute-start(bf16[2,64,128]{2,1,0:T(8,128)(2,1)S(1)} %shard_map.97), channel_id=1, source_target_pairs={{0,7},{1,2},{2,1},{3,4},{4,3},{5,6},{6,5},{7,0},{8,15},{9,10},{10,... | collective-permute-start | bytes 98312 | tf_op jit(solution)/shard_map/ppermute | solution.py:86
  9.5 1.3 %collective-permute-start.3 = (bf16[4,64,128]{2,1,0:T(8,128)(2,1)S(1)}, bf16[4,64,128]{2,1,0:T(8,128)(2,1)S(1)}, u32[]{:S(2)}, u32[]{:S(2)}) collective-permute-start(bf16[4,64,128]{2,1,0:T(8,128)(2,1)S(1)} %shard_map.98.refs_4_), channel_id=1, source_target_pairs={{0,1},{1,0},{2,3},{3,2},{4,5},{5,4},{6,7},{7,6},{8,9},{9,8},{10,11... | collective-permute-start | bytes 196616 | tf_op jit(solution)/shard_map/ppermute | solution.py:86
  10.9 8.4 %collective-permute-start.4 = (bf16[8,64,128]{2,1,0:T(8,128)(2,1)S(1)}, bf16[8,64,128]{2,1,0:T(8,128)(2,1)S(1)}, u32[]{:S(2)}, u32[]{:S(2)}) collective-permute-start(bf16[8,64,128]{2,1,0:T(8,128)(2,1)S(1)} %get-tuple-element.61.refs_9_.refs_8_.refs_0_), channel_id=1, source_target_pairs={{0,8},{1,9},{2,10},{3,11},{4,12},{5,13},{6,14},{7,15},{8,0},{9,1},... | collective-permute-start | bytes 393224 | tf_op jit(solution)/shard_map/ppermute | solution.py:86
  12.3 1.3 %collective-permute-start.6 = (bf16[2,64,128]{2,1,0:T(8,128)(2,1)S(1)}, bf16[2,64,128]{2,1,0:T(8,128)(2,1)S(1)}, u32[]{:S(2)}, u32[]{:S(2)}) collective-permute-start(bf16[2,64,128]{2,1,0:T(8,128)(2,1)S(1)} %get-tuple-element.64), channel_id=1, source_target_pairs={{0,1},{1,0},{2,3},{3,2},{4,5},{5,4},{6,7},{7,6},{8,9},{9,8},{10,11... | collective-permute-start | bytes 98312 | tf_op jit(solution)/shard_map/ppermute | solution.py:86
  12.3 7.0 %collective-permute-start.5 = (bf16[4,64,128]{2,1,0:T(8,128)(2,1)S(1)}, bf16[4,64,128]{2,1,0:T(8,128)(2,1)S(1)}, u32[]{:S(2)}, u32[]{:S(2)}) collective-permute-start(bf16[4,64,128]{2,1,0:T(8,128)(2,1)S(1)} %get-tuple-element.62), channel_id=1, source_target_pairs={{0,12},{1,13},{2,14},{3,15},{4,8},{5,9},{6,10},{7,11},{8,4},{9,5},... | collective-permute-start | bytes 196616 | tf_op jit(solution)/shard_map/ppermute | solution.py:86
  13.6 5.7 %collective-permute-start.7 = (bf16[2,64,128]{2,1,0:T(8,128)(2,1)S(1)}, bf16[2,64,128]{2,1,0:T(8,128)(2,1)S(1)}, u32[]{:S(2)}, u32[]{:S(2)}) collective-permute-start(bf16[2,64,128]{2,1,0:T(8,128)(2,1)S(1)} %shard_map.102), channel_id=1, source_target_pairs={{0,15},{1,10},{2,9},{3,12},{4,11},{5,14},{6,13},{7,8},{8,7},{9,2},... | collective-permute-start | bytes 98312 | tf_op jit(solution)/shard_map/ppermute | solution.py:86
  15.7 4.8 %collective-permute-start.9 = (bf16[4,64,128]{2,1,0:T(8,128)(2,1)S(1)}, bf16[4,64,128]{2,1,0:T(8,128)(2,1)S(1)}, u32[]{:S(2)}, u32[]{:S(2)}) collective-permute-start(bf16[4,64,128]{2,1,0:T(8,128)(2,1)S(1)} %get-tuple-element.66), channel_id=1, source_target_pairs={{0,4},{1,5},{2,6},{3,7},{4,0},{5,1},{6,2},{7,3},{8,12},{9,13},{10,... | collective-permute-start | bytes 196616 | tf_op jit(solution)/shard_map/ppermute | solution.py:86
  16.6 4.6 %collective-permute-start.10 = (bf16[4,64,128]{2,1,0:T(8,128)(2,1)S(1)}, bf16[4,64,128]{2,1,0:T(8,128)(2,1)S(1)}, u32[]{:S(2)}, u32[]{:S(2)}) collective-permute-start(bf16[4,64,128]{2,1,0:T(8,128)(2,1)S(1)} %get-tuple-element.67), channel_id=1, source_target_pairs={{0,7},{1,2},{2,1},{3,4},{4,3},{5,6},{6,5},{7,0},{8,15},{9,10},{10,... | collective-permute-start | bytes 196616 | tf_op jit(solution)/shard_map/ppermute | solution.py:86
  19.4 1.9 %collective-permute-start.8 = (bf16[4,64,128]{2,1,0:T(8,128)(2,1)S(1)}, bf16[4,64,128]{2,1,0:T(8,128)(2,1)S(1)}, u32[]{:S(2)}, u32[]{:S(2)}) collective-permute-start(bf16[4,64,128]{2,1,0:T(8,128)(2,1)S(1)} %shard_map.103.refs_7_), channel_id=1, source_target_pairs={{0,1},{1,0},{2,3},{3,2},{4,5},{5,4},{6,7},{7,6},{8,9},{9,8},{10,11... | collective-permute-start | bytes 196616 | tf_op jit(solution)/shard_map/ppermute | solution.py:86
  21.3 2.6 %collective-permute-start.11 = (bf16[8,64,128]{2,1,0:T(8,128)(2,1)S(1)}, bf16[8,64,128]{2,1,0:T(8,128)(2,1)S(1)}, u32[]{:S(2)}, u32[]{:S(2)}) collective-permute-start(bf16[8,64,128]{2,1,0:T(8,128)(2,1)S(1)} %get-tuple-element.72.refs_10_.one_ref.refs_1_), channel_id=1, source_target_pairs={{0,1},{1,0},{2,3},{3,2},{4,5},{5,4},{6,7},{7,6},{8,16},{9,17},{10,... | collective-permute-start | bytes 393224 | tf_op jit(solution)/shard_map/ppermute | solution.py:86
  21.3 1.4 %collective-permute-start.13 = (bf16[2,64,128]{2,1,0:T(8,128)(2,1)S(1)}, bf16[2,64,128]{2,1,0:T(8,128)(2,1)S(1)}, u32[]{:S(2)}, u32[]{:S(2)}) collective-permute-start(bf16[2,64,128]{2,1,0:T(8,128)(2,1)S(1)} %get-tuple-element.75), channel_id=1, source_target_pairs={{0,1},{1,0},{2,3},{3,2},{4,5},{5,4},{6,7},{7,6},{8,9},{9,8},{10,11... | collective-permute-start | bytes 98312 | tf_op jit(solution)/shard_map/ppermute | solution.py:86
  21.8 2.1 %collective-permute-start.12 = (bf16[4,64,128]{2,1,0:T(8,128)(2,1)S(1)}, bf16[4,64,128]{2,1,0:T(8,128)(2,1)S(1)}, u32[]{:S(2)}, u32[]{:S(2)}) collective-permute-start(bf16[4,64,128]{2,1,0:T(8,128)(2,1)S(1)} %get-tuple-element.73), channel_id=1, source_target_pairs={{0,1},{1,0},{2,3},{3,2},{4,5},{5,4},{6,7},{7,6},{8,20},{9,21},{10,... | collective-permute-start | bytes 196616 | tf_op jit(solution)/shard_map/ppermute | solution.py:86
  22.7 1.2 %collective-permute-start.14 = (bf16[2,64,128]{2,1,0:T(8,128)(2,1)S(1)}, bf16[2,64,128]{2,1,0:T(8,128)(2,1)S(1)}, u32[]{:S(2)}, u32[]{:S(2)}) collective-permute-start(bf16[2,64,128]{2,1,0:T(8,128)(2,1)S(1)} %shard_map.107), channel_id=1, source_target_pairs={{0,1},{1,0},{2,3},{3,2},{4,5},{5,4},{6,7},{7,6},{8,23},{9,18},{10,... | collective-permute-start | bytes 98312 | tf_op jit(solution)/shard_map/ppermute | solution.py:86
  23.9 1.3 %collective-permute-start.15 = (bf16[5,64,128]{2,1,0:T(8,128)(2,1)S(1)}, bf16[5,64,128]{2,1,0:T(8,128)(2,1)S(1)}, u32[]{:S(2)}, u32[]{:S(2)}) collective-permute-start(bf16[5,64,128]{2,1,0:T(8,128)(2,1)S(1)} %shard_map.108.refs_7_), channel_id=1, source_target_pairs={{0,1},{1,0},{2,3},{3,2},{4,5},{5,4},{6,7},{7,6},{8,9},{9,8},{10,11... | collective-permute-start | bytes 245768 | tf_op jit(solution)/shard_map/ppermute | solution.py:86
  25.2 14.6 %collective-permute-start.16 = (bf16[8,64,128]{2,1,0:T(8,128)(2,1)S(1)}, bf16[8,64,128]{2,1,0:T(8,128)(2,1)S(1)}, u32[]{:S(2)}, u32[]{:S(2)}) collective-permute-start(bf16[8,64,128]{2,1,0:T(8,128)(2,1)S(1)} %get-tuple-element.81.refs_11_.other_ref.refs_2_), channel_id=1, source_target_pairs={{0,8},{1,9},{2,10},{3,11},{4,12},{5,13},{6,14},{7,15},{8,0},{9,1},... | collective-permute-start | bytes 393224 | tf_op jit(solution)/shard_map/ppermute | solution.py:86
  33.4 1.2 %collective-permute-start.18 = (bf16[2,64,128]{2,1,0:T(8,128)(2,1)S(1)}, bf16[2,64,128]{2,1,0:T(8,128)(2,1)S(1)}, u32[]{:S(2)}, u32[]{:S(2)}) collective-permute-start(bf16[2,64,128]{2,1,0:T(8,128)(2,1)S(1)} %get-tuple-element.84), channel_id=1, source_target_pairs={{0,1},{1,0},{2,3},{3,2},{4,5},{5,4},{6,7},{7,6},{8,9},{9,8},{10,11... | collective-permute-start | bytes 98312 | tf_op jit(solution)/shard_map/ppermute | solution.py:86
  33.4 6.0 %collective-permute-start.17 = (bf16[4,64,128]{2,1,0:T(8,128)(2,1)S(1)}, bf16[4,64,128]{2,1,0:T(8,128)(2,1)S(1)}, u32[]{:S(2)}, u32[]{:S(2)}) collective-permute-start(bf16[4,64,128]{2,1,0:T(8,128)(2,1)S(1)} %get-tuple-element.82), channel_id=1, source_target_pairs={{0,12},{1,13},{2,14},{3,15},{4,8},{5,9},{6,10},{7,11},{8,4},{9,5},... | collective-permute-start | bytes 196616 | tf_op jit(solution)/shard_map/ppermute | solution.py:86
  34.6 5.3 %collective-permute-start.19 = (bf16[2,64,128]{2,1,0:T(8,128)(2,1)S(1)}, bf16[2,64,128]{2,1,0:T(8,128)(2,1)S(1)}, u32[]{:S(2)}, u32[]{:S(2)}) collective-permute-start(bf16[2,64,128]{2,1,0:T(8,128)(2,1)S(1)} %shard_map.112), channel_id=1, source_target_pairs={{0,15},{1,10},{2,9},{3,12},{4,11},{5,14},{6,13},{7,8},{8,7},{9,2},... | collective-permute-start | bytes 98312 | tf_op jit(solution)/shard_map/ppermute | solution.py:86
  36.1 4.8 %collective-permute-start.21 = (f32[128,128]{1,0:T(8,128)S(1)}, f32[128,128]{1,0:T(8,128)S(1)}, u32[]{:S(2)}, u32[]{:S(2)}) collective-permute-start(f32[128,128]{1,0:T(8,128)S(1)} %shard_map.115), channel_id=1, source_target_pairs={{0,8},{1,9},{2,10},{3,11},{4,12},{5,13},{6,14},{7,15},{8,0},{9,1},... | collective-permute-start | bytes 196616 | tf_op jit(solution)/shard_map/ppermute | solution.py:86
  39.9 1.3 %collective-permute-start.20 = (bf16[4,64,128]{2,1,0:T(8,128)(2,1)S(1)}, bf16[4,64,128]{2,1,0:T(8,128)(2,1)S(1)}, u32[]{:S(2)}, u32[]{:S(2)}) collective-permute-start(bf16[4,64,128]{2,1,0:T(8,128)(2,1)S(1)} %shard_map.113.refs_7_), channel_id=1, source_target_pairs={{0,1},{1,0},{2,3},{3,2},{4,5},{5,4},{6,7},{7,6},{8,9},{9,8},{10,11... | collective-permute-start | bytes 196616 | tf_op jit(solution)/shard_map/ppermute | solution.py:86
  41.4 5.5 %collective-permute-start.22 = (f32[2,8,128]{2,1,0:T(8,128)S(1)}, f32[2,8,128]{2,1,0:T(8,128)S(1)}, u32[]{:S(2)}, u32[]{:S(2)}) collective-permute-start(f32[2,8,128]{2,1,0:T(8,128)S(1)} %shard_map.118), channel_id=1, source_target_pairs={{0,24},{1,25},{2,26},{3,27},{4,28},{5,29},{6,30},{7,31},{8,16},{9,... | collective-permute-start | bytes 24584 | tf_op jit(solution)/shard_map/ppermute | solution.py:86
  44.0 4.5 %collective-permute-start.24 = (f32[8,128]{1,0:T(8,128)S(1)}, f32[8,128]{1,0:T(8,128)S(1)}, u32[]{:S(2)}, u32[]{:S(2)}) collective-permute-start(f32[8,128]{1,0:T(8,128)S(1)} %get-tuple-element.91.own_ref), channel_id=1, source_target_pairs={{0,16},{1,17},{2,18},{3,19},{4,20},{5,21},{6,22},{7,23},{8,24},{9,... | collective-permute-start | bytes 12296 | tf_op jit(solution)/shard_map/ppermute | solution.py:86
  44.2 4.2 %collective-permute-start.23 = (f32[8,128]{1,0:T(8,128)S(1)}, f32[8,128]{1,0:T(8,128)S(1)}, u32[]{:S(2)}, u32[]{:S(2)}) collective-permute-start(f32[8,128]{1,0:T(8,128)S(1)} %get-tuple-element.91.own_ref), channel_id=1, source_target_pairs={{0,8},{1,9},{2,10},{3,11},{4,12},{5,13},{6,14},{7,15},{8,0},{9,1},... | collective-permute-start | bytes 12296 | tf_op jit(solution)/shard_map/ppermute | solution.py:86

commit v7 on v6

--- a/solution.py
+++ b/solution.py
@@ -68,7 +68,7 @@
     tiles = tiles_x * tiles_y
     groups = coupling.shape[0]
     layers, rows, cols = (lax.axis_size(axis) for axis in AXES)
-    if cols != 4 or layers % 2 or rows % 2:
+    if cols != 4 or layers % 2 or layers < 4 or rows % 2:
         raise ValueError("unsupported mesh")
     row_pairs = pairings(rows)
     halos = len(row_pairs)
@@ -216,8 +216,8 @@
 
     def setup_kernel(pattern_hbm, coupling_hbm, group_hbm, blocks_hbm, *refs):
         take = taker(refs)
-        flat_ref, cells_ref, corner_ref, source_ref, front_ref, kappa_ref, member_ref = (take() for _ in range(7))
-        late_refs, carried_refs = take(halos), take(halos)
+        flat_ref, cells_ref, source_ref, front_ref, kappa_ref, member_ref = (take() for _ in range(6))
+        late_refs, late_column_ref, late_corner_refs = take(halos), take(), take(halos)
         pattern_ref, coupling_ref, group_ref, blocks_ref, sems, block_sems = (take() for _ in range(6))
         scalars = [
             pltpu.make_async_copy(src, dst, sems.at[i])
@@ -237,15 +237,11 @@
         for pairing, rim_ref in zip(row_pairs, late_refs):
             row = Side(pairing, "row", tiles_x).edge
             rim_ref[...] = source_ref[1, pl.ds(row * tiles_y, tiles_y)]
-        beyond = Side(far, "col", tiles_y)
-        for h, carried_ref in enumerate(carried_refs):
-            for x in range(tiles_x):
-                carried_ref[x] = source_ref[1, x * tiles_y + beyond.edge]
-
-            @pl.when(jnp.logical_not(beyond.real))
-            def _(h=h, carried_ref=carried_ref):
-                carried_ref[0] = corner_ref[h, 1]
-
+        edge = Side(far, "col", tiles_y).edge
+        for x in range(tiles_x):
+            late_column_ref[x] = source_ref[1, x * tiles_y + edge]
+        for pairing, corner_ref in zip(row_pairs, late_corner_refs):
+            corner_ref[0] = source_ref[1, Side(pairing, "row", tiles_x).edge * tiles_y + edge]
         for copy in scalars:
             copy.wait()
         for t in range(tiles):
@@ -272,14 +268,13 @@
             ((groups, layers, tiles, cells), f32),
         ]
         + [((tiles_y, *tile), bf16)] * halos
-        + [((max(tiles_x, tiles_y), *tile), bf16)] * halos,
+        + [((max(tiles_x, tiles_y), *tile), bf16)] * (halos + 1),
         pattern[0],
         coupling,
         layer_group,
         blocks.reshape(tiles, OFFSETS, cells, cells),
         flat,
         port_row,
-        corner,
         far_args=4,
         scratch=[
             pltpu.SMEM(pattern.shape[1:], jnp.int32),
@@ -291,10 +286,21 @@
         ],
     )
 
-    late = [
-        to_layer(None, beside(pairing))(part)
-        for part, (beside, pairing) in zip(late, [(b, p) for b in (other_row, other_chip) for p in row_pairs])
+    late_rims, late_sides = late[:halos], late[halos:]
+    late_rims = [to_layer(None, other_row(pairing))(part) for part, pairing in zip(late_rims, row_pairs)]
+
+    def inner_only(beside, pairing):
+        def target(l, r, c):
+            return (l, *beside(r, c)) if abs(far(c, cols) - c) == 1 else (l, pairing(r, rows), c)
+
+        return target
+
+    late_corners = [
+        permuted(part, inner_only(lambda r, c, pairing=pairing: (pairing(r, rows), far(c, cols)), pairing))
+        for part, pairing in zip(late_sides[1:], row_pairs)
     ]
+    late_sides = [permuted(late_sides[0], inner_only(lambda r, c: (r, far(c, cols)), near))] + late_corners
+    turn = layers // 2
 
     def waves(phase, kappa_ref):
         def wave(base, field=None, real=None):
@@ -309,7 +315,8 @@
         return [Side(pairing, "row", tiles_x).real for pairing in row_pairs]
 
     def step_inputs(step, take):
-        source_ref, kappa_ref, rim_refs, column_refs = take(), take(), take(halos), take(halos)
+        source_ref, kappa_ref, rim_refs = take(), take(), take(halos)
+        column_refs = take(halos if step < turn else 0 if step == turn else 1)
         if step == 0:
             return source_ref, kappa_ref, rim_refs, column_refs, None, [None] * halos, column_refs
         return source_ref, kappa_ref, rim_refs, column_refs, take(), take(halos), take(halos)
@@ -321,8 +328,6 @@
         core_ref = take()
         for h in range(halos):
             core_ref[ext + h] = carried[h][0]
-            if step == layers // 2:
-                core_ref[ext + halos + h] = column_refs[h][0]
 
         @pl.when(is_active(step))
         def _():
@@ -355,17 +360,21 @@
         t = side.edge * tiles_y + across.edge
         return t, product(corner, front_ref[t, 3 * (side.step + 1) + 1 + across.step])
 
-    def early_tiles():
+    def early_tiles(step):
         edge = Side(far, "col", tiles_y).edge
         inside = [(x, y) for x in range(tiles_x) for y in range(1, tiles_y - 1)]
+        if step == turn:
+            return inside
         if halos > 1:
             return inside + [(x, edge) for x in range(1, tiles_x - 1)]
         low = jnp.where(Side(near, "row", tiles_x).edge == 0, 1, 0)
         return inside + [(low + i, edge) for i in range(tiles_x - 1)]
 
-    def late_tiles():
+    def late_tiles(step):
         beside, beyond = (Side(pairing, "col", tiles_y).edge for pairing in (near, far))
         corners = [(Side(pairing, "row", tiles_x).edge, beyond) for pairing in row_pairs]
+        if step == turn:
+            corners = [(x, beyond) for x in range(tiles_x)]
         return [(x, beside) for x in range(tiles_x)] + corners
 
     def add_parts(some, one_ref, other_ref, part_ref):
@@ -390,7 +399,8 @@
                 for y in range(tiles_y):
                     t = x * tiles_y + y
                     wave_ref[x, y] = wave(source_ref[phase, t], None if step == 0 else field_ref[t])
-                side_ref[x] = wave(column_refs[0][x], None if step == 0 else carried[0][x])
+                if step != turn:
+                    side_ref[x] = wave(column_refs[0][x], None if step == 0 else carried[0][x])
             for h in range(halos):
                 for y in range(tiles_y):
                     wave_ref[tiles_x + h, y] = wave(
@@ -427,8 +437,9 @@
                 for x, total in enumerate(column_products(across, front_ref, side_ref)):
                     sum_ref[x * tiles_y + across.edge] += total
 
-            across.when(beyond)
-            some = early_tiles()
+            if step != turn:
+                across.when(beyond)
+            some = early_tiles(step)
             for x, y in some:
                 out_ref[x * tiles_y + y] = sum_ref[x * tiles_y + y].astype(bf16)
             if last:
@@ -450,32 +461,39 @@
                 def _(k=k):
                     add_parts(whole, earlier[k], earlier[layers - 1 - k], rest[0])
 
-    def add_far_corners(step, sum_ref, front_ref, kappa_ref, core_ref, base_ref):
-        phase = int(step >= layers // 2)
-        wave = waves(phase, kappa_ref)
+    def add_far_corners(step, sum_ref, front_ref, kappa_ref, core_ref, bases, column_ref=None, carried_ref=None):
+        wave = waves(int(step >= turn), kappa_ref)
         real = row_real()
         beyond = Side(far, "col", tiles_y)
 
         def corners():
+            if step == turn:
+                side = [wave(column_ref[x], carried_ref[x]) for x in range(tiles_x)]
+                for x, total in enumerate(column_products(beyond, front_ref, side)):
+                    sum_ref[x * tiles_y + beyond.edge] += total
             for h, pairing in enumerate(row_pairs):
-                base = base_ref[ext + phase * halos + h]
-                corner = wave(base, None if step == 0 else core_ref[ext + h], real[h])
+                corner = wave(bases[h], None if step == 0 else core_ref[ext + h], real[h])
                 t, total = corner_product(beyond, pairing, front_ref, corner)
                 sum_ref[t] += total
 
         beyond.when(corners)
+
+    def corner_bases(step, refs):
+        return [refs[0][ext + h] for h in range(halos)] if step < turn else [ref[0] for ref in refs]
 
     def corner_front_kernel(step, *refs):
         take = taker(refs)
         take()
-        front_ref, kappa_ref, core_ref, base_ref = (take() for _ in range(4))
+        front_ref, kappa_ref, core_ref = take(), take(), take()
+        bases = corner_bases(step, take(1 if step < turn else halos))
+        extra = take(2 if step == turn else 0)
         if step == 1:
-            take(2 * halos)
+            take(halos)
         sum_ref, corner_ref = take(), take()
 
         @pl.when(is_active(step))
         def _():
-            add_far_corners(step, sum_ref, front_ref, kappa_ref, core_ref, base_ref)
+            add_far_corners(step, sum_ref, front_ref, kappa_ref, core_ref, bases, *extra)
             edge = Side(far, "col", tiles_y).edge
             for h, pairing in enumerate(row_pairs):
                 row = Side(pairing, "row", tiles_x).edge
@@ -488,13 +506,14 @@
         front_ref, core_ref = take(), take()
         if last and layers == 4:
             take()
-        kappa_ref, base_ref, first_ref = (take(), take(), take()) if last else (None, None, None)
+        kappa_ref, bases = (take(), corner_bases(step, take(halos))) if last else (None, None)
+        first_ref = take() if last else None
         sum_ref, field_ref, rest = take(), take(), take(1 if last else halos + 1)
 
         @pl.when(is_active(step))
         def _():
             if last:
-                add_far_corners(step, sum_ref, front_ref, kappa_ref, core_ref, base_ref)
+                add_far_corners(step, sum_ref, front_ref, kappa_ref, core_ref, bases)
             across, beyond = Side(near, "col", tiles_y), Side(far, "col", tiles_y)
             totals = column_products(across, front_ref, core_ref)
             corners = [
@@ -508,16 +527,16 @@
                 for edge, corner in zip(edges, corners):
                     total = total + jnp.where(edge == x, corner, 0.0)
                 field_ref[t] = total.astype(bf16)
-            for edge in edges:
-                t = edge * tiles_y + beyond.edge
-                field_ref[t] = sum_ref[t].astype(bf16)
-            some = late_tiles()
+            some = late_tiles(step)
+            for x, y in some[tiles_x:]:
+                field_ref[x * tiles_y + y] = sum_ref[x * tiles_y + y].astype(bf16)
             if last:
                 add_parts(some, first_ref, field_ref, rest[0])
             else:
+                for x, y in some[tiles_x:]:
+                    rest[halos][x] = field_ref[x * tiles_y + y]
                 for h, pairing in enumerate(row_pairs):
                     row = Side(pairing, "row", tiles_x).edge
-                    rest[halos][row] = field_ref[row * tiles_y + beyond.edge]
                     for edge in (across.edge, beyond.edge):
                         rest[h][edge] = field_ref[row * tiles_y + edge]
 
@@ -532,10 +551,11 @@
     fields, field_arrived = [], []
     for step in range(layers):
         last = step == layers - 1
-        inputs = [source, kappa, *(source_beside if step < layers // 2 else late), *field_arrived]
+        halo = source_beside if step < turn else [*late_rims, *(late_sides[:1] if step > turn else [])]
+        inputs = [source, kappa, *halo, *field_arrived]
         (core_out,) = call(
             functools.partial(core_kernel, step),
-            [((ext + halos * (2 if step == layers // 2 else 1), *tile), bf16)],
+            [((ext + halos, *tile), bf16)],
             *inputs,
         )
         core = to_core(core_out)
@@ -549,8 +569,10 @@
             *(fields if last else []),
             scratch=[pltpu.VMEM((ext, tiles_y, *tile), bf16), pltpu.VMEM((tiles_x, *tile), bf16)],
         )
-        if step in (0, layers // 2):
-            base = core
+        if step == 0:
+            base = [core]
+        elif step == turn:
+            base = late_sides[1:]
         if not last:
             summed, corner = call(
                 functools.partial(corner_front_kernel, step),
@@ -559,8 +581,9 @@
                 front,
                 kappa,
                 core,
-                base,
-                *(late if step == 1 else []),
+                *base,
+                *([late_sides[0], field_arrived[1 + halos]] if step == turn else []),
+                *(late_rims if step == 1 else []),
                 aliases={0: 0},
             )
             corner = to_core(corner)
@@ -572,7 +595,7 @@
             front,
             core,
             *([beside] if last and layers == 4 else []),
-            *([kappa, base, fields[0]] if last else []),
+            *([kappa, *base, fields[0]] if last else []),
             aliases={i: i for i in range(1 + len(partial_out))},
         )
         fields.append(field)

time: 48.6 us -> 48.5 us (level)
  starting transfers between devices: 28.6 us -> 26.5 us
  waiting for transfers between devices: 13 us -> 14.9 us
    ppermute x25 -> x26, starting transfers between devices: 28.6 us -> 26.5 us  [permuted(): return lax.ppermute(array, AXES, pairs)]
    ppermute x25 -> x26, waiting for transfers between devices: 13 us -> 14.9 us  [permuted(): return lax.ppermute(array, AXES, pairs)]
  transfers between devices with their start and end apart: 25 -> 26, of which waited for: 15 -> 14; matrix products, arithmetic and copies ran while one was open for 0% -> 0% of each run, Pallas kernels for 9% -> 10%
where the time goes in v7:
time: 48.5 us; the launch traced here: 48.3 us
  starting transfers between devices  26.5 us (55%)
  waiting for transfers between devices  14.9 us (31%)
  Pallas kernels  6.16 us (13%)
  between operations  0.78 us (2%)
    ppermute x26, starting transfers between devices, permuted(): return lax.ppermute(array, AXES, pairs)  26.5 us
    ppermute x26, waiting for transfers between devices, permuted(): return lax.ppermute(array, AXES, pairs)  14.9 us
    pallas_call x26, Pallas kernels, call(): pl.pallas_call(kernel, out_shape=[jax.ShapeDtypeStruct(shape, dtype) for...  6.15 us
  transfers between devices with their start and end apart: 26, of which 14 were waited for; matrix products, arithmetic and copies ran while one was open for 0% of the time, Pallas kernels for 10%

profile of v7, /device:TPU:0, one launch (start us, length us, event | category | flops | bytes accessed | tf_op | source)
XLA Modules:
  0.0 48.3 jit_solution(17737254181984940418)
XLA Ops:
  0.6 1.1 %shard_map.94 = (f32[2,512,128]{2,1,0:T(8,128)S(1)}, s32[1,64]{1,0:T(1,128)S(1)}, bf16[2,2,64,128]{3,2,1,0:T(8,128)(2,1)S(1)}) custom-call(bf16[64,8,128]{2,1,0:T(8,128)(2,1)} %bitcast.8, bf16[64,8,128]{2,1,0:T(8,128)(2,1)} %bitcast.9, s32[1,64]{1,0:T(1,128)} %bitcast.11), custom_call_target="tpu_custom_call" | custom-call | tf_op jit(solution)/shard_map/pallas_call | solution.py:23
  1.7 0.5 %collective-permute-start.1 = (bf16[2,2,64,128]{3,2,1,0:T(8,128)(2,1)S(1)}, bf16[2,2,64,128]{3,2,1,0:T(8,128)(2,1)S(1)}, u32[]{:S(2)}, u32[]{:S(2)}) collective-permute-start(bf16[2,2,64,128]{3,2,1,0:T(8,128)(2,1)S(1)} %get-tuple-element.55), channel_id=1, source_target_pairs={{0,1},{1,0},{2,3},{3,2},{4,5},{5,4},{6,7},{7,6},{8,9},{9,8},{10,11... | collective-permute-start | bytes 196616 | tf_op jit(solution)/shard_map/ppermute | solution.py:86
  2.3 0.2 shard_map.96
  2.5 2.6 %collective-permute-start = (bf16[4,64,128]{2,1,0:T(8,128)(2,1)S(1)}, bf16[4,64,128]{2,1,0:T(8,128)(2,1)S(1)}, u32[]{:S(2)}, u32[]{:S(2)}) collective-permute-start(bf16[4,64,128]{2,1,0:T(8,128)(2,1)S(1)} %get-tuple-element.53), channel_id=1, source_target_pairs={{0,4},{1,5},{2,6},{3,7},{4,0},{5,1},{6,2},{7,3},{8,12},{9,13},{10,... | collective-permute-start | bytes 196616 | tf_op jit(solution)/shard_map/ppermute | solution.py:86
  5.1 0.0 collective-permute-done.1.refs_1_
  5.1 1.7 %collective-permute-start.2 = (bf16[2,64,128]{2,1,0:T(8,128)(2,1)S(1)}, bf16[2,64,128]{2,1,0:T(8,128)(2,1)S(1)}, u32[]{:S(2)}, u32[]{:S(2)}) collective-permute-start(bf16[2,64,128]{2,1,0:T(8,128)(2,1)S(1)} %shard_map.97), channel_id=1, source_target_pairs={{0,7},{1,2},{2,1},{3,4},{4,3},{5,6},{6,5},{7,0},{8,15},{9,10},{10,... | collective-permute-start | bytes 98312 | tf_op jit(solution)/shard_map/ppermute | solution.py:86
  6.7 1.9 %shard_map.95 = (bf16[2,8,64,128]{3,2,1,0:T(8,128)(2,1)S(1)}, bf16[8,9,128,128]{3,2,1,0:T(8,128)(2,1)S(1)}, f32[2,8,128]{2,1,0:T(8,128)S(1)}, f32[4,4,8,128]{3,2...) custom-call(s32[2,4,9]{2,1,0:T(4,128)} %bitcast.10, ...), custom_call_target="tpu_custom_call" | custom-call | tf_op jit(solution)/shard_map/pallas_call | solution.py:23
  8.6 0.9 %collective-permute-done.2.refs_3_ = bf16[2,64,128]{2,1,0:T(8,128)(2,1)S(1)} collective-permute-done((bf16[2,64,128]{2,1,0:T(8,128)(2,1)S(1)}, bf16[2,64,128]{2,1,0:T(8,128)(2,1)S(1)}, u32[]{:S(2)}, u32[]{:S(2)}) %collective-permute-start.2) | collective-permute-done | bytes 32800 | tf_op jit(solution)/shard_map/ppermute | solution.py:86
  9.5 0.0 collective-permute-start.3
  9.5 0.5 %shard_map.99 = (f32[8,64,128]{2,1,0:T(8,128)S(1)}, bf16[8,64,128]{2,1,0:T(8,128)(2,1)S(1)}, bf16[4,64,128]{2,1,0:T(8,128)(2,1)S(1)}, bf16[2,64,128]{2,1,0:T(8,128)(2,1)S(1)}) custom-call(bf16[2,8,64,128]{3,2,1,0:T(8,128)(2,1)S(1)} %get-tuple-element.51.refs_0_, f32[2,8,128]{2,1,0:T(8,128)S(1)} %get-tuple-element.52.refs_1_.refs_2_.refs_6_, ...), custom_call_target="tpu_custom_call" | custom-call | tf_op jit(solution)/shard_map/pallas_call | solution.py:23
  10.0 0.8 %collective-permute-done.3.refs_3_.refs_4_.refs_5_ = bf16[4,64,128]{2,1,0:T(8,128)(2,1)S(1)} collective-permute-done((bf16[4,64,128]{2,1,0:T(8,128)(2,1)S(1)}, bf16[4,64,128]{2,1,0:T(8,128)(2,1)S(1)}, u32[]{:S(2)}, u32[]{:S(2)}) %collective-permute-start.3) | collective-permute-done | bytes 65568 | tf_op jit(solution)/shard_map/ppermute | solution.py:86
  10.8 0.2 shard_map.101
  11.0 1.4 %collective-permute-start.4 = (bf16[8,64,128]{2,1,0:T(8,128)(2,1)S(1)}, bf16[8,64,128]{2,1,0:T(8,128)(2,1)S(1)}, u32[]{:S(2)}, u32[]{:S(2)}) collective-permute-start(bf16[8,64,128]{2,1,0:T(8,128)(2,1)S(1)} %get-tuple-element.62.refs_9_.refs_8_.refs_0_), channel_id=1, source_target_pairs={{0,8},{1,9},{2,10},{3,11},{4,12},{5,13},{6,14},{7,15},{8,0},{9,1},... | collective-permute-start | bytes 393224 | tf_op jit(solution)/shard_map/ppermute | solution.py:86
  12.3 1.3 %collective-permute-start.5 = (bf16[4,64,128]{2,1,0:T(8,128)(2,1)S(1)}, bf16[4,64,128]{2,1,0:T(8,128)(2,1)S(1)}, u32[]{:S(2)}, u32[]{:S(2)}) collective-permute-start(bf16[4,64,128]{2,1,0:T(8,128)(2,1)S(1)} %get-tuple-element.63), channel_id=1, source_target_pairs={{0,12},{1,13},{2,14},{3,15},{4,8},{5,9},{6,10},{7,11},{8,4},{9,5},... | collective-permute-start | bytes 196616 | tf_op jit(solution)/shard_map/ppermute | solution.py:86
  13.6 2.1 %collective-permute-start.7 = (bf16[2,64,128]{2,1,0:T(8,128)(2,1)S(1)}, bf16[2,64,128]{2,1,0:T(8,128)(2,1)S(1)}, u32[]{:S(2)}, u32[]{:S(2)}) collective-permute-start(bf16[2,64,128]{2,1,0:T(8,128)(2,1)S(1)} %shard_map.102), channel_id=1, source_target_pairs={{0,15},{1,10},{2,9},{3,12},{4,11},{5,14},{6,13},{7,8},{8,7},{9,2},... | collective-permute-start | bytes 98312 | tf_op jit(solution)/shard_map/ppermute | solution.py:86
  15.7 0.9 %collective-permute-start.9 = (bf16[4,64,128]{2,1,0:T(8,128)(2,1)S(1)}, bf16[4,64,128]{2,1,0:T(8,128)(2,1)S(1)}, u32[]{:S(2)}, u32[]{:S(2)}) collective-permute-start(bf16[4,64,128]{2,1,0:T(8,128)(2,1)S(1)} %get-tuple-element.67), channel_id=1, source_target_pairs={{0,4},{1,5},{2,6},{3,7},{4,0},{5,1},{6,2},{7,3},{8,12},{9,13},{10,... | collective-permute-start | bytes 196616 | tf_op jit(solution)/shard_map/ppermute | solution.py:86
  16.6 2.7 %collective-permute-done.7.refs_6_ = bf16[2,64,128]{2,1,0:T(8,128)(2,1)S(1)} collective-permute-done((bf16[2,64,128]{2,1,0:T(8,128)(2,1)S(1)}, bf16[2,64,128]{2,1,0:T(8,128)(2,1)S(1)}, u32[]{:S(2)}, u32[]{:S(2)}) %collective-permute-start.7) | collective-permute-done | bytes 32800 | tf_op jit(solution)/shard_map/ppermute | solution.py:86
  19.3 0.1 collective-permute-start.8
  19.4 1.0 %collective-permute-done.9.refs_5_.refs_2_ = bf16[4,64,128]{2,1,0:T(8,128)(2,1)S(1)} collective-permute-done((bf16[4,64,128]{2,1,0:T(8,128)(2,1)S(1)}, bf16[4,64,128]{2,1,0:T(8,128)(2,1)S(1)}, u32[]{:S(2)}, u32[]{:S(2)}) %collective-permute-start.9) | collective-permute-done | bytes 65568 | tf_op jit(solution)/shard_map/ppermute | solution.py:86
  20.5 0.2 collective-permute-done.8.refs_3_.refs_5_
  20.7 0.2 collective-permute-start.10
  20.8 0.4 collective-permute-start.12
  21.2 0.2 collective-permute-start.11
  21.3 0.7 %collective-permute-done.12.refs_1_ = bf16[2,64,128]{2,1,0:T(8,128)(2,1)S(1)} collective-permute-done((bf16[2,64,128]{2,1,0:T(8,128)(2,1)S(1)}, bf16[2,64,128]{2,1,0:T(8,128)(2,1)S(1)}, u32[]{:S(2)}, u32[]{:S(2)}) %collective-permute-start.12) | collective-permute-done | bytes 32800 | tf_op jit(solution)/shard_map/ppermute | solution.py:86
  22.1 0.3 collective-permute-start.13
  22.4 1.0 %collective-permute-start.15 = (bf16[4,64,128]{2,1,0:T(8,128)(2,1)S(1)}, bf16[4,64,128]{2,1,0:T(8,128)(2,1)S(1)}, u32[]{:S(2)}, u32[]{:S(2)}) collective-permute-start(bf16[4,64,128]{2,1,0:T(8,128)(2,1)S(1)} %get-tuple-element.77), channel_id=1, source_target_pairs={{0,4},{1,6},{2,5},{3,7},{4,0},{5,2},{6,1},{7,3},{8,12},{9,14},{10,... | collective-permute-start | bytes 196616 | tf_op jit(solution)/shard_map/ppermute | solution.py:86
  23.4 1.0 %collective-permute-start.16 = (bf16[4,64,128]{2,1,0:T(8,128)(2,1)S(1)}, bf16[4,64,128]{2,1,0:T(8,128)(2,1)S(1)}, u32[]{:S(2)}, u32[]{:S(2)}) collective-permute-start(bf16[4,64,128]{2,1,0:T(8,128)(2,1)S(1)} %get-tuple-element.78), channel_id=1, source_target_pairs={{0,4},{1,2},{2,1},{3,7},{4,0},{5,6},{6,5},{7,3},{8,12},{9,10},{10,... | collective-permute-start | bytes 196616 | tf_op jit(solution)/shard_map/ppermute | solution.py:86
  24.4 0.4 collective-permute-start.14
  24.9 1.8 %collective-permute-done.15.refs_4_.refs_7_ = bf16[4,64,128]{2,1,0:T(8,128)(2,1)S(1)} collective-permute-done((bf16[4,64,128]{2,1,0:T(8,128)(2,1)S(1)}, bf16[4,64,128]{2,1,0:T(8,128)(2,1)S(1)}, u32[]{:S(2)}, u32[]{:S(2)}) %collective-permute-start.15) | collective-permute-done | bytes 65568 | tf_op jit(solution)/shard_map/ppermute | solution.py:86
  26.7 1.4 %collective-permute-done.16.refs_5_.refs_3_ = bf16[4,64,128]{2,1,0:T(8,128)(2,1)S(1)} collective-permute-done((bf16[4,64,128]{2,1,0:T(8,128)(2,1)S(1)}, bf16[4,64,128]{2,1,0:T(8,128)(2,1)S(1)}, u32[]{:S(2)}, u32[]{:S(2)}) %collective-permute-start.16) | collective-permute-done | bytes 65568 | tf_op jit(solution)/shard_map/ppermute | solution.py:86
  28.1 5.3 %collective-permute-start.17 = (bf16[8,64,128]{2,1,0:T(8,128)(2,1)S(1)}, bf16[8,64,128]{2,1,0:T(8,128)(2,1)S(1)}, u32[]{:S(2)}, u32[]{:S(2)}) collective-permute-start(bf16[8,64,128]{2,1,0:T(8,128)(2,1)S(1)} %get-tuple-element.83.refs_11_.other_ref.refs_2_), channel_id=1, source_target_pairs={{0,8},{1,9},{2,10},{3,11},{4,12},{5,13},{6,14},{7,15},{8,0},{9,1},... | collective-permute-start | bytes 393224 | tf_op jit(solution)/shard_map/ppermute | solution.py:86
  33.3 0.7 %collective-permute-start.18 = (bf16[4,64,128]{2,1,0:T(8,128)(2,1)S(1)}, bf16[4,64,128]{2,1,0:T(8,128)(2,1)S(1)}, u32[]{:S(2)}, u32[]{:S(2)}) collective-permute-start(bf16[4,64,128]{2,1,0:T(8,128)(2,1)S(1)} %get-tuple-element.84), channel_id=1, source_target_pairs={{0,12},{1,13},{2,14},{3,15},{4,8},{5,9},{6,10},{7,11},{8,4},{9,5},... | collective-permute-start | bytes 196616 | tf_op jit(solution)/shard_map/ppermute | solution.py:86
  34.0 0.6 %collective-permute-done.19.refs_1_ = bf16[2,64,128]{2,1,0:T(8,128)(2,1)S(1)} collective-permute-done((bf16[2,64,128]{2,1,0:T(8,128)(2,1)S(1)}, bf16[2,64,128]{2,1,0:T(8,128)(2,1)S(1)}, u32[]{:S(2)}, u32[]{:S(2)}) %collective-permute-start.19) | collective-permute-done | bytes 32800 | tf_op jit(solution)/shard_map/ppermute | solution.py:86
  34.5 1.3 %collective-permute-start.20 = (bf16[2,64,128]{2,1,0:T(8,128)(2,1)S(1)}, bf16[2,64,128]{2,1,0:T(8,128)(2,1)S(1)}, u32[]{:S(2)}, u32[]{:S(2)}) collective-permute-start(bf16[2,64,128]{2,1,0:T(8,128)(2,1)S(1)} %shard_map.112), channel_id=1, source_target_pairs={{0,15},{1,10},{2,9},{3,12},{4,11},{5,14},{6,13},{7,8},{8,7},{9,2},... | collective-permute-start | bytes 98312 | tf_op jit(solution)/shard_map/ppermute | solution.py:86
  35.8 0.8 %collective-permute-start.22 = (f32[128,128]{1,0:T(8,128)S(1)}, f32[128,128]{1,0:T(8,128)S(1)}, u32[]{:S(2)}, u32[]{:S(2)}) collective-permute-start(f32[128,128]{1,0:T(8,128)S(1)} %shard_map.115), channel_id=1, source_target_pairs={{0,8},{1,9},{2,10},{3,11},{4,12},{5,13},{6,14},{7,15},{8,0},{9,1},... | collective-permute-start | bytes 196616 | tf_op jit(solution)/shard_map/ppermute | solution.py:86
  36.6 2.5 %collective-permute-done.18.refs_5_ = bf16[4,64,128]{2,1,0:T(8,128)(2,1)S(1)} collective-permute-done((bf16[4,64,128]{2,1,0:T(8,128)(2,1)S(1)}, bf16[4,64,128]{2,1,0:T(8,128)(2,1)S(1)}, u32[]{:S(2)}, u32[]{:S(2)}) %collective-permute-start.18) | collective-permute-done | bytes 65568 | tf_op jit(solution)/shard_map/ppermute | solution.py:86
  39.1 0.8 %collective-permute-done.20.refs_6_ = bf16[2,64,128]{2,1,0:T(8,128)(2,1)S(1)} collective-permute-done((bf16[2,64,128]{2,1,0:T(8,128)(2,1)S(1)}, bf16[2,64,128]{2,1,0:T(8,128)(2,1)S(1)}, u32[]{:S(2)}, u32[]{:S(2)}) %collective-permute-start.20) | collective-permute-done | bytes 32800 | tf_op jit(solution)/shard_map/ppermute | solution.py:86
  40.0 0.1 collective-permute-start.21
  40.1 0.5 %shard_map.114 = (f32[8,64,128]{2,1,0:T(8,128)S(1)}, bf16[8,64,128]{2,1,0:T(8,128)(2,1)S(1)}, f32[8,128]{1,0:T(8,128)S(1)}) custom-call(bf16[2,8,64,128]{3,2,1,0:T(8,128)(2,1)S(1)} %get-tuple-element.51.refs_0_, f32[2,8,128]{2,1,0:T(8,128)S(1)} %get-tuple-element.52.refs_1_.refs_2_.refs_6_, bf16[4,64,128]{2,1,0:T(8,128)(2,1)S(1)} %collective-permute-done.9.refs_5_.refs_2_, ...), custom_call_target="tpu_custom_call" | custom-call | tf_op jit(solution)/shard_map/pallas_call | solution.py:23
  40.6 0.7 %collective-permute-done.21.refs_4_ = bf16[4,64,128]{2,1,0:T(8,128)(2,1)S(1)} collective-permute-done((bf16[4,64,128]{2,1,0:T(8,128)(2,1)S(1)}, bf16[4,64,128]{2,1,0:T(8,128)(2,1)S(1)}, u32[]{:S(2)}, u32[]{:S(2)}) %collective-permute-start.21) | collective-permute-done | bytes 65568 | tf_op jit(solution)/shard_map/ppermute | solution.py:86
  41.3 0.2 shard_map.116
  41.5 2.3 %collective-permute-start.23 = (f32[2,8,128]{2,1,0:T(8,128)S(1)}, f32[2,8,128]{2,1,0:T(8,128)S(1)}, u32[]{:S(2)}, u32[]{:S(2)}) collective-permute-start(f32[2,8,128]{2,1,0:T(8,128)S(1)} %shard_map.118), channel_id=1, source_target_pairs={{0,24},{1,25},{2,26},{3,27},{4,28},{5,29},{6,30},{7,31},{8,16},{9,... | collective-permute-start | bytes 24584 | tf_op jit(solution)/shard_map/ppermute | solution.py:86
  43.8 0.4 collective-permute-start.25
  44.2 1.8 %collective-permute-start.24 = (f32[8,128]{1,0:T(8,128)S(1)}, f32[8,128]{1,0:T(8,128)S(1)}, u32[]{:S(2)}, u32[]{:S(2)}) collective-permute-start(f32[8,128]{1,0:T(8,128)S(1)} %get-tuple-element.93.own_ref), channel_id=1, source_target_pairs={{0,8},{1,9},{2,10},{3,11},{4,12},{5,13},{6,14},{7,15},{8,0},{9,1},... | collective-permute-start | bytes 12296 | tf_op jit(solution)/shard_map/ppermute | solution.py:86
  46.0 0.8 %shard_map.117 = (bf16[64,8,128]{2,1,0:T(8,128)(2,1)}, bf16[64,8,128]{2,1,0:T(8,128)(2,1)}) custom-call(bf16[8,64,128]{2,1,0:T(8,128)(2,1)S(1)} %get-tuple-element.62.refs_9_.refs_8_.refs_0_, bf16[8,64,128]{2,1,0:T(8,128)(2,1)S(1)} %get-tuple-element.72.refs_10_.one_ref.refs_1_, bf16[8,64,128]{2,1,0:T(8,128)(2,1)S(1)} %get-tuple-element.83.refs_11_.other_ref.refs_2_, ...), custom_call_target="tpu_custom_call" | custom-call | tf_op jit(solution)/shard_map/pallas_call | solution.py:23
  46.8 0.2 collective-permute-done.23.across_ref
  47.0 0.6 %shard_map.119.ends_ref = f32[4,2,4,128]{3,2,1,0:T(4,128)} custom-call(f32[8,128]{1,0:T(8,128)S(1)} %get-tuple-element.93.own_ref, f32[128,128]{1,0:T(8,128)S(1)} %collective-permute-done.22.refs_5_.beside_ref, f32[2,8,128]{2,1,0:T(8,128)S(1)} %collective-permute-done.23.across_ref, f32[4,4,8,128]{3,2,1,0:T(8,128)S(1)} %get-tuple-element.94.member_ref), custom_call_target="tpu_custom_call" | custom-call | tf_op jit(solution)/shard_map/pallas_call | solution.py:23
  47.6 0.7 %collective-permute-done.25.other_ref = f32[8,128]{1,0:T(8,128)S(1)} collective-permute-done((f32[8,128]{1,0:T(8,128)S(1)}, f32[8,128]{1,0:T(8,128)S(1)}, u32[]{:S(2)}, u32[]{:S(2)}) %collective-permute-start.25) | collective-permute-done | bytes 4128 | tf_op jit(solution)/shard_map/ppermute | solution.py:86
  (31 shorter events, 0.1 us)
Async XLA Ops:
  1.7 3.3 %collective-permute-start.1 = (bf16[2,2,64,128]{3,2,1,0:T(8,128)(2,1)S(1)}, bf16[2,2,64,128]{3,2,1,0:T(8,128)(2,1)S(1)}, u32[]{:S(2)}, u32[]{:S(2)}) collective-permute-start(bf16[2,2,64,128]{3,2,1,0:T(8,128)(2,1)S(1)} %get-tuple-element.55), channel_id=1, source_target_pairs={{0,1},{1,0},{2,3},{3,2},{4,5},{5,4},{6,7},{7,6},{8,9},{9,8},{10,11... | collective-permute-start | bytes 196616 | tf_op jit(solution)/shard_map/ppermute | solution.py:86
  2.5 6.2 %collective-permute-start = (bf16[4,64,128]{2,1,0:T(8,128)(2,1)S(1)}, bf16[4,64,128]{2,1,0:T(8,128)(2,1)S(1)}, u32[]{:S(2)}, u32[]{:S(2)}) collective-permute-start(bf16[4,64,128]{2,1,0:T(8,128)(2,1)S(1)} %get-tuple-element.53), channel_id=1, source_target_pairs={{0,4},{1,5},{2,6},{3,7},{4,0},{5,1},{6,2},{7,3},{8,12},{9,13},{10,... | collective-permute-start | bytes 196616 | tf_op jit(solution)/shard_map/ppermute | solution.py:86
  5.1 4.4 %collective-permute-start.2 = (bf16[2,64,128]{2,1,0:T(8,128)(2,1)S(1)}, bf16[2,64,128]{2,1,0:T(8,128)(2,1)S(1)}, u32[]{:S(2)}, u32[]{:S(2)}) collective-permute-start(bf16[2,64,128]{2,1,0:T(8,128)(2,1)S(1)} %shard_map.97), channel_id=1, source_target_pairs={{0,7},{1,2},{2,1},{3,4},{4,3},{5,6},{6,5},{7,0},{8,15},{9,10},{10,... | collective-permute-start | bytes 98312 | tf_op jit(solution)/shard_map/ppermute | solution.py:86
  9.5 1.3 %collective-permute-start.3 = (bf16[4,64,128]{2,1,0:T(8,128)(2,1)S(1)}, bf16[4,64,128]{2,1,0:T(8,128)(2,1)S(1)}, u32[]{:S(2)}, u32[]{:S(2)}) collective-permute-start(bf16[4,64,128]{2,1,0:T(8,128)(2,1)S(1)} %shard_map.98.refs_4_), channel_id=1, source_target_pairs={{0,1},{1,0},{2,3},{3,2},{4,5},{5,4},{6,7},{7,6},{8,9},{9,8},{10,11... | collective-permute-start | bytes 196616 | tf_op jit(solution)/shard_map/ppermute | solution.py:86
  11.0 8.4 %collective-permute-start.4 = (bf16[8,64,128]{2,1,0:T(8,128)(2,1)S(1)}, bf16[8,64,128]{2,1,0:T(8,128)(2,1)S(1)}, u32[]{:S(2)}, u32[]{:S(2)}) collective-permute-start(bf16[8,64,128]{2,1,0:T(8,128)(2,1)S(1)} %get-tuple-element.62.refs_9_.refs_8_.refs_0_), channel_id=1, source_target_pairs={{0,8},{1,9},{2,10},{3,11},{4,12},{5,13},{6,14},{7,15},{8,0},{9,1},... | collective-permute-start | bytes 393224 | tf_op jit(solution)/shard_map/ppermute | solution.py:86
  12.3 1.3 %collective-permute-start.6 = (bf16[2,64,128]{2,1,0:T(8,128)(2,1)S(1)}, bf16[2,64,128]{2,1,0:T(8,128)(2,1)S(1)}, u32[]{:S(2)}, u32[]{:S(2)}) collective-permute-start(bf16[2,64,128]{2,1,0:T(8,128)(2,1)S(1)} %get-tuple-element.65), channel_id=1, source_target_pairs={{0,1},{1,0},{2,3},{3,2},{4,5},{5,4},{6,7},{7,6},{8,9},{9,8},{10,11... | collective-permute-start | bytes 98312 | tf_op jit(solution)/shard_map/ppermute | solution.py:86
  12.3 7.0 %collective-permute-start.5 = (bf16[4,64,128]{2,1,0:T(8,128)(2,1)S(1)}, bf16[4,64,128]{2,1,0:T(8,128)(2,1)S(1)}, u32[]{:S(2)}, u32[]{:S(2)}) collective-permute-start(bf16[4,64,128]{2,1,0:T(8,128)(2,1)S(1)} %get-tuple-element.63), channel_id=1, source_target_pairs={{0,12},{1,13},{2,14},{3,15},{4,8},{5,9},{6,10},{7,11},{8,4},{9,5},... | collective-permute-start | bytes 196616 | tf_op jit(solution)/shard_map/ppermute | solution.py:86
  13.6 5.7 %collective-permute-start.7 = (bf16[2,64,128]{2,1,0:T(8,128)(2,1)S(1)}, bf16[2,64,128]{2,1,0:T(8,128)(2,1)S(1)}, u32[]{:S(2)}, u32[]{:S(2)}) collective-permute-start(bf16[2,64,128]{2,1,0:T(8,128)(2,1)S(1)} %shard_map.102), channel_id=1, source_target_pairs={{0,15},{1,10},{2,9},{3,12},{4,11},{5,14},{6,13},{7,8},{8,7},{9,2},... | collective-permute-start | bytes 98312 | tf_op jit(solution)/shard_map/ppermute | solution.py:86
  15.7 4.8 %collective-permute-start.9 = (bf16[4,64,128]{2,1,0:T(8,128)(2,1)S(1)}, bf16[4,64,128]{2,1,0:T(8,128)(2,1)S(1)}, u32[]{:S(2)}, u32[]{:S(2)}) collective-permute-start(bf16[4,64,128]{2,1,0:T(8,128)(2,1)S(1)} %get-tuple-element.67), channel_id=1, source_target_pairs={{0,4},{1,5},{2,6},{3,7},{4,0},{5,1},{6,2},{7,3},{8,12},{9,13},{10,... | collective-permute-start | bytes 196616 | tf_op jit(solution)/shard_map/ppermute | solution.py:86
  19.3 1.3 %collective-permute-start.8 = (bf16[4,64,128]{2,1,0:T(8,128)(2,1)S(1)}, bf16[4,64,128]{2,1,0:T(8,128)(2,1)S(1)}, u32[]{:S(2)}, u32[]{:S(2)}) collective-permute-start(bf16[4,64,128]{2,1,0:T(8,128)(2,1)S(1)} %shard_map.103.refs_7_), channel_id=1, source_target_pairs={{0,1},{1,0},{2,3},{3,2},{4,5},{5,4},{6,7},{7,6},{8,9},{9,8},{10,11... | collective-permute-start | bytes 196616 | tf_op jit(solution)/shard_map/ppermute | solution.py:86
  20.7 3.8 %collective-permute-start.10 = (bf16[8,64,128]{2,1,0:T(8,128)(2,1)S(1)}, bf16[8,64,128]{2,1,0:T(8,128)(2,1)S(1)}, u32[]{:S(2)}, u32[]{:S(2)}) collective-permute-start(bf16[8,64,128]{2,1,0:T(8,128)(2,1)S(1)} %get-tuple-element.72.refs_10_.one_ref.refs_1_), channel_id=1, source_target_pairs={{0,1},{1,0},{2,3},{3,2},{4,5},{5,4},{6,7},{7,6},{8,16},{9,17},{10,... | collective-permute-start | bytes 393224 | tf_op jit(solution)/shard_map/ppermute | solution.py:86
  20.8 1.2 %collective-permute-start.12 = (bf16[2,64,128]{2,1,0:T(8,128)(2,1)S(1)}, bf16[2,64,128]{2,1,0:T(8,128)(2,1)S(1)}, u32[]{:S(2)}, u32[]{:S(2)}) collective-permute-start(bf16[2,64,128]{2,1,0:T(8,128)(2,1)S(1)} %get-tuple-element.75), channel_id=1, source_target_pairs={{0,1},{1,0},{2,3},{3,2},{4,5},{5,4},{6,7},{7,6},{8,9},{9,8},{10,11... | collective-permute-start | bytes 98312 | tf_op jit(solution)/shard_map/ppermute | solution.py:86
  21.2 3.2 %collective-permute-start.11 = (bf16[4,64,128]{2,1,0:T(8,128)(2,1)S(1)}, bf16[4,64,128]{2,1,0:T(8,128)(2,1)S(1)}, u32[]{:S(2)}, u32[]{:S(2)}) collective-permute-start(bf16[4,64,128]{2,1,0:T(8,128)(2,1)S(1)} %get-tuple-element.73), channel_id=1, source_target_pairs={{0,1},{1,0},{2,3},{3,2},{4,5},{5,4},{6,7},{7,6},{8,20},{9,21},{10,... | collective-permute-start | bytes 196616 | tf_op jit(solution)/shard_map/ppermute | solution.py:86
  22.1 2.4 %collective-permute-start.13 = (bf16[2,64,128]{2,1,0:T(8,128)(2,1)S(1)}, bf16[2,64,128]{2,1,0:T(8,128)(2,1)S(1)}, u32[]{:S(2)}, u32[]{:S(2)}) collective-permute-start(bf16[2,64,128]{2,1,0:T(8,128)(2,1)S(1)} %shard_map.107), channel_id=1, source_target_pairs={{0,1},{1,0},{2,3},{3,2},{4,5},{5,4},{6,7},{7,6},{8,23},{9,18},{10,... | collective-permute-start | bytes 98312 | tf_op jit(solution)/shard_map/ppermute | solution.py:86
  22.4 4.3 %collective-permute-start.15 = (bf16[4,64,128]{2,1,0:T(8,128)(2,1)S(1)}, bf16[4,64,128]{2,1,0:T(8,128)(2,1)S(1)}, u32[]{:S(2)}, u32[]{:S(2)}) collective-permute-start(bf16[4,64,128]{2,1,0:T(8,128)(2,1)S(1)} %get-tuple-element.77), channel_id=1, source_target_pairs={{0,4},{1,6},{2,5},{3,7},{4,0},{5,2},{6,1},{7,3},{8,12},{9,14},{10,... | collective-permute-start | bytes 196616 | tf_op jit(solution)/shard_map/ppermute | solution.py:86
  23.4 4.7 %collective-permute-start.16 = (bf16[4,64,128]{2,1,0:T(8,128)(2,1)S(1)}, bf16[4,64,128]{2,1,0:T(8,128)(2,1)S(1)}, u32[]{:S(2)}, u32[]{:S(2)}) collective-permute-start(bf16[4,64,128]{2,1,0:T(8,128)(2,1)S(1)} %get-tuple-element.78), channel_id=1, source_target_pairs={{0,4},{1,2},{2,1},{3,7},{4,0},{5,6},{6,5},{7,3},{8,12},{9,10},{10,... | collective-permute-start | bytes 196616 | tf_op jit(solution)/shard_map/ppermute | solution.py:86
  24.4 3.6 %collective-permute-start.14 = (bf16[4,64,128]{2,1,0:T(8,128)(2,1)S(1)}, bf16[4,64,128]{2,1,0:T(8,128)(2,1)S(1)}, u32[]{:S(2)}, u32[]{:S(2)}) collective-permute-start(bf16[4,64,128]{2,1,0:T(8,128)(2,1)S(1)} %shard_map.108.refs_6_), channel_id=1, source_target_pairs={{0,1},{1,0},{2,3},{3,2},{4,5},{5,4},{6,7},{7,6},{8,9},{9,8},{10,11... | collective-permute-start | bytes 196616 | tf_op jit(solution)/shard_map/ppermute | solution.py:86
  28.1 11.9 %collective-permute-start.17 = (bf16[8,64,128]{2,1,0:T(8,128)(2,1)S(1)}, bf16[8,64,128]{2,1,0:T(8,128)(2,1)S(1)}, u32[]{:S(2)}, u32[]{:S(2)}) collective-permute-start(bf16[8,64,128]{2,1,0:T(8,128)(2,1)S(1)} %get-tuple-element.83.refs_11_.other_ref.refs_2_), channel_id=1, source_target_pairs={{0,8},{1,9},{2,10},{3,11},{4,12},{5,13},{6,14},{7,15},{8,0},{9,1},... | collective-permute-start | bytes 393224 | tf_op jit(solution)/shard_map/ppermute | solution.py:86
  33.3 1.2 %collective-permute-start.19 = (bf16[2,64,128]{2,1,0:T(8,128)(2,1)S(1)}, bf16[2,64,128]{2,1,0:T(8,128)(2,1)S(1)}, u32[]{:S(2)}, u32[]{:S(2)}) collective-permute-start(bf16[2,64,128]{2,1,0:T(8,128)(2,1)S(1)} %get-tuple-element.86), channel_id=1, source_target_pairs={{0,1},{1,0},{2,3},{3,2},{4,5},{5,4},{6,7},{7,6},{8,9},{9,8},{10,11... | collective-permute-start | bytes 98312 | tf_op jit(solution)/shard_map/ppermute | solution.py:86
  33.3 5.8 %collective-permute-start.18 = (bf16[4,64,128]{2,1,0:T(8,128)(2,1)S(1)}, bf16[4,64,128]{2,1,0:T(8,128)(2,1)S(1)}, u32[]{:S(2)}, u32[]{:S(2)}) collective-permute-start(bf16[4,64,128]{2,1,0:T(8,128)(2,1)S(1)} %get-tuple-element.84), channel_id=1, source_target_pairs={{0,12},{1,13},{2,14},{3,15},{4,8},{5,9},{6,10},{7,11},{8,4},{9,5},... | collective-permute-start | bytes 196616 | tf_op jit(solution)/shard_map/ppermute | solution.py:86
  34.5 5.4 %collective-permute-start.20 = (bf16[2,64,128]{2,1,0:T(8,128)(2,1)S(1)}, bf16[2,64,128]{2,1,0:T(8,128)(2,1)S(1)}, u32[]{:S(2)}, u32[]{:S(2)}) collective-permute-start(bf16[2,64,128]{2,1,0:T(8,128)(2,1)S(1)} %shard_map.112), channel_id=1, source_target_pairs={{0,15},{1,10},{2,9},{3,12},{4,11},{5,14},{6,13},{7,8},{8,7},{9,2},... | collective-permute-start | bytes 98312 | tf_op jit(solution)/shard_map/ppermute | solution.py:86
  35.8 4.8 %collective-permute-start.22 = (f32[128,128]{1,0:T(8,128)S(1)}, f32[128,128]{1,0:T(8,128)S(1)}, u32[]{:S(2)}, u32[]{:S(2)}) collective-permute-start(f32[128,128]{1,0:T(8,128)S(1)} %shard_map.115), channel_id=1, source_target_pairs={{0,8},{1,9},{2,10},{3,11},{4,12},{5,13},{6,14},{7,15},{8,0},{9,1},... | collective-permute-start | bytes 196616 | tf_op jit(solution)/shard_map/ppermute | solution.py:86
  40.0 1.3 %collective-permute-start.21 = (bf16[4,64,128]{2,1,0:T(8,128)(2,1)S(1)}, bf16[4,64,128]{2,1,0:T(8,128)(2,1)S(1)}, u32[]{:S(2)}, u32[]{:S(2)}) collective-permute-start(bf16[4,64,128]{2,1,0:T(8,128)(2,1)S(1)} %shard_map.113.refs_7_), channel_id=1, source_target_pairs={{0,1},{1,0},{2,3},{3,2},{4,5},{5,4},{6,7},{7,6},{8,9},{9,8},{10,11... | collective-permute-start | bytes 196616 | tf_op jit(solution)/shard_map/ppermute | solution.py:86
  41.5 5.5 %collective-permute-start.23 = (f32[2,8,128]{2,1,0:T(8,128)S(1)}, f32[2,8,128]{2,1,0:T(8,128)S(1)}, u32[]{:S(2)}, u32[]{:S(2)}) collective-permute-start(f32[2,8,128]{2,1,0:T(8,128)S(1)} %shard_map.118), channel_id=1, source_target_pairs={{0,24},{1,25},{2,26},{3,27},{4,28},{5,29},{6,30},{7,31},{8,16},{9,... | collective-permute-start | bytes 24584 | tf_op jit(solution)/shard_map/ppermute | solution.py:86
  43.8 4.5 %collective-permute-start.25 = (f32[8,128]{1,0:T(8,128)S(1)}, f32[8,128]{1,0:T(8,128)S(1)}, u32[]{:S(2)}, u32[]{:S(2)}) collective-permute-start(f32[8,128]{1,0:T(8,128)S(1)} %get-tuple-element.93.own_ref), channel_id=1, source_target_pairs={{0,16},{1,17},{2,18},{3,19},{4,20},{5,21},{6,22},{7,23},{8,24},{9,... | collective-permute-start | bytes 12296 | tf_op jit(solution)/shard_map/ppermute | solution.py:86
  44.2 4.1 %collective-permute-start.24 = (f32[8,128]{1,0:T(8,128)S(1)}, f32[8,128]{1,0:T(8,128)S(1)}, u32[]{:S(2)}, u32[]{:S(2)}) collective-permute-start(f32[8,128]{1,0:T(8,128)S(1)} %get-tuple-element.93.own_ref), channel_id=1, source_target_pairs={{0,8},{1,9},{2,10},{3,11},{4,12},{5,13},{6,14},{7,15},{8,0},{9,1},... | collective-permute-start | bytes 12296 | tf_op jit(solution)/shard_map/ppermute | solution.py:86

commit v8 on v7

--- a/solution.py
+++ b/solution.py
@@ -163,7 +163,8 @@
             flat_ref[phase] = raw_ref[first_sweep() ^ phase].astype(f32).reshape(ports * tiles, cells)
             for h, pairing in enumerate(row_pairs):
                 row = Side(pairing, "row", tiles_x).edge
-                corner_ref[h, phase] = source_tile(flat_ref, cells_ref, phase, row, edge)
+                if phase == 0:
+                    corner_ref[h] = source_tile(flat_ref, cells_ref, phase, row, edge)
 
     def rims_kernel(flat_ref, cells_ref, *refs):
         take = taker(refs)
@@ -179,7 +180,7 @@
     raw_shape = (ports, tiles, cells)
     flat, port_row, corner = call(
         corner_kernel,
-        [((2, ports * tiles, cells), f32), ((1, ports), jnp.int32), ((SPARE * halos, 2, *tile), bf16)],
+        [((2, ports * tiles, cells), f32), ((1, ports), jnp.int32), ((SPARE * halos, *tile), bf16)],
         sources.reshape(raw_shape),
         adjoint_sources.reshape(raw_shape),
         port_cells.reshape(1, ports),
@@ -202,7 +203,7 @@
         @pl.when(jnp.logical_not(inner))
         def _():
             for h, out_ref in enumerate(out_refs):
-                out_ref[0] = corner_ref[h] if phase is None else corner_ref[h, phase]
+                out_ref[0] = corner_ref[h]
 
     def exchange(step, corner, outward, field=None):
         rims, column = outward[:halos], outward[halos]

time: 48.5 us -> 48.5 us (level)
  transfers between devices with their start and end apart: 26 -> 26, of which waited for: 14 -> 15; matrix products, arithmetic and copies ran while one was open for 0% -> 0% of each run, Pallas kernels for 10% -> 10%
where the time goes in v8:
time: 48.5 us; the launch traced here: 48.3 us
  starting transfers between devices  26.5 us (55%)
  waiting for transfers between devices  14.9 us (31%)
  Pallas kernels  6.15 us (13%)
  between operations  0.77 us (2%)
    ppermute x26, starting transfers between devices, permuted(): return lax.ppermute(array, AXES, pairs)  26.5 us
    ppermute x26, waiting for transfers between devices, permuted(): return lax.ppermute(array, AXES, pairs)  14.9 us
    pallas_call x26, Pallas kernels, call(): pl.pallas_call(kernel, out_shape=[jax.ShapeDtypeStruct(shape, dtype) for...  6.14 us
  transfers between devices with their start and end apart: 26, of which 15 were waited for; matrix products, arithmetic and copies ran while one was open for 0% of the time, Pallas kernels for 10%

profile of v8, /device:TPU:0, one launch (start us, length us, event | category | flops | bytes accessed | tf_op | source)
XLA Modules:
  0.0 48.3 jit_solution(6619799247092005453)
XLA Ops:
  0.6 1.1 %shard_map.94 = (f32[2,512,128]{2,1,0:T(8,128)S(1)}, s32[1,64]{1,0:T(1,128)S(1)}, bf16[2,64,128]{2,1,0:T(8,128)(2,1)S(1)}) custom-call(bf16[64,8,128]{2,1,0:T(8,128)(2,1)} %bitcast.8, bf16[64,8,128]{2,1,0:T(8,128)(2,1)} %bitcast.9, s32[1,64]{1,0:T(1,128)} %bitcast.11), custom_call_target="tpu_custom_call" | custom-call | tf_op jit(solution)/shard_map/pallas_call | solution.py:23
  1.7 0.5 %collective-permute-start.1 = (bf16[2,64,128]{2,1,0:T(8,128)(2,1)S(1)}, bf16[2,64,128]{2,1,0:T(8,128)(2,1)S(1)}, u32[]{:S(2)}, u32[]{:S(2)}) collective-permute-start(bf16[2,64,128]{2,1,0:T(8,128)(2,1)S(1)} %get-tuple-element.55), channel_id=1, source_target_pairs={{0,1},{1,0},{2,3},{3,2},{4,5},{5,4},{6,7},{7,6},{8,9},{9,8},{10,11... | collective-permute-start | bytes 98312 | tf_op jit(solution)/shard_map/ppermute | solution.py:86
  2.3 0.2 shard_map.96
  2.4 2.6 %collective-permute-start = (bf16[4,64,128]{2,1,0:T(8,128)(2,1)S(1)}, bf16[4,64,128]{2,1,0:T(8,128)(2,1)S(1)}, u32[]{:S(2)}, u32[]{:S(2)}) collective-permute-start(bf16[4,64,128]{2,1,0:T(8,128)(2,1)S(1)} %get-tuple-element.53), channel_id=1, source_target_pairs={{0,4},{1,5},{2,6},{3,7},{4,0},{5,1},{6,2},{7,3},{8,12},{9,13},{10,... | collective-permute-start | bytes 196616 | tf_op jit(solution)/shard_map/ppermute | solution.py:86
  5.0 1.6 %collective-permute-start.2 = (bf16[2,64,128]{2,1,0:T(8,128)(2,1)S(1)}, bf16[2,64,128]{2,1,0:T(8,128)(2,1)S(1)}, u32[]{:S(2)}, u32[]{:S(2)}) collective-permute-start(bf16[2,64,128]{2,1,0:T(8,128)(2,1)S(1)} %shard_map.97), channel_id=1, source_target_pairs={{0,7},{1,2},{2,1},{3,4},{4,3},{5,6},{6,5},{7,0},{8,15},{9,10},{10,... | collective-permute-start | bytes 98312 | tf_op jit(solution)/shard_map/ppermute | solution.py:86
  6.7 1.9 %shard_map.95 = (bf16[2,8,64,128]{3,2,1,0:T(8,128)(2,1)S(1)}, bf16[8,9,128,128]{3,2,1,0:T(8,128)(2,1)S(1)}, f32[2,8,128]{2,1,0:T(8,128)S(1)}, f32[4,4,8,128]{3,2...) custom-call(s32[2,4,9]{2,1,0:T(4,128)} %bitcast.10, ...), custom_call_target="tpu_custom_call" | custom-call | tf_op jit(solution)/shard_map/pallas_call | solution.py:23
  8.6 0.9 %collective-permute-done.2.refs_3_ = bf16[2,64,128]{2,1,0:T(8,128)(2,1)S(1)} collective-permute-done((bf16[2,64,128]{2,1,0:T(8,128)(2,1)S(1)}, bf16[2,64,128]{2,1,0:T(8,128)(2,1)S(1)}, u32[]{:S(2)}, u32[]{:S(2)}) %collective-permute-start.2) | collective-permute-done | bytes 32800 | tf_op jit(solution)/shard_map/ppermute | solution.py:86
  9.5 0.1 collective-permute-start.3
  9.5 0.5 %shard_map.99 = (f32[8,64,128]{2,1,0:T(8,128)S(1)}, bf16[8,64,128]{2,1,0:T(8,128)(2,1)S(1)}, bf16[4,64,128]{2,1,0:T(8,128)(2,1)S(1)}, bf16[2,64,128]{2,1,0:T(8,128)(2,1)S(1)}) custom-call(bf16[2,8,64,128]{3,2,1,0:T(8,128)(2,1)S(1)} %get-tuple-element.51.refs_0_, f32[2,8,128]{2,1,0:T(8,128)S(1)} %get-tuple-element.52.refs_1_.refs_2_.refs_6_, ...), custom_call_target="tpu_custom_call" | custom-call | tf_op jit(solution)/shard_map/pallas_call | solution.py:23
  10.0 0.7 %collective-permute-done.3.refs_3_.refs_4_.refs_5_ = bf16[4,64,128]{2,1,0:T(8,128)(2,1)S(1)} collective-permute-done((bf16[4,64,128]{2,1,0:T(8,128)(2,1)S(1)}, bf16[4,64,128]{2,1,0:T(8,128)(2,1)S(1)}, u32[]{:S(2)}, u32[]{:S(2)}) %collective-permute-start.3) | collective-permute-done | bytes 65568 | tf_op jit(solution)/shard_map/ppermute | solution.py:86
  10.8 0.2 shard_map.101
  11.0 1.3 %collective-permute-start.4 = (bf16[8,64,128]{2,1,0:T(8,128)(2,1)S(1)}, bf16[8,64,128]{2,1,0:T(8,128)(2,1)S(1)}, u32[]{:S(2)}, u32[]{:S(2)}) collective-permute-start(bf16[8,64,128]{2,1,0:T(8,128)(2,1)S(1)} %get-tuple-element.62.refs_9_.refs_8_.refs_0_), channel_id=1, source_target_pairs={{0,8},{1,9},{2,10},{3,11},{4,12},{5,13},{6,14},{7,15},{8,0},{9,1},... | collective-permute-start | bytes 393224 | tf_op jit(solution)/shard_map/ppermute | solution.py:86
  12.3 1.3 %collective-permute-start.5 = (bf16[4,64,128]{2,1,0:T(8,128)(2,1)S(1)}, bf16[4,64,128]{2,1,0:T(8,128)(2,1)S(1)}, u32[]{:S(2)}, u32[]{:S(2)}) collective-permute-start(bf16[4,64,128]{2,1,0:T(8,128)(2,1)S(1)} %get-tuple-element.63), channel_id=1, source_target_pairs={{0,12},{1,13},{2,14},{3,15},{4,8},{5,9},{6,10},{7,11},{8,4},{9,5},... | collective-permute-start | bytes 196616 | tf_op jit(solution)/shard_map/ppermute | solution.py:86
  13.6 2.1 %collective-permute-start.7 = (bf16[2,64,128]{2,1,0:T(8,128)(2,1)S(1)}, bf16[2,64,128]{2,1,0:T(8,128)(2,1)S(1)}, u32[]{:S(2)}, u32[]{:S(2)}) collective-permute-start(bf16[2,64,128]{2,1,0:T(8,128)(2,1)S(1)} %shard_map.102), channel_id=1, source_target_pairs={{0,15},{1,10},{2,9},{3,12},{4,11},{5,14},{6,13},{7,8},{8,7},{9,2},... | collective-permute-start | bytes 98312 | tf_op jit(solution)/shard_map/ppermute | solution.py:86
  15.7 0.9 %collective-permute-start.9 = (bf16[4,64,128]{2,1,0:T(8,128)(2,1)S(1)}, bf16[4,64,128]{2,1,0:T(8,128)(2,1)S(1)}, u32[]{:S(2)}, u32[]{:S(2)}) collective-permute-start(bf16[4,64,128]{2,1,0:T(8,128)(2,1)S(1)} %get-tuple-element.67), channel_id=1, source_target_pairs={{0,4},{1,5},{2,6},{3,7},{4,0},{5,1},{6,2},{7,3},{8,12},{9,13},{10,... | collective-permute-start | bytes 196616 | tf_op jit(solution)/shard_map/ppermute | solution.py:86
  16.6 2.7 %collective-permute-done.5.refs_5_ = bf16[4,64,128]{2,1,0:T(8,128)(2,1)S(1)} collective-permute-done((bf16[4,64,128]{2,1,0:T(8,128)(2,1)S(1)}, bf16[4,64,128]{2,1,0:T(8,128)(2,1)S(1)}, u32[]{:S(2)}, u32[]{:S(2)}) %collective-permute-start.5) | collective-permute-done | bytes 65568 | tf_op jit(solution)/shard_map/ppermute | solution.py:86
  19.3 0.1 collective-permute-done.7.refs_6_
  19.3 0.0 collective-permute-start.8
  19.4 1.0 %collective-permute-done.9.refs_5_.refs_2_ = bf16[4,64,128]{2,1,0:T(8,128)(2,1)S(1)} collective-permute-done((bf16[4,64,128]{2,1,0:T(8,128)(2,1)S(1)}, bf16[4,64,128]{2,1,0:T(8,128)(2,1)S(1)}, u32[]{:S(2)}, u32[]{:S(2)}) %collective-permute-start.9) | collective-permute-done | bytes 65568 | tf_op jit(solution)/shard_map/ppermute | solution.py:86
  20.4 0.2 collective-permute-done.8.refs_3_.refs_5_
  20.6 0.2 collective-permute-start.10
  20.8 0.4 collective-permute-start.12
  21.1 0.2 collective-permute-start.11
  21.3 0.7 %collective-permute-done.12.refs_1_ = bf16[2,64,128]{2,1,0:T(8,128)(2,1)S(1)} collective-permute-done((bf16[2,64,128]{2,1,0:T(8,128)(2,1)S(1)}, bf16[2,64,128]{2,1,0:T(8,128)(2,1)S(1)}, u32[]{:S(2)}, u32[]{:S(2)}) %collective-permute-start.12) | collective-permute-done | bytes 32800 | tf_op jit(solution)/shard_map/ppermute | solution.py:86
  22.0 0.3 collective-permute-start.13
  22.3 1.0 %collective-permute-start.15 = (bf16[4,64,128]{2,1,0:T(8,128)(2,1)S(1)}, bf16[4,64,128]{2,1,0:T(8,128)(2,1)S(1)}, u32[]{:S(2)}, u32[]{:S(2)}) collective-permute-start(bf16[4,64,128]{2,1,0:T(8,128)(2,1)S(1)} %get-tuple-element.77), channel_id=1, source_target_pairs={{0,4},{1,6},{2,5},{3,7},{4,0},{5,2},{6,1},{7,3},{8,12},{9,14},{10,... | collective-permute-start | bytes 196616 | tf_op jit(solution)/shard_map/ppermute | solution.py:86
  23.4 1.0 %collective-permute-start.16 = (bf16[4,64,128]{2,1,0:T(8,128)(2,1)S(1)}, bf16[4,64,128]{2,1,0:T(8,128)(2,1)S(1)}, u32[]{:S(2)}, u32[]{:S(2)}) collective-permute-start(bf16[4,64,128]{2,1,0:T(8,128)(2,1)S(1)} %get-tuple-element.78), channel_id=1, source_target_pairs={{0,4},{1,2},{2,1},{3,7},{4,0},{5,6},{6,5},{7,3},{8,12},{9,10},{10,... | collective-permute-start | bytes 196616 | tf_op jit(solution)/shard_map/ppermute | solution.py:86
  24.4 0.4 collective-permute-start.14
  24.8 1.8 %collective-permute-done.15.refs_4_.refs_7_ = bf16[4,64,128]{2,1,0:T(8,128)(2,1)S(1)} collective-permute-done((bf16[4,64,128]{2,1,0:T(8,128)(2,1)S(1)}, bf16[4,64,128]{2,1,0:T(8,128)(2,1)S(1)}, u32[]{:S(2)}, u32[]{:S(2)}) %collective-permute-start.15) | collective-permute-done | bytes 65568 | tf_op jit(solution)/shard_map/ppermute | solution.py:86
  26.6 1.4 %collective-permute-done.16.refs_5_.refs_3_ = bf16[4,64,128]{2,1,0:T(8,128)(2,1)S(1)} collective-permute-done((bf16[4,64,128]{2,1,0:T(8,128)(2,1)S(1)}, bf16[4,64,128]{2,1,0:T(8,128)(2,1)S(1)}, u32[]{:S(2)}, u32[]{:S(2)}) %collective-permute-start.16) | collective-permute-done | bytes 65568 | tf_op jit(solution)/shard_map/ppermute | solution.py:86
  28.0 5.3 %collective-permute-start.17 = (bf16[8,64,128]{2,1,0:T(8,128)(2,1)S(1)}, bf16[8,64,128]{2,1,0:T(8,128)(2,1)S(1)}, u32[]{:S(2)}, u32[]{:S(2)}) collective-permute-start(bf16[8,64,128]{2,1,0:T(8,128)(2,1)S(1)} %get-tuple-element.83.refs_11_.other_ref.refs_2_), channel_id=1, source_target_pairs={{0,8},{1,9},{2,10},{3,11},{4,12},{5,13},{6,14},{7,15},{8,0},{9,1},... | collective-permute-start | bytes 393224 | tf_op jit(solution)/shard_map/ppermute | solution.py:86
  33.3 0.7 %collective-permute-start.18 = (bf16[4,64,128]{2,1,0:T(8,128)(2,1)S(1)}, bf16[4,64,128]{2,1,0:T(8,128)(2,1)S(1)}, u32[]{:S(2)}, u32[]{:S(2)}) collective-permute-start(bf16[4,64,128]{2,1,0:T(8,128)(2,1)S(1)} %get-tuple-element.84), channel_id=1, source_target_pairs={{0,12},{1,13},{2,14},{3,15},{4,8},{5,9},{6,10},{7,11},{8,4},{9,5},... | collective-permute-start | bytes 196616 | tf_op jit(solution)/shard_map/ppermute | solution.py:86
  34.0 0.5 collective-permute-done.19.refs_1_
  34.5 1.3 %collective-permute-start.20 = (bf16[2,64,128]{2,1,0:T(8,128)(2,1)S(1)}, bf16[2,64,128]{2,1,0:T(8,128)(2,1)S(1)}, u32[]{:S(2)}, u32[]{:S(2)}) collective-permute-start(bf16[2,64,128]{2,1,0:T(8,128)(2,1)S(1)} %shard_map.112), channel_id=1, source_target_pairs={{0,15},{1,10},{2,9},{3,12},{4,11},{5,14},{6,13},{7,8},{8,7},{9,2},... | collective-permute-start | bytes 98312 | tf_op jit(solution)/shard_map/ppermute | solution.py:86
  35.8 0.8 %collective-permute-start.22 = (f32[128,128]{1,0:T(8,128)S(1)}, f32[128,128]{1,0:T(8,128)S(1)}, u32[]{:S(2)}, u32[]{:S(2)}) collective-permute-start(f32[128,128]{1,0:T(8,128)S(1)} %shard_map.115), channel_id=1, source_target_pairs={{0,8},{1,9},{2,10},{3,11},{4,12},{5,13},{6,14},{7,15},{8,0},{9,1},... | collective-permute-start | bytes 196616 | tf_op jit(solution)/shard_map/ppermute | solution.py:86
  36.6 2.5 %collective-permute-done.18.refs_5_ = bf16[4,64,128]{2,1,0:T(8,128)(2,1)S(1)} collective-permute-done((bf16[4,64,128]{2,1,0:T(8,128)(2,1)S(1)}, bf16[4,64,128]{2,1,0:T(8,128)(2,1)S(1)}, u32[]{:S(2)}, u32[]{:S(2)}) %collective-permute-start.18) | collective-permute-done | bytes 65568 | tf_op jit(solution)/shard_map/ppermute | solution.py:86
  39.1 0.9 %collective-permute-done.20.refs_6_ = bf16[2,64,128]{2,1,0:T(8,128)(2,1)S(1)} collective-permute-done((bf16[2,64,128]{2,1,0:T(8,128)(2,1)S(1)}, bf16[2,64,128]{2,1,0:T(8,128)(2,1)S(1)}, u32[]{:S(2)}, u32[]{:S(2)}) %collective-permute-start.20) | collective-permute-done | bytes 32800 | tf_op jit(solution)/shard_map/ppermute | solution.py:86
  40.0 0.1 collective-permute-start.21
  40.1 0.5 %shard_map.114 = (f32[8,64,128]{2,1,0:T(8,128)S(1)}, bf16[8,64,128]{2,1,0:T(8,128)(2,1)S(1)}, f32[8,128]{1,0:T(8,128)S(1)}) custom-call(bf16[2,8,64,128]{3,2,1,0:T(8,128)(2,1)S(1)} %get-tuple-element.51.refs_0_, f32[2,8,128]{2,1,0:T(8,128)S(1)} %get-tuple-element.52.refs_1_.refs_2_.refs_6_, bf16[4,64,128]{2,1,0:T(8,128)(2,1)S(1)} %collective-permute-done.9.refs_5_.refs_2_, ...), custom_call_target="tpu_custom_call" | custom-call | tf_op jit(solution)/shard_map/pallas_call | solution.py:23
  40.6 0.7 %collective-permute-done.21.refs_4_ = bf16[4,64,128]{2,1,0:T(8,128)(2,1)S(1)} collective-permute-done((bf16[4,64,128]{2,1,0:T(8,128)(2,1)S(1)}, bf16[4,64,128]{2,1,0:T(8,128)(2,1)S(1)}, u32[]{:S(2)}, u32[]{:S(2)}) %collective-permute-start.21) | collective-permute-done | bytes 65568 | tf_op jit(solution)/shard_map/ppermute | solution.py:86
  41.3 0.2 shard_map.116
  41.5 2.3 %collective-permute-start.23 = (f32[2,8,128]{2,1,0:T(8,128)S(1)}, f32[2,8,128]{2,1,0:T(8,128)S(1)}, u32[]{:S(2)}, u32[]{:S(2)}) collective-permute-start(f32[2,8,128]{2,1,0:T(8,128)S(1)} %shard_map.118), channel_id=1, source_target_pairs={{0,24},{1,25},{2,26},{3,27},{4,28},{5,29},{6,30},{7,31},{8,16},{9,... | collective-permute-start | bytes 24584 | tf_op jit(solution)/shard_map/ppermute | solution.py:86
  43.8 0.5 collective-permute-start.25
  44.3 1.7 %collective-permute-start.24 = (f32[8,128]{1,0:T(8,128)S(1)}, f32[8,128]{1,0:T(8,128)S(1)}, u32[]{:S(2)}, u32[]{:S(2)}) collective-permute-start(f32[8,128]{1,0:T(8,128)S(1)} %get-tuple-element.93.own_ref), channel_id=1, source_target_pairs={{0,8},{1,9},{2,10},{3,11},{4,12},{5,13},{6,14},{7,15},{8,0},{9,1},... | collective-permute-start | bytes 12296 | tf_op jit(solution)/shard_map/ppermute | solution.py:86
  46.0 0.8 %shard_map.117 = (bf16[64,8,128]{2,1,0:T(8,128)(2,1)}, bf16[64,8,128]{2,1,0:T(8,128)(2,1)}) custom-call(bf16[8,64,128]{2,1,0:T(8,128)(2,1)S(1)} %get-tuple-element.62.refs_9_.refs_8_.refs_0_, bf16[8,64,128]{2,1,0:T(8,128)(2,1)S(1)} %get-tuple-element.72.refs_10_.one_ref.refs_1_, bf16[8,64,128]{2,1,0:T(8,128)(2,1)S(1)} %get-tuple-element.83.refs_11_.other_ref.refs_2_, ...), custom_call_target="tpu_custom_call" | custom-call | tf_op jit(solution)/shard_map/pallas_call | solution.py:23
  46.8 0.2 collective-permute-done.23.across_ref
  47.1 0.6 %shard_map.119.ends_ref = f32[4,2,4,128]{3,2,1,0:T(4,128)} custom-call(f32[8,128]{1,0:T(8,128)S(1)} %get-tuple-element.93.own_ref, f32[128,128]{1,0:T(8,128)S(1)} %collective-permute-done.22.refs_5_.beside_ref, f32[2,8,128]{2,1,0:T(8,128)S(1)} %collective-permute-done.23.across_ref, f32[4,4,8,128]{3,2,1,0:T(8,128)S(1)} %get-tuple-element.94.member_ref), custom_call_target="tpu_custom_call" | custom-call | tf_op jit(solution)/shard_map/pallas_call | solution.py:23
  47.7 0.6 %collective-permute-done.25.other_ref = f32[8,128]{1,0:T(8,128)S(1)} collective-permute-done((f32[8,128]{1,0:T(8,128)S(1)}, f32[8,128]{1,0:T(8,128)S(1)}, u32[]{:S(2)}, u32[]{:S(2)}) %collective-permute-start.25) | collective-permute-done | bytes 4128 | tf_op jit(solution)/shard_map/ppermute | solution.py:86
  (31 shorter events, 0.1 us)
Async XLA Ops:
  1.7 3.3 %collective-permute-start.1 = (bf16[2,64,128]{2,1,0:T(8,128)(2,1)S(1)}, bf16[2,64,128]{2,1,0:T(8,128)(2,1)S(1)}, u32[]{:S(2)}, u32[]{:S(2)}) collective-permute-start(bf16[2,64,128]{2,1,0:T(8,128)(2,1)S(1)} %get-tuple-element.55), channel_id=1, source_target_pairs={{0,1},{1,0},{2,3},{3,2},{4,5},{5,4},{6,7},{7,6},{8,9},{9,8},{10,11... | collective-permute-start | bytes 98312 | tf_op jit(solution)/shard_map/ppermute | solution.py:86
  2.4 7.0 %collective-permute-start = (bf16[4,64,128]{2,1,0:T(8,128)(2,1)S(1)}, bf16[4,64,128]{2,1,0:T(8,128)(2,1)S(1)}, u32[]{:S(2)}, u32[]{:S(2)}) collective-permute-start(bf16[4,64,128]{2,1,0:T(8,128)(2,1)S(1)} %get-tuple-element.53), channel_id=1, source_target_pairs={{0,4},{1,5},{2,6},{3,7},{4,0},{5,1},{6,2},{7,3},{8,12},{9,13},{10,... | collective-permute-start | bytes 196616 | tf_op jit(solution)/shard_map/ppermute | solution.py:86
  5.0 4.4 %collective-permute-start.2 = (bf16[2,64,128]{2,1,0:T(8,128)(2,1)S(1)}, bf16[2,64,128]{2,1,0:T(8,128)(2,1)S(1)}, u32[]{:S(2)}, u32[]{:S(2)}) collective-permute-start(bf16[2,64,128]{2,1,0:T(8,128)(2,1)S(1)} %shard_map.97), channel_id=1, source_target_pairs={{0,7},{1,2},{2,1},{3,4},{4,3},{5,6},{6,5},{7,0},{8,15},{9,10},{10,... | collective-permute-start | bytes 98312 | tf_op jit(solution)/shard_map/ppermute | solution.py:86
  9.5 1.3 %collective-permute-start.3 = (bf16[4,64,128]{2,1,0:T(8,128)(2,1)S(1)}, bf16[4,64,128]{2,1,0:T(8,128)(2,1)S(1)}, u32[]{:S(2)}, u32[]{:S(2)}) collective-permute-start(bf16[4,64,128]{2,1,0:T(8,128)(2,1)S(1)} %shard_map.98.refs_4_), channel_id=1, source_target_pairs={{0,1},{1,0},{2,3},{3,2},{4,5},{5,4},{6,7},{7,6},{8,9},{9,8},{10,11... | collective-permute-start | bytes 196616 | tf_op jit(solution)/shard_map/ppermute | solution.py:86
  11.0 8.3 %collective-permute-start.4 = (bf16[8,64,128]{2,1,0:T(8,128)(2,1)S(1)}, bf16[8,64,128]{2,1,0:T(8,128)(2,1)S(1)}, u32[]{:S(2)}, u32[]{:S(2)}) collective-permute-start(bf16[8,64,128]{2,1,0:T(8,128)(2,1)S(1)} %get-tuple-element.62.refs_9_.refs_8_.refs_0_), channel_id=1, source_target_pairs={{0,8},{1,9},{2,10},{3,11},{4,12},{5,13},{6,14},{7,15},{8,0},{9,1},... | collective-permute-start | bytes 393224 | tf_op jit(solution)/shard_map/ppermute | solution.py:86
  12.3 1.3 %collective-permute-start.6 = (bf16[2,64,128]{2,1,0:T(8,128)(2,1)S(1)}, bf16[2,64,128]{2,1,0:T(8,128)(2,1)S(1)}, u32[]{:S(2)}, u32[]{:S(2)}) collective-permute-start(bf16[2,64,128]{2,1,0:T(8,128)(2,1)S(1)} %get-tuple-element.65), channel_id=1, source_target_pairs={{0,1},{1,0},{2,3},{3,2},{4,5},{5,4},{6,7},{7,6},{8,9},{9,8},{10,11... | collective-permute-start | bytes 98312 | tf_op jit(solution)/shard_map/ppermute | solution.py:86
  12.3 7.0 %collective-permute-start.5 = (bf16[4,64,128]{2,1,0:T(8,128)(2,1)S(1)}, bf16[4,64,128]{2,1,0:T(8,128)(2,1)S(1)}, u32[]{:S(2)}, u32[]{:S(2)}) collective-permute-start(bf16[4,64,128]{2,1,0:T(8,128)(2,1)S(1)} %get-tuple-element.63), channel_id=1, source_target_pairs={{0,12},{1,13},{2,14},{3,15},{4,8},{5,9},{6,10},{7,11},{8,4},{9,5},... | collective-permute-start | bytes 196616 | tf_op jit(solution)/shard_map/ppermute | solution.py:86
  13.6 5.7 %collective-permute-start.7 = (bf16[2,64,128]{2,1,0:T(8,128)(2,1)S(1)}, bf16[2,64,128]{2,1,0:T(8,128)(2,1)S(1)}, u32[]{:S(2)}, u32[]{:S(2)}) collective-permute-start(bf16[2,64,128]{2,1,0:T(8,128)(2,1)S(1)} %shard_map.102), channel_id=1, source_target_pairs={{0,15},{1,10},{2,9},{3,12},{4,11},{5,14},{6,13},{7,8},{8,7},{9,2},... | collective-permute-start | bytes 98312 | tf_op jit(solution)/shard_map/ppermute | solution.py:86
  15.7 4.7 %collective-permute-start.9 = (bf16[4,64,128]{2,1,0:T(8,128)(2,1)S(1)}, bf16[4,64,128]{2,1,0:T(8,128)(2,1)S(1)}, u32[]{:S(2)}, u32[]{:S(2)}) collective-permute-start(bf16[4,64,128]{2,1,0:T(8,128)(2,1)S(1)} %get-tuple-element.67), channel_id=1, source_target_pairs={{0,4},{1,5},{2,6},{3,7},{4,0},{5,1},{6,2},{7,3},{8,12},{9,13},{10,... | collective-permute-start | bytes 196616 | tf_op jit(solution)/shard_map/ppermute | solution.py:86
  19.3 1.3 %collective-permute-start.8 = (bf16[4,64,128]{2,1,0:T(8,128)(2,1)S(1)}, bf16[4,64,128]{2,1,0:T(8,128)(2,1)S(1)}, u32[]{:S(2)}, u32[]{:S(2)}) collective-permute-start(bf16[4,64,128]{2,1,0:T(8,128)(2,1)S(1)} %shard_map.103.refs_7_), channel_id=1, source_target_pairs={{0,1},{1,0},{2,3},{3,2},{4,5},{5,4},{6,7},{7,6},{8,9},{9,8},{10,11... | collective-permute-start | bytes 196616 | tf_op jit(solution)/shard_map/ppermute | solution.py:86
  20.6 3.8 %collective-permute-start.10 = (bf16[8,64,128]{2,1,0:T(8,128)(2,1)S(1)}, bf16[8,64,128]{2,1,0:T(8,128)(2,1)S(1)}, u32[]{:S(2)}, u32[]{:S(2)}) collective-permute-start(bf16[8,64,128]{2,1,0:T(8,128)(2,1)S(1)} %get-tuple-element.72.refs_10_.one_ref.refs_1_), channel_id=1, source_target_pairs={{0,1},{1,0},{2,3},{3,2},{4,5},{5,4},{6,7},{7,6},{8,16},{9,17},{10,... | collective-permute-start | bytes 393224 | tf_op jit(solution)/shard_map/ppermute | solution.py:86
  20.8 1.2 %collective-permute-start.12 = (bf16[2,64,128]{2,1,0:T(8,128)(2,1)S(1)}, bf16[2,64,128]{2,1,0:T(8,128)(2,1)S(1)}, u32[]{:S(2)}, u32[]{:S(2)}) collective-permute-start(bf16[2,64,128]{2,1,0:T(8,128)(2,1)S(1)} %get-tuple-element.75), channel_id=1, source_target_pairs={{0,1},{1,0},{2,3},{3,2},{4,5},{5,4},{6,7},{7,6},{8,9},{9,8},{10,11... | collective-permute-start | bytes 98312 | tf_op jit(solution)/shard_map/ppermute | solution.py:86
  21.1 3.2 %collective-permute-start.11 = (bf16[4,64,128]{2,1,0:T(8,128)(2,1)S(1)}, bf16[4,64,128]{2,1,0:T(8,128)(2,1)S(1)}, u32[]{:S(2)}, u32[]{:S(2)}) collective-permute-start(bf16[4,64,128]{2,1,0:T(8,128)(2,1)S(1)} %get-tuple-element.73), channel_id=1, source_target_pairs={{0,1},{1,0},{2,3},{3,2},{4,5},{5,4},{6,7},{7,6},{8,20},{9,21},{10,... | collective-permute-start | bytes 196616 | tf_op jit(solution)/shard_map/ppermute | solution.py:86
  22.0 2.4 %collective-permute-start.13 = (bf16[2,64,128]{2,1,0:T(8,128)(2,1)S(1)}, bf16[2,64,128]{2,1,0:T(8,128)(2,1)S(1)}, u32[]{:S(2)}, u32[]{:S(2)}) collective-permute-start(bf16[2,64,128]{2,1,0:T(8,128)(2,1)S(1)} %shard_map.107), channel_id=1, source_target_pairs={{0,1},{1,0},{2,3},{3,2},{4,5},{5,4},{6,7},{7,6},{8,23},{9,18},{10,... | collective-permute-start | bytes 98312 | tf_op jit(solution)/shard_map/ppermute | solution.py:86
  22.3 4.3 %collective-permute-start.15 = (bf16[4,64,128]{2,1,0:T(8,128)(2,1)S(1)}, bf16[4,64,128]{2,1,0:T(8,128)(2,1)S(1)}, u32[]{:S(2)}, u32[]{:S(2)}) collective-permute-start(bf16[4,64,128]{2,1,0:T(8,128)(2,1)S(1)} %get-tuple-element.77), channel_id=1, source_target_pairs={{0,4},{1,6},{2,5},{3,7},{4,0},{5,2},{6,1},{7,3},{8,12},{9,14},{10,... | collective-permute-start | bytes 196616 | tf_op jit(solution)/shard_map/ppermute | solution.py:86
  23.4 4.7 %collective-permute-start.16 = (bf16[4,64,128]{2,1,0:T(8,128)(2,1)S(1)}, bf16[4,64,128]{2,1,0:T(8,128)(2,1)S(1)}, u32[]{:S(2)}, u32[]{:S(2)}) collective-permute-start(bf16[4,64,128]{2,1,0:T(8,128)(2,1)S(1)} %get-tuple-element.78), channel_id=1, source_target_pairs={{0,4},{1,2},{2,1},{3,7},{4,0},{5,6},{6,5},{7,3},{8,12},{9,10},{10,... | collective-permute-start | bytes 196616 | tf_op jit(solution)/shard_map/ppermute | solution.py:86
  24.4 3.6 %collective-permute-start.14 = (bf16[4,64,128]{2,1,0:T(8,128)(2,1)S(1)}, bf16[4,64,128]{2,1,0:T(8,128)(2,1)S(1)}, u32[]{:S(2)}, u32[]{:S(2)}) collective-permute-start(bf16[4,64,128]{2,1,0:T(8,128)(2,1)S(1)} %shard_map.108.refs_6_), channel_id=1, source_target_pairs={{0,1},{1,0},{2,3},{3,2},{4,5},{5,4},{6,7},{7,6},{8,9},{9,8},{10,11... | collective-permute-start | bytes 196616 | tf_op jit(solution)/shard_map/ppermute | solution.py:86
  28.0 12.0 %collective-permute-start.17 = (bf16[8,64,128]{2,1,0:T(8,128)(2,1)S(1)}, bf16[8,64,128]{2,1,0:T(8,128)(2,1)S(1)}, u32[]{:S(2)}, u32[]{:S(2)}) collective-permute-start(bf16[8,64,128]{2,1,0:T(8,128)(2,1)S(1)} %get-tuple-element.83.refs_11_.other_ref.refs_2_), channel_id=1, source_target_pairs={{0,8},{1,9},{2,10},{3,11},{4,12},{5,13},{6,14},{7,15},{8,0},{9,1},... | collective-permute-start | bytes 393224 | tf_op jit(solution)/shard_map/ppermute | solution.py:86
  33.3 1.2 %collective-permute-start.19 = (bf16[2,64,128]{2,1,0:T(8,128)(2,1)S(1)}, bf16[2,64,128]{2,1,0:T(8,128)(2,1)S(1)}, u32[]{:S(2)}, u32[]{:S(2)}) collective-permute-start(bf16[2,64,128]{2,1,0:T(8,128)(2,1)S(1)} %get-tuple-element.86), channel_id=1, source_target_pairs={{0,1},{1,0},{2,3},{3,2},{4,5},{5,4},{6,7},{7,6},{8,9},{9,8},{10,11... | collective-permute-start | bytes 98312 | tf_op jit(solution)/shard_map/ppermute | solution.py:86
  33.3 5.8 %collective-permute-start.18 = (bf16[4,64,128]{2,1,0:T(8,128)(2,1)S(1)}, bf16[4,64,128]{2,1,0:T(8,128)(2,1)S(1)}, u32[]{:S(2)}, u32[]{:S(2)}) collective-permute-start(bf16[4,64,128]{2,1,0:T(8,128)(2,1)S(1)} %get-tuple-element.84), channel_id=1, source_target_pairs={{0,12},{1,13},{2,14},{3,15},{4,8},{5,9},{6,10},{7,11},{8,4},{9,5},... | collective-permute-start | bytes 196616 | tf_op jit(solution)/shard_map/ppermute | solution.py:86
  34.5 5.5 %collective-permute-start.20 = (bf16[2,64,128]{2,1,0:T(8,128)(2,1)S(1)}, bf16[2,64,128]{2,1,0:T(8,128)(2,1)S(1)}, u32[]{:S(2)}, u32[]{:S(2)}) collective-permute-start(bf16[2,64,128]{2,1,0:T(8,128)(2,1)S(1)} %shard_map.112), channel_id=1, source_target_pairs={{0,15},{1,10},{2,9},{3,12},{4,11},{5,14},{6,13},{7,8},{8,7},{9,2},... | collective-permute-start | bytes 98312 | tf_op jit(solution)/shard_map/ppermute | solution.py:86
  35.8 4.8 %collective-permute-start.22 = (f32[128,128]{1,0:T(8,128)S(1)}, f32[128,128]{1,0:T(8,128)S(1)}, u32[]{:S(2)}, u32[]{:S(2)}) collective-permute-start(f32[128,128]{1,0:T(8,128)S(1)} %shard_map.115), channel_id=1, source_target_pairs={{0,8},{1,9},{2,10},{3,11},{4,12},{5,13},{6,14},{7,15},{8,0},{9,1},... | collective-permute-start | bytes 196616 | tf_op jit(solution)/shard_map/ppermute | solution.py:86
  40.0 1.3 %collective-permute-start.21 = (bf16[4,64,128]{2,1,0:T(8,128)(2,1)S(1)}, bf16[4,64,128]{2,1,0:T(8,128)(2,1)S(1)}, u32[]{:S(2)}, u32[]{:S(2)}) collective-permute-start(bf16[4,64,128]{2,1,0:T(8,128)(2,1)S(1)} %shard_map.113.refs_7_), channel_id=1, source_target_pairs={{0,1},{1,0},{2,3},{3,2},{4,5},{5,4},{6,7},{7,6},{8,9},{9,8},{10,11... | collective-permute-start | bytes 196616 | tf_op jit(solution)/shard_map/ppermute | solution.py:86
  41.5 5.5 %collective-permute-start.23 = (f32[2,8,128]{2,1,0:T(8,128)S(1)}, f32[2,8,128]{2,1,0:T(8,128)S(1)}, u32[]{:S(2)}, u32[]{:S(2)}) collective-permute-start(f32[2,8,128]{2,1,0:T(8,128)S(1)} %shard_map.118), channel_id=1, source_target_pairs={{0,24},{1,25},{2,26},{3,27},{4,28},{5,29},{6,30},{7,31},{8,16},{9,... | collective-permute-start | bytes 24584 | tf_op jit(solution)/shard_map/ppermute | solution.py:86
  43.8 4.5 %collective-permute-start.25 = (f32[8,128]{1,0:T(8,128)S(1)}, f32[8,128]{1,0:T(8,128)S(1)}, u32[]{:S(2)}, u32[]{:S(2)}) collective-permute-start(f32[8,128]{1,0:T(8,128)S(1)} %get-tuple-element.93.own_ref), channel_id=1, source_target_pairs={{0,16},{1,17},{2,18},{3,19},{4,20},{5,21},{6,22},{7,23},{8,24},{9,... | collective-permute-start | bytes 12296 | tf_op jit(solution)/shard_map/ppermute | solution.py:86
  44.3 4.0 %collective-permute-start.24 = (f32[8,128]{1,0:T(8,128)S(1)}, f32[8,128]{1,0:T(8,128)S(1)}, u32[]{:S(2)}, u32[]{:S(2)}) collective-permute-start(f32[8,128]{1,0:T(8,128)S(1)} %get-tuple-element.93.own_ref), channel_id=1, source_target_pairs={{0,8},{1,9},{2,10},{3,11},{4,12},{5,13},{6,14},{7,15},{8,0},{9,1},... | collective-permute-start | bytes 12296 | tf_op jit(solution)/shard_map/ppermute | solution.py:86

commit v9 on v8

--- a/solution.py
+++ b/solution.py
@@ -288,7 +288,6 @@
     )
 
     late_rims, late_sides = late[:halos], late[halos:]
-    late_rims = [to_layer(None, other_row(pairing))(part) for part, pairing in zip(late_rims, row_pairs)]
 
     def inner_only(beside, pairing):
         def target(l, r, c):
@@ -301,6 +300,7 @@
         for part, pairing in zip(late_sides[1:], row_pairs)
     ]
     late_sides = [permuted(late_sides[0], inner_only(lambda r, c: (r, far(c, cols)), near))] + late_corners
+    late_rims = [to_layer(None, other_row(pairing))(part) for part, pairing in zip(late_rims, row_pairs)]
     turn = layers // 2
 
     def waves(phase, kappa_ref):
@@ -468,13 +468,15 @@
         beyond = Side(far, "col", tiles_y)
 
         def corners():
+            totals = []
+            for h, pairing in enumerate(row_pairs):
+                corner = wave(bases[h], None if step == 0 else core_ref[ext + h], real[h])
+                totals.append(corner_product(beyond, pairing, front_ref, corner))
             if step == turn:
                 side = [wave(column_ref[x], carried_ref[x]) for x in range(tiles_x)]
-                for x, total in enumerate(column_products(beyond, front_ref, side)):
-                    sum_ref[x * tiles_y + beyond.edge] += total
-            for h, pairing in enumerate(row_pairs):
-                corner = wave(bases[h], None if step == 0 else core_ref[ext + h], real[h])
-                t, total = corner_product(beyond, pairing, front_ref, corner)
+                products = column_products(beyond, front_ref, side)
+                totals += [(x * tiles_y + beyond.edge, total) for x, total in enumerate(products)]
+            for t, total in totals:
                 sum_ref[t] += total
 
         beyond.when(corners)
@@ -489,7 +491,7 @@
         bases = corner_bases(step, take(1 if step < turn else halos))
         extra = take(2 if step == turn else 0)
         if step == 1:
-            take(halos)
+            take(halos + 1)
         sum_ref, corner_ref = take(), take()
 
         @pl.when(is_active(step))
@@ -584,7 +586,7 @@
                 core,
                 *base,
                 *([late_sides[0], field_arrived[1 + halos]] if step == turn else []),
-                *(late_rims if step == 1 else []),
+                *([*late_rims, late_sides[0]] if step == 1 else []),
                 aliases={0: 0},
             )
             corner = to_core(corner)

time: 48.5 us -> 48.4 us (level)
  waiting for transfers between devices: 14.9 us -> 13.5 us
  starting transfers between devices: 26.5 us -> 27.8 us
    ppermute x26, waiting for transfers between devices: 14.9 us -> 13.5 us  [permuted(): return lax.ppermute(array, AXES, pairs)]
    ppermute x26, starting transfers between devices: 26.5 us -> 27.8 us  [permuted(): return lax.ppermute(array, AXES, pairs)]
where the time goes in v9:
time: 48.4 us; the launch traced here: 48.2 us
  starting transfers between devices  27.8 us (57%)
  waiting for transfers between devices  13.5 us (28%)
  Pallas kernels  6.15 us (13%)
  between operations  0.77 us (2%)
    ppermute x26, starting transfers between devices, permuted(): return lax.ppermute(array, AXES, pairs)  27.8 us
    ppermute x26, waiting for transfers between devices, permuted(): return lax.ppermute(array, AXES, pairs)  13.5 us
    pallas_call x26, Pallas kernels, call(): pl.pallas_call(kernel, out_shape=[jax.ShapeDtypeStruct(shape, dtype) for...  6.14 us
  transfers between devices with their start and end apart: 26, of which 15 were waited for; matrix products, arithmetic and copies ran while one was open for 0% of the time, Pallas kernels for 10%

profile of v9, /device:TPU:0, one launch (start us, length us, event | category | flops | bytes accessed | tf_op | source)
XLA Modules:
  0.0 48.2 jit_solution(1093742688167533771)
XLA Ops:
  0.6 1.1 %shard_map.94 = (f32[2,512,128]{2,1,0:T(8,128)S(1)}, s32[1,64]{1,0:T(1,128)S(1)}, bf16[2,64,128]{2,1,0:T(8,128)(2,1)S(1)}) custom-call(bf16[64,8,128]{2,1,0:T(8,128)(2,1)} %bitcast.8, bf16[64,8,128]{2,1,0:T(8,128)(2,1)} %bitcast.9, s32[1,64]{1,0:T(1,128)} %bitcast.11), custom_call_target="tpu_custom_call" | custom-call | tf_op jit(solution)/shard_map/pallas_call | solution.py:23
  1.7 0.5 %collective-permute-start.1 = (bf16[2,64,128]{2,1,0:T(8,128)(2,1)S(1)}, bf16[2,64,128]{2,1,0:T(8,128)(2,1)S(1)}, u32[]{:S(2)}, u32[]{:S(2)}) collective-permute-start(bf16[2,64,128]{2,1,0:T(8,128)(2,1)S(1)} %get-tuple-element.55), channel_id=1, source_target_pairs={{0,1},{1,0},{2,3},{3,2},{4,5},{5,4},{6,7},{7,6},{8,9},{9,8},{10,11... | collective-permute-start | bytes 98312 | tf_op jit(solution)/shard_map/ppermute | solution.py:86
  2.3 0.2 shard_map.96
  2.4 2.6 %collective-permute-start = (bf16[4,64,128]{2,1,0:T(8,128)(2,1)S(1)}, bf16[4,64,128]{2,1,0:T(8,128)(2,1)S(1)}, u32[]{:S(2)}, u32[]{:S(2)}) collective-permute-start(bf16[4,64,128]{2,1,0:T(8,128)(2,1)S(1)} %get-tuple-element.53), channel_id=1, source_target_pairs={{0,4},{1,5},{2,6},{3,7},{4,0},{5,1},{6,2},{7,3},{8,12},{9,13},{10,... | collective-permute-start | bytes 196616 | tf_op jit(solution)/shard_map/ppermute | solution.py:86
  5.0 1.6 %collective-permute-start.2 = (bf16[2,64,128]{2,1,0:T(8,128)(2,1)S(1)}, bf16[2,64,128]{2,1,0:T(8,128)(2,1)S(1)}, u32[]{:S(2)}, u32[]{:S(2)}) collective-permute-start(bf16[2,64,128]{2,1,0:T(8,128)(2,1)S(1)} %shard_map.97), channel_id=1, source_target_pairs={{0,7},{1,2},{2,1},{3,4},{4,3},{5,6},{6,5},{7,0},{8,15},{9,10},{10,... | collective-permute-start | bytes 98312 | tf_op jit(solution)/shard_map/ppermute | solution.py:86
  6.7 1.9 %shard_map.95 = (bf16[2,8,64,128]{3,2,1,0:T(8,128)(2,1)S(1)}, bf16[8,9,128,128]{3,2,1,0:T(8,128)(2,1)S(1)}, f32[2,8,128]{2,1,0:T(8,128)S(1)}, f32[4,4,8,128]{3,2...) custom-call(s32[2,4,9]{2,1,0:T(4,128)} %bitcast.10, ...), custom_call_target="tpu_custom_call" | custom-call | tf_op jit(solution)/shard_map/pallas_call | solution.py:23
  8.6 0.9 %collective-permute-done.2.refs_3_ = bf16[2,64,128]{2,1,0:T(8,128)(2,1)S(1)} collective-permute-done((bf16[2,64,128]{2,1,0:T(8,128)(2,1)S(1)}, bf16[2,64,128]{2,1,0:T(8,128)(2,1)S(1)}, u32[]{:S(2)}, u32[]{:S(2)}) %collective-permute-start.2) | collective-permute-done | bytes 32800 | tf_op jit(solution)/shard_map/ppermute | solution.py:86
  9.5 0.1 collective-permute-start.3
  9.5 0.5 %shard_map.99 = (f32[8,64,128]{2,1,0:T(8,128)S(1)}, bf16[8,64,128]{2,1,0:T(8,128)(2,1)S(1)}, bf16[4,64,128]{2,1,0:T(8,128)(2,1)S(1)}, bf16[2,64,128]{2,1,0:T(8,128)(2,1)S(1)}) custom-call(bf16[2,8,64,128]{3,2,1,0:T(8,128)(2,1)S(1)} %get-tuple-element.51.refs_0_, f32[2,8,128]{2,1,0:T(8,128)S(1)} %get-tuple-element.52.refs_1_.refs_2_.refs_6_, ...), custom_call_target="tpu_custom_call" | custom-call | tf_op jit(solution)/shard_map/pallas_call | solution.py:23
  10.0 0.7 %collective-permute-done.3.refs_3_.refs_4_.refs_5_ = bf16[4,64,128]{2,1,0:T(8,128)(2,1)S(1)} collective-permute-done((bf16[4,64,128]{2,1,0:T(8,128)(2,1)S(1)}, bf16[4,64,128]{2,1,0:T(8,128)(2,1)S(1)}, u32[]{:S(2)}, u32[]{:S(2)}) %collective-permute-start.3) | collective-permute-done | bytes 65568 | tf_op jit(solution)/shard_map/ppermute | solution.py:86
  10.8 0.2 shard_map.101
  11.0 1.3 %collective-permute-start.4 = (bf16[8,64,128]{2,1,0:T(8,128)(2,1)S(1)}, bf16[8,64,128]{2,1,0:T(8,128)(2,1)S(1)}, u32[]{:S(2)}, u32[]{:S(2)}) collective-permute-start(bf16[8,64,128]{2,1,0:T(8,128)(2,1)S(1)} %get-tuple-element.62.refs_9_.refs_8_.refs_0_), channel_id=1, source_target_pairs={{0,8},{1,9},{2,10},{3,11},{4,12},{5,13},{6,14},{7,15},{8,0},{9,1},... | collective-permute-start | bytes 393224 | tf_op jit(solution)/shard_map/ppermute | solution.py:86
  12.3 1.3 %collective-permute-start.5 = (bf16[4,64,128]{2,1,0:T(8,128)(2,1)S(1)}, bf16[4,64,128]{2,1,0:T(8,128)(2,1)S(1)}, u32[]{:S(2)}, u32[]{:S(2)}) collective-permute-start(bf16[4,64,128]{2,1,0:T(8,128)(2,1)S(1)} %get-tuple-element.63), channel_id=1, source_target_pairs={{0,12},{1,13},{2,14},{3,15},{4,8},{5,9},{6,10},{7,11},{8,4},{9,5},... | collective-permute-start | bytes 196616 | tf_op jit(solution)/shard_map/ppermute | solution.py:86
  13.6 2.1 %collective-permute-start.7 = (bf16[2,64,128]{2,1,0:T(8,128)(2,1)S(1)}, bf16[2,64,128]{2,1,0:T(8,128)(2,1)S(1)}, u32[]{:S(2)}, u32[]{:S(2)}) collective-permute-start(bf16[2,64,128]{2,1,0:T(8,128)(2,1)S(1)} %shard_map.102), channel_id=1, source_target_pairs={{0,15},{1,10},{2,9},{3,12},{4,11},{5,14},{6,13},{7,8},{8,7},{9,2},... | collective-permute-start | bytes 98312 | tf_op jit(solution)/shard_map/ppermute | solution.py:86
  15.7 0.9 %collective-permute-start.9 = (bf16[4,64,128]{2,1,0:T(8,128)(2,1)S(1)}, bf16[4,64,128]{2,1,0:T(8,128)(2,1)S(1)}, u32[]{:S(2)}, u32[]{:S(2)}) collective-permute-start(bf16[4,64,128]{2,1,0:T(8,128)(2,1)S(1)} %get-tuple-element.67), channel_id=1, source_target_pairs={{0,4},{1,5},{2,6},{3,7},{4,0},{5,1},{6,2},{7,3},{8,12},{9,13},{10,... | collective-permute-start | bytes 196616 | tf_op jit(solution)/shard_map/ppermute | solution.py:86
  16.6 1.1 %collective-permute-start.10 = (bf16[4,64,128]{2,1,0:T(8,128)(2,1)S(1)}, bf16[4,64,128]{2,1,0:T(8,128)(2,1)S(1)}, u32[]{:S(2)}, u32[]{:S(2)}) collective-permute-start(bf16[4,64,128]{2,1,0:T(8,128)(2,1)S(1)} %get-tuple-element.68), channel_id=1, source_target_pairs={{0,4},{1,2},{2,1},{3,7},{4,0},{5,6},{6,5},{7,3},{8,12},{9,10},{10,... | collective-permute-start | bytes 196616 | tf_op jit(solution)/shard_map/ppermute | solution.py:86
  17.7 1.5 %collective-permute-done.5.refs_5_ = bf16[4,64,128]{2,1,0:T(8,128)(2,1)S(1)} collective-permute-done((bf16[4,64,128]{2,1,0:T(8,128)(2,1)S(1)}, bf16[4,64,128]{2,1,0:T(8,128)(2,1)S(1)}, u32[]{:S(2)}, u32[]{:S(2)}) %collective-permute-start.5) | collective-permute-done | bytes 65568 | tf_op jit(solution)/shard_map/ppermute | solution.py:86
  19.3 0.1 collective-permute-done.7.refs_6_
  19.3 0.0 collective-permute-start.8
  19.4 1.0 %collective-permute-done.9.refs_5_.refs_2_ = bf16[4,64,128]{2,1,0:T(8,128)(2,1)S(1)} collective-permute-done((bf16[4,64,128]{2,1,0:T(8,128)(2,1)S(1)}, bf16[4,64,128]{2,1,0:T(8,128)(2,1)S(1)}, u32[]{:S(2)}, u32[]{:S(2)}) %collective-permute-start.9) | collective-permute-done | bytes 65568 | tf_op jit(solution)/shard_map/ppermute | solution.py:86
  20.4 0.7 %collective-permute-done.10.refs_6_.refs_5_.refs_3_ = bf16[4,64,128]{2,1,0:T(8,128)(2,1)S(1)} collective-permute-done((bf16[4,64,128]{2,1,0:T(8,128)(2,1)S(1)}, bf16[4,64,128]{2,1,0:T(8,128)(2,1)S(1)}, u32[]{:S(2)}, u32[]{:S(2)}) %collective-permute-start.10) | collective-permute-done | bytes 65568 | tf_op jit(solution)/shard_map/ppermute | solution.py:86
  21.1 0.5 %collective-permute-start.13 = (bf16[2,64,128]{2,1,0:T(8,128)(2,1)S(1)}, bf16[2,64,128]{2,1,0:T(8,128)(2,1)S(1)}, u32[]{:S(2)}, u32[]{:S(2)}) collective-permute-start(bf16[2,64,128]{2,1,0:T(8,128)(2,1)S(1)} %get-tuple-element.76), channel_id=1, source_target_pairs={{0,1},{1,0},{2,3},{3,2},{4,5},{5,4},{6,7},{7,6},{8,9},{9,8},{10,11... | collective-permute-start | bytes 98312 | tf_op jit(solution)/shard_map/ppermute | solution.py:86
  21.6 0.1 collective-permute-start.12
  21.7 0.8 %collective-permute-done.13.refs_1_ = bf16[2,64,128]{2,1,0:T(8,128)(2,1)S(1)} collective-permute-done((bf16[2,64,128]{2,1,0:T(8,128)(2,1)S(1)}, bf16[2,64,128]{2,1,0:T(8,128)(2,1)S(1)}, u32[]{:S(2)}, u32[]{:S(2)}) %collective-permute-start.13) | collective-permute-done | bytes 32800 | tf_op jit(solution)/shard_map/ppermute | solution.py:86
  22.5 0.3 collective-permute-start.14
  22.9 1.0 %collective-permute-start.16 = (bf16[4,64,128]{2,1,0:T(8,128)(2,1)S(1)}, bf16[4,64,128]{2,1,0:T(8,128)(2,1)S(1)}, u32[]{:S(2)}, u32[]{:S(2)}) collective-permute-start(bf16[4,64,128]{2,1,0:T(8,128)(2,1)S(1)} %get-tuple-element.78), channel_id=1, source_target_pairs={{0,4},{1,6},{2,5},{3,7},{4,0},{5,2},{6,1},{7,3},{8,12},{9,14},{10,... | collective-permute-start | bytes 196616 | tf_op jit(solution)/shard_map/ppermute | solution.py:86
  23.9 0.4 collective-permute-start.15
  24.4 2.8 %collective-permute-done.16.refs_4_.refs_7_ = bf16[4,64,128]{2,1,0:T(8,128)(2,1)S(1)} collective-permute-done((bf16[4,64,128]{2,1,0:T(8,128)(2,1)S(1)}, bf16[4,64,128]{2,1,0:T(8,128)(2,1)S(1)}, u32[]{:S(2)}, u32[]{:S(2)}) %collective-permute-start.16) | collective-permute-done | bytes 65568 | tf_op jit(solution)/shard_map/ppermute | solution.py:86
  27.1 5.9 %collective-permute-start.17 = (bf16[8,64,128]{2,1,0:T(8,128)(2,1)S(1)}, bf16[8,64,128]{2,1,0:T(8,128)(2,1)S(1)}, u32[]{:S(2)}, u32[]{:S(2)}) collective-permute-start(bf16[8,64,128]{2,1,0:T(8,128)(2,1)S(1)} %get-tuple-element.83.refs_11_.other_ref.refs_2_), channel_id=1, source_target_pairs={{0,8},{1,9},{2,10},{3,11},{4,12},{5,13},{6,14},{7,15},{8,0},{9,1},... | collective-permute-start | bytes 393224 | tf_op jit(solution)/shard_map/ppermute | solution.py:86
  33.0 0.1 collective-permute-start.19
  33.1 0.8 %collective-permute-start.18 = (bf16[4,64,128]{2,1,0:T(8,128)(2,1)S(1)}, bf16[4,64,128]{2,1,0:T(8,128)(2,1)S(1)}, u32[]{:S(2)}, u32[]{:S(2)}) collective-permute-start(bf16[4,64,128]{2,1,0:T(8,128)(2,1)S(1)} %get-tuple-element.84), channel_id=1, source_target_pairs={{0,12},{1,13},{2,14},{3,15},{4,8},{5,9},{6,10},{7,11},{8,4},{9,5},... | collective-permute-start | bytes 196616 | tf_op jit(solution)/shard_map/ppermute | solution.py:86
  33.9 0.4 collective-permute-done.19.refs_1_
  34.2 1.7 %collective-permute-start.20 = (bf16[2,64,128]{2,1,0:T(8,128)(2,1)S(1)}, bf16[2,64,128]{2,1,0:T(8,128)(2,1)S(1)}, u32[]{:S(2)}, u32[]{:S(2)}) collective-permute-start(bf16[2,64,128]{2,1,0:T(8,128)(2,1)S(1)} %shard_map.112), channel_id=1, source_target_pairs={{0,15},{1,10},{2,9},{3,12},{4,11},{5,14},{6,13},{7,8},{8,7},{9,2},... | collective-permute-start | bytes 98312 | tf_op jit(solution)/shard_map/ppermute | solution.py:86
  36.0 0.9 %collective-permute-start.22 = (f32[128,128]{1,0:T(8,128)S(1)}, f32[128,128]{1,0:T(8,128)S(1)}, u32[]{:S(2)}, u32[]{:S(2)}) collective-permute-start(f32[128,128]{1,0:T(8,128)S(1)} %shard_map.115), channel_id=1, source_target_pairs={{0,8},{1,9},{2,10},{3,11},{4,12},{5,13},{6,14},{7,15},{8,0},{9,1},... | collective-permute-start | bytes 196616 | tf_op jit(solution)/shard_map/ppermute | solution.py:86
  36.8 2.3 %collective-permute-done.18.refs_5_ = bf16[4,64,128]{2,1,0:T(8,128)(2,1)S(1)} collective-permute-done((bf16[4,64,128]{2,1,0:T(8,128)(2,1)S(1)}, bf16[4,64,128]{2,1,0:T(8,128)(2,1)S(1)}, u32[]{:S(2)}, u32[]{:S(2)}) %collective-permute-start.18) | collective-permute-done | bytes 65568 | tf_op jit(solution)/shard_map/ppermute | solution.py:86
  39.1 0.5 %collective-permute-done.20.refs_6_ = bf16[2,64,128]{2,1,0:T(8,128)(2,1)S(1)} collective-permute-done((bf16[2,64,128]{2,1,0:T(8,128)(2,1)S(1)}, bf16[2,64,128]{2,1,0:T(8,128)(2,1)S(1)}, u32[]{:S(2)}, u32[]{:S(2)}) %collective-permute-start.20) | collective-permute-done | bytes 32800 | tf_op jit(solution)/shard_map/ppermute | solution.py:86
  39.7 0.1 collective-permute-start.21
  39.7 0.5 %shard_map.114 = (f32[8,64,128]{2,1,0:T(8,128)S(1)}, bf16[8,64,128]{2,1,0:T(8,128)(2,1)S(1)}, f32[8,128]{1,0:T(8,128)S(1)}) custom-call(bf16[2,8,64,128]{3,2,1,0:T(8,128)(2,1)S(1)} %get-tuple-element.51.refs_0_, f32[2,8,128]{2,1,0:T(8,128)S(1)} %get-tuple-element.52.refs_1_.refs_2_.refs_6_, bf16[4,64,128]{2,1,0:T(8,128)(2,1)S(1)} %collective-permute-done.9.refs_5_.refs_2_, ...), custom_call_target="tpu_custom_call" | custom-call | tf_op jit(solution)/shard_map/pallas_call | solution.py:23
  40.3 0.3 collective-permute-done.22.refs_5_.beside_ref
  40.6 0.4 collective-permute-done.21.refs_4_
  41.0 0.2 shard_map.116
  41.2 2.5 %collective-permute-start.23 = (f32[2,8,128]{2,1,0:T(8,128)S(1)}, f32[2,8,128]{2,1,0:T(8,128)S(1)}, u32[]{:S(2)}, u32[]{:S(2)}) collective-permute-start(f32[2,8,128]{2,1,0:T(8,128)S(1)} %shard_map.118), channel_id=1, source_target_pairs={{0,24},{1,25},{2,26},{3,27},{4,28},{5,29},{6,30},{7,31},{8,16},{9,... | collective-permute-start | bytes 24584 | tf_op jit(solution)/shard_map/ppermute | solution.py:86
  43.7 0.3 collective-permute-start.25
  44.0 1.6 %collective-permute-start.24 = (f32[8,128]{1,0:T(8,128)S(1)}, f32[8,128]{1,0:T(8,128)S(1)}, u32[]{:S(2)}, u32[]{:S(2)}) collective-permute-start(f32[8,128]{1,0:T(8,128)S(1)} %get-tuple-element.93.own_ref), channel_id=1, source_target_pairs={{0,8},{1,9},{2,10},{3,11},{4,12},{5,13},{6,14},{7,15},{8,0},{9,1},... | collective-permute-start | bytes 12296 | tf_op jit(solution)/shard_map/ppermute | solution.py:86
  45.6 0.8 %shard_map.117 = (bf16[64,8,128]{2,1,0:T(8,128)(2,1)}, bf16[64,8,128]{2,1,0:T(8,128)(2,1)}) custom-call(bf16[8,64,128]{2,1,0:T(8,128)(2,1)S(1)} %get-tuple-element.62.refs_9_.refs_8_.refs_0_, bf16[8,64,128]{2,1,0:T(8,128)(2,1)S(1)} %get-tuple-element.73.refs_10_.one_ref.refs_1_, bf16[8,64,128]{2,1,0:T(8,128)(2,1)S(1)} %get-tuple-element.83.refs_11_.other_ref.refs_2_, ...), custom_call_target="tpu_custom_call" | custom-call | tf_op jit(solution)/shard_map/pallas_call | solution.py:23
  46.5 0.2 collective-permute-done.23.across_ref
  46.7 0.6 %shard_map.119.ends_ref = f32[4,2,4,128]{3,2,1,0:T(4,128)} custom-call(f32[8,128]{1,0:T(8,128)S(1)} %get-tuple-element.93.own_ref, f32[128,128]{1,0:T(8,128)S(1)} %collective-permute-done.22.refs_5_.beside_ref, f32[2,8,128]{2,1,0:T(8,128)S(1)} %collective-permute-done.23.across_ref, f32[4,4,8,128]{3,2,1,0:T(8,128)S(1)} %get-tuple-element.94.member_ref), custom_call_target="tpu_custom_call" | custom-call | tf_op jit(solution)/shard_map/pallas_call | solution.py:23
  47.3 0.8 %collective-permute-done.25.other_ref = f32[8,128]{1,0:T(8,128)S(1)} collective-permute-done((f32[8,128]{1,0:T(8,128)S(1)}, f32[8,128]{1,0:T(8,128)S(1)}, u32[]{:S(2)}, u32[]{:S(2)}) %collective-permute-start.25) | collective-permute-done | bytes 4128 | tf_op jit(solution)/shard_map/ppermute | solution.py:86
  (31 shorter events, 0.1 us)
Async XLA Ops:
  1.7 3.3 %collective-permute-start.1 = (bf16[2,64,128]{2,1,0:T(8,128)(2,1)S(1)}, bf16[2,64,128]{2,1,0:T(8,128)(2,1)S(1)}, u32[]{:S(2)}, u32[]{:S(2)}) collective-permute-start(bf16[2,64,128]{2,1,0:T(8,128)(2,1)S(1)} %get-tuple-element.55), channel_id=1, source_target_pairs={{0,1},{1,0},{2,3},{3,2},{4,5},{5,4},{6,7},{7,6},{8,9},{9,8},{10,11... | collective-permute-start | bytes 98312 | tf_op jit(solution)/shard_map/ppermute | solution.py:86
  2.4 7.0 %collective-permute-start = (bf16[4,64,128]{2,1,0:T(8,128)(2,1)S(1)}, bf16[4,64,128]{2,1,0:T(8,128)(2,1)S(1)}, u32[]{:S(2)}, u32[]{:S(2)}) collective-permute-start(bf16[4,64,128]{2,1,0:T(8,128)(2,1)S(1)} %get-tuple-element.53), channel_id=1, source_target_pairs={{0,4},{1,5},{2,6},{3,7},{4,0},{5,1},{6,2},{7,3},{8,12},{9,13},{10,... | collective-permute-start | bytes 196616 | tf_op jit(solution)/shard_map/ppermute | solution.py:86
  5.0 4.4 %collective-permute-start.2 = (bf16[2,64,128]{2,1,0:T(8,128)(2,1)S(1)}, bf16[2,64,128]{2,1,0:T(8,128)(2,1)S(1)}, u32[]{:S(2)}, u32[]{:S(2)}) collective-permute-start(bf16[2,64,128]{2,1,0:T(8,128)(2,1)S(1)} %shard_map.97), channel_id=1, source_target_pairs={{0,7},{1,2},{2,1},{3,4},{4,3},{5,6},{6,5},{7,0},{8,15},{9,10},{10,... | collective-permute-start | bytes 98312 | tf_op jit(solution)/shard_map/ppermute | solution.py:86
  9.5 1.3 %collective-permute-start.3 = (bf16[4,64,128]{2,1,0:T(8,128)(2,1)S(1)}, bf16[4,64,128]{2,1,0:T(8,128)(2,1)S(1)}, u32[]{:S(2)}, u32[]{:S(2)}) collective-permute-start(bf16[4,64,128]{2,1,0:T(8,128)(2,1)S(1)} %shard_map.98.refs_4_), channel_id=1, source_target_pairs={{0,1},{1,0},{2,3},{3,2},{4,5},{5,4},{6,7},{7,6},{8,9},{9,8},{10,11... | collective-permute-start | bytes 196616 | tf_op jit(solution)/shard_map/ppermute | solution.py:86
  11.0 8.3 %collective-permute-start.4 = (bf16[8,64,128]{2,1,0:T(8,128)(2,1)S(1)}, bf16[8,64,128]{2,1,0:T(8,128)(2,1)S(1)}, u32[]{:S(2)}, u32[]{:S(2)}) collective-permute-start(bf16[8,64,128]{2,1,0:T(8,128)(2,1)S(1)} %get-tuple-element.62.refs_9_.refs_8_.refs_0_), channel_id=1, source_target_pairs={{0,8},{1,9},{2,10},{3,11},{4,12},{5,13},{6,14},{7,15},{8,0},{9,1},... | collective-permute-start | bytes 393224 | tf_op jit(solution)/shard_map/ppermute | solution.py:86
  12.3 1.3 %collective-permute-start.6 = (bf16[2,64,128]{2,1,0:T(8,128)(2,1)S(1)}, bf16[2,64,128]{2,1,0:T(8,128)(2,1)S(1)}, u32[]{:S(2)}, u32[]{:S(2)}) collective-permute-start(bf16[2,64,128]{2,1,0:T(8,128)(2,1)S(1)} %get-tuple-element.65), channel_id=1, source_target_pairs={{0,1},{1,0},{2,3},{3,2},{4,5},{5,4},{6,7},{7,6},{8,9},{9,8},{10,11... | collective-permute-start | bytes 98312 | tf_op jit(solution)/shard_map/ppermute | solution.py:86
  12.3 7.0 %collective-permute-start.5 = (bf16[4,64,128]{2,1,0:T(8,128)(2,1)S(1)}, bf16[4,64,128]{2,1,0:T(8,128)(2,1)S(1)}, u32[]{:S(2)}, u32[]{:S(2)}) collective-permute-start(bf16[4,64,128]{2,1,0:T(8,128)(2,1)S(1)} %get-tuple-element.63), channel_id=1, source_target_pairs={{0,12},{1,13},{2,14},{3,15},{4,8},{5,9},{6,10},{7,11},{8,4},{9,5},... | collective-permute-start | bytes 196616 | tf_op jit(solution)/shard_map/ppermute | solution.py:86
  13.6 5.7 %collective-permute-start.7 = (bf16[2,64,128]{2,1,0:T(8,128)(2,1)S(1)}, bf16[2,64,128]{2,1,0:T(8,128)(2,1)S(1)}, u32[]{:S(2)}, u32[]{:S(2)}) collective-permute-start(bf16[2,64,128]{2,1,0:T(8,128)(2,1)S(1)} %shard_map.102), channel_id=1, source_target_pairs={{0,15},{1,10},{2,9},{3,12},{4,11},{5,14},{6,13},{7,8},{8,7},{9,2},... | collective-permute-start | bytes 98312 | tf_op jit(solution)/shard_map/ppermute | solution.py:86
  15.7 4.7 %collective-permute-start.9 = (bf16[4,64,128]{2,1,0:T(8,128)(2,1)S(1)}, bf16[4,64,128]{2,1,0:T(8,128)(2,1)S(1)}, u32[]{:S(2)}, u32[]{:S(2)}) collective-permute-start(bf16[4,64,128]{2,1,0:T(8,128)(2,1)S(1)} %get-tuple-element.67), channel_id=1, source_target_pairs={{0,4},{1,5},{2,6},{3,7},{4,0},{5,1},{6,2},{7,3},{8,12},{9,13},{10,... | collective-permute-start | bytes 196616 | tf_op jit(solution)/shard_map/ppermute | solution.py:86
  16.6 4.6 %collective-permute-start.10 = (bf16[4,64,128]{2,1,0:T(8,128)(2,1)S(1)}, bf16[4,64,128]{2,1,0:T(8,128)(2,1)S(1)}, u32[]{:S(2)}, u32[]{:S(2)}) collective-permute-start(bf16[4,64,128]{2,1,0:T(8,128)(2,1)S(1)} %get-tuple-element.68), channel_id=1, source_target_pairs={{0,4},{1,2},{2,1},{3,7},{4,0},{5,6},{6,5},{7,3},{8,12},{9,10},{10,... | collective-permute-start | bytes 196616 | tf_op jit(solution)/shard_map/ppermute | solution.py:86
  19.3 1.8 %collective-permute-start.8 = (bf16[4,64,128]{2,1,0:T(8,128)(2,1)S(1)}, bf16[4,64,128]{2,1,0:T(8,128)(2,1)S(1)}, u32[]{:S(2)}, u32[]{:S(2)}) collective-permute-start(bf16[4,64,128]{2,1,0:T(8,128)(2,1)S(1)} %shard_map.103.refs_7_), channel_id=1, source_target_pairs={{0,1},{1,0},{2,3},{3,2},{4,5},{5,4},{6,7},{7,6},{8,9},{9,8},{10,11... | collective-permute-start | bytes 196616 | tf_op jit(solution)/shard_map/ppermute | solution.py:86
  21.1 2.8 %collective-permute-start.11 = (bf16[8,64,128]{2,1,0:T(8,128)(2,1)S(1)}, bf16[8,64,128]{2,1,0:T(8,128)(2,1)S(1)}, u32[]{:S(2)}, u32[]{:S(2)}) collective-permute-start(bf16[8,64,128]{2,1,0:T(8,128)(2,1)S(1)} %get-tuple-element.73.refs_10_.one_ref.refs_1_), channel_id=1, source_target_pairs={{0,1},{1,0},{2,3},{3,2},{4,5},{5,4},{6,7},{7,6},{8,16},{9,17},{10,... | collective-permute-start | bytes 393224 | tf_op jit(solution)/shard_map/ppermute | solution.py:86
  21.1 1.4 %collective-permute-start.13 = (bf16[2,64,128]{2,1,0:T(8,128)(2,1)S(1)}, bf16[2,64,128]{2,1,0:T(8,128)(2,1)S(1)}, u32[]{:S(2)}, u32[]{:S(2)}) collective-permute-start(bf16[2,64,128]{2,1,0:T(8,128)(2,1)S(1)} %get-tuple-element.76), channel_id=1, source_target_pairs={{0,1},{1,0},{2,3},{3,2},{4,5},{5,4},{6,7},{7,6},{8,9},{9,8},{10,11... | collective-permute-start | bytes 98312 | tf_op jit(solution)/shard_map/ppermute | solution.py:86
  21.6 2.3 %collective-permute-start.12 = (bf16[4,64,128]{2,1,0:T(8,128)(2,1)S(1)}, bf16[4,64,128]{2,1,0:T(8,128)(2,1)S(1)}, u32[]{:S(2)}, u32[]{:S(2)}) collective-permute-start(bf16[4,64,128]{2,1,0:T(8,128)(2,1)S(1)} %get-tuple-element.74), channel_id=1, source_target_pairs={{0,1},{1,0},{2,3},{3,2},{4,5},{5,4},{6,7},{7,6},{8,20},{9,21},{10,... | collective-permute-start | bytes 196616 | tf_op jit(solution)/shard_map/ppermute | solution.py:86
  22.5 1.4 %collective-permute-start.14 = (bf16[2,64,128]{2,1,0:T(8,128)(2,1)S(1)}, bf16[2,64,128]{2,1,0:T(8,128)(2,1)S(1)}, u32[]{:S(2)}, u32[]{:S(2)}) collective-permute-start(bf16[2,64,128]{2,1,0:T(8,128)(2,1)S(1)} %shard_map.107), channel_id=1, source_target_pairs={{0,1},{1,0},{2,3},{3,2},{4,5},{5,4},{6,7},{7,6},{8,23},{9,18},{10,... | collective-permute-start | bytes 98312 | tf_op jit(solution)/shard_map/ppermute | solution.py:86
  22.9 4.3 %collective-permute-start.16 = (bf16[4,64,128]{2,1,0:T(8,128)(2,1)S(1)}, bf16[4,64,128]{2,1,0:T(8,128)(2,1)S(1)}, u32[]{:S(2)}, u32[]{:S(2)}) collective-permute-start(bf16[4,64,128]{2,1,0:T(8,128)(2,1)S(1)} %get-tuple-element.78), channel_id=1, source_target_pairs={{0,4},{1,6},{2,5},{3,7},{4,0},{5,2},{6,1},{7,3},{8,12},{9,14},{10,... | collective-permute-start | bytes 196616 | tf_op jit(solution)/shard_map/ppermute | solution.py:86
  23.9 3.2 %collective-permute-start.15 = (bf16[4,64,128]{2,1,0:T(8,128)(2,1)S(1)}, bf16[4,64,128]{2,1,0:T(8,128)(2,1)S(1)}, u32[]{:S(2)}, u32[]{:S(2)}) collective-permute-start(bf16[4,64,128]{2,1,0:T(8,128)(2,1)S(1)} %shard_map.108.refs_6_), channel_id=1, source_target_pairs={{0,1},{1,0},{2,3},{3,2},{4,5},{5,4},{6,7},{7,6},{8,9},{9,8},{10,11... | collective-permute-start | bytes 196616 | tf_op jit(solution)/shard_map/ppermute | solution.py:86
  27.1 12.5 %collective-permute-start.17 = (bf16[8,64,128]{2,1,0:T(8,128)(2,1)S(1)}, bf16[8,64,128]{2,1,0:T(8,128)(2,1)S(1)}, u32[]{:S(2)}, u32[]{:S(2)}) collective-permute-start(bf16[8,64,128]{2,1,0:T(8,128)(2,1)S(1)} %get-tuple-element.83.refs_11_.other_ref.refs_2_), channel_id=1, source_target_pairs={{0,8},{1,9},{2,10},{3,11},{4,12},{5,13},{6,14},{7,15},{8,0},{9,1},... | collective-permute-start | bytes 393224 | tf_op jit(solution)/shard_map/ppermute | solution.py:86
  33.0 1.2 %collective-permute-start.19 = (bf16[2,64,128]{2,1,0:T(8,128)(2,1)S(1)}, bf16[2,64,128]{2,1,0:T(8,128)(2,1)S(1)}, u32[]{:S(2)}, u32[]{:S(2)}) collective-permute-start(bf16[2,64,128]{2,1,0:T(8,128)(2,1)S(1)} %get-tuple-element.86), channel_id=1, source_target_pairs={{0,1},{1,0},{2,3},{3,2},{4,5},{5,4},{6,7},{7,6},{8,9},{9,8},{10,11... | collective-permute-start | bytes 98312 | tf_op jit(solution)/shard_map/ppermute | solution.py:86
  33.1 6.0 %collective-permute-start.18 = (bf16[4,64,128]{2,1,0:T(8,128)(2,1)S(1)}, bf16[4,64,128]{2,1,0:T(8,128)(2,1)S(1)}, u32[]{:S(2)}, u32[]{:S(2)}) collective-permute-start(bf16[4,64,128]{2,1,0:T(8,128)(2,1)S(1)} %get-tuple-element.84), channel_id=1, source_target_pairs={{0,12},{1,13},{2,14},{3,15},{4,8},{5,9},{6,10},{7,11},{8,4},{9,5},... | collective-permute-start | bytes 196616 | tf_op jit(solution)/shard_map/ppermute | solution.py:86
  34.2 5.4 %collective-permute-start.20 = (bf16[2,64,128]{2,1,0:T(8,128)(2,1)S(1)}, bf16[2,64,128]{2,1,0:T(8,128)(2,1)S(1)}, u32[]{:S(2)}, u32[]{:S(2)}) collective-permute-start(bf16[2,64,128]{2,1,0:T(8,128)(2,1)S(1)} %shard_map.112), channel_id=1, source_target_pairs={{0,15},{1,10},{2,9},{3,12},{4,11},{5,14},{6,13},{7,8},{8,7},{9,2},... | collective-permute-start | bytes 98312 | tf_op jit(solution)/shard_map/ppermute | solution.py:86
  36.0 4.6 %collective-permute-start.22 = (f32[128,128]{1,0:T(8,128)S(1)}, f32[128,128]{1,0:T(8,128)S(1)}, u32[]{:S(2)}, u32[]{:S(2)}) collective-permute-start(f32[128,128]{1,0:T(8,128)S(1)} %shard_map.115), channel_id=1, source_target_pairs={{0,8},{1,9},{2,10},{3,11},{4,12},{5,13},{6,14},{7,15},{8,0},{9,1},... | collective-permute-start | bytes 196616 | tf_op jit(solution)/shard_map/ppermute | solution.py:86
  39.7 1.3 %collective-permute-start.21 = (bf16[4,64,128]{2,1,0:T(8,128)(2,1)S(1)}, bf16[4,64,128]{2,1,0:T(8,128)(2,1)S(1)}, u32[]{:S(2)}, u32[]{:S(2)}) collective-permute-start(bf16[4,64,128]{2,1,0:T(8,128)(2,1)S(1)} %shard_map.113.refs_7_), channel_id=1, source_target_pairs={{0,1},{1,0},{2,3},{3,2},{4,5},{5,4},{6,7},{7,6},{8,9},{9,8},{10,11... | collective-permute-start | bytes 196616 | tf_op jit(solution)/shard_map/ppermute | solution.py:86
  41.2 5.5 %collective-permute-start.23 = (f32[2,8,128]{2,1,0:T(8,128)S(1)}, f32[2,8,128]{2,1,0:T(8,128)S(1)}, u32[]{:S(2)}, u32[]{:S(2)}) collective-permute-start(f32[2,8,128]{2,1,0:T(8,128)S(1)} %shard_map.118), channel_id=1, source_target_pairs={{0,24},{1,25},{2,26},{3,27},{4,28},{5,29},{6,30},{7,31},{8,16},{9,... | collective-permute-start | bytes 24584 | tf_op jit(solution)/shard_map/ppermute | solution.py:86
  43.7 4.5 %collective-permute-start.25 = (f32[8,128]{1,0:T(8,128)S(1)}, f32[8,128]{1,0:T(8,128)S(1)}, u32[]{:S(2)}, u32[]{:S(2)}) collective-permute-start(f32[8,128]{1,0:T(8,128)S(1)} %get-tuple-element.93.own_ref), channel_id=1, source_target_pairs={{0,16},{1,17},{2,18},{3,19},{4,20},{5,21},{6,22},{7,23},{8,24},{9,... | collective-permute-start | bytes 12296 | tf_op jit(solution)/shard_map/ppermute | solution.py:86
  44.0 4.2 %collective-permute-start.24 = (f32[8,128]{1,0:T(8,128)S(1)}, f32[8,128]{1,0:T(8,128)S(1)}, u32[]{:S(2)}, u32[]{:S(2)}) collective-permute-start(f32[8,128]{1,0:T(8,128)S(1)} %get-tuple-element.93.own_ref), channel_id=1, source_target_pairs={{0,8},{1,9},{2,10},{3,11},{4,12},{5,13},{6,14},{7,15},{8,0},{9,1},... | collective-permute-start | bytes 12296 | tf_op jit(solution)/shard_map/ppermute | solution.py:86

commit v10 on v9

--- a/solution.py
+++ b/solution.py
@@ -518,11 +518,11 @@
             if last:
                 add_far_corners(step, sum_ref, front_ref, kappa_ref, core_ref, bases)
             across, beyond = Side(near, "col", tiles_y), Side(far, "col", tiles_y)
-            totals = column_products(across, front_ref, core_ref)
             corners = [
                 corner_product(across, pairing, front_ref, core_ref[tiles_x + h])[1]
                 for h, pairing in enumerate(row_pairs)
             ]
+            totals = column_products(across, front_ref, core_ref)
             edges = [Side(pairing, "row", tiles_x).edge for pairing in row_pairs]
             for x, total in enumerate(totals):
                 t = x * tiles_y + across.edge

time: 48.4 us -> 48.4 us (level)
  no operation moved by 1% of the time
where the time goes in v10:
time: 48.4 us; the launch traced here: 48.2 us
  starting transfers between devices  27.8 us (57%)
  waiting for transfers between devices  13.5 us (28%)
  Pallas kernels  6.17 us (13%)
  between operations  0.78 us (2%)
    ppermute x26, starting transfers between devices, permuted(): return lax.ppermute(array, AXES, pairs)  27.8 us
    ppermute x26, waiting for transfers between devices, permuted(): return lax.ppermute(array, AXES, pairs)  13.5 us
    pallas_call x26, Pallas kernels, call(): pl.pallas_call(kernel, out_shape=[jax.ShapeDtypeStruct(shape, dtype) for...  6.16 us
  transfers between devices with their start and end apart: 26, of which 15 were waited for; matrix products, arithmetic and copies ran while one was open for 0% of the time, Pallas kernels for 10%

profile of v10, /device:TPU:0, one launch (start us, length us, event | category | flops | bytes accessed | tf_op | source)
XLA Modules:
  0.0 48.2 jit_solution(12365421759512246949)
XLA Ops:
  0.6 1.1 %shard_map.94 = (f32[2,512,128]{2,1,0:T(8,128)S(1)}, s32[1,64]{1,0:T(1,128)S(1)}, bf16[2,64,128]{2,1,0:T(8,128)(2,1)S(1)}) custom-call(bf16[64,8,128]{2,1,0:T(8,128)(2,1)} %bitcast.8, bf16[64,8,128]{2,1,0:T(8,128)(2,1)} %bitcast.9, s32[1,64]{1,0:T(1,128)} %bitcast.11), custom_call_target="tpu_custom_call" | custom-call | tf_op jit(solution)/shard_map/pallas_call | solution.py:23
  1.7 0.5 %collective-permute-start.1 = (bf16[2,64,128]{2,1,0:T(8,128)(2,1)S(1)}, bf16[2,64,128]{2,1,0:T(8,128)(2,1)S(1)}, u32[]{:S(2)}, u32[]{:S(2)}) collective-permute-start(bf16[2,64,128]{2,1,0:T(8,128)(2,1)S(1)} %get-tuple-element.55), channel_id=1, source_target_pairs={{0,1},{1,0},{2,3},{3,2},{4,5},{5,4},{6,7},{7,6},{8,9},{9,8},{10,11... | collective-permute-start | bytes 98312 | tf_op jit(solution)/shard_map/ppermute | solution.py:86
  2.3 0.2 shard_map.96
  2.4 2.6 %collective-permute-start = (bf16[4,64,128]{2,1,0:T(8,128)(2,1)S(1)}, bf16[4,64,128]{2,1,0:T(8,128)(2,1)S(1)}, u32[]{:S(2)}, u32[]{:S(2)}) collective-permute-start(bf16[4,64,128]{2,1,0:T(8,128)(2,1)S(1)} %get-tuple-element.53), channel_id=1, source_target_pairs={{0,4},{1,5},{2,6},{3,7},{4,0},{5,1},{6,2},{7,3},{8,12},{9,13},{10,... | collective-permute-start | bytes 196616 | tf_op jit(solution)/shard_map/ppermute | solution.py:86
  5.0 1.6 %collective-permute-start.2 = (bf16[2,64,128]{2,1,0:T(8,128)(2,1)S(1)}, bf16[2,64,128]{2,1,0:T(8,128)(2,1)S(1)}, u32[]{:S(2)}, u32[]{:S(2)}) collective-permute-start(bf16[2,64,128]{2,1,0:T(8,128)(2,1)S(1)} %shard_map.97), channel_id=1, source_target_pairs={{0,7},{1,2},{2,1},{3,4},{4,3},{5,6},{6,5},{7,0},{8,15},{9,10},{10,... | collective-permute-start | bytes 98312 | tf_op jit(solution)/shard_map/ppermute | solution.py:86
  6.7 1.9 %shard_map.95 = (bf16[2,8,64,128]{3,2,1,0:T(8,128)(2,1)S(1)}, bf16[8,9,128,128]{3,2,1,0:T(8,128)(2,1)S(1)}, f32[2,8,128]{2,1,0:T(8,128)S(1)}, f32[4,4,8,128]{3,2...) custom-call(s32[2,4,9]{2,1,0:T(4,128)} %bitcast.10, ...), custom_call_target="tpu_custom_call" | custom-call | tf_op jit(solution)/shard_map/pallas_call | solution.py:23
  8.6 0.9 %collective-permute-done.2.refs_3_ = bf16[2,64,128]{2,1,0:T(8,128)(2,1)S(1)} collective-permute-done((bf16[2,64,128]{2,1,0:T(8,128)(2,1)S(1)}, bf16[2,64,128]{2,1,0:T(8,128)(2,1)S(1)}, u32[]{:S(2)}, u32[]{:S(2)}) %collective-permute-start.2) | collective-permute-done | bytes 32800 | tf_op jit(solution)/shard_map/ppermute | solution.py:86
  9.5 0.1 collective-permute-start.3
  9.5 0.5 %shard_map.99 = (f32[8,64,128]{2,1,0:T(8,128)S(1)}, bf16[8,64,128]{2,1,0:T(8,128)(2,1)S(1)}, bf16[4,64,128]{2,1,0:T(8,128)(2,1)S(1)}, bf16[2,64,128]{2,1,0:T(8,128)(2,1)S(1)}) custom-call(bf16[2,8,64,128]{3,2,1,0:T(8,128)(2,1)S(1)} %get-tuple-element.51.refs_0_, f32[2,8,128]{2,1,0:T(8,128)S(1)} %get-tuple-element.52.refs_1_.refs_2_.refs_6_, ...), custom_call_target="tpu_custom_call" | custom-call | tf_op jit(solution)/shard_map/pallas_call | solution.py:23
  10.0 0.7 %collective-permute-done.3.refs_3_.refs_4_.refs_5_ = bf16[4,64,128]{2,1,0:T(8,128)(2,1)S(1)} collective-permute-done((bf16[4,64,128]{2,1,0:T(8,128)(2,1)S(1)}, bf16[4,64,128]{2,1,0:T(8,128)(2,1)S(1)}, u32[]{:S(2)}, u32[]{:S(2)}) %collective-permute-start.3) | collective-permute-done | bytes 65568 | tf_op jit(solution)/shard_map/ppermute | solution.py:86
  10.8 0.2 shard_map.101
  11.0 1.3 %collective-permute-start.4 = (bf16[8,64,128]{2,1,0:T(8,128)(2,1)S(1)}, bf16[8,64,128]{2,1,0:T(8,128)(2,1)S(1)}, u32[]{:S(2)}, u32[]{:S(2)}) collective-permute-start(bf16[8,64,128]{2,1,0:T(8,128)(2,1)S(1)} %get-tuple-element.62.refs_9_.refs_8_.refs_0_), channel_id=1, source_target_pairs={{0,8},{1,9},{2,10},{3,11},{4,12},{5,13},{6,14},{7,15},{8,0},{9,1},... | collective-permute-start | bytes 393224 | tf_op jit(solution)/shard_map/ppermute | solution.py:86
  12.3 1.3 %collective-permute-start.5 = (bf16[4,64,128]{2,1,0:T(8,128)(2,1)S(1)}, bf16[4,64,128]{2,1,0:T(8,128)(2,1)S(1)}, u32[]{:S(2)}, u32[]{:S(2)}) collective-permute-start(bf16[4,64,128]{2,1,0:T(8,128)(2,1)S(1)} %get-tuple-element.63), channel_id=1, source_target_pairs={{0,12},{1,13},{2,14},{3,15},{4,8},{5,9},{6,10},{7,11},{8,4},{9,5},... | collective-permute-start | bytes 196616 | tf_op jit(solution)/shard_map/ppermute | solution.py:86
  13.6 2.1 %collective-permute-start.7 = (bf16[2,64,128]{2,1,0:T(8,128)(2,1)S(1)}, bf16[2,64,128]{2,1,0:T(8,128)(2,1)S(1)}, u32[]{:S(2)}, u32[]{:S(2)}) collective-permute-start(bf16[2,64,128]{2,1,0:T(8,128)(2,1)S(1)} %shard_map.102), channel_id=1, source_target_pairs={{0,15},{1,10},{2,9},{3,12},{4,11},{5,14},{6,13},{7,8},{8,7},{9,2},... | collective-permute-start | bytes 98312 | tf_op jit(solution)/shard_map/ppermute | solution.py:86
  15.7 0.9 %collective-permute-start.9 = (bf16[4,64,128]{2,1,0:T(8,128)(2,1)S(1)}, bf16[4,64,128]{2,1,0:T(8,128)(2,1)S(1)}, u32[]{:S(2)}, u32[]{:S(2)}) collective-permute-start(bf16[4,64,128]{2,1,0:T(8,128)(2,1)S(1)} %get-tuple-element.67), channel_id=1, source_target_pairs={{0,4},{1,5},{2,6},{3,7},{4,0},{5,1},{6,2},{7,3},{8,12},{9,13},{10,... | collective-permute-start | bytes 196616 | tf_op jit(solution)/shard_map/ppermute | solution.py:86
  16.6 1.1 %collective-permute-start.10 = (bf16[4,64,128]{2,1,0:T(8,128)(2,1)S(1)}, bf16[4,64,128]{2,1,0:T(8,128)(2,1)S(1)}, u32[]{:S(2)}, u32[]{:S(2)}) collective-permute-start(bf16[4,64,128]{2,1,0:T(8,128)(2,1)S(1)} %get-tuple-element.68), channel_id=1, source_target_pairs={{0,4},{1,2},{2,1},{3,7},{4,0},{5,6},{6,5},{7,3},{8,12},{9,10},{10,... | collective-permute-start | bytes 196616 | tf_op jit(solution)/shard_map/ppermute | solution.py:86
  17.7 1.5 %collective-permute-done.5.refs_5_ = bf16[4,64,128]{2,1,0:T(8,128)(2,1)S(1)} collective-permute-done((bf16[4,64,128]{2,1,0:T(8,128)(2,1)S(1)}, bf16[4,64,128]{2,1,0:T(8,128)(2,1)S(1)}, u32[]{:S(2)}, u32[]{:S(2)}) %collective-permute-start.5) | collective-permute-done | bytes 65568 | tf_op jit(solution)/shard_map/ppermute | solution.py:86
  19.3 0.1 collective-permute-done.7.refs_6_
  19.3 0.0 collective-permute-start.8
  19.4 1.0 %collective-permute-done.9.refs_5_.refs_2_ = bf16[4,64,128]{2,1,0:T(8,128)(2,1)S(1)} collective-permute-done((bf16[4,64,128]{2,1,0:T(8,128)(2,1)S(1)}, bf16[4,64,128]{2,1,0:T(8,128)(2,1)S(1)}, u32[]{:S(2)}, u32[]{:S(2)}) %collective-permute-start.9) | collective-permute-done | bytes 65568 | tf_op jit(solution)/shard_map/ppermute | solution.py:86
  20.4 0.7 %collective-permute-done.10.refs_6_.refs_5_.refs_3_ = bf16[4,64,128]{2,1,0:T(8,128)(2,1)S(1)} collective-permute-done((bf16[4,64,128]{2,1,0:T(8,128)(2,1)S(1)}, bf16[4,64,128]{2,1,0:T(8,128)(2,1)S(1)}, u32[]{:S(2)}, u32[]{:S(2)}) %collective-permute-start.10) | collective-permute-done | bytes 65568 | tf_op jit(solution)/shard_map/ppermute | solution.py:86
  21.2 0.5 %collective-permute-start.13 = (bf16[2,64,128]{2,1,0:T(8,128)(2,1)S(1)}, bf16[2,64,128]{2,1,0:T(8,128)(2,1)S(1)}, u32[]{:S(2)}, u32[]{:S(2)}) collective-permute-start(bf16[2,64,128]{2,1,0:T(8,128)(2,1)S(1)} %get-tuple-element.76), channel_id=1, source_target_pairs={{0,1},{1,0},{2,3},{3,2},{4,5},{5,4},{6,7},{7,6},{8,9},{9,8},{10,11... | collective-permute-start | bytes 98312 | tf_op jit(solution)/shard_map/ppermute | solution.py:86
  21.7 0.1 collective-permute-start.12
  21.7 0.8 %collective-permute-done.13.refs_1_ = bf16[2,64,128]{2,1,0:T(8,128)(2,1)S(1)} collective-permute-done((bf16[2,64,128]{2,1,0:T(8,128)(2,1)S(1)}, bf16[2,64,128]{2,1,0:T(8,128)(2,1)S(1)}, u32[]{:S(2)}, u32[]{:S(2)}) %collective-permute-start.13) | collective-permute-done | bytes 32800 | tf_op jit(solution)/shard_map/ppermute | solution.py:86
  22.5 0.3 collective-permute-start.14
  22.9 1.0 %collective-permute-start.16 = (bf16[4,64,128]{2,1,0:T(8,128)(2,1)S(1)}, bf16[4,64,128]{2,1,0:T(8,128)(2,1)S(1)}, u32[]{:S(2)}, u32[]{:S(2)}) collective-permute-start(bf16[4,64,128]{2,1,0:T(8,128)(2,1)S(1)} %get-tuple-element.78), channel_id=1, source_target_pairs={{0,4},{1,6},{2,5},{3,7},{4,0},{5,2},{6,1},{7,3},{8,12},{9,14},{10,... | collective-permute-start | bytes 196616 | tf_op jit(solution)/shard_map/ppermute | solution.py:86
  24.0 0.4 collective-permute-start.15
  24.4 2.8 %collective-permute-done.16.refs_4_.refs_7_ = bf16[4,64,128]{2,1,0:T(8,128)(2,1)S(1)} collective-permute-done((bf16[4,64,128]{2,1,0:T(8,128)(2,1)S(1)}, bf16[4,64,128]{2,1,0:T(8,128)(2,1)S(1)}, u32[]{:S(2)}, u32[]{:S(2)}) %collective-permute-start.16) | collective-permute-done | bytes 65568 | tf_op jit(solution)/shard_map/ppermute | solution.py:86
  27.2 5.9 %collective-permute-start.17 = (bf16[8,64,128]{2,1,0:T(8,128)(2,1)S(1)}, bf16[8,64,128]{2,1,0:T(8,128)(2,1)S(1)}, u32[]{:S(2)}, u32[]{:S(2)}) collective-permute-start(bf16[8,64,128]{2,1,0:T(8,128)(2,1)S(1)} %get-tuple-element.83.refs_11_.other_ref.refs_2_), channel_id=1, source_target_pairs={{0,8},{1,9},{2,10},{3,11},{4,12},{5,13},{6,14},{7,15},{8,0},{9,1},... | collective-permute-start | bytes 393224 | tf_op jit(solution)/shard_map/ppermute | solution.py:86
  33.1 0.1 collective-permute-start.19
  33.1 0.7 %collective-permute-start.18 = (bf16[4,64,128]{2,1,0:T(8,128)(2,1)S(1)}, bf16[4,64,128]{2,1,0:T(8,128)(2,1)S(1)}, u32[]{:S(2)}, u32[]{:S(2)}) collective-permute-start(bf16[4,64,128]{2,1,0:T(8,128)(2,1)S(1)} %get-tuple-element.84), channel_id=1, source_target_pairs={{0,12},{1,13},{2,14},{3,15},{4,8},{5,9},{6,10},{7,11},{8,4},{9,5},... | collective-permute-start | bytes 196616 | tf_op jit(solution)/shard_map/ppermute | solution.py:86
  33.9 0.4 collective-permute-done.19.refs_1_
  34.3 1.7 %collective-permute-start.20 = (bf16[2,64,128]{2,1,0:T(8,128)(2,1)S(1)}, bf16[2,64,128]{2,1,0:T(8,128)(2,1)S(1)}, u32[]{:S(2)}, u32[]{:S(2)}) collective-permute-start(bf16[2,64,128]{2,1,0:T(8,128)(2,1)S(1)} %shard_map.112), channel_id=1, source_target_pairs={{0,15},{1,10},{2,9},{3,12},{4,11},{5,14},{6,13},{7,8},{8,7},{9,2},... | collective-permute-start | bytes 98312 | tf_op jit(solution)/shard_map/ppermute | solution.py:86
  36.0 0.9 %collective-permute-start.22 = (f32[128,128]{1,0:T(8,128)S(1)}, f32[128,128]{1,0:T(8,128)S(1)}, u32[]{:S(2)}, u32[]{:S(2)}) collective-permute-start(f32[128,128]{1,0:T(8,128)S(1)} %shard_map.115), channel_id=1, source_target_pairs={{0,8},{1,9},{2,10},{3,11},{4,12},{5,13},{6,14},{7,15},{8,0},{9,1},... | collective-permute-start | bytes 196616 | tf_op jit(solution)/shard_map/ppermute | solution.py:86
  36.9 2.3 %collective-permute-done.18.refs_5_ = bf16[4,64,128]{2,1,0:T(8,128)(2,1)S(1)} collective-permute-done((bf16[4,64,128]{2,1,0:T(8,128)(2,1)S(1)}, bf16[4,64,128]{2,1,0:T(8,128)(2,1)S(1)}, u32[]{:S(2)}, u32[]{:S(2)}) %collective-permute-start.18) | collective-permute-done | bytes 65568 | tf_op jit(solution)/shard_map/ppermute | solution.py:86
  39.2 0.5 %collective-permute-done.20.refs_6_ = bf16[2,64,128]{2,1,0:T(8,128)(2,1)S(1)} collective-permute-done((bf16[2,64,128]{2,1,0:T(8,128)(2,1)S(1)}, bf16[2,64,128]{2,1,0:T(8,128)(2,1)S(1)}, u32[]{:S(2)}, u32[]{:S(2)}) %collective-permute-start.20) | collective-permute-done | bytes 32800 | tf_op jit(solution)/shard_map/ppermute | solution.py:86
  39.7 0.1 collective-permute-start.21
  39.8 0.5 %shard_map.114 = (f32[8,64,128]{2,1,0:T(8,128)S(1)}, bf16[8,64,128]{2,1,0:T(8,128)(2,1)S(1)}, f32[8,128]{1,0:T(8,128)S(1)}) custom-call(bf16[2,8,64,128]{3,2,1,0:T(8,128)(2,1)S(1)} %get-tuple-element.51.refs_0_, f32[2,8,128]{2,1,0:T(8,128)S(1)} %get-tuple-element.52.refs_1_.refs_2_.refs_6_, bf16[4,64,128]{2,1,0:T(8,128)(2,1)S(1)} %collective-permute-done.9.refs_5_.refs_2_, ...), custom_call_target="tpu_custom_call" | custom-call | tf_op jit(solution)/shard_map/pallas_call | solution.py:23
  40.3 0.3 collective-permute-done.22.refs_5_.beside_ref
  40.6 0.4 collective-permute-done.21.refs_4_
  41.0 0.2 shard_map.116
  41.2 2.5 %collective-permute-start.23 = (f32[2,8,128]{2,1,0:T(8,128)S(1)}, f32[2,8,128]{2,1,0:T(8,128)S(1)}, u32[]{:S(2)}, u32[]{:S(2)}) collective-permute-start(f32[2,8,128]{2,1,0:T(8,128)S(1)} %shard_map.118), channel_id=1, source_target_pairs={{0,24},{1,25},{2,26},{3,27},{4,28},{5,29},{6,30},{7,31},{8,16},{9,... | collective-permute-start | bytes 24584 | tf_op jit(solution)/shard_map/ppermute | solution.py:86
  43.7 0.3 collective-permute-start.25
  44.0 1.7 %collective-permute-start.24 = (f32[8,128]{1,0:T(8,128)S(1)}, f32[8,128]{1,0:T(8,128)S(1)}, u32[]{:S(2)}, u32[]{:S(2)}) collective-permute-start(f32[8,128]{1,0:T(8,128)S(1)} %get-tuple-element.93.own_ref), channel_id=1, source_target_pairs={{0,8},{1,9},{2,10},{3,11},{4,12},{5,13},{6,14},{7,15},{8,0},{9,1},... | collective-permute-start | bytes 12296 | tf_op jit(solution)/shard_map/ppermute | solution.py:86
  45.7 0.8 %shard_map.117 = (bf16[64,8,128]{2,1,0:T(8,128)(2,1)}, bf16[64,8,128]{2,1,0:T(8,128)(2,1)}) custom-call(bf16[8,64,128]{2,1,0:T(8,128)(2,1)S(1)} %get-tuple-element.62.refs_9_.refs_8_.refs_0_, bf16[8,64,128]{2,1,0:T(8,128)(2,1)S(1)} %get-tuple-element.73.refs_10_.one_ref.refs_1_, bf16[8,64,128]{2,1,0:T(8,128)(2,1)S(1)} %get-tuple-element.83.refs_11_.other_ref.refs_2_, ...), custom_call_target="tpu_custom_call" | custom-call | tf_op jit(solution)/shard_map/pallas_call | solution.py:23
  46.5 0.2 collective-permute-done.23.across_ref
  46.7 0.6 %shard_map.119.ends_ref = f32[4,2,4,128]{3,2,1,0:T(4,128)} custom-call(f32[8,128]{1,0:T(8,128)S(1)} %get-tuple-element.93.own_ref, f32[128,128]{1,0:T(8,128)S(1)} %collective-permute-done.22.refs_5_.beside_ref, f32[2,8,128]{2,1,0:T(8,128)S(1)} %collective-permute-done.23.across_ref, f32[4,4,8,128]{3,2,1,0:T(8,128)S(1)} %get-tuple-element.94.member_ref), custom_call_target="tpu_custom_call" | custom-call | tf_op jit(solution)/shard_map/pallas_call | solution.py:23
  47.4 0.8 %collective-permute-done.25.other_ref = f32[8,128]{1,0:T(8,128)S(1)} collective-permute-done((f32[8,128]{1,0:T(8,128)S(1)}, f32[8,128]{1,0:T(8,128)S(1)}, u32[]{:S(2)}, u32[]{:S(2)}) %collective-permute-start.25) | collective-permute-done | bytes 4128 | tf_op jit(solution)/shard_map/ppermute | solution.py:86
  (31 shorter events, 0.1 us)
Async XLA Ops:
  1.7 3.3 %collective-permute-start.1 = (bf16[2,64,128]{2,1,0:T(8,128)(2,1)S(1)}, bf16[2,64,128]{2,1,0:T(8,128)(2,1)S(1)}, u32[]{:S(2)}, u32[]{:S(2)}) collective-permute-start(bf16[2,64,128]{2,1,0:T(8,128)(2,1)S(1)} %get-tuple-element.55), channel_id=1, source_target_pairs={{0,1},{1,0},{2,3},{3,2},{4,5},{5,4},{6,7},{7,6},{8,9},{9,8},{10,11... | collective-permute-start | bytes 98312 | tf_op jit(solution)/shard_map/ppermute | solution.py:86
  2.4 7.0 %collective-permute-start = (bf16[4,64,128]{2,1,0:T(8,128)(2,1)S(1)}, bf16[4,64,128]{2,1,0:T(8,128)(2,1)S(1)}, u32[]{:S(2)}, u32[]{:S(2)}) collective-permute-start(bf16[4,64,128]{2,1,0:T(8,128)(2,1)S(1)} %get-tuple-element.53), channel_id=1, source_target_pairs={{0,4},{1,5},{2,6},{3,7},{4,0},{5,1},{6,2},{7,3},{8,12},{9,13},{10,... | collective-permute-start | bytes 196616 | tf_op jit(solution)/shard_map/ppermute | solution.py:86
  5.0 4.4 %collective-permute-start.2 = (bf16[2,64,128]{2,1,0:T(8,128)(2,1)S(1)}, bf16[2,64,128]{2,1,0:T(8,128)(2,1)S(1)}, u32[]{:S(2)}, u32[]{:S(2)}) collective-permute-start(bf16[2,64,128]{2,1,0:T(8,128)(2,1)S(1)} %shard_map.97), channel_id=1, source_target_pairs={{0,7},{1,2},{2,1},{3,4},{4,3},{5,6},{6,5},{7,0},{8,15},{9,10},{10,... | collective-permute-start | bytes 98312 | tf_op jit(solution)/shard_map/ppermute | solution.py:86
  9.5 1.3 %collective-permute-start.3 = (bf16[4,64,128]{2,1,0:T(8,128)(2,1)S(1)}, bf16[4,64,128]{2,1,0:T(8,128)(2,1)S(1)}, u32[]{:S(2)}, u32[]{:S(2)}) collective-permute-start(bf16[4,64,128]{2,1,0:T(8,128)(2,1)S(1)} %shard_map.98.refs_4_), channel_id=1, source_target_pairs={{0,1},{1,0},{2,3},{3,2},{4,5},{5,4},{6,7},{7,6},{8,9},{9,8},{10,11... | collective-permute-start | bytes 196616 | tf_op jit(solution)/shard_map/ppermute | solution.py:86
  11.0 8.3 %collective-permute-start.4 = (bf16[8,64,128]{2,1,0:T(8,128)(2,1)S(1)}, bf16[8,64,128]{2,1,0:T(8,128)(2,1)S(1)}, u32[]{:S(2)}, u32[]{:S(2)}) collective-permute-start(bf16[8,64,128]{2,1,0:T(8,128)(2,1)S(1)} %get-tuple-element.62.refs_9_.refs_8_.refs_0_), channel_id=1, source_target_pairs={{0,8},{1,9},{2,10},{3,11},{4,12},{5,13},{6,14},{7,15},{8,0},{9,1},... | collective-permute-start | bytes 393224 | tf_op jit(solution)/shard_map/ppermute | solution.py:86
  12.3 1.3 %collective-permute-start.6 = (bf16[2,64,128]{2,1,0:T(8,128)(2,1)S(1)}, bf16[2,64,128]{2,1,0:T(8,128)(2,1)S(1)}, u32[]{:S(2)}, u32[]{:S(2)}) collective-permute-start(bf16[2,64,128]{2,1,0:T(8,128)(2,1)S(1)} %get-tuple-element.65), channel_id=1, source_target_pairs={{0,1},{1,0},{2,3},{3,2},{4,5},{5,4},{6,7},{7,6},{8,9},{9,8},{10,11... | collective-permute-start | bytes 98312 | tf_op jit(solution)/shard_map/ppermute | solution.py:86
  12.3 7.0 %collective-permute-start.5 = (bf16[4,64,128]{2,1,0:T(8,128)(2,1)S(1)}, bf16[4,64,128]{2,1,0:T(8,128)(2,1)S(1)}, u32[]{:S(2)}, u32[]{:S(2)}) collective-permute-start(bf16[4,64,128]{2,1,0:T(8,128)(2,1)S(1)} %get-tuple-element.63), channel_id=1, source_target_pairs={{0,12},{1,13},{2,14},{3,15},{4,8},{5,9},{6,10},{7,11},{8,4},{9,5},... | collective-permute-start | bytes 196616 | tf_op jit(solution)/shard_map/ppermute | solution.py:86
  13.6 5.7 %collective-permute-start.7 = (bf16[2,64,128]{2,1,0:T(8,128)(2,1)S(1)}, bf16[2,64,128]{2,1,0:T(8,128)(2,1)S(1)}, u32[]{:S(2)}, u32[]{:S(2)}) collective-permute-start(bf16[2,64,128]{2,1,0:T(8,128)(2,1)S(1)} %shard_map.102), channel_id=1, source_target_pairs={{0,15},{1,10},{2,9},{3,12},{4,11},{5,14},{6,13},{7,8},{8,7},{9,2},... | collective-permute-start | bytes 98312 | tf_op jit(solution)/shard_map/ppermute | solution.py:86
  15.7 4.7 %collective-permute-start.9 = (bf16[4,64,128]{2,1,0:T(8,128)(2,1)S(1)}, bf16[4,64,128]{2,1,0:T(8,128)(2,1)S(1)}, u32[]{:S(2)}, u32[]{:S(2)}) collective-permute-start(bf16[4,64,128]{2,1,0:T(8,128)(2,1)S(1)} %get-tuple-element.67), channel_id=1, source_target_pairs={{0,4},{1,5},{2,6},{3,7},{4,0},{5,1},{6,2},{7,3},{8,12},{9,13},{10,... | collective-permute-start | bytes 196616 | tf_op jit(solution)/shard_map/ppermute | solution.py:86
  16.6 4.6 %collective-permute-start.10 = (bf16[4,64,128]{2,1,0:T(8,128)(2,1)S(1)}, bf16[4,64,128]{2,1,0:T(8,128)(2,1)S(1)}, u32[]{:S(2)}, u32[]{:S(2)}) collective-permute-start(bf16[4,64,128]{2,1,0:T(8,128)(2,1)S(1)} %get-tuple-element.68), channel_id=1, source_target_pairs={{0,4},{1,2},{2,1},{3,7},{4,0},{5,6},{6,5},{7,3},{8,12},{9,10},{10,... | collective-permute-start | bytes 196616 | tf_op jit(solution)/shard_map/ppermute | solution.py:86
  19.3 1.8 %collective-permute-start.8 = (bf16[4,64,128]{2,1,0:T(8,128)(2,1)S(1)}, bf16[4,64,128]{2,1,0:T(8,128)(2,1)S(1)}, u32[]{:S(2)}, u32[]{:S(2)}) collective-permute-start(bf16[4,64,128]{2,1,0:T(8,128)(2,1)S(1)} %shard_map.103.refs_7_), channel_id=1, source_target_pairs={{0,1},{1,0},{2,3},{3,2},{4,5},{5,4},{6,7},{7,6},{8,9},{9,8},{10,11... | collective-permute-start | bytes 196616 | tf_op jit(solution)/shard_map/ppermute | solution.py:86
  21.1 2.8 %collective-permute-start.11 = (bf16[8,64,128]{2,1,0:T(8,128)(2,1)S(1)}, bf16[8,64,128]{2,1,0:T(8,128)(2,1)S(1)}, u32[]{:S(2)}, u32[]{:S(2)}) collective-permute-start(bf16[8,64,128]{2,1,0:T(8,128)(2,1)S(1)} %get-tuple-element.73.refs_10_.one_ref.refs_1_), channel_id=1, source_target_pairs={{0,1},{1,0},{2,3},{3,2},{4,5},{5,4},{6,7},{7,6},{8,16},{9,17},{10,... | collective-permute-start | bytes 393224 | tf_op jit(solution)/shard_map/ppermute | solution.py:86
  21.2 1.4 %collective-permute-start.13 = (bf16[2,64,128]{2,1,0:T(8,128)(2,1)S(1)}, bf16[2,64,128]{2,1,0:T(8,128)(2,1)S(1)}, u32[]{:S(2)}, u32[]{:S(2)}) collective-permute-start(bf16[2,64,128]{2,1,0:T(8,128)(2,1)S(1)} %get-tuple-element.76), channel_id=1, source_target_pairs={{0,1},{1,0},{2,3},{3,2},{4,5},{5,4},{6,7},{7,6},{8,9},{9,8},{10,11... | collective-permute-start | bytes 98312 | tf_op jit(solution)/shard_map/ppermute | solution.py:86
  21.7 2.3 %collective-permute-start.12 = (bf16[4,64,128]{2,1,0:T(8,128)(2,1)S(1)}, bf16[4,64,128]{2,1,0:T(8,128)(2,1)S(1)}, u32[]{:S(2)}, u32[]{:S(2)}) collective-permute-start(bf16[4,64,128]{2,1,0:T(8,128)(2,1)S(1)} %get-tuple-element.74), channel_id=1, source_target_pairs={{0,1},{1,0},{2,3},{3,2},{4,5},{5,4},{6,7},{7,6},{8,20},{9,21},{10,... | collective-permute-start | bytes 196616 | tf_op jit(solution)/shard_map/ppermute | solution.py:86
  22.5 1.4 %collective-permute-start.14 = (bf16[2,64,128]{2,1,0:T(8,128)(2,1)S(1)}, bf16[2,64,128]{2,1,0:T(8,128)(2,1)S(1)}, u32[]{:S(2)}, u32[]{:S(2)}) collective-permute-start(bf16[2,64,128]{2,1,0:T(8,128)(2,1)S(1)} %shard_map.107), channel_id=1, source_target_pairs={{0,1},{1,0},{2,3},{3,2},{4,5},{5,4},{6,7},{7,6},{8,23},{9,18},{10,... | collective-permute-start | bytes 98312 | tf_op jit(solution)/shard_map/ppermute | solution.py:86
  22.9 4.3 %collective-permute-start.16 = (bf16[4,64,128]{2,1,0:T(8,128)(2,1)S(1)}, bf16[4,64,128]{2,1,0:T(8,128)(2,1)S(1)}, u32[]{:S(2)}, u32[]{:S(2)}) collective-permute-start(bf16[4,64,128]{2,1,0:T(8,128)(2,1)S(1)} %get-tuple-element.78), channel_id=1, source_target_pairs={{0,4},{1,6},{2,5},{3,7},{4,0},{5,2},{6,1},{7,3},{8,12},{9,14},{10,... | collective-permute-start | bytes 196616 | tf_op jit(solution)/shard_map/ppermute | solution.py:86
  24.0 3.2 %collective-permute-start.15 = (bf16[4,64,128]{2,1,0:T(8,128)(2,1)S(1)}, bf16[4,64,128]{2,1,0:T(8,128)(2,1)S(1)}, u32[]{:S(2)}, u32[]{:S(2)}) collective-permute-start(bf16[4,64,128]{2,1,0:T(8,128)(2,1)S(1)} %shard_map.108.refs_6_), channel_id=1, source_target_pairs={{0,1},{1,0},{2,3},{3,2},{4,5},{5,4},{6,7},{7,6},{8,9},{9,8},{10,11... | collective-permute-start | bytes 196616 | tf_op jit(solution)/shard_map/ppermute | solution.py:86
  27.2 12.5 %collective-permute-start.17 = (bf16[8,64,128]{2,1,0:T(8,128)(2,1)S(1)}, bf16[8,64,128]{2,1,0:T(8,128)(2,1)S(1)}, u32[]{:S(2)}, u32[]{:S(2)}) collective-permute-start(bf16[8,64,128]{2,1,0:T(8,128)(2,1)S(1)} %get-tuple-element.83.refs_11_.other_ref.refs_2_), channel_id=1, source_target_pairs={{0,8},{1,9},{2,10},{3,11},{4,12},{5,13},{6,14},{7,15},{8,0},{9,1},... | collective-permute-start | bytes 393224 | tf_op jit(solution)/shard_map/ppermute | solution.py:86
  33.1 1.2 %collective-permute-start.19 = (bf16[2,64,128]{2,1,0:T(8,128)(2,1)S(1)}, bf16[2,64,128]{2,1,0:T(8,128)(2,1)S(1)}, u32[]{:S(2)}, u32[]{:S(2)}) collective-permute-start(bf16[2,64,128]{2,1,0:T(8,128)(2,1)S(1)} %get-tuple-element.86), channel_id=1, source_target_pairs={{0,1},{1,0},{2,3},{3,2},{4,5},{5,4},{6,7},{7,6},{8,9},{9,8},{10,11... | collective-permute-start | bytes 98312 | tf_op jit(solution)/shard_map/ppermute | solution.py:86
  33.1 6.0 %collective-permute-start.18 = (bf16[4,64,128]{2,1,0:T(8,128)(2,1)S(1)}, bf16[4,64,128]{2,1,0:T(8,128)(2,1)S(1)}, u32[]{:S(2)}, u32[]{:S(2)}) collective-permute-start(bf16[4,64,128]{2,1,0:T(8,128)(2,1)S(1)} %get-tuple-element.84), channel_id=1, source_target_pairs={{0,12},{1,13},{2,14},{3,15},{4,8},{5,9},{6,10},{7,11},{8,4},{9,5},... | collective-permute-start | bytes 196616 | tf_op jit(solution)/shard_map/ppermute | solution.py:86
  34.3 5.4 %collective-permute-start.20 = (bf16[2,64,128]{2,1,0:T(8,128)(2,1)S(1)}, bf16[2,64,128]{2,1,0:T(8,128)(2,1)S(1)}, u32[]{:S(2)}, u32[]{:S(2)}) collective-permute-start(bf16[2,64,128]{2,1,0:T(8,128)(2,1)S(1)} %shard_map.112), channel_id=1, source_target_pairs={{0,15},{1,10},{2,9},{3,12},{4,11},{5,14},{6,13},{7,8},{8,7},{9,2},... | collective-permute-start | bytes 98312 | tf_op jit(solution)/shard_map/ppermute | solution.py:86
  36.0 4.6 %collective-permute-start.22 = (f32[128,128]{1,0:T(8,128)S(1)}, f32[128,128]{1,0:T(8,128)S(1)}, u32[]{:S(2)}, u32[]{:S(2)}) collective-permute-start(f32[128,128]{1,0:T(8,128)S(1)} %shard_map.115), channel_id=1, source_target_pairs={{0,8},{1,9},{2,10},{3,11},{4,12},{5,13},{6,14},{7,15},{8,0},{9,1},... | collective-permute-start | bytes 196616 | tf_op jit(solution)/shard_map/ppermute | solution.py:86
  39.7 1.3 %collective-permute-start.21 = (bf16[4,64,128]{2,1,0:T(8,128)(2,1)S(1)}, bf16[4,64,128]{2,1,0:T(8,128)(2,1)S(1)}, u32[]{:S(2)}, u32[]{:S(2)}) collective-permute-start(bf16[4,64,128]{2,1,0:T(8,128)(2,1)S(1)} %shard_map.113.refs_7_), channel_id=1, source_target_pairs={{0,1},{1,0},{2,3},{3,2},{4,5},{5,4},{6,7},{7,6},{8,9},{9,8},{10,11... | collective-permute-start | bytes 196616 | tf_op jit(solution)/shard_map/ppermute | solution.py:86
  41.2 5.5 %collective-permute-start.23 = (f32[2,8,128]{2,1,0:T(8,128)S(1)}, f32[2,8,128]{2,1,0:T(8,128)S(1)}, u32[]{:S(2)}, u32[]{:S(2)}) collective-permute-start(f32[2,8,128]{2,1,0:T(8,128)S(1)} %shard_map.118), channel_id=1, source_target_pairs={{0,24},{1,25},{2,26},{3,27},{4,28},{5,29},{6,30},{7,31},{8,16},{9,... | collective-permute-start | bytes 24584 | tf_op jit(solution)/shard_map/ppermute | solution.py:86
  43.7 4.5 %collective-permute-start.25 = (f32[8,128]{1,0:T(8,128)S(1)}, f32[8,128]{1,0:T(8,128)S(1)}, u32[]{:S(2)}, u32[]{:S(2)}) collective-permute-start(f32[8,128]{1,0:T(8,128)S(1)} %get-tuple-element.93.own_ref), channel_id=1, source_target_pairs={{0,16},{1,17},{2,18},{3,19},{4,20},{5,21},{6,22},{7,23},{8,24},{9,... | collective-permute-start | bytes 12296 | tf_op jit(solution)/shard_map/ppermute | solution.py:86
  44.0 4.2 %collective-permute-start.24 = (f32[8,128]{1,0:T(8,128)S(1)}, f32[8,128]{1,0:T(8,128)S(1)}, u32[]{:S(2)}, u32[]{:S(2)}) collective-permute-start(f32[8,128]{1,0:T(8,128)S(1)} %get-tuple-element.93.own_ref), channel_id=1, source_target_pairs={{0,8},{1,9},{2,10},{3,11},{4,12},{5,13},{6,14},{7,15},{8,0},{9,1},... | collective-permute-start | bytes 12296 | tf_op jit(solution)/shard_map/ppermute | solution.py:86
